TPU v7x, 32 devices: a whole 2x2x4 slice. The times are simulated.
32 devices in a mesh: cols: 8 (over z, y), rows: 4 (over x, core).
Axes of the slice: x: 2, y: 2, z: 4, core: 2. Of those that a mesh axis runs over, the one named last changes fastest.
Arguments:
- observed: float32 [1024, 8192], P('rows', 'cols'), may hold values from -14 to 14
- class_map: int32 [1024, 8192], P('rows', 'cols'), may hold values from 0 to 3
- class_weights: float32 [4], replicated, may hold values from 0.5 to 8
- blur_kernel: float32 [3, 3], replicated, may hold values from 0.02 to 0.25
Outputs:
- solution: float32 [1024, 8192], P('rows', 'cols')
- residual: float32 [1024, 8192], P('rows', 'cols')
All inputs are finite; a program needn't handle non-finite values.
Results may differ from a plain program's by a relative error of at most 0.0003.
Values sent between devices are 32-bit elements; how exact they have to be, the bound alone decides.
No kernel may reach another device: no remote copies, remote signals or barrier semaphores. Data moves between devices by JAX's collectives and lax.ppermute only.
A program may use at most 128 MiB of HBM per device.

v0:
```python
import jax
import jax.numpy as jnp
from jax import lax
from jax.sharding import PartitionSpec as P

COARSE = 8
SWEEPS = 8
ITERS = 2
CLASSES = 4


OMEGA = 0.8


def padded_2(cells, sides, width):
    for axis, dim in sides:
        count = lax.axis_size(axis)
        ends = count - 1
        head = lax.slice_in_dim(cells, 0, width, axis=dim)
        tail = lax.slice_in_dim(cells, cells.shape[dim] - width, cells.shape[dim], axis=dim)
        cells = jnp.concatenate(
            [
                lax.ppermute(tail, axis, [(i, (i + 1) % count) for i in range(ends)]),
                cells,
                lax.ppermute(head, axis, [((i + 1) % count, i) for i in range(ends)]),
            ],
            axis=dim,
        )
    return cells


def blurred(padded, kernel):
    height = padded.shape[0] - 2
    breadth = padded.shape[1] - 2
    summed = jnp.zeros((height, breadth), jnp.float32)
    for across in range(3):
        for along in range(3):
            summed = (
                summed
                + kernel[across, along] * padded[across : across + height, along : along + breadth]
            )
    return summed


def adjoint(padded, kernel):
    height = padded.shape[0] - 2
    breadth = padded.shape[1] - 2
    summed = jnp.zeros((height, breadth), jnp.float32)
    for across in range(3):
        for along in range(3):
            summed = (
                summed
                + kernel[across, along]
                * padded[2 - across : 2 - across + height, 2 - along : 2 - along + breadth]
            )
    return summed


def edge_weights(cond_pad):
    center = cond_pad[1:-1, 1:-1]
    return (
        0.5 * (center + cond_pad[1:-1, 2:]),
        0.5 * (center + cond_pad[1:-1, :-2]),
        0.5 * (center + cond_pad[:-2, 1:-1]),
        0.5 * (center + cond_pad[2:, 1:-1]),
    )


def laplace(padded, edge_set):
    east, west, north, south = edge_set
    center = padded[1:-1, 1:-1]
    return (
        (east + west + north + south) * center
        - east * padded[1:-1, 2:]
        - west * padded[1:-1, :-2]
        - north * padded[:-2, 1:-1]
        - south * padded[2:, 1:-1]
    )


def coarse_weights(edge_set, kernel):
    east, west, north, south = edge_set
    blocks_down = east.shape[0] // COARSE
    blocks_across = east.shape[1] // COARSE
    c_east = east[:, COARSE - 1 :: COARSE].reshape(blocks_down, COARSE, blocks_across).sum(axis=1)
    c_west = west[:, 0::COARSE].reshape(blocks_down, COARSE, blocks_across).sum(axis=1)
    c_north = north[0::COARSE, :].reshape(blocks_down, blocks_across, COARSE).sum(axis=2)
    c_south = south[COARSE - 1 :: COARSE, :].reshape(blocks_down, blocks_across, COARSE).sum(axis=2)
    c_diag = COARSE * COARSE * jnp.square(jnp.sum(kernel)) + c_east + c_west + c_north + c_south
    return jnp.stack([c_east, c_west, c_north, c_south, c_diag])


def jacobi(source, coarse_table, widen):
    c_east, c_west, c_north, c_south, c_diag = (
        coarse_table[0],
        coarse_table[1],
        coarse_table[2],
        coarse_table[3],
        coarse_table[4],
    )
    iterate = OMEGA * source / c_diag
    for repeat in range(SWEEPS - 1):
        padded = widen(iterate)
        applied = (
            c_diag * iterate
            - c_east * padded[1:-1, 2:]
            - c_west * padded[1:-1, :-2]
            - c_north * padded[:-2, 1:-1]
            - c_south * padded[2:, 1:-1]
        )
        iterate = iterate + OMEGA * (source - applied) / c_diag
    return iterate


def body(observed, class_map, class_weights, blur_kernel):
    rows_here = observed.shape[0]
    cols_here = observed.shape[1]
    conductance = jnp.zeros(observed.shape, jnp.float32)
    for class_id in range(CLASSES):
        conductance = conductance + jnp.where(class_map == class_id, class_weights[class_id], 0.0)
    rim_pair = padded_2(jnp.stack([observed, conductance]), (("cols", 2), ("rows", 1)), 1)
    edge_set = edge_weights(rim_pair[1])
    right_side = adjoint(rim_pair[0], blur_kernel)
    fine_diag = (
        jnp.sum(blur_kernel * blur_kernel) + edge_set[0] + edge_set[1] + edge_set[2] + edge_set[3]
    )
    coarse_table = coarse_weights(edge_set, blur_kernel)
    blocks_down = coarse_table.shape[1]
    blocks_across = coarse_table.shape[2]

    def widen_both(iterate):
        return padded_2(iterate, (("cols", 1), ("rows", 0)), 1)

    def coarse_part(source):
        return jacobi(source, coarse_table, widen_both)

    def precondition(residual):
        source = residual.reshape(blocks_down, COARSE, blocks_across, COARSE).sum(axis=(1, 3))
        coarse = coarse_part(source)
        spread = jnp.broadcast_to(
            coarse[:, None, :, None], (blocks_down, COARSE, blocks_across, COARSE)
        )
        return residual / fine_diag + spread.reshape(rows_here, cols_here)

    solution = jnp.zeros(observed.shape, jnp.float32)
    residual = right_side

    def measure(first, second):
        return lax.psum(jnp.sum(first * second), ("cols", "rows"))

    precond = precondition(residual)
    gamma_now = measure(residual, precond)
    direction = precond
    for iteration in range(ITERS):
        padded = padded_2(direction, (("cols", 1), ("rows", 0)), 1)
        image = blurred(padded, blur_kernel)
        blurred_rim = padded_2(image, (("cols", 1), ("rows", 0)), 1)
        product_field = adjoint(blurred_rim, blur_kernel) + laplace(padded, edge_set)
        step_size = gamma_now / lax.psum(jnp.sum(direction * product_field), ("cols", "rows"))
        solution = solution + step_size * direction
        residual = residual - step_size * product_field
        if iteration + 1 < ITERS:
            precond = precondition(residual)
            gamma_next = measure(residual, precond)
            direction = precond + gamma_next / gamma_now * direction
            gamma_now = gamma_next
    return (solution, residual)


def solution(mesh):
    return jax.shard_map(
        body,
        mesh=mesh,
        in_specs=(P("rows", "cols"), P("rows", "cols"), P(), P()),
        out_specs=(P("rows", "cols"), P("rows", "cols")),
        check_vma=False,
    )
```

profile of v0, /device:TPU:0, one launch (start us, length us, event | category | flops | bytes accessed | tf_op | source)
XLA Modules:
  0.0 667.6 jit_solution(1161200545796063400)
XLA Ops:
  2.1 4.1 add_bitcast_fusion
  7.7 5.5 collective-permute-start
  17.6 5.8 collective-permute-done
  23.3 3.1 concatenate.310
  35.3 5.1 slice.756
  40.6 6.1 slice.757
  54.1 7.4 %fusion.78 = f32[256,1024]{1,0:T(8,128)S(1)} fusion(f32[258,1026]{1,0:T(8,128)S(1)} %get-tuple-element.13, f32[]{:T(128)} %bitcast.15, f32[]{:T(128)} %bitcast.14, f32[]{:T(128)} %bitcast.13, f32[]{:T(128)} %bitcast.12, f32[]{:T(128)} %bitcast.11, f32[]{:T(128)} %bitcast.10, f32[]{:T(128)} %bitcast.9, f32[]{:T(128)} %bitcast.8, f32[]{:T(128)} %bitcast), kind=kLoop, calls=%fused_computation.139 | loop fusion | flops 4456448 | bytes 10485796 | tf_op jit(solution)/shard_map/add | solution.py:52
  61.4 11.3 %reshape.30 = f32[32,8,128,8]{3,2,1,0:T(8,128)} reshape(f32[256,1024]{1,0:T(8,128)S(1)} %fusion.78) | data formatting | bytes 2097152 | tf_op jit(solution)/shard_map/reshape | solution.py:138
  73.7 7.0 %reduce_sum.109 = f32[32,128]{1,0:T(8,128)S(1)} reduce(f32[32,8,128,8]{3,2,1,0:T(8,128)} %reshape.30, f32[]{:T(128)} %constant.1.clone.1), dimensions={1,3}, to_apply=%region_1.2 | reduce | flops 258048 | bytes 1064964 | tf_op jit(solution)/shard_map/reduce_sum | solution.py:138
  80.8 4.4 collective-permute-start.5
  86.6 4.2 collective-permute-done.4
  90.9 2.9 collective-permute-start.6
  95.1 3.3 collective-permute-done.7
  98.5 3.4 collective-permute-start.9
  103.4 4.2 collective-permute-done.8
  114.9 4.3 collective-permute-start.13
  120.6 4.2 collective-permute-done.12
  131.9 3.4 collective-permute-start.17
  136.8 4.2 collective-permute-done.16
  141.1 2.8 collective-permute-start.18
  148.1 4.3 collective-permute-start.21
  153.8 4.2 collective-permute-done.20
  165.1 3.4 collective-permute-start.25
  170.0 4.2 collective-permute-done.24
  185.6 4.2 collective-permute-done.28
  196.8 8.0 %broadcast_in_dim.37 = f32[32,8,128,8]{3,2,1,0:T(8,128)} broadcast(f32[32,128]{1,0:T(8,128)S(1)} %fusion.177), dimensions={0,2} | broadcast | bytes 1064960 | tf_op jit(solution)/shard_map/broadcast_in_dim | solution.py:140
  204.8 13.5 %reshape.35 = f32[256,1024]{1,0:T(8,128)} reshape(f32[32,8,128,8]{3,2,1,0:T(8,128)} %broadcast_in_dim.37) | data formatting | bytes 2097152 | tf_op jit(solution)/shard_map/reshape | solution.py:143
  218.3 11.1 %divide_add_fusion.1 = (f32[256,1024]{1,0:T(8,128)S(1)}, f32[256,1024]{1,0:T(8,128)}) fusion(f32[256,1024]{1,0:T(8,128)} %reshape.35, f32[256,1024]{1,0:T(8,128)} %get-tuple-element.22, f32[256,1024]{1,0:T(8,128)} %copy-done.1, f32[256,1024]{1,0:T(8,128)} %get-tuple-element.21, f32[256,1024]{1,0:T(8,128)S(1)} %get-tuple-element.19, f32[]{:T(128)} %get-tuple-element.4, ...), kind=kLoop, calls=%fused_computation.165 | loop fusion | flops 6029312 | bytes 16777256 | tf_op jit(solution)/shard_map/add | solution.py:143
  230.8 5.2 collective-permute-start.32
  236.3 3.1 collective-permute-done.32
  247.9 11.5 %fusion.53 = f32[256,1024]{1,0:T(8,128)S(1)} fusion(f32[256,1026]{1,0:T(8,128)} %concatenate.347, f32[1,1026]{1,0:T(1,128)S(1)} %collective-permute-done.35, f32[1,1026]{1,0:T(1,128)S(1)} %collective-permute-done.34, f32[256,1024]{1,0:T(8,128)S(1)} %get-tuple-element.11, f32[256,1]{1,0:T(8,128)} %collective-permute-done.32, ...), kind=kLoop, calls=%fused_computation.93 | loop fusion | flops 6553600 | bytes 3158068 | tf_op jit(solution)/shard_map/add | solution.py:39
  261.8 5.5 collective-permute-start.36
  267.7 4.4 collective-permute-done.36
  276.6 3.2 collective-permute-start.39
  280.4 19.3 %multiply_reduce_fusion.2 = (f32[]{:T(128)}, f32[]{:T(128)}, f32[256,1024]{1,0:T(8,128)}) fusion(f32[256,1024]{1,0:T(8,128)S(1)} %get-tuple-element.11, f32[256,1024]{1,0:T(8,128)} %get-tuple-element.22, f32[1,1026]{1,0:T(1,128)S(1)} %collective-permute-done.35, f32[256,1026]{1,0:T(8,128)} %concatenate.347, f32[256,1024]{1,0:T(8,128)} %copy-done.1, ...), kind=kLoop, calls=%fused_computation.162 | loop fusion | flops 16515070 | bytes 18899020 | tf_op jit(solution)/shard_map/reduce_sum | solution.py:159
  299.7 43.2 %all-reduce = (f32[]{:T(128)}, f32[]{:T(128)}) all-reduce(f32[]{:T(128)} %get-tuple-element.3, f32[]{:T(128)} %get-tuple-element.2), channel_id=1, replica_groups=mesh['cols'=8,'rows'=4] {'cols','rows'}, use_global_device_ids=true, to_apply=%region_8.9 | all-reduce | flops 2 | bytes 16 | tf_op jit(solution)/shard_map/psum | solution.py:149
  344.1 8.6 %multiply_subtract_fusion.1 = f32[256,1024]{1,0:T(8,128)S(1)} fusion(f32[256,1024]{1,0:T(8,128)} %get-tuple-element.10, f32[]{:T(128)S(6)} %div.72, f32[258,1026]{1,0:T(8,128)S(1)} %get-tuple-element.13, f32[]{:T(128)} %bitcast.15, f32[]{:T(128)} %bitcast.14, f32[]{:T(128)} %bitcast.13, f32[]{:T(128)} %bitcast.12, f32[]{:T(128)} %bitcast.11, f32[]{:T(128)} %bitcast.10, ...), kind=kLoop, calls=%fused_computation.161 | loop fusion | flops 4980736 | bytes 11534376 | tf_op jit(solution)/shard_map/sub | solution.py:161
  352.7 11.3 %reshape.36 = f32[32,8,128,8]{3,2,1,0:T(8,128)} reshape(f32[256,1024]{1,0:T(8,128)S(1)} %multiply_subtract_fusion.1) | data formatting | bytes 2097152 | tf_op jit(solution)/shard_map/reshape | solution.py:138
  364.0 6.9 %reduce_sum.117 = f32[32,128]{1,0:T(8,128)S(1)} reduce(f32[32,8,128,8]{3,2,1,0:T(8,128)} %reshape.36, f32[]{:T(128)} %constant.1.clone.1), dimensions={1,3}, to_apply=%region_11.12 | reduce | flops 258048 | bytes 1064964 | tf_op jit(solution)/shard_map/reduce_sum | solution.py:138
  371.0 4.4 collective-permute-start.41
  376.8 4.2 collective-permute-done.40
  383.7 3.1 collective-permute-done.43
  387.0 3.7 collective-permute-start.45
  392.0 4.2 collective-permute-done.44
  407.6 4.2 collective-permute-done.48
  418.9 4.0 collective-permute-start.53
  424.3 4.2 collective-permute-done.52
  439.9 4.2 collective-permute-done.56
  444.2 3.0 collective-permute-start.58
  451.2 4.7 collective-permute-start.61
  457.3 4.2 collective-permute-done.60
  468.6 3.2 collective-permute-start.65
  473.2 4.2 collective-permute-done.64
  484.5 8.0 %broadcast_in_dim.38 = f32[32,8,128,8]{3,2,1,0:T(8,128)} broadcast(f32[32,128]{1,0:T(8,128)S(1)} %fusion.93), dimensions={0,2} | broadcast | bytes 1064960 | tf_op jit(solution)/shard_map/broadcast_in_dim | solution.py:140
  492.5 13.6 %reshape.37 = f32[256,1024]{1,0:T(8,128)} reshape(f32[32,8,128,8]{3,2,1,0:T(8,128)} %broadcast_in_dim.38) | data formatting | bytes 2097152 | tf_op jit(solution)/shard_map/reshape | solution.py:143
  508.3 38.6 %psum.30 = f32[]{:T(128)} all-reduce(f32[]{:T(128)} %multiply_reduce_fusion.1), channel_id=1, replica_groups=mesh['cols'=8,'rows'=4] {'cols','rows'}, use_global_device_ids=true, to_apply=%region_13.14 | all-reduce | flops 1 | bytes 8 | tf_op jit(solution)/shard_map/psum | solution.py:149
  551.6 5.1 collective-permute-start.68
  564.8 3.4 collective-permute-done.71
  568.2 11.4 %fusion.22 = f32[256,1024]{1,0:T(8,128)S(1)} fusion(f32[256,1026]{1,0:T(8,128)} %concatenate.392, f32[1,1026]{1,0:T(1,128)S(1)} %collective-permute-done.71, f32[1,1026]{1,0:T(1,128)S(1)} %collective-permute-done.70, f32[256,1024]{1,0:T(8,128)S(1)} %multiply_add_fusion.1, f32[256,1]{1,0:T(8,128)S(1)} %collective-permute-done.68, ...), kind=kLoop, calls=%fused_computation.62 | loop fusion | flops 6553600 | bytes 3158068 | tf_op jit(solution)/shard_map/add | solution.py:39
  582.0 5.7 collective-permute-start.72
  588.1 4.4 collective-permute-done.72
  597.0 3.0 collective-permute-start.75
  600.8 18.0 %multiply_reduce_fusion = (f32[]{:T(128)}, f32[256,1024]{1,0:T(8,128)}) fusion(f32[256,1024]{1,0:T(8,128)S(1)} %multiply_add_fusion.1, f32[256,1024]{1,0:T(8,128)} %get-tuple-element.22, f32[1,1026]{1,0:T(1,128)S(1)} %collective-permute-done.71, f32[256,1026]{1,0:T(8,128)} %concatenate.392, f32[256,1024]{1,0:T(8,128)} %copy-done.1, ...), kind=kLoop, calls=%fused_computation.157 | loop fusion | flops 11534335 | bytes 9461832 | tf_op jit(solution)/shard_map/reduce_sum | solution.py:159
  618.8 44.4 %psum.31 = f32[]{:T(128)} all-reduce(f32[]{:T(128)} %get-tuple-element.8), channel_id=1, replica_groups=mesh['cols'=8,'rows'=4] {'cols','rows'}, use_global_device_ids=true, to_apply=%region_15.16 | all-reduce | flops 1 | bytes 8 | tf_op jit(solution)/shard_map/psum | solution.py:159
  (206 shorter events, 177.5 us)
Async XLA Ops:
  6.4 11.2 %collective-permute-start.1 = (f32[2,256,1]{2,1,0:T(8,128)S(1)}, f32[2,256,1]{2,1,0:T(8,128)S(1)}, u32[]{:S(2)}, u32[]{:S(2)}) collective-permute-start(f32[2,256,1]{2,1,0:T(8,128)S(1)} %get-tuple-element.17), channel_id=1, source_target_pairs={{4,0},{8,4},{12,8},{16,12},{20,16},{24,20},{28,24},{5,1},{9,5},{13... | collective-permute-start | bytes 6152 | tf_op jit(solution)/shard_map/ppermute | solution.py:25
  7.7 15.6 %collective-permute-start = (f32[2,256,1]{2,1,0:T(8,128)S(1)}, f32[2,256,1]{2,1,0:T(8,128)S(1)}, u32[]{:S(2)}, u32[]{:S(2)}) collective-permute-start(f32[2,256,1]{2,1,0:T(8,128)S(1)} %get-tuple-element.18), channel_id=1, source_target_pairs={{0,4},{4,8},{8,12},{12,16},{16,20},{20,24},{24,28},{1,5},{5,9},{9,... | collective-permute-start | bytes 6152 | tf_op jit(solution)/shard_map/ppermute | solution.py:23
  26.4 5.2 collective-permute-start.2
  28.4 4.2 collective-permute-start.3
  80.8 5.8 collective-permute-start.5
  85.2 5.6 collective-permute-start.4
  90.9 4.2 collective-permute-start.6
  93.7 4.6 collective-permute-start.7
  98.5 4.9 collective-permute-start.9
  102.0 5.6 collective-permute-start.8
  107.7 4.3 collective-permute-start.10
  110.5 4.2 collective-permute-start.11
  114.9 5.7 collective-permute-start.13
  119.2 5.6 collective-permute-start.12
  124.9 4.1 collective-permute-start.14
  127.7 4.0 collective-permute-start.15
  131.9 4.9 collective-permute-start.17
  135.4 5.6 collective-permute-start.16
  141.1 4.1 collective-permute-start.18
  143.9 4.0 collective-permute-start.19
  148.1 5.7 collective-permute-start.21
  152.4 5.6 collective-permute-start.20
  158.1 4.1 collective-permute-start.22
  161.0 4.0 collective-permute-start.23
  165.1 4.9 collective-permute-start.25
  168.6 5.6 collective-permute-start.24
  174.3 4.1 collective-permute-start.26
  177.1 4.0 collective-permute-start.27
  181.3 4.2 collective-permute-start.29
  184.1 5.6 collective-permute-start.28
  189.8 4.1 collective-permute-start.30
  192.7 4.0 collective-permute-start.31
  229.5 6.9 %collective-permute-start.33 = (f32[256,1]{1,0:T(8,128)S(1)}, f32[256,1]{1,0:T(8,128)S(1)}, u32[]{:S(2)}, u32[]{:S(2)}) collective-permute-start(f32[256,1]{1,0:T(8,128)S(1)} %get-tuple-element.37), channel_id=1, source_target_pairs={{4,0},{8,4},{12,8},{16,12},{20,16},{24,20},{28,24},{5,1},{9,5},{13... | collective-permute-start | bytes 3080 | tf_op jit(solution)/shard_map/ppermute | solution.py:25
  230.8 8.7 %collective-permute-start.32 = (f32[256,1]{1,0:T(8,128)S(1)}, f32[256,1]{1,0:T(8,128)}, u32[]{:S(2)}, u32[]{:S(2)}) collective-permute-start(f32[256,1]{1,0:T(8,128)S(1)} %get-tuple-element.38), channel_id=1, source_target_pairs={{0,4},{4,8},{8,12},{12,16},{16,20},{20,24},{24,28},{1,5},{5,9},{9,... | collective-permute-start | bytes 3080 | tf_op jit(solution)/shard_map/ppermute | solution.py:23
  260.5 7.3 %collective-permute-start.37 = (f32[256,1]{1,0:T(8,128)S(1)}, f32[256,1]{1,0:T(8,128)}, u32[]{:S(2)}, u32[]{:S(2)}) collective-permute-start(f32[256,1]{1,0:T(8,128)S(1)} %get-tuple-element.35), channel_id=1, source_target_pairs={{4,0},{8,4},{12,8},{16,12},{20,16},{24,20},{28,24},{5,1},{9,5},{13... | collective-permute-start | bytes 3080 | tf_op jit(solution)/shard_map/ppermute | solution.py:25
  261.8 10.4 %collective-permute-start.36 = (f32[256,1]{1,0:T(8,128)S(1)}, f32[256,1]{1,0:T(8,128)}, u32[]{:S(2)}, u32[]{:S(2)}) collective-permute-start(f32[256,1]{1,0:T(8,128)S(1)} %get-tuple-element.36), channel_id=1, source_target_pairs={{0,4},{4,8},{8,12},{12,16},{16,20},{20,24},{24,28},{1,5},{5,9},{9,... | collective-permute-start | bytes 3080 | tf_op jit(solution)/shard_map/ppermute | solution.py:23
  275.3 4.5 collective-permute-start.38
  371.0 5.8 collective-permute-start.41
  375.4 5.6 collective-permute-start.40
  382.4 4.4 collective-permute-start.43
  387.0 5.1 collective-permute-start.45
  390.6 5.6 collective-permute-start.44
  396.3 4.1 collective-permute-start.46
  403.3 4.2 collective-permute-start.49
  406.2 5.6 collective-permute-start.48
  411.9 4.1 collective-permute-start.50
  418.9 5.4 collective-permute-start.53
  422.9 5.6 collective-permute-start.52
  428.6 4.1 collective-permute-start.54
  435.6 4.2 collective-permute-start.57
  438.5 5.6 collective-permute-start.56
  444.2 4.3 collective-permute-start.58
  451.2 6.1 collective-permute-start.61
  455.9 5.6 collective-permute-start.60
  461.6 4.1 collective-permute-start.62
  468.6 4.7 collective-permute-start.65
  471.8 5.6 collective-permute-start.64
  477.5 4.4 collective-permute-start.66
  550.3 7.4 %collective-permute-start.69 = (f32[256,1]{1,0:T(8,128)S(1)}, f32[256,1]{1,0:T(8,128)S(1)}, u32[]{:S(2)}, u32[]{:S(2)}) collective-permute-start(f32[256,1]{1,0:T(8,128)S(1)} %get-tuple-element.33), channel_id=1, source_target_pairs={{4,0},{8,4},{12,8},{16,12},{20,16},{24,20},{28,24},{5,1},{9,5},{13... | collective-permute-start | bytes 3080 | tf_op jit(solution)/shard_map/ppermute | solution.py:25
  551.6 8.4 %collective-permute-start.68 = (f32[256,1]{1,0:T(8,128)S(1)}, f32[256,1]{1,0:T(8,128)S(1)}, u32[]{:S(2)}, u32[]{:S(2)}) collective-permute-start(f32[256,1]{1,0:T(8,128)S(1)} %get-tuple-element.34), channel_id=1, source_target_pairs={{0,4},{4,8},{8,12},{12,16},{16,20},{20,24},{24,28},{1,5},{5,9},{9,... | collective-permute-start | bytes 3080 | tf_op jit(solution)/shard_map/ppermute | solution.py:23
  563.5 4.7 collective-permute-start.71
  580.7 7.4 %collective-permute-start.73 = (f32[256,1]{1,0:T(8,128)S(1)}, f32[256,1]{1,0:T(8,128)}, u32[]{:S(2)}, u32[]{:S(2)}) collective-permute-start(f32[256,1]{1,0:T(8,128)S(1)} %get-tuple-element.31), channel_id=1, source_target_pairs={{4,0},{8,4},{12,8},{16,12},{20,16},{24,20},{28,24},{5,1},{9,5},{13... | collective-permute-start | bytes 3080 | tf_op jit(solution)/shard_map/ppermute | solution.py:25
  582.0 10.6 %collective-permute-start.72 = (f32[256,1]{1,0:T(8,128)S(1)}, f32[256,1]{1,0:T(8,128)}, u32[]{:S(2)}, u32[]{:S(2)}) collective-permute-start(f32[256,1]{1,0:T(8,128)S(1)} %get-tuple-element.32), channel_id=1, source_target_pairs={{0,4},{4,8},{8,12},{12,16},{16,20},{20,24},{24,28},{1,5},{5,9},{9,... | collective-permute-start | bytes 3080 | tf_op jit(solution)/shard_map/ppermute | solution.py:23
  595.7 4.3 collective-permute-start.74
  (21 other events, 347.1 us)
where the time goes:
time: 680 us; the launch traced here: 668 us
  starting transfers between devices  178 us (26%)
  waiting for transfers between devices  131 us (19%)
  blocking collectives  126 us (19%)
  other arithmetic  123 us (18%)
  local copies, waits for them, and re-layouts  102 us (15%)
  between operations  7.12 us (1%)
    ppermute x38, starting transfers between devices, padded_2(): lax.ppermute(tail, axis, [(i, (i + 1) % count) for i in range(ends)])  129 us
    ppermute x38, waiting for transfers between devices, padded_2(): lax.ppermute(head, axis, [((i + 1) % count, i) for i in range(ends)])  108 us
    psum x2, blocking collectives, measure(): return lax.psum(jnp.sum(first * second), ('cols', 'rows'))  81.9 us
    ppermute x38, starting transfers between devices, padded_2(): lax.ppermute(head, axis, [((i + 1) % count, i) for i in range(ends)])  49.5 us
    psum x1, blocking collectives, body(): lax.psum(jnp.sum(direction * product_field), ('cols', 'rows'))  44.4 us
    reduce_sum x2, other arithmetic, body(): jnp.sum(direction * product_field)  37.3 us
    reshape x2, local copies, waits for them, and re-layouts, precondition(): return residual / fine_diag + spread.reshape(rows_here, cols_here)  27 us
    ppermute x38, waiting for transfers between devices, padded_2(): lax.ppermute(tail, axis, [(i, (i + 1) % count) for i in range(ends)])  23.2 us
  transfers between devices with their start and end apart: 76, of which 57 were waited for; matrix products, arithmetic and copies ran while one was open for 0% of the time, Pallas kernels for 0%

commit v1 on v0

v1 whole, which is shorter than its diff:
```python
import functools

import jax
import jax.numpy as jnp
from jax import lax
from jax.experimental import pallas as pl
from jax.experimental.pallas import tpu as pltpu
from jax.sharding import PartitionSpec as P

COARSE = 8
SWEEPS = 8
CLASSES = 4
OMEGA = 0.8

LANES = 128
HALF = LANES // 2
EDGE = 8
STRIP = 2 * EDGE
AXES = ("cols", "rows")
LIMIT = 40 * 1024 * 1024


VMEM = pl.BlockSpec(memory_space=pltpu.VMEM)
SMEM = pl.BlockSpec(memory_space=pltpu.SMEM)
HBM = pl.BlockSpec(memory_space=pltpu.HBM)


def params():
    return pltpu.CompilerParams(vmem_limit_bytes=LIMIT)


def floats(*shapes):
    return [jax.ShapeDtypeStruct(shape, jnp.float32) for shape in shapes]


def place():
    at_col, at_row = lax.axis_index("cols"), lax.axis_index("rows")
    n_cols, n_rows = lax.axis_size("cols"), lax.axis_size("rows")
    return at_col, at_row, n_cols, n_rows


def has_sides():
    at_col, at_row, n_cols, n_rows = place()
    flag = lambda test: jnp.where(test, 1.0, 0.0).astype(jnp.float32)
    return (
        flag(at_row > 0),
        flag(at_row < n_rows - 1),
        flag(at_col < n_cols - 1),
        flag(at_col > 0),
    )


def iota(shape, dim):
    return lax.broadcasted_iota(jnp.int32, shape, dim)


def cell_of(pixel, tiles):
    turn = (tiles + 1) * LANES
    return jnp.where(pixel < turn - HALF, pixel >> 3, ((pixel - turn) >> 3) & (2 * LANES - 1))


def gather_matrix(tiles):
    shape = ((tiles + 1) * LANES, 2 * LANES)
    hit = cell_of(iota(shape, 0), tiles) == iota(shape, 1)
    return jnp.where(hit, 1.0, 0.0).astype(jnp.bfloat16)


def spread_matrix(tiles):
    shape = (2 * LANES, (tiles + 1) * LANES)
    hit = cell_of(iota(shape, 1), tiles) == iota(shape, 0)
    return jnp.where(hit, 1.0, 0.0).astype(jnp.bfloat16)


def split_dot(field, matrix):
    rows = field.shape[0]
    high = field.astype(jnp.bfloat16)
    low = (field - high.astype(jnp.float32)).astype(jnp.bfloat16)
    both = jnp.dot(
        jnp.concatenate([high, low], axis=0), matrix, preferred_element_type=jnp.float32
    )
    return both[:rows] + both[rows:]


def roll(field, by, axis):
    return pltpu.roll(field, by % field.shape[axis], axis)


def load(ref, at, rows=STRIP):
    return [ref[t, pl.ds(at, rows), :] for t in range(ref.shape[0])]


def store(ref, at, strip):
    for t, part in enumerate(strip):
        ref[t, pl.ds(at, part.shape[0]), :] = part


def wide(ref, at, rows):
    return jnp.concatenate(load(ref, at, rows), axis=1)


def from_west(strip):
    lane = iota(strip[0].shape, 1)
    turned = [roll(part, 1, 1) for part in strip]
    return [jnp.where(lane == 0, turned[t - 1], turned[t]) for t in range(len(strip))]


def from_east(strip):
    lane = iota(strip[0].shape, 1)
    turned = [roll(part, -1, 1) for part in strip]
    count = len(strip)
    return [
        jnp.where(lane == LANES - 1, turned[(t + 1) % count], turned[t]) for t in range(count)
    ]


def read_taps(taps):
    return [[taps[a, b] for b in range(3)] for a in range(3)]


def tap_total(taps, power):
    return sum(tap * tap if power == 2 else tap for line in taps for tap in line)


def conv(ref, at, taps, flip):
    if flip:
        taps = [line[::-1] for line in taps[::-1]]
    above, here, below = load(ref, at - 1), load(ref, at), load(ref, at + 1)
    sums = [[], [], []]
    for t in range(len(here)):
        for b in range(3):
            sums[b].append(
                taps[0][b] * above[t] + taps[1][b] * here[t] + taps[2][b] * below[t]
            )
    west, east = from_west(sums[0]), from_east(sums[2])
    return [sums[1][t] + west[t] + east[t] for t in range(len(here))]


def laplace(ref, east_ref, south_ref, at):
    above, here, below = load(ref, at - 1), load(ref, at), load(ref, at + 1)
    east, south, north = load(east_ref, at), load(south_ref, at), load(south_ref, at - 1)
    beside = from_east(here)
    flux = [east[t] * (here[t] - beside[t]) for t in range(len(here))]
    back = from_west(flux)
    return here, [
        flux[t]
        - back[t]
        + south[t] * (here[t] - below[t])
        - north[t] * (above[t] - here[t])
        for t in range(len(here))
    ]


def spread_strip(spread, index):
    top, bottom = load(spread, 2 * index + EDGE - 1, 1), load(spread, 2 * index + EDGE, 1)
    shape = (EDGE, LANES)
    return [
        jnp.concatenate([jnp.broadcast_to(a, shape), jnp.broadcast_to(b, shape)], axis=0)
        for a, b in zip(top, bottom)
    ]


def side_lanes(has_e, has_w):
    return jnp.where(iota((STRIP, LANES), 1) < HALF, has_e, has_w)


def mask_rows(ref, has_n, has_s):
    last = ref.shape[1] - 2 * EDGE
    ref[:, EDGE : 2 * EDGE, :] = ref[:, EDGE : 2 * EDGE, :] * has_n
    ref[:, last : last + EDGE, :] = ref[:, last : last + EDGE, :] * has_s


def clear_pads(*refs):
    for ref in refs:
        empty = jnp.zeros((ref.shape[0], EDGE, LANES), jnp.float32)
        ref[:, :EDGE, :] = empty
        ref[:, ref.shape[1] - EDGE :, :] = empty


def product_sum(one, two, count, keep_top=None, keep_bottom=None):
    total = one[0] * two[0]
    for t in range(1, count):
        total = total + one[t] * two[t]
    top, bottom = total[:EDGE], total[EDGE:]
    if keep_top is not None:
        top, bottom = top * keep_top, bottom * keep_bottom
    return top + bottom


def strip_at(index):
    return pl.multiple_of(EDGE + STRIP * index, EDGE)


def jacobi(source, east, south, factor):
    west = roll(east, 1, 1)
    north = roll(south, 1, 0)
    iterate = factor * source
    for _ in range(SWEEPS - 1):
        around = (
            source
            + east * roll(iterate, -1, 1)
            + west * roll(iterate, 1, 1)
            + south * roll(iterate, -1, 0)
            + north * roll(iterate, 1, 0)
        )
        iterate = (1.0 - OMEGA) * iterate + factor * around
    return iterate


def in_pair_order(at, for_before, for_after):
    even = at % 2 == 0
    return jnp.where(even, for_after, for_before), jnp.where(even, for_before, for_after)


def pack_kernel(
    tiles,
    down,
    obs_in,
    class_in,
    weight_in,
    taps_in,
    obs_ref,
    cond_ref,
    coarse_ref,
    send_a,
    send_b,
    classes,
    weights,
    taps,
    sums,
    message,
    obs_sem,
    class_sem,
    small_sem,
):
    height = down * COARSE
    window = down + 2 * EDGE
    own = pl.ds(2 * EDGE, height)
    small = [
        pltpu.make_async_copy(weight_in, weights, small_sem.at[0]),
        pltpu.make_async_copy(taps_in, taps, small_sem.at[1]),
    ]
    moves = []
    for t in range(tiles):
        lanes = pl.ds(t * LANES, LANES)
        moves.append(
            (
                pltpu.make_async_copy(class_in.at[:, lanes], classes.at[t], class_sem.at[t]),
                pltpu.make_async_copy(
                    obs_in.at[:, lanes], obs_ref.at[t, own, :], obs_sem.at[t]
                ),
            )
        )
    for copy in small:
        copy.start()
    for pair in moves:
        for copy in pair:
            copy.start()
    sums[...] = jnp.zeros_like(sums)
    matrix = gather_matrix(tiles)
    for copy in small:
        copy.wait()
    values = [weights[class_id] for class_id in range(CLASSES)]
    fields = (obs_ref, cond_ref)
    for t in range(tiles):
        for copy in moves[t]:
            copy.wait()
        kind = classes[t]
        level = jnp.where(
            kind < 2,
            jnp.where(kind == 0, values[0], values[1]),
            jnp.where(kind == 2, values[2], values[3]),
        )
        cond_ref[t, own, :] = level
        for which, ref in enumerate(fields):
            picked = [
                ref[t, pl.ds(2 * EDGE + k, down, stride=COARSE), :] for k in range(COARSE)
            ]
            sums[3 * which, t, EDGE : EDGE + down, :] = sum(picked[1:], picked[0])
            sums[3 * which + 1, t, EDGE : EDGE + down, :] = picked[0]
            sums[3 * which + 2, t, EDGE : EDGE + down, :] = picked[-1]

    halves = height // LANES
    for which, ref in enumerate(fields):
        for slot, t, begin in ((0, 0, 0), (1, tiles - 1, LANES - EDGE)):
            turned = jnp.transpose(ref[t, own, :])[begin : begin + EDGE]
            for half in range(halves):
                at = (which * halves + half) * EDGE
                message[slot, at : at + EDGE, :] = turned[:, half * LANES : (half + 1) * LANES]
    taps = read_taps(taps)
    whole = lambda index: wide(sums.at[index], 0, window)
    full, head, tail = whole(0), whole(1), whole(2)
    by_tap = [full - head + roll(head, -1, 0), full, full - tail + roll(tail, 1, 0)]
    across = [sum(taps[a][b] * by_tap[a] for a in range(3)) for b in range(3)]
    source = across[1] + roll(across[0], -1, 1) + roll(across[2], 1, 1)
    full, head, tail = whole(3), whole(4), whole(5)
    last = (iota(full.shape, 1) & (COARSE - 1)) == COARSE - 1
    east = jnp.where(last, 0.5 * (full + roll(full, -1, 1)), 0.0)
    south = 0.5 * (tail + roll(head, -1, 0))
    cells = split_dot(jnp.concatenate([source, east, south], axis=0), matrix)
    source, east, south = cells[:window], cells[window : 2 * window], cells[2 * window :]
    around = east + roll(east, 1, 1) + south + roll(south, 1, 0)
    parts = [source, east, south, around]
    for index, part in enumerate(parts):
        coarse_ref[index] = part
    spare = jnp.zeros((2 * LANES - 4 * window, 2 * LANES), jnp.float32)
    stack = jnp.concatenate(parts + [spare], axis=0)
    left = jnp.transpose(stack[:, :LANES])
    right = jnp.transpose(stack[:, LANES:])
    base = 2 * halves * EDGE
    for slot, pieces in (
        (0, (left[:EDGE], right[LANES - EDGE :])),
        (1, (left[LANES - EDGE :], right[:EDGE])),
    ):
        for index, piece in enumerate(pieces):
            for half in range(2):
                at = base + (2 * index + half) * EDGE
                message[slot, at : at + EDGE, :] = piece[:, half * LANES : (half + 1) * LANES]
    send_a[...], send_b[...] = in_pair_order(place()[0], message[0], message[1])


def pack(observed, class_map, class_weights, taps):
    height, breadth = observed.shape
    tiles, down = breadth // LANES, height // COARSE
    window = down + 2 * EDGE
    field = (tiles + 1, height + 4 * EDGE, LANES)
    strip = ((2 * (height // LANES) + 4) * EDGE, LANES)
    return pl.pallas_call(
        functools.partial(pack_kernel, tiles, down),
        in_specs=[HBM] * 4,
        out_specs=[VMEM] * 5,
        out_shape=floats(field, field, (4, window, 2 * LANES), strip, strip),
        scratch_shapes=[
            pltpu.VMEM((tiles, height, LANES), jnp.int32),
            pltpu.SMEM(class_weights.shape, jnp.float32),
            pltpu.SMEM(taps.shape, jnp.float32),
            pltpu.VMEM((6, tiles + 1, window, LANES), jnp.float32),
            pltpu.VMEM((2,) + strip, jnp.float32),
            pltpu.SemaphoreType.DMA((tiles,)),
            pltpu.SemaphoreType.DMA((tiles,)),
            pltpu.SemaphoreType.DMA((2,)),
        ],
        compiler_params=params(),
        name="pack_east_west",
    )(observed, class_map, class_weights, taps)


def middle_kernel(
    tiles, down, got_a, got_b, coarse_in, obs_ref, cond_ref, side_ref, coarse_ref, send_a, send_b, message
):
    height = down * COARSE
    halves = height // LANES
    at_col, at_row, _, _ = place()
    from_e, from_w = in_pair_order(at_col, got_b[...], got_a[...])
    gap = jnp.zeros((LANES - 2 * EDGE, LANES), jnp.float32)

    def turned(low, high):
        return jnp.transpose(jnp.concatenate([low, gap, high], axis=0))

    for which in range(2):
        for half in range(halves):
            at = (which * halves + half) * EDGE
            side_ref[which, half * LANES : (half + 1) * LANES, :] = turned(
                from_e[at : at + EDGE], from_w[at : at + EDGE]
            )
    base = 2 * halves * EDGE

    def piece(strip, index, half):
        at = base + (2 * index + half) * EDGE
        return strip[at : at + EDGE]

    left = [turned(piece(from_w, 1, half), piece(from_e, 1, half)) for half in range(2)]
    right = [turned(piece(from_e, 0, half), piece(from_w, 0, half)) for half in range(2)]
    left = jnp.concatenate(left, axis=0)
    right = jnp.concatenate(right, axis=0)
    window = down + 2 * EDGE
    for index in range(4):
        rows = slice(index * window, (index + 1) * window)
        coarse_ref[index, :, :LANES] = coarse_in[index, :, :LANES] + left[rows]
        coarse_ref[index, :, LANES:] = coarse_in[index, :, LANES:] + right[rows]
    for slot, side_at, coarse_at in ((0, 0, 0), (1, height - EDGE, window - 2 * EDGE)):
        for which, field in enumerate((obs_ref, cond_ref)):
            for t in range(tiles + 1):
                at = (which * (tiles + 1) + t) * EDGE
                if t < tiles:
                    begin = 2 * EDGE + side_at
                    message[slot, at : at + EDGE, :] = field[t, begin : begin + EDGE, :]
                else:
                    message[slot, at : at + EDGE, :] = side_ref[
                        which, side_at : side_at + EDGE, :
                    ]
        for index in range(4):
            for half in range(2):
                at = 2 * (tiles + 1) * EDGE + (2 * index + half) * 2 * EDGE
                message[slot, at : at + 2 * EDGE, :] = coarse_ref[
                    index, coarse_at : coarse_at + 2 * EDGE, half * LANES : (half + 1) * LANES
                ]
    send_a[...], send_b[...] = in_pair_order(at_row, message[0], message[1])


def middle(got_a, got_b, coarse, obs, cond):
    tiles, height = obs.shape[0] - 1, obs.shape[1] - 4 * EDGE
    down = height // COARSE
    long = (2 * (tiles + 1) * EDGE + 16 * EDGE, LANES)
    return pl.pallas_call(
        functools.partial(middle_kernel, tiles, down),
        in_specs=[VMEM] * 5,
        out_specs=[VMEM] * 4,
        out_shape=floats((2, height, LANES), coarse.shape, long, long),
        scratch_shapes=[pltpu.VMEM((2,) + long, jnp.float32)],
        compiler_params=params(),
        name="pack_north_south",
    )(got_a, got_b, coarse, obs, cond)


def first_kernel(
    tiles,
    down,
    taps,
    obs_in,
    cond_in,
    side_ref,
    got_a,
    got_b,
    coarse_in,
    obs,
    cond,
    res_ref,
    p_ref,
    q_ref,
    east_ref,
    south_ref,
    inv_ref,
    table_ref,
    own_ref,
    chunk_ref,
    dots_ref,
    image,
    spread,
):
    height = down * COARSE
    window = down + 2 * EDGE
    strips = height // STRIP + 1
    at_col, at_row, n_cols, n_rows = place()
    has_n, has_s, has_e, has_w = has_sides()
    from_s, from_n = in_pair_order(at_row, got_b[...], got_a[...])
    clear_pads(obs, cond, p_ref, image, res_ref, q_ref, east_ref, south_ref, inv_ref)
    for which, field in enumerate((obs, cond)):
        field[tiles, 2 * EDGE : 2 * EDGE + height, :] = side_ref[which]
        for t in range(tiles + 1):
            at = (which * (tiles + 1) + t) * EDGE
            field[t, EDGE : 2 * EDGE, :] = from_n[at : at + EDGE]
            field[t, 2 * EDGE + height : 3 * EDGE + height, :] = from_s[at : at + EDGE]

    base = 2 * (tiles + 1) * EDGE

    def joined(index):
        def part(strip):
            at = [base + (2 * index + half) * 2 * EDGE for half in range(2)]
            return jnp.concatenate([strip[a : a + 2 * EDGE] for a in at], axis=1)

        gap = jnp.zeros((window - 4 * EDGE, 2 * LANES), jnp.float32)
        return coarse_in[index] + jnp.concatenate([part(from_n), gap, part(from_s)], axis=0)

    source, east, south, around = [joined(index) for index in range(4)]
    row = iota(source.shape, 0)
    lane = iota(source.shape, 1)
    inside = jnp.where(row < EDGE, has_n, jnp.where(row < window - EDGE, 1.0, has_s))
    inside = inside * jnp.where(
        lane < LANES, 1.0, jnp.where(lane < LANES + HALF, has_e, has_w)
    )
    taps = read_taps(taps)
    total = tap_total(taps, 1)
    factor = inside * OMEGA / (COARSE * COARSE * total * total + around)
    table_ref[0] = east
    table_ref[1] = south
    table_ref[2] = factor
    cells = split_dot(jacobi(source, east, south, factor), spread_matrix(tiles))
    for t in range(tiles + 1):
        spread[t] = cells[:, t * LANES : (t + 1) * LANES]

    squares = tap_total(taps, 2)
    sides = side_lanes(has_e, has_w)

    def keeps(index):
        return jnp.where(index > 0, 1.0, 0.0), jnp.where(index < strips - 1, 1.0, 0.0)

    def start(index, total):
        at = strip_at(index)
        above, here, below = load(cond, at - 1), load(cond, at), load(cond, at + 1)
        right = from_east(here)
        span = range(tiles + 1)
        to_e = [0.5 * (here[t] + right[t]) for t in span]
        to_w = from_west(to_e)
        to_s = [0.5 * (here[t] + below[t]) for t in span]
        inverse = [
            1.0 / (squares + to_e[t] + to_w[t] + to_s[t] + 0.5 * (here[t] + above[t]))
            for t in span
        ]
        inverse[tiles] = inverse[tiles] * sides
        residual = conv(obs, at, taps, True)
        cells = spread_strip(spread, index)
        direction = [residual[t] * inverse[t] + cells[t] for t in span]
        store(east_ref, at, to_e)
        store(south_ref, at, to_s)
        store(inv_ref, at, inverse)
        store(res_ref, at, residual)
        store(p_ref, at, direction)
        return total + product_sum(residual, direction, tiles, *keeps(index))

    def blur(index, _):
        at = strip_at(index)
        blurred = conv(p_ref, at, taps, False)
        blurred[tiles] = blurred[tiles] * sides
        store(image, at, blurred)
        return 0

    def finish(index, total):
        at = strip_at(index)
        here, pulled = laplace(p_ref, east_ref, south_ref, at)
        back = conv(image, at, taps, True)
        product = [back[t] + pulled[t] for t in range(tiles + 1)]
        store(q_ref, at, product)
        return total + product_sum(here, product, tiles, *keeps(index))

    nothing = jnp.zeros((EDGE, LANES), jnp.float32)
    dots_ref[0] = lax.fori_loop(0, strips, start, nothing)
    mask_rows(inv_ref, has_n, has_s)
    mask_rows(p_ref, has_n, has_s)
    lax.fori_loop(0, strips, blur, 0)
    mask_rows(image, has_n, has_s)
    dots_ref[1] = lax.fori_loop(0, strips, finish, nothing)

    shape = (tiles * LANES, LANES)
    matrix = jnp.where(iota(shape, 0) >> 3 == iota(shape, 1), 1.0, 0.0).astype(jnp.bfloat16)
    flat = []
    for t in range(tiles):
        picked = [
            q_ref[t, pl.ds(2 * EDGE + k, down, stride=COARSE), :] for k in range(COARSE)
        ]
        flat.append(sum(picked[1:], picked[0]))
    own = split_dot(jnp.concatenate(flat, axis=1), matrix)
    own_ref[...] = own
    spare = jnp.zeros((LANES - down, LANES), jnp.float32)
    turned = jnp.transpose(jnp.concatenate([own, spare], axis=0))
    chunk_ref[...] = jnp.zeros_like(chunk_ref)
    for down_by in (-1, 0, 1):
        for right_by in (-1, 0, 1):
            if down_by == 0 and right_by == 0:
                continue
            if down_by == 0:
                piece = turned[:EDGE] if right_by < 0 else turned[LANES - EDGE :]
            else:
                piece = own[:EDGE] if down_by < 0 else own[down - EDGE :]
            to_row, to_col = at_row + down_by, at_col + right_by

            @pl.when((to_row >= 0) & (to_row < n_rows) & (to_col >= 0) & (to_col < n_cols))
            def _(piece=piece, to_row=to_row, to_col=to_col):
                chunk_ref[to_col * n_rows + to_row] = piece


def first(taps, obs, cond, side, got_a, got_b, coarse):
    field = obs.shape
    tiles, height = field[0] - 1, field[1] - 4 * EDGE
    down = height // COARSE
    window = down + 2 * EDGE
    count = lax.axis_size("cols") * lax.axis_size("rows")
    shapes = [field] * 8 + [
        (3, window, 2 * LANES),
        (down, LANES),
        (count, EDGE, LANES),
        (2, EDGE, LANES),
    ]
    return pl.pallas_call(
        functools.partial(first_kernel, tiles, down),
        in_specs=[SMEM] + [VMEM] * 6,
        out_specs=[VMEM] * len(shapes),
        out_shape=floats(*shapes),
        input_output_aliases={1: 0, 2: 1},
        scratch_shapes=[
            pltpu.VMEM(field, jnp.float32),
            pltpu.VMEM((tiles + 1, window, LANES), jnp.float32),
        ],
        compiler_params=params(),
        name="first_direction",
    )(taps, obs, cond, side, got_a, got_b, coarse)[2:]


def second_kernel(
    tiles,
    down,
    taps,
    got_ref,
    own_ref,
    table_ref,
    q_ref,
    east_ref,
    south_ref,
    inv_ref,
    dots_in,
    w_ref,
    v_ref,
    out_ref,
    image,
    spread,
):
    height = down * COARSE
    strips = height // STRIP + 1
    has_n, has_s, has_e, has_w = has_sides()
    at_col, at_row, n_cols, n_rows = place()
    me = at_col * n_rows + at_row

    def got(down_by, right_by):
        to_row, to_col = at_row + down_by, at_col + right_by
        there = (to_row >= 0) & (to_row < n_rows) & (to_col >= 0) & (to_col < n_cols)
        return got_ref[jnp.where(there, to_col * n_rows + to_row, me)]

    low = iota((EDGE, LANES), 1) < HALF
    gap = jnp.zeros((LANES - 2 * EDGE, LANES), jnp.float32)
    beside = jnp.transpose(jnp.concatenate([got(0, 1), gap, got(0, -1)], axis=0))[:down]
    source = jnp.concatenate(
        [
            jnp.concatenate([got(-1, 0), jnp.where(low, got(-1, 1), got(-1, -1))], axis=1),
            jnp.concatenate([own_ref[...], beside], axis=1),
            jnp.concatenate([got(1, 0), jnp.where(low, got(1, 1), got(1, -1))], axis=1),
        ],
        axis=0,
    )
    cells = jacobi(source, table_ref[0], table_ref[1], table_ref[2])
    cells = split_dot(cells, spread_matrix(tiles))
    for t in range(tiles + 1):
        spread[t] = cells[:, t * LANES : (t + 1) * LANES]
    clear_pads(w_ref, image, v_ref)
    sides = side_lanes(has_e, has_w)
    taps = read_taps(taps)

    def start(index, _):
        at = strip_at(index)
        field, inverse = load(q_ref, at), load(inv_ref, at)
        cells = spread_strip(spread, index)
        store(w_ref, at, [field[t] * inverse[t] + cells[t] for t in range(tiles + 1)])
        return 0

    def blur(index, _):
        at = strip_at(index)
        blurred = conv(w_ref, at, taps, False)
        blurred[tiles] = blurred[tiles] * sides
        store(image, at, blurred)
        return 0

    def finish(index, totals):
        at = pl.multiple_of(2 * EDGE + STRIP * index, EDGE)
        here, pulled = laplace(w_ref, east_ref, south_ref, at)
        back = conv(image, at, taps, True)
        product = [back[t] + pulled[t] for t in range(tiles + 1)]
        field = load(q_ref, at)
        store(v_ref, at, product)
        return (
            totals[0] + product_sum(field, here, tiles),
            totals[1] + product_sum(here, product, tiles),
        )

    nothing = jnp.zeros((EDGE, LANES), jnp.float32)
    lax.fori_loop(0, strips, start, 0)
    lax.fori_loop(0, strips, blur, 0)
    mask_rows(image, has_n, has_s)
    dot_qw, dot_wv = lax.fori_loop(0, strips - 1, finish, (nothing, nothing))
    line = jnp.zeros((1, LANES), jnp.float32)
    at_lane = iota((1, LANES), 1)
    for index, part in enumerate((dots_in[0], dots_in[1], dot_qw, dot_wv)):
        line = line + jnp.where(at_lane == index, jnp.sum(part), 0.0)
    for index in range(out_ref.shape[0]):
        out_ref[index] = line


def second(taps, got, own, table, q, east, south, inv, dots):
    tiles, height = q.shape[0] - 1, q.shape[1] - 4 * EDGE
    down = height // COARSE
    window = down + 2 * EDGE
    return pl.pallas_call(
        functools.partial(second_kernel, tiles, down),
        in_specs=[SMEM] + [VMEM] * 8,
        out_specs=[VMEM] * 3,
        out_shape=floats(q.shape, q.shape, (got.shape[0], 1, LANES)),
        scratch_shapes=[
            pltpu.VMEM(q.shape, jnp.float32),
            pltpu.VMEM((tiles + 1, window, LANES), jnp.float32),
        ],
        compiler_params=params(),
        name="second_direction",
    )(taps, got, own, table, q, east, south, inv, dots)


def combine_kernel(
    tiles, height, sums_ref, p_ref, w_ref, r_ref, q_ref, v_ref, sol_out, res_out, sol, res, sem
):
    line = sums_ref[0]
    for index in range(1, sums_ref.shape[0]):
        line = line + sums_ref[index]
    lane = iota((1, LANES), 1)
    pick = lambda index: jnp.sum(jnp.where(lane == index, line, 0.0), axis=1, keepdims=True)
    rp, pq, qw, wv = [pick(index) for index in range(4)]
    step = rp / pq
    rp_next = step * step * qw - rp
    ratio = rp_next / rp
    lead = 1.0 + ratio
    curvature = lead * lead * pq - 2.0 * lead * step * qw + step * step * wv
    step_next = rp_next / curvature
    on_p = jnp.broadcast_to(step + step_next * lead, (STRIP, LANES))
    on_w = jnp.broadcast_to(step_next * step, (STRIP, LANES))

    def copies(index):
        rows = pl.ds(pl.multiple_of(index * STRIP, STRIP), STRIP)
        return (
            pltpu.make_async_copy(sol.at[rows, :], sol_out.at[rows, :], sem.at[0, index]),
            pltpu.make_async_copy(res.at[rows, :], res_out.at[rows, :], sem.at[1, index]),
        )

    def work(index, _):
        at = pl.multiple_of(index * STRIP, STRIP)
        p, w, r, q, v = [
            load(ref, at + 2 * EDGE) for ref in (p_ref, w_ref, r_ref, q_ref, v_ref)
        ]
        one = [on_p * p[t] - on_w * w[t] for t in range(tiles)]
        two = [r[t] - on_p * q[t] + on_w * v[t] for t in range(tiles)]
        for t in range(tiles):
            sol[pl.ds(at, STRIP), t * LANES : (t + 1) * LANES] = one[t]
            res[pl.ds(at, STRIP), t * LANES : (t + 1) * LANES] = two[t]
        for copy in copies(index):
            copy.start()
        return 0

    def settle(index, _):
        for copy in copies(index):
            copy.wait()
        return 0

    lax.fori_loop(0, height // STRIP, work, 0)
    lax.fori_loop(0, height // STRIP, settle, 0)


def combine(sums, p, w, r, q, v):
    tiles, height = q.shape[0] - 1, q.shape[1] - 4 * EDGE
    shape = (height, tiles * LANES)
    return pl.pallas_call(
        functools.partial(combine_kernel, tiles, height),
        in_specs=[VMEM] * 6,
        out_specs=[HBM] * 2,
        out_shape=floats(shape, shape),
        scratch_shapes=[
            pltpu.VMEM(shape, jnp.float32),
            pltpu.VMEM(shape, jnp.float32),
            pltpu.SemaphoreType.DMA((2, height // STRIP)),
        ],
        compiler_params=params(),
        name="combine",
    )(sums, p, w, r, q, v)


def exchange(send_a, send_b, axis):
    count = lax.axis_size(axis)

    def pairs(begin):
        return [
            pair for i in range(begin, count - 1, 2) for pair in ((i, i + 1), (i + 1, i))
        ]

    return lax.ppermute(send_a, axis, pairs(0)), lax.ppermute(send_b, axis, pairs(1))


def body(observed, class_map, class_weights, blur_kernel):
    obs, cond, coarse, send_a, send_b = pack(observed, class_map, class_weights, blur_kernel)
    got_a, got_b = exchange(send_a, send_b, "cols")
    side, coarse, send_a, send_b = middle(got_a, got_b, coarse, obs, cond)
    got_a, got_b = exchange(send_a, send_b, "rows")
    r, p, q, east, south, inv, table, own, chunk, dots = first(
        blur_kernel, obs, cond, side, got_a, got_b, coarse
    )
    got = lax.all_to_all(chunk, AXES, 0, 0, tiled=True)
    w, v, line = second(blur_kernel, got, own, table, q, east, south, inv, dots)
    sums = lax.all_to_all(line, AXES, 0, 0, tiled=True)
    return tuple(combine(sums, p, w, r, q, v))


def solution(mesh):
    return jax.shard_map(
        body,
        mesh=mesh,
        in_specs=(P("rows", "cols"), P("rows", "cols"), P(), P()),
        out_specs=(P("rows", "cols"), P("rows", "cols")),
        check_vma=False,
    )
```

time: 680 us -> 63.8 us (0.09); the launches traced: 668 us -> 63.5 us
  starting transfers between devices: 178 us -> 4.42 us
  waiting for transfers between devices: 131 us -> 1.91 us
  other arithmetic: 123 us -> 0 us
  local copies, waits for them, and re-layouts: 102 us -> 3.78 us
  blocking collectives: 126 us -> 31.7 us
  Pallas kernels: 0 us -> 21 us
    ppermute x76 -> x4, starting transfers between devices: 178 us -> 4.42 us  [the longest x2 3.1 us: exchange(): lax.ppermute(send_a, axis, pairs(0))]
    ppermute x76 -> x4, waiting for transfers between devices: 131 us -> 1.91 us  [the longest x2 1.9 us: exchange(): lax.ppermute(send_a, axis, pairs(0))]
    psum x3 -> x0, blocking collectives: 126 us -> none  [the longest x2 81.9 us: measure(): return lax.psum(jnp.sum(first * second), ('cols', 'rows'))]
    reduce_sum x9 -> x0, other arithmetic: 57.5 us -> none  [the longest x2 37.3 us: body(): jnp.sum(direction * product_field)]
    reshape x4 -> x0, local copies, waits for them, and re-layouts: 49.6 us -> none  [the longest x2 27 us: precondition(): return residual / fine_diag + spread.reshape(rows_here, cols_here)]
    add x20 -> x0, other arithmetic: 45.8 us -> none  [the longest x2 22.8 us: blurred(): summed + kernel[across, along] * padded[across:across + height, along:alo...]
    all_to_all x0 -> x2, blocking collectives: none -> 31.7 us  [the longest x1 22.8 us: body(): got = lax.all_to_all(chunk, AXES, 0, 0, tiled=True)]
    slice x31 -> x0, local copies, waits for them, and re-layouts: 22.9 us -> none  [the longest x1 6.1 us: coarse_weights(): west[:, 0::COARSE].reshape(blocks_down, COARSE, blocks_across).sum(axis=1)]
  transfers between devices with their start and end apart: 76 -> 4, of which waited for: 57 -> 2; matrix products, arithmetic and copies ran while one was open for 0% -> 0% of each run, Pallas kernels for 0% -> 0%
where the time goes in v1:
time: 63.8 us; the launch traced here: 63.5 us
  blocking collectives  31.7 us (50%)
  Pallas kernels  21 us (33%)
  starting transfers between devices  4.42 us (7%)
  local copies, waits for them, and re-layouts  3.78 us (6%)
  waiting for transfers between devices  1.91 us (3%)
  between operations  0.7 us (1%)
    all_to_all x1, blocking collectives, body(): got = lax.all_to_all(chunk, AXES, 0, 0, tiled=True)  22.8 us
    pallas_call x1, Pallas kernels, first(): pl.pallas_call(functools.partial(first_kernel, tiles, down), in_specs=[SM...  10.1 us
    all_to_all x1, blocking collectives, body(): sums = lax.all_to_all(line, AXES, 0, 0, tiled=True)  8.93 us
    pallas_call x1, Pallas kernels, second(): pl.pallas_call(functools.partial(second_kernel, tiles, down), in_specs=[S...  6.74 us
    unnamed x10, local copies, waits for them, and re-layouts  3.78 us
    ppermute x2, starting transfers between devices, exchange(): lax.ppermute(send_a, axis, pairs(0))  3.1 us
    pallas_call x1, Pallas kernels, pack(): pl.pallas_call(functools.partial(pack_kernel, tiles, down), in_specs=[HBM...  2.19 us
    ppermute x2, waiting for transfers between devices, exchange(): lax.ppermute(send_a, axis, pairs(0))  1.9 us
  transfers between devices with their start and end apart: 4, of which 2 were waited for; matrix products, arithmetic and copies ran while one was open for 0% of the time, Pallas kernels for 0%

profile of v1, /device:TPU:0, one launch (start us, length us, event | category | flops | bytes accessed | tf_op | source)
XLA Modules:
  0.0 63.5 jit_solution(3233452296313381237)
XLA Ops:
  0.6 0.0 copy-start
  0.6 1.2 %copy-done = f32[256,1024]{1,0:T(8,128)S(1)} copy-done((f32[256,1024]{1,0:T(8,128)S(1)}, f32[256,1024]{1,0:T(8,128)}, u32[]{:S(2)}) %copy-start) | copy-done | bytes 1048600
  1.9 0.0 copy-start.1
  1.9 1.2 %copy-done.1 = s32[256,1024]{1,0:T(8,128)S(1)} copy-done((s32[256,1024]{1,0:T(8,128)S(1)}, s32[256,1024]{1,0:T(8,128)}, u32[]{:S(2)}) %copy-start.1) | copy-done | bytes 1048600
  3.1 0.0 copy-start.2
  3.1 0.7 %copy-done.2 = f32[3,3]{1,0:T(4,128)S(1)} copy-done((f32[3,3]{1,0:T(4,128)S(1)}, f32[3,3]{1,0:T(4,128)}, u32[]{:S(2)}) %copy-start.2) | copy-done | bytes 60
  3.8 0.0 copy-start.4
  3.8 0.7 %copy-done.4 = f32[4]{0:T(128)S(1)} copy-done((f32[4]{0:T(128)S(1)}, f32[4]{0:T(128)}, u32[]{:S(2)}) %copy-start.4) | copy-done | bytes 40
  4.4 2.2 %pack_east_west.1 = (f32[9,288,128]{2,1,0:T(8,128)S(1)}, f32[9,288,128]{2,1,0:T(8,128)S(1)}, f32[4,48,256]{2,1,0:T(8,128)S(1)}, f32[64,128]{1,0:T(8,128)S(1)}, f32[64,128]{1,0:T(8,128)S(1)}) custom-call(f32[256,1024]{1,0:T(8,128)S(1)} %copy-done, s32[256,1024]{1,0:T(8,128)S(1)} %copy-done.1, f32[4]{0:T(128)S(1)} %copy-done.4, f32[3,3]{1,0:T(4,128)S(1)} %copy-done.2), custom_call_target="tpu_custom_call" | custom-call | tf_op jit(solution)/shard_map/pack_east_west/pallas_call | solution.py:327
  6.6 3.0 %collective-permute-start = (f32[64,128]{1,0:T(8,128)S(1)}, f32[64,128]{1,0:T(8,128)S(1)}, u32[]{:S(2)}, u32[]{:S(2)}) collective-permute-start(f32[64,128]{1,0:T(8,128)S(1)} %get-tuple-element.26), channel_id=1, source_target_pairs={{0,4},{4,0},{8,12},{12,8},{16,20},{20,16},{24,28},{28,24},{1,5},{5... | collective-permute-start | bytes 98312 | tf_op jit(solution)/shard_map/ppermute | solution.py:767
  9.6 0.7 %collective-permute-start.1 = (f32[64,128]{1,0:T(8,128)S(1)}, f32[64,128]{1,0:T(8,128)S(1)}, u32[]{:S(2)}, u32[]{:S(2)}) collective-permute-start(f32[64,128]{1,0:T(8,128)S(1)} %get-tuple-element.27), channel_id=1, source_target_pairs={{4,8},{8,4},{12,16},{16,12},{20,24},{24,20},{5,9},{9,5},{13,17},{1... | collective-permute-start | bytes 98312 | tf_op jit(solution)/shard_map/ppermute | solution.py:767
  10.3 1.2 %collective-permute-done.got_a = f32[64,128]{1,0:T(8,128)S(1)} collective-permute-done((f32[64,128]{1,0:T(8,128)S(1)}, f32[64,128]{1,0:T(8,128)S(1)}, u32[]{:S(2)}, u32[]{:S(2)}) %collective-permute-start) | collective-permute-done | bytes 32800 | tf_op jit(solution)/shard_map/ppermute | solution.py:767
  11.5 0.0 collective-permute-done.1.got_b
  11.5 0.0 copy-start.3
  11.5 0.2 pack_north_south.1
  11.8 0.1 collective-permute-start.2
  11.8 0.7 %collective-permute-start.3 = (f32[272,128]{1,0:T(8,128)S(1)}, f32[272,128]{1,0:T(8,128)S(1)}, u32[]{:S(2)}, u32[]{:S(2)}) collective-permute-start(f32[272,128]{1,0:T(8,128)S(1)} %get-tuple-element.31), channel_id=1, source_target_pairs={{1,2},{2,1},{5,6},{6,5},{9,10},{10,9},{13,14},{14,13},{17,18},{18,... | collective-permute-start | bytes 417800 | tf_op jit(solution)/shard_map/ppermute | solution.py:767
  12.5 0.7 %collective-permute-done.2.got_a = f32[272,128]{1,0:T(8,128)S(1)} collective-permute-done((f32[272,128]{1,0:T(8,128)S(1)}, f32[272,128]{1,0:T(8,128)S(1)}, u32[]{:S(2)}, u32[]{:S(2)}) %collective-permute-start.2) | collective-permute-done | bytes 139296 | tf_op jit(solution)/shard_map/ppermute | solution.py:767
  13.2 0.0 collective-permute-done.3.got_b
  13.2 0.0 copy-done.3
  13.2 10.1 %first_direction.1 = (f32[9,288,128]{2,1,0:T(8,128)S(1)}, f32[9,288,128]{2,1,0:T(8,128)S(1)}, f32[9,288,128]{2,1,0:T(8,128)S(1)}, f32[9,288,128]{2,1,0:T(8,128)S...) custom-call(f32[3,3]{1,0:T(4,128)S(1)} %copy-done.3, ...), custom_call_target="tpu_custom_call", output_to_operand_aliasing={{0}: (1, {}), {1}: (2, {})} | custom-call | tf_op jit(solution)/shard_map/first_direction/pallas_call | solution.py:573
  23.3 22.8 %all_to_all.10.got_ref = f32[32,8,128]{2,1,0:T(8,128)S(1)} all-to-all(f32[32,8,128]{2,1,0:T(8,128)S(1)} %get-tuple-element.33), channel_id=1, replica_groups=mesh['cols'=8,'rows'=4] {'cols','rows'}, dimensions={0} | all-to-all | bytes 262144 | tf_op jit(solution)/shard_map/all_to_all | solution.py:778
  46.1 6.7 %second_direction.1 = (f32[9,288,128]{2,1,0:T(8,128)S(1)}, f32[9,288,128]{2,1,0:T(8,128)S(1)}, f32[32,1,128]{2,1,0:T(1,128)S(1)}) custom-call(f32[3,3]{1,0:T(4,128)S(1)} %copy-done.3, f32[32,8,128]{2,1,0:T(8,128)S(1)} %all_to_all.10.got_ref, f32[32,128]{1,0:T(8,128)S(1)} %get-tuple-element.34.own_ref, f32[3,48,256]{2,1,0:T(8,128)S(1)} %get-tuple-element.35.table_ref, ...), custom_call_target="tpu_custom_call" | custom-call | tf_op jit(solution)/shard_map/second_direction/pallas_call | solution.py:679
  52.9 8.9 %all_to_all.11.sums_ref = f32[32,1,128]{2,1,0:T(1,128)S(1)} all-to-all(f32[32,1,128]{2,1,0:T(1,128)S(1)} %get-tuple-element.41), channel_id=1, replica_groups=mesh['cols'=8,'rows'=4] {'cols','rows'}, dimensions={0} | all-to-all | bytes 32768 | tf_op jit(solution)/shard_map/all_to_all | solution.py:780
  61.8 1.7 %combine.1 = (f32[256,1024]{1,0:T(8,128)}, f32[256,1024]{1,0:T(8,128)}) custom-call(f32[32,1,128]{2,1,0:T(1,128)S(1)} %all_to_all.11.sums_ref, f32[9,288,128]{2,1,0:T(8,128)S(1)} %get-tuple-element.42.p_ref, f32[9,288,128]{2,1,0:T(8,128)S(1)} %get-tuple-element.43.w_ref, f32[9,288,128]{2,1,0:T(8,128)S(1)} %get-tuple-element.44.r_ref, ...), custom_call_target="tpu_custom_call" | custom-call | tf_op jit(solution)/shard_map/combine/pallas_call | solution.py:744
Async XLA Ops:
  0.6 1.2 %copy-start = (f32[256,1024]{1,0:T(8,128)S(1)}, f32[256,1024]{1,0:T(8,128)}, u32[]{:S(2)}) copy-start(f32[256,1024]{1,0:T(8,128)} %obs_in.1) | copy-start | bytes 3145732
  1.9 1.2 %copy-start.1 = (s32[256,1024]{1,0:T(8,128)S(1)}, s32[256,1024]{1,0:T(8,128)}, u32[]{:S(2)}) copy-start(s32[256,1024]{1,0:T(8,128)} %class_in.1) | copy-start | bytes 3145732
  3.1 0.7 %copy-start.2 = (f32[3,3]{1,0:T(4,128)S(1)}, f32[3,3]{1,0:T(4,128)}, u32[]{:S(2)}) copy-start(f32[3,3]{1,0:T(4,128)} %taps.3) | copy-start | bytes 112
  3.8 0.7 %copy-start.4 = (f32[4]{0:T(128)S(1)}, f32[4]{0:T(128)}, u32[]{:S(2)}) copy-start(f32[4]{0:T(128)} %weight_in.1) | copy-start | bytes 52
  6.6 4.9 %collective-permute-start = (f32[64,128]{1,0:T(8,128)S(1)}, f32[64,128]{1,0:T(8,128)S(1)}, u32[]{:S(2)}, u32[]{:S(2)}) collective-permute-start(f32[64,128]{1,0:T(8,128)S(1)} %get-tuple-element.26), channel_id=1, source_target_pairs={{0,4},{4,0},{8,12},{12,8},{16,20},{20,16},{24,28},{28,24},{1,5},{5... | collective-permute-start | bytes 98312 | tf_op jit(solution)/shard_map/ppermute | solution.py:767
  9.6 1.9 %collective-permute-start.1 = (f32[64,128]{1,0:T(8,128)S(1)}, f32[64,128]{1,0:T(8,128)S(1)}, u32[]{:S(2)}, u32[]{:S(2)}) collective-permute-start(f32[64,128]{1,0:T(8,128)S(1)} %get-tuple-element.27), channel_id=1, source_target_pairs={{4,8},{8,4},{12,16},{16,12},{20,24},{24,20},{5,9},{9,5},{13,17},{1... | collective-permute-start | bytes 98312 | tf_op jit(solution)/shard_map/ppermute | solution.py:767
  11.5 1.7 %copy-start.3 = (f32[3,3]{1,0:T(4,128)S(1)}, f32[3,3]{1,0:T(4,128)}, u32[]{:S(2)}) copy-start(f32[3,3]{1,0:T(4,128)} %taps.3) | copy-start | bytes 112
  11.8 1.4 %collective-permute-start.2 = (f32[272,128]{1,0:T(8,128)S(1)}, f32[272,128]{1,0:T(8,128)S(1)}, u32[]{:S(2)}, u32[]{:S(2)}) collective-permute-start(f32[272,128]{1,0:T(8,128)S(1)} %get-tuple-element.30), channel_id=1, source_target_pairs={{0,1},{1,0},{2,3},{3,2},{4,5},{5,4},{6,7},{7,6},{8,9},{9,8},{10,11... | collective-permute-start | bytes 417800 | tf_op jit(solution)/shard_map/ppermute | solution.py:767
  11.8 1.3 %collective-permute-start.3 = (f32[272,128]{1,0:T(8,128)S(1)}, f32[272,128]{1,0:T(8,128)S(1)}, u32[]{:S(2)}, u32[]{:S(2)}) collective-permute-start(f32[272,128]{1,0:T(8,128)S(1)} %get-tuple-element.31), channel_id=1, source_target_pairs={{1,2},{2,1},{5,6},{6,5},{9,10},{10,9},{13,14},{14,13},{17,18},{18,... | collective-permute-start | bytes 417800 | tf_op jit(solution)/shard_map/ppermute | solution.py:767

commit v2 on v1

--- a/solution.py
+++ b/solution.py
@@ -27,6 +27,10 @@
 
 def params():
     return pltpu.CompilerParams(vmem_limit_bytes=LIMIT)
+
+
+def in_hbm(array):
+    return pltpu.with_memory_space_constraint(array, pltpu.HBM)
 
 
 def floats(*shapes):
@@ -121,7 +125,7 @@
     return sum(tap * tap if power == 2 else tap for line in taps for tap in line)
 
 
-def conv(ref, at, taps, flip):
+def tap_sums(ref, at, taps, flip):
     if flip:
         taps = [line[::-1] for line in taps[::-1]]
     above, here, below = load(ref, at - 1), load(ref, at), load(ref, at + 1)
@@ -131,23 +135,48 @@
             sums[b].append(
                 taps[0][b] * above[t] + taps[1][b] * here[t] + taps[2][b] * below[t]
             )
+    return sums
+
+
+def conv(ref, at, taps, flip):
+    sums = tap_sums(ref, at, taps, flip)
     west, east = from_west(sums[0]), from_east(sums[2])
-    return [sums[1][t] + west[t] + east[t] for t in range(len(here))]
-
-
-def laplace(ref, east_ref, south_ref, at):
+    return [sums[1][t] + west[t] + east[t] for t in range(len(west))]
+
+
+def operate(ref, image, east_ref, south_ref, at, taps):
     above, here, below = load(ref, at - 1), load(ref, at), load(ref, at + 1)
     east, south, north = load(east_ref, at), load(south_ref, at), load(south_ref, at - 1)
+    sums = tap_sums(image, at, taps, True)
+    span = range(len(here))
     beside = from_east(here)
-    flux = [east[t] * (here[t] - beside[t]) for t in range(len(here))]
-    back = from_west(flux)
+    flux = [east[t] * (here[t] - beside[t]) for t in span]
+    from_left = from_west([sums[0][t] - flux[t] for t in span])
+    from_right = from_east(sums[2])
     return here, [
-        flux[t]
-        - back[t]
+        sums[1][t]
+        + flux[t]
+        + from_left[t]
+        + from_right[t]
         + south[t] * (here[t] - below[t])
         - north[t] * (above[t] - here[t])
-        for t in range(len(here))
+        for t in span
     ]
+
+
+def begin(obs, cond, at, taps, sides):
+    above, here, below = load(cond, at - 1), load(cond, at), load(cond, at + 1)
+    span = range(len(here))
+    right = from_east(here)
+    east = [here[t] + right[t] for t in span]
+    west = from_west(east)
+    south = [here[t] + below[t] for t in span]
+    squares = tap_total(taps, 2)
+    inverse = [
+        1.0 / (squares + east[t] + west[t] + south[t] + (here[t] + above[t])) for t in span
+    ]
+    inverse[-1] = inverse[-1] * sides
+    return east, south, inverse, conv(obs, at, taps, True)
 
 
 def spread_strip(spread, index):
@@ -186,23 +215,34 @@
     return top + bottom
 
 
+def sweep(count, group, body, carry):
+    def some(first_index, width, carry):
+        stores = []
+        for offset in range(width):
+            more, carry = body(first_index + offset, carry)
+            stores += more
+        for ref, at, strip in stores:
+            store(ref, at, strip)
+        return carry
+
+    steps = count // group
+    carry = lax.fori_loop(0, steps, lambda step, c: some(step * group, group, c), carry)
+    left = count - steps * group
+    return some(steps * group, left, carry) if left else carry
+
+
 def strip_at(index):
     return pl.multiple_of(EDGE + STRIP * index, EDGE)
 
 
-def jacobi(source, east, south, factor):
-    west = roll(east, 1, 1)
-    north = roll(south, 1, 0)
-    iterate = factor * source
+def jacobi(source, table):
+    factor, east, west, south, north = table
+    source = factor * source
+    iterate = source
     for _ in range(SWEEPS - 1):
-        around = (
-            source
-            + east * roll(iterate, -1, 1)
-            + west * roll(iterate, 1, 1)
-            + south * roll(iterate, -1, 0)
-            + north * roll(iterate, 1, 0)
-        )
-        iterate = (1.0 - OMEGA) * iterate + factor * around
+        across = east * roll(iterate, -1, 1) + west * roll(iterate, 1, 1)
+        along = south * roll(iterate, -1, 0) + north * roll(iterate, 1, 0)
+        iterate = ((1.0 - OMEGA) * iterate + source) + (across + along)
     return iterate
 
 
@@ -211,42 +251,22 @@
     return jnp.where(even, for_after, for_before), jnp.where(even, for_before, for_after)
 
 
-def pack_kernel(
-    tiles,
-    down,
-    obs_in,
-    class_in,
-    weight_in,
-    taps_in,
-    obs_ref,
-    cond_ref,
-    coarse_ref,
-    send_a,
-    send_b,
-    classes,
-    weights,
-    taps,
-    sums,
-    message,
-    obs_sem,
-    class_sem,
-    small_sem,
-):
-    height = down * COARSE
-    window = down + 2 * EDGE
-    own = pl.ds(2 * EDGE, height)
+def reader(tiles_here, refs, scratch, obs, cond, down):
+    obs_in, class_in, weight_in, taps_in = refs
+    classes, weights, taps, sums, obs_sem, class_sem, small_sem = scratch
+    own = pl.ds(2 * EDGE, down * COARSE)
     small = [
         pltpu.make_async_copy(weight_in, weights, small_sem.at[0]),
         pltpu.make_async_copy(taps_in, taps, small_sem.at[1]),
     ]
     moves = []
-    for t in range(tiles):
+    for slot, t in enumerate(tiles_here):
         lanes = pl.ds(t * LANES, LANES)
         moves.append(
             (
-                pltpu.make_async_copy(class_in.at[:, lanes], classes.at[t], class_sem.at[t]),
+                pltpu.make_async_copy(class_in.at[:, lanes], classes.at[slot], class_sem.at[slot]),
                 pltpu.make_async_copy(
-                    obs_in.at[:, lanes], obs_ref.at[t, own, :], obs_sem.at[t]
+                    obs_in.at[:, lanes], obs.at[slot, own, :], obs_sem.at[slot]
                 ),
             )
         )
@@ -256,37 +276,45 @@
         for copy in pair:
             copy.start()
     sums[...] = jnp.zeros_like(sums)
-    matrix = gather_matrix(tiles)
-    for copy in small:
-        copy.wait()
-    values = [weights[class_id] for class_id in range(CLASSES)]
-    fields = (obs_ref, cond_ref)
-    for t in range(tiles):
-        for copy in moves[t]:
+
+    def settle(slot):
+        if slot == 0:
+            for copy in small:
+                copy.wait()
+        for copy in moves[slot]:
             copy.wait()
-        kind = classes[t]
-        level = jnp.where(
+        values = [0.5 * weights[class_id] for class_id in range(CLASSES)]
+        kind = classes[slot]
+        cond[slot, own, :] = jnp.where(
             kind < 2,
             jnp.where(kind == 0, values[0], values[1]),
             jnp.where(kind == 2, values[2], values[3]),
         )
-        cond_ref[t, own, :] = level
-        for which, ref in enumerate(fields):
+        for which, ref in enumerate((obs, cond)):
             picked = [
-                ref[t, pl.ds(2 * EDGE + k, down, stride=COARSE), :] for k in range(COARSE)
+                ref[slot, pl.ds(2 * EDGE + k, down, stride=COARSE), :] for k in range(COARSE)
             ]
-            sums[3 * which, t, EDGE : EDGE + down, :] = sum(picked[1:], picked[0])
-            sums[3 * which + 1, t, EDGE : EDGE + down, :] = picked[0]
-            sums[3 * which + 2, t, EDGE : EDGE + down, :] = picked[-1]
-
-    halves = height // LANES
-    for which, ref in enumerate(fields):
-        for slot, t, begin in ((0, 0, 0), (1, tiles - 1, LANES - EDGE)):
-            turned = jnp.transpose(ref[t, own, :])[begin : begin + EDGE]
-            for half in range(halves):
-                at = (which * halves + half) * EDGE
-                message[slot, at : at + EDGE, :] = turned[:, half * LANES : (half + 1) * LANES]
-    taps = read_taps(taps)
+            sums[3 * which, slot, EDGE : EDGE + down, :] = sum(picked[1:], picked[0])
+            sums[3 * which + 1, slot, EDGE : EDGE + down, :] = picked[0]
+            sums[3 * which + 2, slot, EDGE : EDGE + down, :] = picked[-1]
+
+    return settle
+
+
+def reader_scratch(tiles, height, window, class_weights, taps):
+    return [
+        pltpu.VMEM((tiles, height, LANES), jnp.int32),
+        pltpu.SMEM(class_weights.shape, jnp.float32),
+        pltpu.SMEM(taps.shape, jnp.float32),
+        pltpu.VMEM((6, tiles + 1, window, LANES), jnp.float32),
+        pltpu.SemaphoreType.DMA((tiles,)),
+        pltpu.SemaphoreType.DMA((tiles,)),
+        pltpu.SemaphoreType.DMA((2,)),
+    ]
+
+
+def coarse_parts(sums, taps, matrix):
+    window = sums.shape[2]
     whole = lambda index: wide(sums.at[index], 0, window)
     full, head, tail = whole(0), whole(1), whole(2)
     by_tap = [full - head + roll(head, -1, 0), full, full - tail + roll(tail, 1, 0)]
@@ -294,22 +322,39 @@
     source = across[1] + roll(across[0], -1, 1) + roll(across[2], 1, 1)
     full, head, tail = whole(3), whole(4), whole(5)
     last = (iota(full.shape, 1) & (COARSE - 1)) == COARSE - 1
-    east = jnp.where(last, 0.5 * (full + roll(full, -1, 1)), 0.0)
-    south = 0.5 * (tail + roll(head, -1, 0))
+    east = jnp.where(last, full + roll(full, -1, 1), 0.0)
+    south = tail + roll(head, -1, 0)
     cells = split_dot(jnp.concatenate([source, east, south], axis=0), matrix)
     source, east, south = cells[:window], cells[window : 2 * window], cells[2 * window :]
     around = east + roll(east, 1, 1) + south + roll(south, 1, 0)
-    parts = [source, east, south, around]
-    for index, part in enumerate(parts):
-        coarse_ref[index] = part
+    return [source, east, south, around]
+
+
+def edge_kernel(tiles, down, *refs):
+    arguments, (send_a, send_b), (obs, cond, message, *scratch) = refs[:4], refs[4:6], refs[6:]
+    height = down * COARSE
+    halves = height // LANES
+    window = down + 2 * EDGE
+    settle = reader((0, tiles - 1), arguments, scratch, obs, cond, down)
+    matrix = gather_matrix(2)
+    for slot, begin_row in ((0, 0), (1, LANES - EDGE)):
+        settle(slot)
+        for which, ref in enumerate((obs, cond)):
+            turned = jnp.transpose(ref[slot, 2 * EDGE : 2 * EDGE + height, :])
+            turned = turned[begin_row : begin_row + EDGE]
+            for half in range(halves):
+                at = (which * halves + half) * EDGE
+                message[slot, at : at + EDGE, :] = turned[:, half * LANES : (half + 1) * LANES]
+    parts = coarse_parts(scratch[3], read_taps(scratch[2]), matrix)
     spare = jnp.zeros((2 * LANES - 4 * window, 2 * LANES), jnp.float32)
     stack = jnp.concatenate(parts + [spare], axis=0)
     left = jnp.transpose(stack[:, :LANES])
     right = jnp.transpose(stack[:, LANES:])
     base = 2 * halves * EDGE
+    past = 2 * LANES // COARSE
     for slot, pieces in (
         (0, (left[:EDGE], right[LANES - EDGE :])),
-        (1, (left[LANES - EDGE :], right[:EDGE])),
+        (1, (left[past - EDGE : past], left[past : past + EDGE])),
     ):
         for index, piece in enumerate(pieces):
             for half in range(2):
@@ -318,34 +363,72 @@
     send_a[...], send_b[...] = in_pair_order(place()[0], message[0], message[1])
 
 
-def pack(observed, class_map, class_weights, taps):
+def edge(observed, class_map, class_weights, taps):
+    height, breadth = observed.shape
+    tiles, down = breadth // LANES, height // COARSE
+    window = down + 2 * EDGE
+    field = (3, height + 4 * EDGE, LANES)
+    strip = ((2 * (height // LANES) + 4) * EDGE, LANES)
+    return pl.pallas_call(
+        functools.partial(edge_kernel, tiles, down),
+        in_specs=[HBM] * 4,
+        out_specs=[VMEM] * 2,
+        out_shape=floats(strip, strip),
+        scratch_shapes=[
+            pltpu.VMEM(field, jnp.float32),
+            pltpu.VMEM(field, jnp.float32),
+            pltpu.VMEM((2,) + strip, jnp.float32),
+        ]
+        + reader_scratch(2, height, window, class_weights, taps),
+        compiler_params=params(),
+        name="pack_east_west",
+    )(*[in_hbm(array) for array in (observed, class_map, class_weights, taps)])
+
+
+def pack_kernel(tiles, down, *refs):
+    arguments, (obs, cond, coarse_ref), scratch = refs[:4], refs[5:8], refs[8:]
+    settle = reader(range(tiles), arguments, scratch, obs, cond, down)
+    matrix = gather_matrix(tiles)
+    for t in range(tiles):
+        settle(t)
+    for index, part in enumerate(coarse_parts(scratch[3], read_taps(scratch[2]), matrix)):
+        coarse_ref[index] = part
+
+
+def pack(observed, class_map, class_weights, taps, after):
     height, breadth = observed.shape
     tiles, down = breadth // LANES, height // COARSE
     window = down + 2 * EDGE
     field = (tiles + 1, height + 4 * EDGE, LANES)
-    strip = ((2 * (height // LANES) + 4) * EDGE, LANES)
+    pixels = height * breadth
     return pl.pallas_call(
         functools.partial(pack_kernel, tiles, down),
-        in_specs=[HBM] * 4,
-        out_specs=[VMEM] * 5,
-        out_shape=floats(field, field, (4, window, 2 * LANES), strip, strip),
-        scratch_shapes=[
-            pltpu.VMEM((tiles, height, LANES), jnp.int32),
-            pltpu.SMEM(class_weights.shape, jnp.float32),
-            pltpu.SMEM(taps.shape, jnp.float32),
-            pltpu.VMEM((6, tiles + 1, window, LANES), jnp.float32),
-            pltpu.VMEM((2,) + strip, jnp.float32),
-            pltpu.SemaphoreType.DMA((tiles,)),
-            pltpu.SemaphoreType.DMA((tiles,)),
-            pltpu.SemaphoreType.DMA((2,)),
-        ],
+        in_specs=[HBM] * 4 + [VMEM],
+        out_specs=[VMEM] * 3,
+        out_shape=floats(field, field, (4, window, 2 * LANES)),
+        scratch_shapes=reader_scratch(tiles, height, window, class_weights, taps),
         compiler_params=params(),
-        name="pack_east_west",
-    )(observed, class_map, class_weights, taps)
+        cost_estimate=pl.CostEstimate(
+            flops=20 * pixels, bytes_accessed=16 * pixels, transcendentals=0
+        ),
+        name="pack_all",
+    )(*[in_hbm(array) for array in (observed, class_map, class_weights, taps)], after)
 
 
 def middle_kernel(
-    tiles, down, got_a, got_b, coarse_in, obs_ref, cond_ref, side_ref, coarse_ref, send_a, send_b, message
+    tiles,
+    down,
+    got_b,
+    got_a,
+    coarse_in,
+    obs_in,
+    cond_in,
+    obs,
+    cond,
+    coarse_ref,
+    send_a,
+    send_b,
+    message,
 ):
     height = down * COARSE
     halves = height // LANES
@@ -356,10 +439,11 @@
     def turned(low, high):
         return jnp.transpose(jnp.concatenate([low, gap, high], axis=0))
 
-    for which in range(2):
+    for which, field in enumerate((obs, cond)):
         for half in range(halves):
             at = (which * halves + half) * EDGE
-            side_ref[which, half * LANES : (half + 1) * LANES, :] = turned(
+            begin_row = 2 * EDGE + half * LANES
+            field[tiles, begin_row : begin_row + LANES, :] = turned(
                 from_e[at : at + EDGE], from_w[at : at + EDGE]
             )
     base = 2 * halves * EDGE
@@ -377,17 +461,14 @@
         rows = slice(index * window, (index + 1) * window)
         coarse_ref[index, :, :LANES] = coarse_in[index, :, :LANES] + left[rows]
         coarse_ref[index, :, LANES:] = coarse_in[index, :, LANES:] + right[rows]
-    for slot, side_at, coarse_at in ((0, 0, 0), (1, height - EDGE, window - 2 * EDGE)):
-        for which, field in enumerate((obs_ref, cond_ref)):
+    for slot, begin_row, coarse_at in (
+        (0, 2 * EDGE, 0),
+        (1, EDGE + height, window - 2 * EDGE),
+    ):
+        for which, field in enumerate((obs, cond)):
             for t in range(tiles + 1):
                 at = (which * (tiles + 1) + t) * EDGE
-                if t < tiles:
-                    begin = 2 * EDGE + side_at
-                    message[slot, at : at + EDGE, :] = field[t, begin : begin + EDGE, :]
-                else:
-                    message[slot, at : at + EDGE, :] = side_ref[
-                        which, side_at : side_at + EDGE, :
-                    ]
+                message[slot, at : at + EDGE, :] = field[t, begin_row : begin_row + EDGE, :]
         for index in range(4):
             for half in range(2):
                 at = 2 * (tiles + 1) * EDGE + (2 * index + half) * 2 * EDGE
@@ -404,12 +485,50 @@
     return pl.pallas_call(
         functools.partial(middle_kernel, tiles, down),
         in_specs=[VMEM] * 5,
-        out_specs=[VMEM] * 4,
-        out_shape=floats((2, height, LANES), coarse.shape, long, long),
+        out_specs=[VMEM] * 5,
+        out_shape=floats(obs.shape, cond.shape, coarse.shape, long, long),
+        input_output_aliases={3: 0, 4: 1},
         scratch_shapes=[pltpu.VMEM((2,) + long, jnp.float32)],
         compiler_params=params(),
         name="pack_north_south",
-    )(got_a, got_b, coarse, obs, cond)
+    )(got_b, got_a, coarse, obs, cond)
+
+
+def inner_kernel(tiles, taps, obs, cond, res_ref, east_ref, south_ref, inv_ref, spread_ref):
+    strips = (obs.shape[1] - 2 * EDGE) // STRIP
+    _, _, has_e, has_w = has_sides()
+    clear_pads(east_ref, south_ref)
+    spread_ref[...] = spread_matrix(tiles)
+    taps = read_taps(taps)
+    sides = side_lanes(has_e, has_w)
+
+    def work(index, _):
+        at = strip_at(index + 1)
+        fields = begin(obs, cond, at, taps, sides)
+        return [
+            (ref, at, strip)
+            for ref, strip in zip((east_ref, south_ref, inv_ref, res_ref), fields)
+        ], 0
+
+    sweep(strips - 2, 1, work, 0)
+
+
+def inner(taps, obs, cond):
+    field = obs.shape
+    tiles = field[0] - 1
+    pixels = field[0] * field[1] * field[2]
+    return pl.pallas_call(
+        functools.partial(inner_kernel, tiles),
+        in_specs=[SMEM] + [VMEM] * 2,
+        out_specs=[VMEM] * 5,
+        out_shape=floats(field, field, field, field)
+        + [jax.ShapeDtypeStruct((2 * LANES, (tiles + 1) * LANES), jnp.bfloat16)],
+        compiler_params=params(),
+        cost_estimate=pl.CostEstimate(
+            flops=45 * pixels, bytes_accessed=24 * pixels, transcendentals=0
+        ),
+        name="inner_strips",
+    )(taps, obs, cond)
 
 
 def first_kernel(
@@ -418,18 +537,22 @@
     taps,
     obs_in,
     cond_in,
-    side_ref,
+    res_in,
+    east_in,
+    south_in,
+    inv_in,
+    got_b,
     got_a,
-    got_b,
     coarse_in,
+    matrix,
     obs,
     cond,
     res_ref,
-    p_ref,
-    q_ref,
     east_ref,
     south_ref,
     inv_ref,
+    p_ref,
+    q_ref,
     table_ref,
     own_ref,
     chunk_ref,
@@ -443,9 +566,8 @@
     at_col, at_row, n_cols, n_rows = place()
     has_n, has_s, has_e, has_w = has_sides()
     from_s, from_n = in_pair_order(at_row, got_b[...], got_a[...])
-    clear_pads(obs, cond, p_ref, image, res_ref, q_ref, east_ref, south_ref, inv_ref)
+    clear_pads(obs, cond, p_ref, image)
     for which, field in enumerate((obs, cond)):
-        field[tiles, 2 * EDGE : 2 * EDGE + height, :] = side_ref[which]
         for t in range(tiles + 1):
             at = (which * (tiles + 1) + t) * EDGE
             field[t, EDGE : 2 * EDGE, :] = from_n[at : at + EDGE]
@@ -471,64 +593,50 @@
     taps = read_taps(taps)
     total = tap_total(taps, 1)
     factor = inside * OMEGA / (COARSE * COARSE * total * total + around)
-    table_ref[0] = east
-    table_ref[1] = south
-    table_ref[2] = factor
-    cells = split_dot(jacobi(source, east, south, factor), spread_matrix(tiles))
+    weights = (east, roll(east, 1, 1), south, roll(south, 1, 0))
+    table = [factor] + [factor * weight for weight in weights]
+    for index, part in enumerate(table):
+        table_ref[index] = part
+    cells = split_dot(jacobi(source, table), matrix[...])
     for t in range(tiles + 1):
         spread[t] = cells[:, t * LANES : (t + 1) * LANES]
 
-    squares = tap_total(taps, 2)
     sides = side_lanes(has_e, has_w)
+    for index in (0, strips - 1):
+        at = EDGE + STRIP * index
+        fields = begin(obs, cond, at, taps, sides)
+        for ref, strip in zip((east_ref, south_ref, inv_ref, res_ref), fields):
+            store(ref, at, strip)
+    mask_rows(inv_ref, has_n, has_s)
 
     def keeps(index):
         return jnp.where(index > 0, 1.0, 0.0), jnp.where(index < strips - 1, 1.0, 0.0)
 
     def start(index, total):
         at = strip_at(index)
-        above, here, below = load(cond, at - 1), load(cond, at), load(cond, at + 1)
-        right = from_east(here)
-        span = range(tiles + 1)
-        to_e = [0.5 * (here[t] + right[t]) for t in span]
-        to_w = from_west(to_e)
-        to_s = [0.5 * (here[t] + below[t]) for t in span]
-        inverse = [
-            1.0 / (squares + to_e[t] + to_w[t] + to_s[t] + 0.5 * (here[t] + above[t]))
-            for t in span
-        ]
-        inverse[tiles] = inverse[tiles] * sides
-        residual = conv(obs, at, taps, True)
+        residual, inverse = load(res_ref, at), load(inv_ref, at)
         cells = spread_strip(spread, index)
-        direction = [residual[t] * inverse[t] + cells[t] for t in span]
-        store(east_ref, at, to_e)
-        store(south_ref, at, to_s)
-        store(inv_ref, at, inverse)
-        store(res_ref, at, residual)
-        store(p_ref, at, direction)
-        return total + product_sum(residual, direction, tiles, *keeps(index))
+        direction = [residual[t] * inverse[t] + cells[t] for t in range(tiles + 1)]
+        return [(p_ref, at, direction)], total + product_sum(
+            residual, direction, tiles, *keeps(index)
+        )
 
     def blur(index, _):
         at = strip_at(index)
         blurred = conv(p_ref, at, taps, False)
         blurred[tiles] = blurred[tiles] * sides
-        store(image, at, blurred)
-        return 0
+        return [(image, at, blurred)], 0
 
     def finish(index, total):
         at = strip_at(index)
-        here, pulled = laplace(p_ref, east_ref, south_ref, at)
-        back = conv(image, at, taps, True)
-        product = [back[t] + pulled[t] for t in range(tiles + 1)]
-        store(q_ref, at, product)
-        return total + product_sum(here, product, tiles, *keeps(index))
+        here, product = operate(p_ref, image, east_ref, south_ref, at, taps)
+        return [(q_ref, at, product)], total + product_sum(here, product, tiles, *keeps(index))
 
     nothing = jnp.zeros((EDGE, LANES), jnp.float32)
-    dots_ref[0] = lax.fori_loop(0, strips, start, nothing)
-    mask_rows(inv_ref, has_n, has_s)
-    mask_rows(p_ref, has_n, has_s)
-    lax.fori_loop(0, strips, blur, 0)
+    dots_ref[0] = sweep(strips, 2, start, nothing)
+    sweep(strips, 2, blur, 0)
     mask_rows(image, has_n, has_s)
-    dots_ref[1] = lax.fori_loop(0, strips, finish, nothing)
+    dots_ref[1] = sweep(strips, 2, finish, nothing)
 
     shape = (tiles * LANES, LANES)
     matrix = jnp.where(iota(shape, 0) >> 3 == iota(shape, 1), 1.0, 0.0).astype(jnp.bfloat16)
@@ -558,31 +666,31 @@
                 chunk_ref[to_col * n_rows + to_row] = piece
 
 
-def first(taps, obs, cond, side, got_a, got_b, coarse):
-    field = obs.shape
+def first(taps, fields, got_a, got_b, coarse, matrix):
+    field = fields[0].shape
     tiles, height = field[0] - 1, field[1] - 4 * EDGE
     down = height // COARSE
     window = down + 2 * EDGE
     count = lax.axis_size("cols") * lax.axis_size("rows")
     shapes = [field] * 8 + [
-        (3, window, 2 * LANES),
+        (5, window, 2 * LANES),
         (down, LANES),
         (count, EDGE, LANES),
         (2, EDGE, LANES),
     ]
     return pl.pallas_call(
         functools.partial(first_kernel, tiles, down),
-        in_specs=[SMEM] + [VMEM] * 6,
+        in_specs=[SMEM] + [VMEM] * 10,
         out_specs=[VMEM] * len(shapes),
         out_shape=floats(*shapes),
-        input_output_aliases={1: 0, 2: 1},
+        input_output_aliases={index + 1: index for index in range(6)},
         scratch_shapes=[
             pltpu.VMEM(field, jnp.float32),
             pltpu.VMEM((tiles + 1, window, LANES), jnp.float32),
         ],
         compiler_params=params(),
         name="first_direction",
-    )(taps, obs, cond, side, got_a, got_b, coarse)[2:]
+    )(taps, *fields, got_b, got_a, coarse, matrix)[2:]
 
 
 def second_kernel(
@@ -597,6 +705,7 @@
     south_ref,
     inv_ref,
     dots_in,
+    matrix,
     w_ref,
     v_ref,
     out_ref,
@@ -625,11 +734,11 @@
         ],
         axis=0,
     )
-    cells = jacobi(source, table_ref[0], table_ref[1], table_ref[2])
-    cells = split_dot(cells, spread_matrix(tiles))
+    cells = jacobi(source, [table_ref[index] for index in range(5)])
+    cells = split_dot(cells, matrix[...])
     for t in range(tiles + 1):
         spread[t] = cells[:, t * LANES : (t + 1) * LANES]
-    clear_pads(w_ref, image, v_ref)
+    clear_pads(w_ref, image)
     sides = side_lanes(has_e, has_w)
     taps = read_taps(taps)
 
@@ -637,57 +746,56 @@
         at = strip_at(index)
         field, inverse = load(q_ref, at), load(inv_ref, at)
         cells = spread_strip(spread, index)
-        store(w_ref, at, [field[t] * inverse[t] + cells[t] for t in range(tiles + 1)])
-        return 0
+        return [(w_ref, at, [field[t] * inverse[t] + cells[t] for t in range(tiles + 1)])], 0
 
     def blur(index, _):
         at = strip_at(index)
         blurred = conv(w_ref, at, taps, False)
         blurred[tiles] = blurred[tiles] * sides
-        store(image, at, blurred)
-        return 0
+        return [(image, at, blurred)], 0
 
     def finish(index, totals):
         at = pl.multiple_of(2 * EDGE + STRIP * index, EDGE)
-        here, pulled = laplace(w_ref, east_ref, south_ref, at)
-        back = conv(image, at, taps, True)
-        product = [back[t] + pulled[t] for t in range(tiles + 1)]
+        here, product = operate(w_ref, image, east_ref, south_ref, at, taps)
         field = load(q_ref, at)
-        store(v_ref, at, product)
-        return (
+        return [(v_ref, at, product[:tiles])], (
             totals[0] + product_sum(field, here, tiles),
             totals[1] + product_sum(here, product, tiles),
         )
 
     nothing = jnp.zeros((EDGE, LANES), jnp.float32)
-    lax.fori_loop(0, strips, start, 0)
-    lax.fori_loop(0, strips, blur, 0)
+    sweep(strips, 2, start, 0)
+    sweep(strips, 2, blur, 0)
     mask_rows(image, has_n, has_s)
-    dot_qw, dot_wv = lax.fori_loop(0, strips - 1, finish, (nothing, nothing))
+    dot_qw, dot_wv = sweep(strips - 1, 2, finish, (nothing, nothing))
     line = jnp.zeros((1, LANES), jnp.float32)
-    at_lane = iota((1, LANES), 1)
+    block = iota((1, LANES), 1) // (LANES // 4)
     for index, part in enumerate((dots_in[0], dots_in[1], dot_qw, dot_wv)):
-        line = line + jnp.where(at_lane == index, jnp.sum(part), 0.0)
+        part = jnp.sum(part, axis=0, keepdims=True)
+        part = part + roll(part, LANES // 2, 1)
+        part = part + roll(part, LANES // 4, 1)
+        line = jnp.where(block == index, part, line)
     for index in range(out_ref.shape[0]):
         out_ref[index] = line
 
 
-def second(taps, got, own, table, q, east, south, inv, dots):
+def second(taps, got, own, table, q, east, south, inv, dots, matrix):
     tiles, height = q.shape[0] - 1, q.shape[1] - 4 * EDGE
     down = height // COARSE
     window = down + 2 * EDGE
+    count = lax.axis_size("cols") * lax.axis_size("rows")
     return pl.pallas_call(
         functools.partial(second_kernel, tiles, down),
-        in_specs=[SMEM] + [VMEM] * 8,
+        in_specs=[SMEM] + [VMEM] * 9,
         out_specs=[VMEM] * 3,
-        out_shape=floats(q.shape, q.shape, (got.shape[0], 1, LANES)),
+        out_shape=floats(q.shape, q.shape, (count, 1, LANES)),
         scratch_shapes=[
             pltpu.VMEM(q.shape, jnp.float32),
             pltpu.VMEM((tiles + 1, window, LANES), jnp.float32),
         ],
         compiler_params=params(),
         name="second_direction",
-    )(taps, got, own, table, q, east, south, inv, dots)
+    )(taps, got, own, table, q, east, south, inv, dots, matrix)
 
 
 def combine_kernel(
@@ -696,8 +804,8 @@
     line = sums_ref[0]
     for index in range(1, sums_ref.shape[0]):
         line = line + sums_ref[index]
-    lane = iota((1, LANES), 1)
-    pick = lambda index: jnp.sum(jnp.where(lane == index, line, 0.0), axis=1, keepdims=True)
+    block = iota((1, LANES), 1) // (LANES // 4)
+    pick = lambda index: jnp.sum(jnp.where(block == index, line, 0.0), axis=1, keepdims=True)
     rp, pq, qw, wv = [pick(index) for index in range(4)]
     step = rp / pq
     rp_next = step * step * qw - rp
@@ -764,19 +872,25 @@
             pair for i in range(begin, count - 1, 2) for pair in ((i, i + 1), (i + 1, i))
         ]
 
-    return lax.ppermute(send_a, axis, pairs(0)), lax.ppermute(send_b, axis, pairs(1))
+    got_b = lax.ppermute(send_b, axis, pairs(1))
+    got_a = lax.ppermute(send_a, axis, pairs(0))
+    return got_a, got_b
 
 
 def body(observed, class_map, class_weights, blur_kernel):
-    obs, cond, coarse, send_a, send_b = pack(observed, class_map, class_weights, blur_kernel)
+    arguments = (observed, class_map, class_weights, blur_kernel)
+    send_a, send_b = edge(*arguments)
     got_a, got_b = exchange(send_a, send_b, "cols")
-    side, coarse, send_a, send_b = middle(got_a, got_b, coarse, obs, cond)
+    obs, cond, coarse = pack(*arguments, send_a)
+    obs, cond, coarse, send_a, send_b = middle(got_a, got_b, coarse, obs, cond)
     got_a, got_b = exchange(send_a, send_b, "rows")
-    r, p, q, east, south, inv, table, own, chunk, dots = first(
-        blur_kernel, obs, cond, side, got_a, got_b, coarse
+    r, east, south, inv, matrix = inner(blur_kernel, obs, cond)
+    fields = (obs, cond, r, east, south, inv)
+    r, east, south, inv, p, q, table, own, chunk, dots = first(
+        blur_kernel, fields, got_a, got_b, coarse, matrix
     )
     got = lax.all_to_all(chunk, AXES, 0, 0, tiled=True)
-    w, v, line = second(blur_kernel, got, own, table, q, east, south, inv, dots)
+    w, v, line = second(blur_kernel, got, own, table, q, east, south, inv, dots, matrix)
     sums = lax.all_to_all(line, AXES, 0, 0, tiled=True)
     return tuple(combine(sums, p, w, r, q, v))
 

time: 63.8 us -> 52.8 us (0.83)
  blocking collectives: 31.7 us -> 21.1 us
  starting transfers between devices: 4.42 us -> 10 us
  local copies, waits for them, and re-layouts: 3.78 us -> 0.01 us
  waiting for transfers between devices: 1.91 us -> 0.01 us
    all_to_all x1, blocking collectives: 22.8 us -> 12.1 us  [body(): got = lax.all_to_all(chunk, AXES, 0, 0, tiled=True)]
    ppermute x4, starting transfers between devices: 4.42 us -> 10 us  [the longest x2 8.71 us: exchange(): got_a = lax.ppermute(send_a, axis, pairs(0))]
    pallas_call x0 -> x2, Pallas kernels: none -> 5.02 us  [the longest x1 3.36 us: inner(): pl.pallas_call(functools.partial(inner_kernel, tiles), in_specs=[SMEM] +...]
    pallas_call x1, Pallas kernels: 10.1 us -> 5.96 us  [first(): pl.pallas_call(functools.partial(first_kernel, tiles, down), in_specs=[SM...]
    unnamed x10 -> x2, local copies, waits for them, and re-layouts: 3.78 us -> 0.01 us
    ppermute x4, waiting for transfers between devices: 1.91 us -> 0.01 us  [the longest x2 0.01 us: exchange(): got_a = lax.ppermute(send_a, axis, pairs(0))]
    pallas_call x1, Pallas kernels: 6.74 us -> 5.32 us  [second(): pl.pallas_call(functools.partial(second_kernel, tiles, down), in_specs=[S...]
  transfers between devices with their start and end apart: 4 -> 4, of which waited for: 2 -> 0; matrix products, arithmetic and copies ran while one was open for 0% -> 0% of each run, Pallas kernels for 0% -> 11%
where the time goes in v2:
time: 52.8 us; the launch traced here: 52.6 us
  blocking collectives  21.1 us (40%)
  Pallas kernels  20.7 us (39%)
  starting transfers between devices  10 us (19%)
  between operations  0.73 us (1%)
    all_to_all x1, blocking collectives, body(): got = lax.all_to_all(chunk, AXES, 0, 0, tiled=True)  12.1 us
    all_to_all x1, blocking collectives, body(): sums = lax.all_to_all(line, AXES, 0, 0, tiled=True)  8.93 us
    ppermute x2, starting transfers between devices, exchange(): got_a = lax.ppermute(send_a, axis, pairs(0))  8.71 us
    pallas_call x1, Pallas kernels, first(): pl.pallas_call(functools.partial(first_kernel, tiles, down), in_specs=[SM...  5.96 us
    pallas_call x1, Pallas kernels, second(): pl.pallas_call(functools.partial(second_kernel, tiles, down), in_specs=[S...  5.32 us
    pallas_call x1, Pallas kernels, inner(): pl.pallas_call(functools.partial(inner_kernel, tiles), in_specs=[SMEM] +...  3.36 us
    pallas_call x1, Pallas kernels, pack(): pl.pallas_call(functools.partial(pack_kernel, tiles, down), in_specs=[HBM...  2.5 us
    pallas_call x1, Pallas kernels, combine(): pl.pallas_call(functools.partial(combine_kernel, tiles, height), in_specs...  1.71 us
  transfers between devices with their start and end apart: 4, of which 0 were waited for; matrix products, arithmetic and copies ran while one was open for 0% of the time, Pallas kernels for 11%

profile of v2, /device:TPU:0, one launch (start us, length us, event | category | flops | bytes accessed | tf_op | source)
XLA Modules:
  0.0 52.6 jit_solution(6775701081454069637)
XLA Ops:
  0.6 1.7 %pack_east_west.1 = (f32[64,128]{1,0:T(8,128)S(1)}, f32[64,128]{1,0:T(8,128)S(1)}) custom-call(f32[256,1024]{1,0:T(8,128)} %refs_0_.3, s32[256,1024]{1,0:T(8,128)} %refs_1_.3, f32[4]{0:T(128)} %refs_2_.3, f32[3,3]{1,0:T(4,128)} %taps.5), custom_call_target="tpu_custom_call" | custom-call | tf_op jit(solution)/shard_map/pack_east_west/pallas_call | solution.py:372
  2.3 0.7 %collective-permute-start = (f32[64,128]{1,0:T(8,128)S(1)}, f32[64,128]{1,0:T(8,128)S(1)}, u32[]{:S(2)}, u32[]{:S(2)}) collective-permute-start(f32[64,128]{1,0:T(8,128)S(1)} %get-tuple-element.30), channel_id=1, source_target_pairs={{4,8},{8,4},{12,16},{16,12},{20,24},{24,20},{5,9},{9,5},{13,17},{1... | collective-permute-start | bytes 98312 | tf_op jit(solution)/shard_map/ppermute | solution.py:875
  3.0 5.8 %collective-permute-start.1 = (f32[64,128]{1,0:T(8,128)S(1)}, f32[64,128]{1,0:T(8,128)S(1)}, u32[]{:S(2)}, u32[]{:S(2)}) collective-permute-start(f32[64,128]{1,0:T(8,128)S(1)} %get-tuple-element.31.refs_4_), channel_id=1, source_target_pairs={{0,4},{4,0},{8,12},{12,8},{16,20},{20,16},{24,28},{28,24},{1,5},{5... | collective-permute-start | bytes 98312 | tf_op jit(solution)/shard_map/ppermute | solution.py:876
  8.8 2.5 %pack_all.1 = (f32[9,288,128]{2,1,0:T(8,128)S(1)}, f32[9,288,128]{2,1,0:T(8,128)S(1)}, f32[4,48,256]{2,1,0:T(8,128)S(1)}) custom-call(f32[256,1024]{1,0:T(8,128)} %refs_0_.3, s32[256,1024]{1,0:T(8,128)} %refs_1_.3, f32[4]{0:T(128)} %refs_2_.3, f32[3,3]{1,0:T(4,128)} %taps.5, f32[64,128]{1,0:T(8,128)S(1)} %get-tuple-element.31.refs_4_), custom_call_target="tpu_custom_call" | custom-call | flops 5242880 | bytes 4194304 | tf_op jit(solution)/shard_map/pack_all/pallas_call | solution.py:404
  11.3 0.0 collective-permute-done.got_b
  11.3 0.0 collective-permute-done.1.got_a
  11.3 0.0 copy-start
  11.3 0.2 pack_north_south.1
  11.5 0.7 %collective-permute-start.2 = (f32[272,128]{1,0:T(8,128)S(1)}, f32[272,128]{1,0:T(8,128)S(1)}, u32[]{:S(2)}, u32[]{:S(2)}) collective-permute-start(f32[272,128]{1,0:T(8,128)S(1)} %get-tuple-element.41), channel_id=1, source_target_pairs={{1,2},{2,1},{5,6},{6,5},{9,10},{10,9},{13,14},{14,13},{17,18},{18,... | collective-permute-start | bytes 417800 | tf_op jit(solution)/shard_map/ppermute | solution.py:875
  12.2 2.9 %collective-permute-start.3 = (f32[272,128]{1,0:T(8,128)S(1)}, f32[272,128]{1,0:T(8,128)S(1)}, u32[]{:S(2)}, u32[]{:S(2)}) collective-permute-start(f32[272,128]{1,0:T(8,128)S(1)} %get-tuple-element.42), channel_id=1, source_target_pairs={{0,1},{1,0},{2,3},{3,2},{4,5},{5,4},{6,7},{7,6},{8,9},{9,8},{10,11... | collective-permute-start | bytes 417800 | tf_op jit(solution)/shard_map/ppermute | solution.py:876
  15.1 0.0 copy-done
  15.1 3.4 %inner_strips.1 = (f32[9,288,128]{2,1,0:T(8,128)S(1)}, f32[9,288,128]{2,1,0:T(8,128)S(1)}, f32[9,288,128]{2,1,0:T(8,128)S(1)}, f32[9,288,128]{2,1,0:T(8,128)S(1)}, bf16[256,1152]{1,0:T(8,128)(2,1)S(1)}) custom-call(f32[3,3]{1,0:T(4,128)S(1)} %copy-done, f32[9,288,128]{2,1,0:T(8,128)S(1)} %get-tuple-element.35.obs.obs_in, ...), custom_call_target="tpu_custom_call" | custom-call | flops 14929920 | bytes 7962624 | tf_op jit(solution)/shard_map/inner_strips/pallas_call | solution.py:520
  18.5 0.0 collective-permute-done.2.got_b
  18.5 0.0 collective-permute-done.3.got_a
  18.5 6.0 %first_direction.1 = (f32[9,288,128]{2,1,0:T(8,128)S(1)}, f32[9,288,128]{2,1,0:T(8,128)S(1)}, f32[9,288,128]{2,1,0:T(8,128)S(1)}, f32[9,288,128]{2,1,0:T(8,128)S...) custom-call(f32[3,3]{1,0:T(4,128)S(1)} %copy-done, ...), custom_call_target="tpu_custom_call", output_to_operand_aliasing={{0}: (1, {}), {1}: (2, {}), {2}: (3, {}), {3}: (4, {}), {4}... | custom-call | tf_op jit(solution)/shard_map/first_direction/pallas_call | solution.py:681
  24.5 12.1 %all_to_all.10.got_ref = f32[32,8,128]{2,1,0:T(8,128)S(1)} all-to-all(f32[32,8,128]{2,1,0:T(8,128)S(1)} %get-tuple-element.45), channel_id=1, replica_groups=mesh['cols'=8,'rows'=4] {'cols','rows'}, dimensions={0} | all-to-all | bytes 262144 | tf_op jit(solution)/shard_map/all_to_all | solution.py:892
  36.6 5.3 %second_direction.1 = (f32[9,288,128]{2,1,0:T(8,128)S(1)}, f32[9,288,128]{2,1,0:T(8,128)S(1)}, f32[32,1,128]{2,1,0:T(1,128)S(1)}) custom-call(f32[3,3]{1,0:T(4,128)S(1)} %copy-done, f32[32,8,128]{2,1,0:T(8,128)S(1)} %all_to_all.10.got_ref, f32[32,128]{1,0:T(8,128)S(1)} %get-tuple-element.46.own_ref, f32[5,48,256]{2,1,0:T(8,128)S(1)} %get-tuple-element.47.table_ref, ...), custom_call_target="tpu_custom_call" | custom-call | tf_op jit(solution)/shard_map/second_direction/pallas_call | solution.py:787
  42.0 8.9 %all_to_all.11.sums_ref = f32[32,1,128]{2,1,0:T(1,128)S(1)} all-to-all(f32[32,1,128]{2,1,0:T(1,128)S(1)} %get-tuple-element.53), channel_id=1, replica_groups=mesh['cols'=8,'rows'=4] {'cols','rows'}, dimensions={0} | all-to-all | bytes 32768 | tf_op jit(solution)/shard_map/all_to_all | solution.py:894
  50.9 1.7 %combine.1 = (f32[256,1024]{1,0:T(8,128)}, f32[256,1024]{1,0:T(8,128)}) custom-call(f32[32,1,128]{2,1,0:T(1,128)S(1)} %all_to_all.11.sums_ref, f32[9,288,128]{2,1,0:T(8,128)S(1)} %get-tuple-element.54.p_ref, f32[9,288,128]{2,1,0:T(8,128)S(1)} %get-tuple-element.55.w_ref, f32[9,288,128]{2,1,0:T(8,128)S(1)} %get-tuple-element.56.r_ref, ...), custom_call_target="tpu_custom_call" | custom-call | tf_op jit(solution)/shard_map/combine/pallas_call | solution.py:852
Async XLA Ops:
  2.3 9.0 %collective-permute-start = (f32[64,128]{1,0:T(8,128)S(1)}, f32[64,128]{1,0:T(8,128)S(1)}, u32[]{:S(2)}, u32[]{:S(2)}) collective-permute-start(f32[64,128]{1,0:T(8,128)S(1)} %get-tuple-element.30), channel_id=1, source_target_pairs={{4,8},{8,4},{12,16},{16,12},{20,24},{24,20},{5,9},{9,5},{13,17},{1... | collective-permute-start | bytes 98312 | tf_op jit(solution)/shard_map/ppermute | solution.py:875
  3.0 8.3 %collective-permute-start.1 = (f32[64,128]{1,0:T(8,128)S(1)}, f32[64,128]{1,0:T(8,128)S(1)}, u32[]{:S(2)}, u32[]{:S(2)}) collective-permute-start(f32[64,128]{1,0:T(8,128)S(1)} %get-tuple-element.31.refs_4_), channel_id=1, source_target_pairs={{0,4},{4,0},{8,12},{12,8},{16,20},{20,16},{24,28},{28,24},{1,5},{5... | collective-permute-start | bytes 98312 | tf_op jit(solution)/shard_map/ppermute | solution.py:876
  11.3 3.8 %copy-start = (f32[3,3]{1,0:T(4,128)S(1)}, f32[3,3]{1,0:T(4,128)}, u32[]{:S(2)}) copy-start(f32[3,3]{1,0:T(4,128)} %taps.5) | copy-start | bytes 112
  11.5 7.0 %collective-permute-start.2 = (f32[272,128]{1,0:T(8,128)S(1)}, f32[272,128]{1,0:T(8,128)S(1)}, u32[]{:S(2)}, u32[]{:S(2)}) collective-permute-start(f32[272,128]{1,0:T(8,128)S(1)} %get-tuple-element.41), channel_id=1, source_target_pairs={{1,2},{2,1},{5,6},{6,5},{9,10},{10,9},{13,14},{14,13},{17,18},{18,... | collective-permute-start | bytes 417800 | tf_op jit(solution)/shard_map/ppermute | solution.py:875
  12.2 6.3 %collective-permute-start.3 = (f32[272,128]{1,0:T(8,128)S(1)}, f32[272,128]{1,0:T(8,128)S(1)}, u32[]{:S(2)}, u32[]{:S(2)}) collective-permute-start(f32[272,128]{1,0:T(8,128)S(1)} %get-tuple-element.42), channel_id=1, source_target_pairs={{0,1},{1,0},{2,3},{3,2},{4,5},{5,4},{6,7},{7,6},{8,9},{9,8},{10,11... | collective-permute-start | bytes 417800 | tf_op jit(solution)/shard_map/ppermute | solution.py:876

commit v3 on v2

--- a/solution.py
+++ b/solution.py
@@ -15,7 +15,7 @@
 LANES = 128
 HALF = LANES // 2
 EDGE = 8
-STRIP = 2 * EDGE
+STRIP = 4 * EDGE
 AXES = ("cols", "rows")
 LIMIT = 40 * 1024 * 1024
 
@@ -69,12 +69,6 @@
     return jnp.where(hit, 1.0, 0.0).astype(jnp.bfloat16)
 
 
-def spread_matrix(tiles):
-    shape = (2 * LANES, (tiles + 1) * LANES)
-    hit = cell_of(iota(shape, 1), tiles) == iota(shape, 0)
-    return jnp.where(hit, 1.0, 0.0).astype(jnp.bfloat16)
-
-
 def split_dot(field, matrix):
     rows = field.shape[0]
     high = field.astype(jnp.bfloat16)
@@ -102,21 +96,6 @@
     return jnp.concatenate(load(ref, at, rows), axis=1)
 
 
-def from_west(strip):
-    lane = iota(strip[0].shape, 1)
-    turned = [roll(part, 1, 1) for part in strip]
-    return [jnp.where(lane == 0, turned[t - 1], turned[t]) for t in range(len(strip))]
-
-
-def from_east(strip):
-    lane = iota(strip[0].shape, 1)
-    turned = [roll(part, -1, 1) for part in strip]
-    count = len(strip)
-    return [
-        jnp.where(lane == LANES - 1, turned[(t + 1) % count], turned[t]) for t in range(count)
-    ]
-
-
 def read_taps(taps):
     return [[taps[a, b] for b in range(3)] for a in range(3)]
 
@@ -125,129 +104,182 @@
     return sum(tap * tap if power == 2 else tap for line in taps for tap in line)
 
 
-def tap_sums(ref, at, taps, flip):
+def shifter(count, rows, make):
+    make = functools.cache(make)
+    west = functools.cache(lambda t: roll(make(t), 1, 1))
+    east = functools.cache(lambda t: roll(make(t), -1, 1))
+
+    def from_west(t):
+        lane = iota((rows, LANES), 1)
+        return jnp.where(lane == 0, west((t - 1) % count), west(t))
+
+    def from_east(t):
+        lane = iota((rows, LANES), 1)
+        return jnp.where(lane == LANES - 1, east((t + 1) % count), east(t))
+
+    return make, from_west, from_east
+
+
+def reader_of(ref, at, rows=STRIP):
+    return functools.cache(lambda t, by=0: ref[t, pl.ds(at + by, rows), :])
+
+
+def tap_sum(field, taps, flip, b):
     if flip:
         taps = [line[::-1] for line in taps[::-1]]
-    above, here, below = load(ref, at - 1), load(ref, at), load(ref, at + 1)
-    sums = [[], [], []]
-    for t in range(len(here)):
-        for b in range(3):
-            sums[b].append(
-                taps[0][b] * above[t] + taps[1][b] * here[t] + taps[2][b] * below[t]
-            )
-    return sums
-
-
-def conv(ref, at, taps, flip):
-    sums = tap_sums(ref, at, taps, flip)
-    west, east = from_west(sums[0]), from_east(sums[2])
-    return [sums[1][t] + west[t] + east[t] for t in range(len(west))]
+    return lambda t: (
+        taps[0][b] * field(t, -1) + taps[1][b] * field(t) + taps[2][b] * field(t, 1)
+    )
+
+
+def conv(ref, at, taps, flip, rows=STRIP):
+    count = ref.shape[0]
+    field = reader_of(ref, at, rows)
+    sums = [tap_sum(field, taps, flip, b) for b in range(3)]
+    _, from_west, _ = shifter(count, rows, sums[0])
+    _, _, from_east = shifter(count, rows, sums[2])
+    return lambda t: sums[1](t) + from_west(t) + from_east(t)
 
 
 def operate(ref, image, east_ref, south_ref, at, taps):
-    above, here, below = load(ref, at - 1), load(ref, at), load(ref, at + 1)
-    east, south, north = load(east_ref, at), load(south_ref, at), load(south_ref, at - 1)
-    sums = tap_sums(image, at, taps, True)
-    span = range(len(here))
-    beside = from_east(here)
-    flux = [east[t] * (here[t] - beside[t]) for t in span]
-    from_left = from_west([sums[0][t] - flux[t] for t in span])
-    from_right = from_east(sums[2])
-    return here, [
-        sums[1][t]
-        + flux[t]
-        + from_left[t]
-        + from_right[t]
-        + south[t] * (here[t] - below[t])
-        - north[t] * (above[t] - here[t])
-        for t in span
+    count = ref.shape[0]
+    field, picture = reader_of(ref, at), reader_of(image, at)
+    east, south = reader_of(east_ref, at), reader_of(south_ref, at)
+    here, _, beside = shifter(count, STRIP, field)
+    flux = functools.cache(lambda t: east(t) * (here(t) - beside(t)))
+    sums = [tap_sum(picture, taps, True, b) for b in range(3)]
+    _, from_west, _ = shifter(count, STRIP, lambda t: sums[0](t) - flux(t))
+    _, _, from_east = shifter(count, STRIP, sums[2])
+
+    def value(t):
+        down = south(t) * (here(t) - field(t, 1)) - south(t, -1) * (field(t, -1) - here(t))
+        return sums[1](t) + flux(t) + from_west(t) + from_east(t) + down
+
+    return here, value
+
+
+def begin(obs, cond, at, taps, sides, rows):
+    count = cond.shape[0]
+    level = reader_of(cond, at, rows)
+    here, _, right = shifter(count, rows, level)
+    east, west, _ = shifter(count, rows, lambda t: here(t) + right(t))
+    squares = tap_total(taps, 2)
+    residual = conv(obs, at, taps, True, rows)
+    fields = [[], [], [], []]
+    for t in range(count):
+        south = here(t) + level(t, 1)
+        diag = squares + east(t) + west(t) + south + (here(t) + level(t, -1))
+        inverse = pl.reciprocal(diag, approx=True)
+        inverse = inverse * (2.0 - diag * inverse)
+        if t == count - 1:
+            inverse = inverse * sides
+        for strip, part in zip(fields, (east(t), south, inverse, residual(t))):
+            strip.append(part)
+    return fields
+
+
+def pick_lanes(field, lanes):
+    return jnp.take_along_axis(field, lanes, axis=1, mode="promise_in_bounds")
+
+
+def spread_cells(cells, spread):
+    tiles = spread.shape[0] - 1
+    lane = iota((cells.shape[0], LANES), 1)
+    for t in range(tiles):
+        spread[t] = pick_lanes(cells[:, :LANES], (lane >> 3) + t * (LANES // COARSE))
+    turn = jnp.where(lane < HALF, 0, LANES - LANES // COARSE)
+    spread[tiles] = pick_lanes(cells[:, LANES:], (lane >> 3) + turn)
+
+
+def cells_at(spread, at, rows, t):
+    first = at // EDGE + EDGE - 2
+    parts = [
+        jnp.broadcast_to(spread[t, pl.ds(first + index, 1), :], (EDGE, LANES))
+        for index in range(rows // EDGE)
     ]
-
-
-def begin(obs, cond, at, taps, sides):
-    above, here, below = load(cond, at - 1), load(cond, at), load(cond, at + 1)
-    span = range(len(here))
-    right = from_east(here)
-    east = [here[t] + right[t] for t in span]
-    west = from_west(east)
-    south = [here[t] + below[t] for t in span]
-    squares = tap_total(taps, 2)
-    inverse = [
-        1.0 / (squares + east[t] + west[t] + south[t] + (here[t] + above[t])) for t in span
-    ]
-    inverse[-1] = inverse[-1] * sides
-    return east, south, inverse, conv(obs, at, taps, True)
-
-
-def spread_strip(spread, index):
-    top, bottom = load(spread, 2 * index + EDGE - 1, 1), load(spread, 2 * index + EDGE, 1)
-    shape = (EDGE, LANES)
-    return [
-        jnp.concatenate([jnp.broadcast_to(a, shape), jnp.broadcast_to(b, shape)], axis=0)
-        for a, b in zip(top, bottom)
-    ]
-
-
-def side_lanes(has_e, has_w):
-    return jnp.where(iota((STRIP, LANES), 1) < HALF, has_e, has_w)
+    return jnp.concatenate(parts, axis=0)
+
+
+def cell_sums(ref, tiles, down):
+    lane = iota((down, LANES), 1)
+    total = jnp.zeros((down, LANES), jnp.float32)
+    for t in range(tiles):
+        picked = [
+            ref[t, pl.ds(2 * EDGE + k, down, stride=COARSE), :] for k in range(COARSE)
+        ]
+        part = sum(picked[1:], picked[0])
+        for by in (1, 2, 4):
+            part = part + roll(part, -by, 1)
+        part = pick_lanes(part, (lane & (LANES // COARSE - 1)) * COARSE)
+        total = jnp.where(lane // (LANES // COARSE) == t, part, total)
+    return total
+
+
+def side_lanes(has_e, has_w, rows=STRIP):
+    return jnp.where(iota((rows, LANES), 1) < HALF, has_e, has_w)
 
 
 def mask_rows(ref, has_n, has_s):
     last = ref.shape[1] - 2 * EDGE
-    ref[:, EDGE : 2 * EDGE, :] = ref[:, EDGE : 2 * EDGE, :] * has_n
-    ref[:, last : last + EDGE, :] = ref[:, last : last + EDGE, :] * has_s
+
+    def work(t, _):
+        for at, flag in ((EDGE, has_n), (last, has_s)):
+            ref[t, at : at + EDGE, :] = ref[t, at : at + EDGE, :] * flag
+        return 0
+
+    lax.fori_loop(0, ref.shape[0], work, 0)
 
 
 def clear_pads(*refs):
-    for ref in refs:
-        empty = jnp.zeros((ref.shape[0], EDGE, LANES), jnp.float32)
-        ref[:, :EDGE, :] = empty
-        ref[:, ref.shape[1] - EDGE :, :] = empty
-
-
-def product_sum(one, two, count, keep_top=None, keep_bottom=None):
-    total = one[0] * two[0]
-    for t in range(1, count):
-        total = total + one[t] * two[t]
-    top, bottom = total[:EDGE], total[EDGE:]
-    if keep_top is not None:
-        top, bottom = top * keep_top, bottom * keep_bottom
-    return top + bottom
-
-
-def sweep(count, group, body, carry):
-    def some(first_index, width, carry):
-        stores = []
-        for offset in range(width):
-            more, carry = body(first_index + offset, carry)
-            stores += more
-        for ref, at, strip in stores:
+    def work(t, _):
+        empty = jnp.zeros((EDGE, LANES), jnp.float32)
+        for ref in refs:
+            ref[t, :EDGE, :] = empty
+            ref[t, ref.shape[1] - EDGE :, :] = empty
+        return 0
+
+    lax.fori_loop(0, refs[0].shape[0], work, 0)
+
+
+def fold(total, flags=None):
+    parts = [total[at : at + EDGE] for at in range(0, total.shape[0], EDGE)]
+    if flags is not None:
+        parts = [part * flag for part, flag in zip(parts, flags)]
+    return sum(parts[1:], parts[0])
+
+
+def sweep(first, last, body, carry):
+    steps = -(-(last - first) // STRIP)
+
+    def work(index, carry):
+        start = first + index * STRIP
+        at = pl.multiple_of(jnp.minimum(start, last - STRIP), EDGE)
+        stores, carry = body(at, start, carry)
+        for ref, strip in stores:
             store(ref, at, strip)
         return carry
 
-    steps = count // group
-    carry = lax.fori_loop(0, steps, lambda step, c: some(step * group, group, c), carry)
-    left = count - steps * group
-    return some(steps * group, left, carry) if left else carry
-
-
-def strip_at(index):
-    return pl.multiple_of(EDGE + STRIP * index, EDGE)
+    return lax.fori_loop(0, steps, work, carry)
 
 
 def jacobi(source, table):
-    factor, east, west, south, north = table
-    source = factor * source
-    iterate = source
-    for _ in range(SWEEPS - 1):
-        across = east * roll(iterate, -1, 1) + west * roll(iterate, 1, 1)
-        along = south * roll(iterate, -1, 0) + north * roll(iterate, 1, 0)
-        iterate = ((1.0 - OMEGA) * iterate + source) + (across + along)
-    return iterate
+    source = table[0] * source
+
+    def work(_, iterate):
+        across = table[1] * roll(iterate, -1, 1) + table[2] * roll(iterate, 1, 1)
+        along = table[3] * roll(iterate, -1, 0) + table[4] * roll(iterate, 1, 0)
+        return ((1.0 - OMEGA) * iterate + source) + (across + along)
+
+    return lax.fori_loop(0, SWEEPS - 1, work, source)
 
 
 def in_pair_order(at, for_before, for_after):
     even = at % 2 == 0
+    if callable(for_before):
+        return (
+            lambda index: jnp.where(even, for_after(index), for_before(index)),
+            lambda index: jnp.where(even, for_before(index), for_after(index)),
+        )
     return jnp.where(even, for_after, for_before), jnp.where(even, for_before, for_after)
 
 
@@ -415,6 +447,22 @@
     )(*[in_hbm(array) for array in (observed, class_map, class_weights, taps)], after)
 
 
+def merge_sides(parts):
+    block = iota((EDGE, LANES), 1) // (2 * EDGE)
+    merged = jnp.zeros((EDGE, LANES), jnp.float32)
+    for index, part in enumerate(parts):
+        merged = jnp.where(block == index, roll(part, (2 * index + 1) * EDGE, 1), merged)
+    return merged
+
+
+def split_sides(merged, count):
+    lane = iota((EDGE, LANES), 1)
+    outer = (lane < EDGE) | (lane >= LANES - EDGE)
+    return [
+        jnp.where(outer, roll(merged, -(2 * index + 1) * EDGE, 1), 0.0) for index in range(count)
+    ]
+
+
 def middle_kernel(
     tiles,
     down,
@@ -461,27 +509,36 @@
         rows = slice(index * window, (index + 1) * window)
         coarse_ref[index, :, :LANES] = coarse_in[index, :, :LANES] + left[rows]
         coarse_ref[index, :, LANES:] = coarse_in[index, :, LANES:] + right[rows]
-    for slot, begin_row, coarse_at in (
-        (0, 2 * EDGE, 0),
-        (1, EDGE + height, window - 2 * EDGE),
+    fields = (obs, cond)
+    for slot, begin_row, first_row, over_row in (
+        (0, 2 * EDGE, EDGE, EDGE - 1),
+        (1, EDGE + height, window - 2 * EDGE, window - EDGE),
     ):
-        for which, field in enumerate((obs, cond)):
-            for t in range(tiles + 1):
-                at = (which * (tiles + 1) + t) * EDGE
-                message[slot, at : at + EDGE, :] = field[t, begin_row : begin_row + EDGE, :]
-        for index in range(4):
-            for half in range(2):
-                at = 2 * (tiles + 1) * EDGE + (2 * index + half) * 2 * EDGE
-                message[slot, at : at + 2 * EDGE, :] = coarse_ref[
-                    index, coarse_at : coarse_at + 2 * EDGE, half * LANES : (half + 1) * LANES
-                ]
+        pieces = [field[t, begin_row : begin_row + EDGE, :] for field in fields for t in range(tiles)]
+        rows = slice(first_row, first_row + EDGE)
+        pieces += [coarse_ref[index, rows, :LANES] for index in range(4)]
+        beyond = [coarse_ref[index, rows, LANES:] for index in range(4)]
+        beyond += [field[tiles, begin_row : begin_row + EDGE, :] for field in fields]
+        pieces.append(merge_sides(beyond))
+        pieces.append(
+            jnp.concatenate(
+                [
+                    coarse_ref[index, over_row : over_row + 1, half * LANES : (half + 1) * LANES]
+                    for index in range(4)
+                    for half in range(2)
+                ],
+                axis=0,
+            )
+        )
+        for index, piece in enumerate(pieces):
+            message[slot, index] = piece
     send_a[...], send_b[...] = in_pair_order(at_row, message[0], message[1])
 
 
 def middle(got_a, got_b, coarse, obs, cond):
     tiles, height = obs.shape[0] - 1, obs.shape[1] - 4 * EDGE
     down = height // COARSE
-    long = (2 * (tiles + 1) * EDGE + 16 * EDGE, LANES)
+    long = (2 * tiles + 6, EDGE, LANES)
     return pl.pallas_call(
         functools.partial(middle_kernel, tiles, down),
         in_specs=[VMEM] * 5,
@@ -494,35 +551,27 @@
     )(got_b, got_a, coarse, obs, cond)
 
 
-def inner_kernel(tiles, taps, obs, cond, res_ref, east_ref, south_ref, inv_ref, spread_ref):
-    strips = (obs.shape[1] - 2 * EDGE) // STRIP
+def inner_kernel(taps, obs, cond, res_ref, east_ref, south_ref, inv_ref):
     _, _, has_e, has_w = has_sides()
     clear_pads(east_ref, south_ref)
-    spread_ref[...] = spread_matrix(tiles)
     taps = read_taps(taps)
     sides = side_lanes(has_e, has_w)
 
-    def work(index, _):
-        at = strip_at(index + 1)
-        fields = begin(obs, cond, at, taps, sides)
-        return [
-            (ref, at, strip)
-            for ref, strip in zip((east_ref, south_ref, inv_ref, res_ref), fields)
-        ], 0
-
-    sweep(strips - 2, 1, work, 0)
+    def work(at, _, carry):
+        fields = begin(obs, cond, at, taps, sides, STRIP)
+        return list(zip((east_ref, south_ref, inv_ref, res_ref), fields)), carry
+
+    sweep(3 * EDGE, obs.shape[1] - 3 * EDGE, work, 0)
 
 
 def inner(taps, obs, cond):
     field = obs.shape
-    tiles = field[0] - 1
     pixels = field[0] * field[1] * field[2]
     return pl.pallas_call(
-        functools.partial(inner_kernel, tiles),
+        inner_kernel,
         in_specs=[SMEM] + [VMEM] * 2,
-        out_specs=[VMEM] * 5,
-        out_shape=floats(field, field, field, field)
-        + [jax.ShapeDtypeStruct((2 * LANES, (tiles + 1) * LANES), jnp.bfloat16)],
+        out_specs=[VMEM] * 4,
+        out_shape=floats(field, field, field, field),
         compiler_params=params(),
         cost_estimate=pl.CostEstimate(
             flops=45 * pixels, bytes_accessed=24 * pixels, transcendentals=0
@@ -544,7 +593,6 @@
     got_b,
     got_a,
     coarse_in,
-    matrix,
     obs,
     cond,
     res_ref,
@@ -562,26 +610,39 @@
 ):
     height = down * COARSE
     window = down + 2 * EDGE
-    strips = height // STRIP + 1
     at_col, at_row, n_cols, n_rows = place()
     has_n, has_s, has_e, has_w = has_sides()
-    from_s, from_n = in_pair_order(at_row, got_b[...], got_a[...])
     clear_pads(obs, cond, p_ref, image)
+    from_s, from_n = in_pair_order(
+        at_row, lambda index: got_b[index], lambda index: got_a[index]
+    )
+
+    def fill(t, _):
+        for which, field in enumerate((obs, cond)):
+            field[t, EDGE : 2 * EDGE, :] = from_n(which * tiles + t)
+            field[t, 2 * EDGE + height : 3 * EDGE + height, :] = from_s(which * tiles + t)
+        return 0
+
+    lax.fori_loop(0, tiles, fill, 0)
+    sides_n, sides_s = [split_sides(strip(2 * tiles + 4), 6) for strip in (from_n, from_s)]
     for which, field in enumerate((obs, cond)):
-        for t in range(tiles + 1):
-            at = (which * (tiles + 1) + t) * EDGE
-            field[t, EDGE : 2 * EDGE, :] = from_n[at : at + EDGE]
-            field[t, 2 * EDGE + height : 3 * EDGE + height, :] = from_s[at : at + EDGE]
-
-    base = 2 * (tiles + 1) * EDGE
+        field[tiles, EDGE : 2 * EDGE, :] = sides_n[4 + which]
+        field[tiles, 2 * EDGE + height : 3 * EDGE + height, :] = sides_s[4 + which]
 
     def joined(index):
-        def part(strip):
-            at = [base + (2 * index + half) * 2 * EDGE for half in range(2)]
-            return jnp.concatenate([strip[a : a + 2 * EDGE] for a in at], axis=1)
-
+        def parts(strip, beyond):
+            rows = jnp.concatenate([strip(2 * tiles + index), beyond[index]], axis=1)
+            over = strip(2 * tiles + 5)
+            over = [over[2 * index + half : 2 * index + half + 1] for half in range(2)]
+            return rows, jnp.concatenate(over, axis=1)
+
+        rows_n, over_n = parts(from_n, sides_n)
+        rows_s, over_s = parts(from_s, sides_s)
+        empty = jnp.zeros((EDGE - 1, 2 * LANES), jnp.float32)
         gap = jnp.zeros((window - 4 * EDGE, 2 * LANES), jnp.float32)
-        return coarse_in[index] + jnp.concatenate([part(from_n), gap, part(from_s)], axis=0)
+        return coarse_in[index] + jnp.concatenate(
+            [rows_n, over_n, empty, gap, empty, over_s, rows_s], axis=0
+        )
 
     source, east, south, around = [joined(index) for index in range(4)]
     row = iota(source.shape, 0)
@@ -597,60 +658,66 @@
     table = [factor] + [factor * weight for weight in weights]
     for index, part in enumerate(table):
         table_ref[index] = part
-    cells = split_dot(jacobi(source, table), matrix[...])
-    for t in range(tiles + 1):
-        spread[t] = cells[:, t * LANES : (t + 1) * LANES]
-
-    sides = side_lanes(has_e, has_w)
-    for index in (0, strips - 1):
-        at = EDGE + STRIP * index
-        fields = begin(obs, cond, at, taps, sides)
+    spread_cells(jacobi(source, table_ref), spread)
+
+    end_rows = 2 * EDGE
+    end_sides = side_lanes(has_e, has_w, end_rows)
+
+    def ends(index, _):
+        at = pl.multiple_of(EDGE + index * height, EDGE)
+        fields = begin(obs, cond, at, taps, end_sides, end_rows)
         for ref, strip in zip((east_ref, south_ref, inv_ref, res_ref), fields):
             store(ref, at, strip)
+        return 0
+
+    lax.fori_loop(0, 2, ends, 0)
     mask_rows(inv_ref, has_n, has_s)
-
-    def keeps(index):
-        return jnp.where(index > 0, 1.0, 0.0), jnp.where(index < strips - 1, 1.0, 0.0)
-
-    def start(index, total):
-        at = strip_at(index)
-        residual, inverse = load(res_ref, at), load(inv_ref, at)
-        cells = spread_strip(spread, index)
-        direction = [residual[t] * inverse[t] + cells[t] for t in range(tiles + 1)]
-        return [(p_ref, at, direction)], total + product_sum(
-            residual, direction, tiles, *keeps(index)
-        )
-
-    def blur(index, _):
-        at = strip_at(index)
-        blurred = conv(p_ref, at, taps, False)
-        blurred[tiles] = blurred[tiles] * sides
-        return [(image, at, blurred)], 0
-
-    def finish(index, total):
-        at = strip_at(index)
-        here, product = operate(p_ref, image, east_ref, south_ref, at, taps)
-        return [(q_ref, at, product)], total + product_sum(here, product, tiles, *keeps(index))
+    sides = side_lanes(has_e, has_w)
+
+    def flags(at, start):
+        rows = [at + by for by in range(0, STRIP, EDGE)]
+        first_row = jnp.maximum(start, 2 * EDGE)
+        return [
+            jnp.where((row >= first_row) & (row < 2 * EDGE + height), 1.0, 0.0) for row in rows
+        ]
+
+    def begin_p(at, start, total):
+        residual, inverse = reader_of(res_ref, at), reader_of(inv_ref, at)
+        strip = [
+            residual(t) * inverse(t) + cells_at(spread, at, STRIP, t) for t in range(tiles + 1)
+        ]
+        terms = [residual(t) * strip[t] for t in range(tiles)]
+        return [(p_ref, strip)], total + fold(sum(terms[1:], terms[0]), flags(at, start))
+
+    def blur(at, _, carry):
+        value = conv(p_ref, at, taps, False)
+        return [(image, [value(t) for t in range(tiles)] + [value(tiles) * sides])], carry
+
+    def finish(at, start, total):
+        here, value = operate(p_ref, image, east_ref, south_ref, at, taps)
+        product, term = [], 0.0
+        for t in range(tiles + 1):
+            product.append(value(t))
+            if t < tiles:
+                term = term + here(t) * product[t]
+        return [(q_ref, product)], total + fold(term, flags(at, start))
 
     nothing = jnp.zeros((EDGE, LANES), jnp.float32)
-    dots_ref[0] = sweep(strips, 2, start, nothing)
-    sweep(strips, 2, blur, 0)
+    span = (EDGE, 3 * EDGE + height)
+    dots_ref[0] = sweep(*span, begin_p, nothing)
+    sweep(*span, blur, 0)
     mask_rows(image, has_n, has_s)
-    dots_ref[1] = sweep(strips, 2, finish, nothing)
-
-    shape = (tiles * LANES, LANES)
-    matrix = jnp.where(iota(shape, 0) >> 3 == iota(shape, 1), 1.0, 0.0).astype(jnp.bfloat16)
-    flat = []
-    for t in range(tiles):
-        picked = [
-            q_ref[t, pl.ds(2 * EDGE + k, down, stride=COARSE), :] for k in range(COARSE)
-        ]
-        flat.append(sum(picked[1:], picked[0]))
-    own = split_dot(jnp.concatenate(flat, axis=1), matrix)
+    dots_ref[1] = sweep(*span, finish, nothing)
+
+    own = cell_sums(q_ref, tiles, down)
     own_ref[...] = own
     spare = jnp.zeros((LANES - down, LANES), jnp.float32)
     turned = jnp.transpose(jnp.concatenate([own, spare], axis=0))
-    chunk_ref[...] = jnp.zeros_like(chunk_ref)
+    def empty(index, _):
+        chunk_ref[index] = jnp.zeros((EDGE, LANES), jnp.float32)
+        return 0
+
+    lax.fori_loop(0, chunk_ref.shape[0], empty, 0)
     for down_by in (-1, 0, 1):
         for right_by in (-1, 0, 1):
             if down_by == 0 and right_by == 0:
@@ -666,7 +733,7 @@
                 chunk_ref[to_col * n_rows + to_row] = piece
 
 
-def first(taps, fields, got_a, got_b, coarse, matrix):
+def first(taps, fields, got_a, got_b, coarse):
     field = fields[0].shape
     tiles, height = field[0] - 1, field[1] - 4 * EDGE
     down = height // COARSE
@@ -680,7 +747,7 @@
     ]
     return pl.pallas_call(
         functools.partial(first_kernel, tiles, down),
-        in_specs=[SMEM] + [VMEM] * 10,
+        in_specs=[SMEM] + [VMEM] * 9,
         out_specs=[VMEM] * len(shapes),
         out_shape=floats(*shapes),
         input_output_aliases={index + 1: index for index in range(6)},
@@ -690,7 +757,7 @@
         ],
         compiler_params=params(),
         name="first_direction",
-    )(taps, *fields, got_b, got_a, coarse, matrix)[2:]
+    )(taps, *fields, got_b, got_a, coarse)[2:]
 
 
 def second_kernel(
@@ -705,7 +772,6 @@
     south_ref,
     inv_ref,
     dots_in,
-    matrix,
     w_ref,
     v_ref,
     out_ref,
@@ -713,7 +779,6 @@
     spread,
 ):
     height = down * COARSE
-    strips = height // STRIP + 1
     has_n, has_s, has_e, has_w = has_sides()
     at_col, at_row, n_cols, n_rows = place()
     me = at_col * n_rows + at_row
@@ -734,40 +799,39 @@
         ],
         axis=0,
     )
-    cells = jacobi(source, [table_ref[index] for index in range(5)])
-    cells = split_dot(cells, matrix[...])
-    for t in range(tiles + 1):
-        spread[t] = cells[:, t * LANES : (t + 1) * LANES]
+    spread_cells(jacobi(source, table_ref), spread)
     clear_pads(w_ref, image)
     sides = side_lanes(has_e, has_w)
     taps = read_taps(taps)
 
-    def start(index, _):
-        at = strip_at(index)
-        field, inverse = load(q_ref, at), load(inv_ref, at)
-        cells = spread_strip(spread, index)
-        return [(w_ref, at, [field[t] * inverse[t] + cells[t] for t in range(tiles + 1)])], 0
-
-    def blur(index, _):
-        at = strip_at(index)
-        blurred = conv(w_ref, at, taps, False)
-        blurred[tiles] = blurred[tiles] * sides
-        return [(image, at, blurred)], 0
-
-    def finish(index, totals):
-        at = pl.multiple_of(2 * EDGE + STRIP * index, EDGE)
-        here, product = operate(w_ref, image, east_ref, south_ref, at, taps)
-        field = load(q_ref, at)
-        return [(v_ref, at, product[:tiles])], (
-            totals[0] + product_sum(field, here, tiles),
-            totals[1] + product_sum(here, product, tiles),
+    def begin_w(at, _, carry):
+        field, inverse = reader_of(q_ref, at), reader_of(inv_ref, at)
+        strip = [
+            field(t) * inverse(t) + cells_at(spread, at, STRIP, t) for t in range(tiles + 1)
+        ]
+        return [(w_ref, strip)], carry
+
+    def blur(at, _, carry):
+        value = conv(w_ref, at, taps, False)
+        return [(image, [value(t) for t in range(tiles)] + [value(tiles) * sides])], carry
+
+    def finish(at, _, totals):
+        here, value = operate(w_ref, image, east_ref, south_ref, at, taps)
+        field = reader_of(q_ref, at)
+        product, terms = [], [0.0, 0.0]
+        for t in range(tiles):
+            product.append(value(t))
+            terms = [terms[0] + field(t) * here(t), terms[1] + here(t) * product[t]]
+        return [(v_ref, product)], tuple(
+            total + fold(term) for total, term in zip(totals, terms)
         )
 
     nothing = jnp.zeros((EDGE, LANES), jnp.float32)
-    sweep(strips, 2, start, 0)
-    sweep(strips, 2, blur, 0)
+    span = (EDGE, 3 * EDGE + height)
+    sweep(*span, begin_w, 0)
+    sweep(*span, blur, 0)
     mask_rows(image, has_n, has_s)
-    dot_qw, dot_wv = sweep(strips - 1, 2, finish, (nothing, nothing))
+    dot_qw, dot_wv = sweep(2 * EDGE, 2 * EDGE + height, finish, (nothing, nothing))
     line = jnp.zeros((1, LANES), jnp.float32)
     block = iota((1, LANES), 1) // (LANES // 4)
     for index, part in enumerate((dots_in[0], dots_in[1], dot_qw, dot_wv)):
@@ -779,14 +843,14 @@
         out_ref[index] = line
 
 
-def second(taps, got, own, table, q, east, south, inv, dots, matrix):
+def second(taps, got, own, table, q, east, south, inv, dots):
     tiles, height = q.shape[0] - 1, q.shape[1] - 4 * EDGE
     down = height // COARSE
     window = down + 2 * EDGE
     count = lax.axis_size("cols") * lax.axis_size("rows")
     return pl.pallas_call(
         functools.partial(second_kernel, tiles, down),
-        in_specs=[SMEM] + [VMEM] * 9,
+        in_specs=[SMEM] + [VMEM] * 8,
         out_specs=[VMEM] * 3,
         out_shape=floats(q.shape, q.shape, (count, 1, LANES)),
         scratch_shapes=[
@@ -795,7 +859,7 @@
         ],
         compiler_params=params(),
         name="second_direction",
-    )(taps, got, own, table, q, east, south, inv, dots, matrix)
+    )(taps, got, own, table, q, east, south, inv, dots)
 
 
 def combine_kernel(
@@ -884,13 +948,13 @@
     obs, cond, coarse = pack(*arguments, send_a)
     obs, cond, coarse, send_a, send_b = middle(got_a, got_b, coarse, obs, cond)
     got_a, got_b = exchange(send_a, send_b, "rows")
-    r, east, south, inv, matrix = inner(blur_kernel, obs, cond)
+    r, east, south, inv = inner(blur_kernel, obs, cond)
     fields = (obs, cond, r, east, south, inv)
     r, east, south, inv, p, q, table, own, chunk, dots = first(
-        blur_kernel, fields, got_a, got_b, coarse, matrix
+        blur_kernel, fields, got_a, got_b, coarse
     )
     got = lax.all_to_all(chunk, AXES, 0, 0, tiled=True)
-    w, v, line = second(blur_kernel, got, own, table, q, east, south, inv, dots, matrix)
+    w, v, line = second(blur_kernel, got, own, table, q, east, south, inv, dots)
     sums = lax.all_to_all(line, AXES, 0, 0, tiled=True)
     return tuple(combine(sums, p, w, r, q, v))
 

time: 52.8 us -> 53.3 us (level)
  Pallas kernels: 20.7 us -> 21.5 us
    pallas_call x1, Pallas kernels: 5.96 us -> 6.88 us  [first(): pl.pallas_call(functools.partial(first_kernel, tiles, down), in_specs=[SM...]
where the time goes in v3:
time: 53.3 us; the launch traced here: 53.1 us
  Pallas kernels  21.5 us (40%)
  blocking collectives  20.8 us (39%)
  starting transfers between devices  10 us (19%)
  between operations  0.73 us (1%)
    all_to_all x1, blocking collectives, body(): got = lax.all_to_all(chunk, AXES, 0, 0, tiled=True)  11.8 us
    all_to_all x1, blocking collectives, body(): sums = lax.all_to_all(line, AXES, 0, 0, tiled=True)  8.92 us
    ppermute x2, starting transfers between devices, exchange(): got_a = lax.ppermute(send_a, axis, pairs(0))  8.71 us
    pallas_call x1, Pallas kernels, first(): pl.pallas_call(functools.partial(first_kernel, tiles, down), in_specs=[SM...  6.88 us
    pallas_call x1, Pallas kernels, second(): pl.pallas_call(functools.partial(second_kernel, tiles, down), in_specs=[S...  5.38 us
    pallas_call x1, Pallas kernels, inner(): pl.pallas_call(inner_kernel, in_specs=[SMEM] + [VMEM] * 2, out_specs=[VME...  3.24 us
    pallas_call x1, Pallas kernels, pack(): pl.pallas_call(functools.partial(pack_kernel, tiles, down), in_specs=[HBM...  2.5 us
    pallas_call x1, Pallas kernels, edge(): pl.pallas_call(functools.partial(edge_kernel, tiles, down), in_specs=[HBM...  1.66 us
  transfers between devices with their start and end apart: 4, of which 0 were waited for; matrix products, arithmetic and copies ran while one was open for 0% of the time, Pallas kernels for 11%

profile of v3, /device:TPU:0, one launch (start us, length us, event | category | flops | bytes accessed | tf_op | source)
XLA Modules:
  0.0 53.1 jit_solution(12676843040056438019)
XLA Ops:
  0.6 1.7 %pack_east_west.1 = (f32[64,128]{1,0:T(8,128)S(1)}, f32[64,128]{1,0:T(8,128)S(1)}) custom-call(f32[256,1024]{1,0:T(8,128)} %refs_0_.3, s32[256,1024]{1,0:T(8,128)} %refs_1_.3, f32[4]{0:T(128)} %refs_2_.3, f32[3,3]{1,0:T(4,128)} %taps.5), custom_call_target="tpu_custom_call" | custom-call | tf_op jit(solution)/shard_map/pack_east_west/pallas_call | solution.py:404
  2.3 0.7 %collective-permute-start = (f32[64,128]{1,0:T(8,128)S(1)}, f32[64,128]{1,0:T(8,128)S(1)}, u32[]{:S(2)}, u32[]{:S(2)}) collective-permute-start(f32[64,128]{1,0:T(8,128)S(1)} %get-tuple-element.29), channel_id=1, source_target_pairs={{4,8},{8,4},{12,16},{16,12},{20,24},{24,20},{5,9},{9,5},{13,17},{1... | collective-permute-start | bytes 98312 | tf_op jit(solution)/shard_map/ppermute | solution.py:939
  3.0 5.8 %collective-permute-start.1 = (f32[64,128]{1,0:T(8,128)S(1)}, f32[64,128]{1,0:T(8,128)S(1)}, u32[]{:S(2)}, u32[]{:S(2)}) collective-permute-start(f32[64,128]{1,0:T(8,128)S(1)} %get-tuple-element.30.refs_4_), channel_id=1, source_target_pairs={{0,4},{4,0},{8,12},{12,8},{16,20},{20,16},{24,28},{28,24},{1,5},{5... | collective-permute-start | bytes 98312 | tf_op jit(solution)/shard_map/ppermute | solution.py:940
  8.8 2.5 %pack_all.1 = (f32[9,288,128]{2,1,0:T(8,128)S(1)}, f32[9,288,128]{2,1,0:T(8,128)S(1)}, f32[4,48,256]{2,1,0:T(8,128)S(1)}) custom-call(f32[256,1024]{1,0:T(8,128)} %refs_0_.3, s32[256,1024]{1,0:T(8,128)} %refs_1_.3, f32[4]{0:T(128)} %refs_2_.3, f32[3,3]{1,0:T(4,128)} %taps.5, f32[64,128]{1,0:T(8,128)S(1)} %get-tuple-element.30.refs_4_), custom_call_target="tpu_custom_call" | custom-call | flops 5242880 | bytes 4194304 | tf_op jit(solution)/shard_map/pack_all/pallas_call | solution.py:436
  11.3 0.0 collective-permute-done.got_b
  11.3 0.0 collective-permute-done.1.got_a
  11.3 0.0 copy-start
  11.3 0.3 pack_north_south.1
  11.6 0.7 %collective-permute-start.2 = (f32[22,8,128]{2,1,0:T(8,128)S(1)}, f32[22,8,128]{2,1,0:T(8,128)S(1)}, u32[]{:S(2)}, u32[]{:S(2)}) collective-permute-start(f32[22,8,128]{2,1,0:T(8,128)S(1)} %get-tuple-element.40), channel_id=1, source_target_pairs={{1,2},{2,1},{5,6},{6,5},{9,10},{10,9},{13,14},{14,13},{17,18},{18,... | collective-permute-start | bytes 270344 | tf_op jit(solution)/shard_map/ppermute | solution.py:939
  12.2 2.9 %collective-permute-start.3 = (f32[22,8,128]{2,1,0:T(8,128)S(1)}, f32[22,8,128]{2,1,0:T(8,128)S(1)}, u32[]{:S(2)}, u32[]{:S(2)}) collective-permute-start(f32[22,8,128]{2,1,0:T(8,128)S(1)} %get-tuple-element.41), channel_id=1, source_target_pairs={{0,1},{1,0},{2,3},{3,2},{4,5},{5,4},{6,7},{7,6},{8,9},{9,8},{10,11... | collective-permute-start | bytes 270344 | tf_op jit(solution)/shard_map/ppermute | solution.py:940
  15.2 0.0 copy-done
  15.2 3.2 %inner_strips.1 = (f32[9,288,128]{2,1,0:T(8,128)S(1)}, f32[9,288,128]{2,1,0:T(8,128)S(1)}, f32[9,288,128]{2,1,0:T(8,128)S(1)}, f32[9,288,128]{2,1,0:T(8,128)S(1)}) custom-call(f32[3,3]{1,0:T(4,128)S(1)} %copy-done, f32[9,288,128]{2,1,0:T(8,128)S(1)} %get-tuple-element.34.obs.obs_in, f32[9,288,128]{2,1,0:T(8,128)S(1)} %get-tuple-element.35.cond.cond_in), custom_call_target="tpu_custom_call" | custom-call | flops 14929920 | bytes 7962624 | tf_op jit(solution)/shard_map/inner_strips/pallas_call | solution.py:570
  18.4 0.0 collective-permute-done.2.got_b
  18.4 0.0 collective-permute-done.3.got_a
  18.4 6.9 %first_direction.1 = (f32[9,288,128]{2,1,0:T(8,128)S(1)}, f32[9,288,128]{2,1,0:T(8,128)S(1)}, f32[9,288,128]{2,1,0:T(8,128)S(1)}, f32[9,288,128]{2,1,0:T(8,128)S...) custom-call(f32[3,3]{1,0:T(4,128)S(1)} %copy-done, ...), custom_call_target="tpu_custom_call", output_to_operand_aliasing={{0}: (1, {}), {1}: (2, {}), {2}: (3, {}), {3}: (4, {}), {4}... | custom-call | tf_op jit(solution)/shard_map/first_direction/pallas_call | solution.py:748
  25.3 11.8 %all_to_all.10.got_ref = f32[32,8,128]{2,1,0:T(8,128)S(1)} all-to-all(f32[32,8,128]{2,1,0:T(8,128)S(1)} %get-tuple-element.43), channel_id=1, replica_groups=mesh['cols'=8,'rows'=4] {'cols','rows'}, dimensions={0} | all-to-all | bytes 262144 | tf_op jit(solution)/shard_map/all_to_all | solution.py:956
  37.1 5.4 %second_direction.1 = (f32[9,288,128]{2,1,0:T(8,128)S(1)}, f32[9,288,128]{2,1,0:T(8,128)S(1)}, f32[32,1,128]{2,1,0:T(1,128)S(1)}) custom-call(f32[3,3]{1,0:T(4,128)S(1)} %copy-done, f32[32,8,128]{2,1,0:T(8,128)S(1)} %all_to_all.10.got_ref, f32[32,128]{1,0:T(8,128)S(1)} %get-tuple-element.44.own_ref, f32[5,48,256]{2,1,0:T(8,128)S(1)} %get-tuple-element.45.table_ref, ...), custom_call_target="tpu_custom_call" | custom-call | tf_op jit(solution)/shard_map/second_direction/pallas_call | solution.py:851
  42.5 8.9 %all_to_all.11.sums_ref = f32[32,1,128]{2,1,0:T(1,128)S(1)} all-to-all(f32[32,1,128]{2,1,0:T(1,128)S(1)} %get-tuple-element.51), channel_id=1, replica_groups=mesh['cols'=8,'rows'=4] {'cols','rows'}, dimensions={0} | all-to-all | bytes 32768 | tf_op jit(solution)/shard_map/all_to_all | solution.py:958
  51.5 1.6 %combine.1 = (f32[256,1024]{1,0:T(8,128)}, f32[256,1024]{1,0:T(8,128)}) custom-call(f32[32,1,128]{2,1,0:T(1,128)S(1)} %all_to_all.11.sums_ref, f32[9,288,128]{2,1,0:T(8,128)S(1)} %get-tuple-element.52.p_ref, f32[9,288,128]{2,1,0:T(8,128)S(1)} %get-tuple-element.53.w_ref, f32[9,288,128]{2,1,0:T(8,128)S(1)} %get-tuple-element.54.r_ref, ...), custom_call_target="tpu_custom_call" | custom-call | tf_op jit(solution)/shard_map/combine/pallas_call | solution.py:916
Async XLA Ops:
  2.3 9.0 %collective-permute-start = (f32[64,128]{1,0:T(8,128)S(1)}, f32[64,128]{1,0:T(8,128)S(1)}, u32[]{:S(2)}, u32[]{:S(2)}) collective-permute-start(f32[64,128]{1,0:T(8,128)S(1)} %get-tuple-element.29), channel_id=1, source_target_pairs={{4,8},{8,4},{12,16},{16,12},{20,24},{24,20},{5,9},{9,5},{13,17},{1... | collective-permute-start | bytes 98312 | tf_op jit(solution)/shard_map/ppermute | solution.py:939
  3.0 8.3 %collective-permute-start.1 = (f32[64,128]{1,0:T(8,128)S(1)}, f32[64,128]{1,0:T(8,128)S(1)}, u32[]{:S(2)}, u32[]{:S(2)}) collective-permute-start(f32[64,128]{1,0:T(8,128)S(1)} %get-tuple-element.30.refs_4_), channel_id=1, source_target_pairs={{0,4},{4,0},{8,12},{12,8},{16,20},{20,16},{24,28},{28,24},{1,5},{5... | collective-permute-start | bytes 98312 | tf_op jit(solution)/shard_map/ppermute | solution.py:940
  11.3 3.9 %copy-start = (f32[3,3]{1,0:T(4,128)S(1)}, f32[3,3]{1,0:T(4,128)}, u32[]{:S(2)}) copy-start(f32[3,3]{1,0:T(4,128)} %taps.5) | copy-start | bytes 112
  11.6 6.8 %collective-permute-start.2 = (f32[22,8,128]{2,1,0:T(8,128)S(1)}, f32[22,8,128]{2,1,0:T(8,128)S(1)}, u32[]{:S(2)}, u32[]{:S(2)}) collective-permute-start(f32[22,8,128]{2,1,0:T(8,128)S(1)} %get-tuple-element.40), channel_id=1, source_target_pairs={{1,2},{2,1},{5,6},{6,5},{9,10},{10,9},{13,14},{14,13},{17,18},{18,... | collective-permute-start | bytes 270344 | tf_op jit(solution)/shard_map/ppermute | solution.py:939
  12.2 6.2 %collective-permute-start.3 = (f32[22,8,128]{2,1,0:T(8,128)S(1)}, f32[22,8,128]{2,1,0:T(8,128)S(1)}, u32[]{:S(2)}, u32[]{:S(2)}) collective-permute-start(f32[22,8,128]{2,1,0:T(8,128)S(1)} %get-tuple-element.41), channel_id=1, source_target_pairs={{0,1},{1,0},{2,3},{3,2},{4,5},{5,4},{6,7},{7,6},{8,9},{9,8},{10,11... | collective-permute-start | bytes 270344 | tf_op jit(solution)/shard_map/ppermute | solution.py:940

commit v4 on v3

--- a/solution.py
+++ b/solution.py
@@ -15,7 +15,9 @@
 LANES = 128
 HALF = LANES // 2
 EDGE = 8
-STRIP = 4 * EDGE
+STRIP = 2 * EDGE
+GROUP = 2
+CHUNK = 32
 AXES = ("cols", "rows")
 LIMIT = 40 * 1024 * 1024
 
@@ -104,78 +106,73 @@
     return sum(tap * tap if power == 2 else tap for line in taps for tap in line)
 
 
-def shifter(count, rows, make):
-    make = functools.cache(make)
-    west = functools.cache(lambda t: roll(make(t), 1, 1))
-    east = functools.cache(lambda t: roll(make(t), -1, 1))
-
-    def from_west(t):
-        lane = iota((rows, LANES), 1)
-        return jnp.where(lane == 0, west((t - 1) % count), west(t))
-
-    def from_east(t):
-        lane = iota((rows, LANES), 1)
-        return jnp.where(lane == LANES - 1, east((t + 1) % count), east(t))
-
-    return make, from_west, from_east
-
-
-def reader_of(ref, at, rows=STRIP):
-    return functools.cache(lambda t, by=0: ref[t, pl.ds(at + by, rows), :])
-
-
-def tap_sum(field, taps, flip, b):
+def from_west(strip):
+    lane = iota(strip[0].shape, 1)
+    turned = [roll(part, 1, 1) for part in strip]
+    return [jnp.where(lane == 0, turned[t - 1], turned[t]) for t in range(len(strip))]
+
+
+def from_east(strip):
+    lane = iota(strip[0].shape, 1)
+    turned = [roll(part, -1, 1) for part in strip]
+    count = len(strip)
+    return [
+        jnp.where(lane == LANES - 1, turned[(t + 1) % count], turned[t]) for t in range(count)
+    ]
+
+
+def tap_sums(ref, at, taps, flip):
     if flip:
         taps = [line[::-1] for line in taps[::-1]]
-    return lambda t: (
-        taps[0][b] * field(t, -1) + taps[1][b] * field(t) + taps[2][b] * field(t, 1)
-    )
-
-
-def conv(ref, at, taps, flip, rows=STRIP):
-    count = ref.shape[0]
-    field = reader_of(ref, at, rows)
-    sums = [tap_sum(field, taps, flip, b) for b in range(3)]
-    _, from_west, _ = shifter(count, rows, sums[0])
-    _, _, from_east = shifter(count, rows, sums[2])
-    return lambda t: sums[1](t) + from_west(t) + from_east(t)
+    above, here, below = load(ref, at - 1), load(ref, at), load(ref, at + 1)
+    sums = [[], [], []]
+    for t in range(len(here)):
+        for b in range(3):
+            sums[b].append(
+                taps[0][b] * above[t] + taps[1][b] * here[t] + taps[2][b] * below[t]
+            )
+    return sums
+
+
+def conv(ref, at, taps, flip):
+    sums = tap_sums(ref, at, taps, flip)
+    west, east = from_west(sums[0]), from_east(sums[2])
+    return [sums[1][t] + west[t] + east[t] for t in range(len(west))]
 
 
 def operate(ref, image, east_ref, south_ref, at, taps):
-    count = ref.shape[0]
-    field, picture = reader_of(ref, at), reader_of(image, at)
-    east, south = reader_of(east_ref, at), reader_of(south_ref, at)
-    here, _, beside = shifter(count, STRIP, field)
-    flux = functools.cache(lambda t: east(t) * (here(t) - beside(t)))
-    sums = [tap_sum(picture, taps, True, b) for b in range(3)]
-    _, from_west, _ = shifter(count, STRIP, lambda t: sums[0](t) - flux(t))
-    _, _, from_east = shifter(count, STRIP, sums[2])
-
-    def value(t):
-        down = south(t) * (here(t) - field(t, 1)) - south(t, -1) * (field(t, -1) - here(t))
-        return sums[1](t) + flux(t) + from_west(t) + from_east(t) + down
-
-    return here, value
-
-
-def begin(obs, cond, at, taps, sides, rows):
-    count = cond.shape[0]
-    level = reader_of(cond, at, rows)
-    here, _, right = shifter(count, rows, level)
-    east, west, _ = shifter(count, rows, lambda t: here(t) + right(t))
+    above, here, below = load(ref, at - 1), load(ref, at), load(ref, at + 1)
+    east, south, north = load(east_ref, at), load(south_ref, at), load(south_ref, at - 1)
+    sums = tap_sums(image, at, taps, True)
+    span = range(len(here))
+    beside = from_east(here)
+    flux = [east[t] * (here[t] - beside[t]) for t in span]
+    from_left = from_west([sums[0][t] - flux[t] for t in span])
+    from_right = from_east(sums[2])
+    return here, [
+        sums[1][t]
+        + flux[t]
+        + from_left[t]
+        + from_right[t]
+        + south[t] * (here[t] - below[t])
+        - north[t] * (above[t] - here[t])
+        for t in span
+    ]
+
+
+def begin(obs, cond, at, taps, sides):
+    above, here, below = load(cond, at - 1), load(cond, at), load(cond, at + 1)
+    span = range(len(here))
+    right = from_east(here)
+    east = [here[t] + right[t] for t in span]
+    west = from_west(east)
+    south = [here[t] + below[t] for t in span]
     squares = tap_total(taps, 2)
-    residual = conv(obs, at, taps, True, rows)
-    fields = [[], [], [], []]
-    for t in range(count):
-        south = here(t) + level(t, 1)
-        diag = squares + east(t) + west(t) + south + (here(t) + level(t, -1))
-        inverse = pl.reciprocal(diag, approx=True)
-        inverse = inverse * (2.0 - diag * inverse)
-        if t == count - 1:
-            inverse = inverse * sides
-        for strip, part in zip(fields, (east(t), south, inverse, residual(t))):
-            strip.append(part)
-    return fields
+    diag = [squares + east[t] + west[t] + south[t] + (here[t] + above[t]) for t in span]
+    inverse = [pl.reciprocal(part, approx=True) for part in diag]
+    inverse = [inverse[t] * (2.0 - diag[t] * inverse[t]) for t in span]
+    inverse[-1] = inverse[-1] * sides
+    return east, south, inverse, conv(obs, at, taps, True)
 
 
 def pick_lanes(field, lanes):
@@ -191,13 +188,13 @@
     spread[tiles] = pick_lanes(cells[:, LANES:], (lane >> 3) + turn)
 
 
-def cells_at(spread, at, rows, t):
+def cells_at(spread, at):
     first = at // EDGE + EDGE - 2
-    parts = [
-        jnp.broadcast_to(spread[t, pl.ds(first + index, 1), :], (EDGE, LANES))
-        for index in range(rows // EDGE)
+    rows = [load(spread, first + index, 1) for index in range(STRIP // EDGE)]
+    return [
+        jnp.concatenate([jnp.broadcast_to(row, (EDGE, LANES)) for row in parts], axis=0)
+        for parts in zip(*rows)
     ]
-    return jnp.concatenate(parts, axis=0)
 
 
 def cell_sums(ref, tiles, down):
@@ -215,8 +212,8 @@
     return total
 
 
-def side_lanes(has_e, has_w, rows=STRIP):
-    return jnp.where(iota((rows, LANES), 1) < HALF, has_e, has_w)
+def side_lanes(has_e, has_w):
+    return jnp.where(iota((STRIP, LANES), 1) < HALF, has_e, has_w)
 
 
 def mask_rows(ref, has_n, has_s):
@@ -241,6 +238,13 @@
     lax.fori_loop(0, refs[0].shape[0], work, 0)
 
 
+def product_sum(one, two, count, flags=None):
+    total = one[0] * two[0]
+    for t in range(1, count):
+        total = total + one[t] * two[t]
+    return fold(total, flags)
+
+
 def fold(total, flags=None):
     parts = [total[at : at + EDGE] for at in range(0, total.shape[0], EDGE)]
     if flags is not None:
@@ -249,14 +253,18 @@
 
 
 def sweep(first, last, body, carry):
-    steps = -(-(last - first) // STRIP)
+    width = GROUP * STRIP
+    steps = -(-(last - first) // width)
 
     def work(index, carry):
-        start = first + index * STRIP
-        at = pl.multiple_of(jnp.minimum(start, last - STRIP), EDGE)
-        stores, carry = body(at, start, carry)
-        for ref, strip in stores:
-            store(ref, at, strip)
+        start = first + index * width
+        at = pl.multiple_of(jnp.minimum(start, last - width), EDGE)
+        pending = []
+        for by in range(0, width, STRIP):
+            stores, carry = body(at + by, start, carry)
+            pending += [(ref, at + by, strip) for ref, strip in stores]
+        for ref, row, strip in pending:
+            store(ref, row, strip)
         return carry
 
     return lax.fori_loop(0, steps, work, carry)
@@ -558,7 +566,7 @@
     sides = side_lanes(has_e, has_w)
 
     def work(at, _, carry):
-        fields = begin(obs, cond, at, taps, sides, STRIP)
+        fields = begin(obs, cond, at, taps, sides)
         return list(zip((east_ref, south_ref, inv_ref, res_ref), fields)), carry
 
     sweep(3 * EDGE, obs.shape[1] - 3 * EDGE, work, 0)
@@ -660,19 +668,17 @@
         table_ref[index] = part
     spread_cells(jacobi(source, table_ref), spread)
 
-    end_rows = 2 * EDGE
-    end_sides = side_lanes(has_e, has_w, end_rows)
+    sides = side_lanes(has_e, has_w)
 
     def ends(index, _):
         at = pl.multiple_of(EDGE + index * height, EDGE)
-        fields = begin(obs, cond, at, taps, end_sides, end_rows)
+        fields = begin(obs, cond, at, taps, sides)
         for ref, strip in zip((east_ref, south_ref, inv_ref, res_ref), fields):
             store(ref, at, strip)
         return 0
 
     lax.fori_loop(0, 2, ends, 0)
     mask_rows(inv_ref, has_n, has_s)
-    sides = side_lanes(has_e, has_w)
 
     def flags(at, start):
         rows = [at + by for by in range(0, STRIP, EDGE)]
@@ -682,25 +688,18 @@
         ]
 
     def begin_p(at, start, total):
-        residual, inverse = reader_of(res_ref, at), reader_of(inv_ref, at)
-        strip = [
-            residual(t) * inverse(t) + cells_at(spread, at, STRIP, t) for t in range(tiles + 1)
-        ]
-        terms = [residual(t) * strip[t] for t in range(tiles)]
-        return [(p_ref, strip)], total + fold(sum(terms[1:], terms[0]), flags(at, start))
+        residual, inverse, cells = load(res_ref, at), load(inv_ref, at), cells_at(spread, at)
+        strip = [residual[t] * inverse[t] + cells[t] for t in range(tiles + 1)]
+        return [(p_ref, strip)], total + product_sum(residual, strip, tiles, flags(at, start))
 
     def blur(at, _, carry):
-        value = conv(p_ref, at, taps, False)
-        return [(image, [value(t) for t in range(tiles)] + [value(tiles) * sides])], carry
+        strip = conv(p_ref, at, taps, False)
+        strip[tiles] = strip[tiles] * sides
+        return [(image, strip)], carry
 
     def finish(at, start, total):
-        here, value = operate(p_ref, image, east_ref, south_ref, at, taps)
-        product, term = [], 0.0
-        for t in range(tiles + 1):
-            product.append(value(t))
-            if t < tiles:
-                term = term + here(t) * product[t]
-        return [(q_ref, product)], total + fold(term, flags(at, start))
+        here, product = operate(p_ref, image, east_ref, south_ref, at, taps)
+        return [(q_ref, product)], total + product_sum(here, product, tiles, flags(at, start))
 
     nothing = jnp.zeros((EDGE, LANES), jnp.float32)
     span = (EDGE, 3 * EDGE + height)
@@ -805,25 +804,20 @@
     taps = read_taps(taps)
 
     def begin_w(at, _, carry):
-        field, inverse = reader_of(q_ref, at), reader_of(inv_ref, at)
-        strip = [
-            field(t) * inverse(t) + cells_at(spread, at, STRIP, t) for t in range(tiles + 1)
-        ]
-        return [(w_ref, strip)], carry
+        field, inverse, cells = load(q_ref, at), load(inv_ref, at), cells_at(spread, at)
+        return [(w_ref, [field[t] * inverse[t] + cells[t] for t in range(tiles + 1)])], carry
 
     def blur(at, _, carry):
-        value = conv(w_ref, at, taps, False)
-        return [(image, [value(t) for t in range(tiles)] + [value(tiles) * sides])], carry
+        strip = conv(w_ref, at, taps, False)
+        strip[tiles] = strip[tiles] * sides
+        return [(image, strip)], carry
 
     def finish(at, _, totals):
-        here, value = operate(w_ref, image, east_ref, south_ref, at, taps)
-        field = reader_of(q_ref, at)
-        product, terms = [], [0.0, 0.0]
-        for t in range(tiles):
-            product.append(value(t))
-            terms = [terms[0] + field(t) * here(t), terms[1] + here(t) * product[t]]
-        return [(v_ref, product)], tuple(
-            total + fold(term) for total, term in zip(totals, terms)
+        here, product = operate(w_ref, image, east_ref, south_ref, at, taps)
+        field = load(q_ref, at)
+        return [(v_ref, product[:tiles])], (
+            totals[0] + product_sum(field, here, tiles),
+            totals[1] + product_sum(here, product, tiles),
         )
 
     nothing = jnp.zeros((EDGE, LANES), jnp.float32)
@@ -877,26 +871,26 @@
     lead = 1.0 + ratio
     curvature = lead * lead * pq - 2.0 * lead * step * qw + step * step * wv
     step_next = rp_next / curvature
-    on_p = jnp.broadcast_to(step + step_next * lead, (STRIP, LANES))
-    on_w = jnp.broadcast_to(step_next * step, (STRIP, LANES))
+    on_p = jnp.broadcast_to(step + step_next * lead, (CHUNK, LANES))
+    on_w = jnp.broadcast_to(step_next * step, (CHUNK, LANES))
 
     def copies(index):
-        rows = pl.ds(pl.multiple_of(index * STRIP, STRIP), STRIP)
+        rows = pl.ds(pl.multiple_of(index * CHUNK, CHUNK), CHUNK)
         return (
             pltpu.make_async_copy(sol.at[rows, :], sol_out.at[rows, :], sem.at[0, index]),
             pltpu.make_async_copy(res.at[rows, :], res_out.at[rows, :], sem.at[1, index]),
         )
 
     def work(index, _):
-        at = pl.multiple_of(index * STRIP, STRIP)
+        at = pl.multiple_of(index * CHUNK, CHUNK)
         p, w, r, q, v = [
-            load(ref, at + 2 * EDGE) for ref in (p_ref, w_ref, r_ref, q_ref, v_ref)
+            load(ref, at + 2 * EDGE, CHUNK) for ref in (p_ref, w_ref, r_ref, q_ref, v_ref)
         ]
         one = [on_p * p[t] - on_w * w[t] for t in range(tiles)]
         two = [r[t] - on_p * q[t] + on_w * v[t] for t in range(tiles)]
         for t in range(tiles):
-            sol[pl.ds(at, STRIP), t * LANES : (t + 1) * LANES] = one[t]
-            res[pl.ds(at, STRIP), t * LANES : (t + 1) * LANES] = two[t]
+            sol[pl.ds(at, CHUNK), t * LANES : (t + 1) * LANES] = one[t]
+            res[pl.ds(at, CHUNK), t * LANES : (t + 1) * LANES] = two[t]
         for copy in copies(index):
             copy.start()
         return 0
@@ -906,8 +900,8 @@
             copy.wait()
         return 0
 
-    lax.fori_loop(0, height // STRIP, work, 0)
-    lax.fori_loop(0, height // STRIP, settle, 0)
+    lax.fori_loop(0, height // CHUNK, work, 0)
+    lax.fori_loop(0, height // CHUNK, settle, 0)
 
 
 def combine(sums, p, w, r, q, v):
@@ -921,7 +915,7 @@
         scratch_shapes=[
             pltpu.VMEM(shape, jnp.float32),
             pltpu.VMEM(shape, jnp.float32),
-            pltpu.SemaphoreType.DMA((2, height // STRIP)),
+            pltpu.SemaphoreType.DMA((2, height // CHUNK)),
         ],
         compiler_params=params(),
         name="combine",

time: 53.3 us -> 53.2 us (level)
  transfers between devices with their start and end apart: 4 -> 4, of which waited for: 0 -> 0; matrix products, arithmetic and copies ran while one was open for 0% -> 0% of each run, Pallas kernels for 11% -> 10%
where the time goes in v4:
time: 53.2 us; the launch traced here: 53 us
  Pallas kernels  21.4 us (40%)
  blocking collectives  20.9 us (39%)
  starting transfers between devices  10 us (19%)
  between operations  0.73 us (1%)
    all_to_all x1, blocking collectives, body(): got = lax.all_to_all(chunk, AXES, 0, 0, tiled=True)  11.9 us
    all_to_all x1, blocking collectives, body(): sums = lax.all_to_all(line, AXES, 0, 0, tiled=True)  8.92 us
    ppermute x2, starting transfers between devices, exchange(): got_a = lax.ppermute(send_a, axis, pairs(0))  8.71 us
    pallas_call x1, Pallas kernels, first(): pl.pallas_call(functools.partial(first_kernel, tiles, down), in_specs=[SM...  6.96 us
    pallas_call x1, Pallas kernels, second(): pl.pallas_call(functools.partial(second_kernel, tiles, down), in_specs=[S...  5.34 us
    pallas_call x1, Pallas kernels, inner(): pl.pallas_call(inner_kernel, in_specs=[SMEM] + [VMEM] * 2, out_specs=[VME...  3.05 us
    pallas_call x1, Pallas kernels, pack(): pl.pallas_call(functools.partial(pack_kernel, tiles, down), in_specs=[HBM...  2.5 us
    pallas_call x1, Pallas kernels, edge(): pl.pallas_call(functools.partial(edge_kernel, tiles, down), in_specs=[HBM...  1.66 us
  transfers between devices with their start and end apart: 4, of which 0 were waited for; matrix products, arithmetic and copies ran while one was open for 0% of the time, Pallas kernels for 10%

profile of v4, /device:TPU:0, one launch (start us, length us, event | category | flops | bytes accessed | tf_op | source)
XLA Modules:
  0.0 53.0 jit_solution(15286330808362409580)
XLA Ops:
  0.6 1.7 %pack_east_west.1 = (f32[64,128]{1,0:T(8,128)S(1)}, f32[64,128]{1,0:T(8,128)S(1)}) custom-call(f32[256,1024]{1,0:T(8,128)} %refs_0_.3, s32[256,1024]{1,0:T(8,128)} %refs_1_.3, f32[4]{0:T(128)} %refs_2_.3, f32[3,3]{1,0:T(4,128)} %taps.5), custom_call_target="tpu_custom_call" | custom-call | tf_op jit(solution)/shard_map/pack_east_west/pallas_call | solution.py:412
  2.3 0.7 %collective-permute-start = (f32[64,128]{1,0:T(8,128)S(1)}, f32[64,128]{1,0:T(8,128)S(1)}, u32[]{:S(2)}, u32[]{:S(2)}) collective-permute-start(f32[64,128]{1,0:T(8,128)S(1)} %get-tuple-element.29), channel_id=1, source_target_pairs={{4,8},{8,4},{12,16},{16,12},{20,24},{24,20},{5,9},{9,5},{13,17},{1... | collective-permute-start | bytes 98312 | tf_op jit(solution)/shard_map/ppermute | solution.py:933
  3.0 5.8 %collective-permute-start.1 = (f32[64,128]{1,0:T(8,128)S(1)}, f32[64,128]{1,0:T(8,128)S(1)}, u32[]{:S(2)}, u32[]{:S(2)}) collective-permute-start(f32[64,128]{1,0:T(8,128)S(1)} %get-tuple-element.30.refs_4_), channel_id=1, source_target_pairs={{0,4},{4,0},{8,12},{12,8},{16,20},{20,16},{24,28},{28,24},{1,5},{5... | collective-permute-start | bytes 98312 | tf_op jit(solution)/shard_map/ppermute | solution.py:934
  8.8 2.5 %pack_all.1 = (f32[9,288,128]{2,1,0:T(8,128)S(1)}, f32[9,288,128]{2,1,0:T(8,128)S(1)}, f32[4,48,256]{2,1,0:T(8,128)S(1)}) custom-call(f32[256,1024]{1,0:T(8,128)} %refs_0_.3, s32[256,1024]{1,0:T(8,128)} %refs_1_.3, f32[4]{0:T(128)} %refs_2_.3, f32[3,3]{1,0:T(4,128)} %taps.5, f32[64,128]{1,0:T(8,128)S(1)} %get-tuple-element.30.refs_4_), custom_call_target="tpu_custom_call" | custom-call | flops 5242880 | bytes 4194304 | tf_op jit(solution)/shard_map/pack_all/pallas_call | solution.py:444
  11.3 0.0 collective-permute-done.got_b
  11.3 0.0 collective-permute-done.1.got_a
  11.3 0.0 copy-start
  11.3 0.3 pack_north_south.1
  11.6 0.7 %collective-permute-start.2 = (f32[22,8,128]{2,1,0:T(8,128)S(1)}, f32[22,8,128]{2,1,0:T(8,128)S(1)}, u32[]{:S(2)}, u32[]{:S(2)}) collective-permute-start(f32[22,8,128]{2,1,0:T(8,128)S(1)} %get-tuple-element.40), channel_id=1, source_target_pairs={{1,2},{2,1},{5,6},{6,5},{9,10},{10,9},{13,14},{14,13},{17,18},{18,... | collective-permute-start | bytes 270344 | tf_op jit(solution)/shard_map/ppermute | solution.py:933
  12.2 2.9 %collective-permute-start.3 = (f32[22,8,128]{2,1,0:T(8,128)S(1)}, f32[22,8,128]{2,1,0:T(8,128)S(1)}, u32[]{:S(2)}, u32[]{:S(2)}) collective-permute-start(f32[22,8,128]{2,1,0:T(8,128)S(1)} %get-tuple-element.41), channel_id=1, source_target_pairs={{0,1},{1,0},{2,3},{3,2},{4,5},{5,4},{6,7},{7,6},{8,9},{9,8},{10,11... | collective-permute-start | bytes 270344 | tf_op jit(solution)/shard_map/ppermute | solution.py:934
  15.2 0.0 copy-done
  15.2 3.1 %inner_strips.1 = (f32[9,288,128]{2,1,0:T(8,128)S(1)}, f32[9,288,128]{2,1,0:T(8,128)S(1)}, f32[9,288,128]{2,1,0:T(8,128)S(1)}, f32[9,288,128]{2,1,0:T(8,128)S(1)}) custom-call(f32[3,3]{1,0:T(4,128)S(1)} %copy-done, f32[9,288,128]{2,1,0:T(8,128)S(1)} %get-tuple-element.34.obs.obs_in, f32[9,288,128]{2,1,0:T(8,128)S(1)} %get-tuple-element.35.cond.cond_in), custom_call_target="tpu_custom_call" | custom-call | flops 14929920 | bytes 7962624 | tf_op jit(solution)/shard_map/inner_strips/pallas_call | solution.py:578
  18.2 0.0 collective-permute-done.2.got_b
  18.2 0.0 collective-permute-done.3.got_a
  18.2 7.0 %first_direction.1 = (f32[9,288,128]{2,1,0:T(8,128)S(1)}, f32[9,288,128]{2,1,0:T(8,128)S(1)}, f32[9,288,128]{2,1,0:T(8,128)S(1)}, f32[9,288,128]{2,1,0:T(8,128)S...) custom-call(f32[3,3]{1,0:T(4,128)S(1)} %copy-done, ...), custom_call_target="tpu_custom_call", output_to_operand_aliasing={{0}: (1, {}), {1}: (2, {}), {2}: (3, {}), {3}: (4, {}), {4}... | custom-call | tf_op jit(solution)/shard_map/first_direction/pallas_call | solution.py:747
  25.2 11.9 %all_to_all.10.got_ref = f32[32,8,128]{2,1,0:T(8,128)S(1)} all-to-all(f32[32,8,128]{2,1,0:T(8,128)S(1)} %get-tuple-element.43), channel_id=1, replica_groups=mesh['cols'=8,'rows'=4] {'cols','rows'}, dimensions={0} | all-to-all | bytes 262144 | tf_op jit(solution)/shard_map/all_to_all | solution.py:950
  37.1 5.3 %second_direction.1 = (f32[9,288,128]{2,1,0:T(8,128)S(1)}, f32[9,288,128]{2,1,0:T(8,128)S(1)}, f32[32,1,128]{2,1,0:T(1,128)S(1)}) custom-call(f32[3,3]{1,0:T(4,128)S(1)} %copy-done, f32[32,8,128]{2,1,0:T(8,128)S(1)} %all_to_all.10.got_ref, f32[32,128]{1,0:T(8,128)S(1)} %get-tuple-element.44.own_ref, f32[5,48,256]{2,1,0:T(8,128)S(1)} %get-tuple-element.45.table_ref, ...), custom_call_target="tpu_custom_call" | custom-call | tf_op jit(solution)/shard_map/second_direction/pallas_call | solution.py:845
  42.5 8.9 %all_to_all.11.sums_ref = f32[32,1,128]{2,1,0:T(1,128)S(1)} all-to-all(f32[32,1,128]{2,1,0:T(1,128)S(1)} %get-tuple-element.51), channel_id=1, replica_groups=mesh['cols'=8,'rows'=4] {'cols','rows'}, dimensions={0} | all-to-all | bytes 32768 | tf_op jit(solution)/shard_map/all_to_all | solution.py:952
  51.4 1.6 %combine.1 = (f32[256,1024]{1,0:T(8,128)}, f32[256,1024]{1,0:T(8,128)}) custom-call(f32[32,1,128]{2,1,0:T(1,128)S(1)} %all_to_all.11.sums_ref, f32[9,288,128]{2,1,0:T(8,128)S(1)} %get-tuple-element.52.p_ref, f32[9,288,128]{2,1,0:T(8,128)S(1)} %get-tuple-element.53.w_ref, f32[9,288,128]{2,1,0:T(8,128)S(1)} %get-tuple-element.54.r_ref, ...), custom_call_target="tpu_custom_call" | custom-call | tf_op jit(solution)/shard_map/combine/pallas_call | solution.py:910
Async XLA Ops:
  2.3 9.0 %collective-permute-start = (f32[64,128]{1,0:T(8,128)S(1)}, f32[64,128]{1,0:T(8,128)S(1)}, u32[]{:S(2)}, u32[]{:S(2)}) collective-permute-start(f32[64,128]{1,0:T(8,128)S(1)} %get-tuple-element.29), channel_id=1, source_target_pairs={{4,8},{8,4},{12,16},{16,12},{20,24},{24,20},{5,9},{9,5},{13,17},{1... | collective-permute-start | bytes 98312 | tf_op jit(solution)/shard_map/ppermute | solution.py:933
  3.0 8.3 %collective-permute-start.1 = (f32[64,128]{1,0:T(8,128)S(1)}, f32[64,128]{1,0:T(8,128)S(1)}, u32[]{:S(2)}, u32[]{:S(2)}) collective-permute-start(f32[64,128]{1,0:T(8,128)S(1)} %get-tuple-element.30.refs_4_), channel_id=1, source_target_pairs={{0,4},{4,0},{8,12},{12,8},{16,20},{20,16},{24,28},{28,24},{1,5},{5... | collective-permute-start | bytes 98312 | tf_op jit(solution)/shard_map/ppermute | solution.py:934
  11.3 3.9 %copy-start = (f32[3,3]{1,0:T(4,128)S(1)}, f32[3,3]{1,0:T(4,128)}, u32[]{:S(2)}) copy-start(f32[3,3]{1,0:T(4,128)} %taps.5) | copy-start | bytes 112
  11.6 6.6 %collective-permute-start.2 = (f32[22,8,128]{2,1,0:T(8,128)S(1)}, f32[22,8,128]{2,1,0:T(8,128)S(1)}, u32[]{:S(2)}, u32[]{:S(2)}) collective-permute-start(f32[22,8,128]{2,1,0:T(8,128)S(1)} %get-tuple-element.40), channel_id=1, source_target_pairs={{1,2},{2,1},{5,6},{6,5},{9,10},{10,9},{13,14},{14,13},{17,18},{18,... | collective-permute-start | bytes 270344 | tf_op jit(solution)/shard_map/ppermute | solution.py:933
  12.2 6.0 %collective-permute-start.3 = (f32[22,8,128]{2,1,0:T(8,128)S(1)}, f32[22,8,128]{2,1,0:T(8,128)S(1)}, u32[]{:S(2)}, u32[]{:S(2)}) collective-permute-start(f32[22,8,128]{2,1,0:T(8,128)S(1)} %get-tuple-element.41), channel_id=1, source_target_pairs={{0,1},{1,0},{2,3},{3,2},{4,5},{5,4},{6,7},{7,6},{8,9},{9,8},{10,11... | collective-permute-start | bytes 270344 | tf_op jit(solution)/shard_map/ppermute | solution.py:934

commit v5 on v4

--- a/solution.py
+++ b/solution.py
@@ -218,24 +218,15 @@
 
 def mask_rows(ref, has_n, has_s):
     last = ref.shape[1] - 2 * EDGE
-
-    def work(t, _):
-        for at, flag in ((EDGE, has_n), (last, has_s)):
-            ref[t, at : at + EDGE, :] = ref[t, at : at + EDGE, :] * flag
-        return 0
-
-    lax.fori_loop(0, ref.shape[0], work, 0)
+    for at, flag in ((EDGE, has_n), (last, has_s)):
+        ref[:, at : at + EDGE, :] = ref[:, at : at + EDGE, :] * flag
 
 
 def clear_pads(*refs):
-    def work(t, _):
-        empty = jnp.zeros((EDGE, LANES), jnp.float32)
-        for ref in refs:
-            ref[t, :EDGE, :] = empty
-            ref[t, ref.shape[1] - EDGE :, :] = empty
-        return 0
-
-    lax.fori_loop(0, refs[0].shape[0], work, 0)
+    empty = jnp.zeros((refs[0].shape[0], EDGE, LANES), jnp.float32)
+    for ref in refs:
+        ref[:, :EDGE, :] = empty
+        ref[:, ref.shape[1] - EDGE :, :] = empty
 
 
 def product_sum(one, two, count, flags=None):
@@ -271,14 +262,14 @@
 
 
 def jacobi(source, table):
-    source = table[0] * source
-
-    def work(_, iterate):
-        across = table[1] * roll(iterate, -1, 1) + table[2] * roll(iterate, 1, 1)
-        along = table[3] * roll(iterate, -1, 0) + table[4] * roll(iterate, 1, 0)
-        return ((1.0 - OMEGA) * iterate + source) + (across + along)
-
-    return lax.fori_loop(0, SWEEPS - 1, work, source)
+    factor, east, west, south, north = [table[index] for index in range(5)]
+    source = factor * source
+    iterate = source
+    for _ in range(SWEEPS - 1):
+        across = east * roll(iterate, -1, 1) + west * roll(iterate, 1, 1)
+        along = south * roll(iterate, -1, 0) + north * roll(iterate, 1, 0)
+        iterate = ((1.0 - OMEGA) * iterate + source) + (across + along)
+    return iterate
 
 
 def in_pair_order(at, for_before, for_after):
@@ -625,32 +616,36 @@
         at_row, lambda index: got_b[index], lambda index: got_a[index]
     )
 
-    def fill(t, _):
-        for which, field in enumerate((obs, cond)):
+    for which, field in enumerate((obs, cond)):
+        for t in range(tiles):
             field[t, EDGE : 2 * EDGE, :] = from_n(which * tiles + t)
             field[t, 2 * EDGE + height : 3 * EDGE + height, :] = from_s(which * tiles + t)
-        return 0
-
-    lax.fori_loop(0, tiles, fill, 0)
     sides_n, sides_s = [split_sides(strip(2 * tiles + 4), 6) for strip in (from_n, from_s)]
     for which, field in enumerate((obs, cond)):
         field[tiles, EDGE : 2 * EDGE, :] = sides_n[4 + which]
         field[tiles, 2 * EDGE + height : 3 * EDGE + height, :] = sides_s[4 + which]
 
+    edge_row = iota((EDGE, 2 * LANES), 0)
+
     def joined(index):
-        def parts(strip, beyond):
-            rows = jnp.concatenate([strip(2 * tiles + index), beyond[index]], axis=1)
-            over = strip(2 * tiles + 5)
-            over = [over[2 * index + half : 2 * index + half + 1] for half in range(2)]
-            return rows, jnp.concatenate(over, axis=1)
-
-        rows_n, over_n = parts(from_n, sides_n)
-        rows_s, over_s = parts(from_s, sides_s)
-        empty = jnp.zeros((EDGE - 1, 2 * LANES), jnp.float32)
-        gap = jnp.zeros((window - 4 * EDGE, 2 * LANES), jnp.float32)
-        return coarse_in[index] + jnp.concatenate(
-            [rows_n, over_n, empty, gap, empty, over_s, rows_s], axis=0
-        )
+        def over(strip, row):
+            line = [
+                jnp.broadcast_to(
+                    strip((2 * tiles + 5, pl.ds(2 * index + half, 1))), (EDGE, LANES)
+                )
+                for half in range(2)
+            ]
+            return jnp.where(edge_row == row, jnp.concatenate(line, axis=1), 0.0)
+
+        def rows(strip, beyond):
+            return jnp.concatenate([strip(2 * tiles + index), beyond[index]], axis=1)
+
+        parts = [coarse_in[index, at : at + EDGE, :] for at in range(0, window, EDGE)]
+        parts[0] = parts[0] + rows(from_n, sides_n)
+        parts[1] = parts[1] + over(from_n, 0)
+        parts[-2] = parts[-2] + over(from_s, EDGE - 1)
+        parts[-1] = parts[-1] + rows(from_s, sides_s)
+        return jnp.concatenate(parts, axis=0)
 
     source, east, south, around = [joined(index) for index in range(4)]
     row = iota(source.shape, 0)
@@ -666,19 +661,21 @@
     table = [factor] + [factor * weight for weight in weights]
     for index, part in enumerate(table):
         table_ref[index] = part
-    spread_cells(jacobi(source, table_ref), spread)
-
     sides = side_lanes(has_e, has_w)
-
-    def ends(index, _):
-        at = pl.multiple_of(EDGE + index * height, EDGE)
+    half = iota((STRIP, LANES), 0) // EDGE
+    pending = []
+    for index, known in ((0, has_n), (1, has_s)):
+        at = EDGE + index * height
         fields = begin(obs, cond, at, taps, sides)
-        for ref, strip in zip((east_ref, south_ref, inv_ref, res_ref), fields):
-            store(ref, at, strip)
-        return 0
-
-    lax.fori_loop(0, 2, ends, 0)
-    mask_rows(inv_ref, has_n, has_s)
+        flag = jnp.where(half == index, known, 1.0)
+        fields = (*fields[:2], [part * flag for part in fields[2]], fields[3])
+        pending += [
+            (ref, at, strip)
+            for ref, strip in zip((east_ref, south_ref, inv_ref, res_ref), fields)
+        ]
+    spread_cells(jacobi(source, table), spread)
+    for ref, at, strip in pending:
+        store(ref, at, strip)
 
     def flags(at, start):
         rows = [at + by for by in range(0, STRIP, EDGE)]
@@ -712,11 +709,7 @@
     own_ref[...] = own
     spare = jnp.zeros((LANES - down, LANES), jnp.float32)
     turned = jnp.transpose(jnp.concatenate([own, spare], axis=0))
-    def empty(index, _):
-        chunk_ref[index] = jnp.zeros((EDGE, LANES), jnp.float32)
-        return 0
-
-    lax.fori_loop(0, chunk_ref.shape[0], empty, 0)
+    chunk_ref[...] = jnp.zeros_like(chunk_ref)
     for down_by in (-1, 0, 1):
         for right_by in (-1, 0, 1):
             if down_by == 0 and right_by == 0:

time: 53.2 us -> 52.4 us (0.985)
  Pallas kernels: 21.4 us -> 20.5 us
    pallas_call x1, Pallas kernels: 6.96 us -> 6.23 us  [first(): pl.pallas_call(functools.partial(first_kernel, tiles, down), in_specs=[SM...]
  transfers between devices with their start and end apart: 4 -> 4, of which waited for: 0 -> 0; matrix products, arithmetic and copies ran while one was open for 0% -> 0% of each run, Pallas kernels for 10% -> 11%
where the time goes in v5:
time: 52.4 us; the launch traced here: 52.2 us
  blocking collectives  20.9 us (40%)
  Pallas kernels  20.5 us (39%)
  starting transfers between devices  10 us (19%)
  between operations  0.73 us (1%)
    all_to_all x1, blocking collectives, body(): got = lax.all_to_all(chunk, AXES, 0, 0, tiled=True)  12 us
    all_to_all x1, blocking collectives, body(): sums = lax.all_to_all(line, AXES, 0, 0, tiled=True)  8.92 us
    ppermute x2, starting transfers between devices, exchange(): got_a = lax.ppermute(send_a, axis, pairs(0))  8.71 us
    pallas_call x1, Pallas kernels, first(): pl.pallas_call(functools.partial(first_kernel, tiles, down), in_specs=[SM...  6.23 us
    pallas_call x1, Pallas kernels, second(): pl.pallas_call(functools.partial(second_kernel, tiles, down), in_specs=[S...  5.26 us
    pallas_call x1, Pallas kernels, inner(): pl.pallas_call(inner_kernel, in_specs=[SMEM] + [VMEM] * 2, out_specs=[VME...  3 us
    pallas_call x1, Pallas kernels, pack(): pl.pallas_call(functools.partial(pack_kernel, tiles, down), in_specs=[HBM...  2.5 us
    pallas_call x1, Pallas kernels, edge(): pl.pallas_call(functools.partial(edge_kernel, tiles, down), in_specs=[HBM...  1.66 us
  transfers between devices with their start and end apart: 4, of which 0 were waited for; matrix products, arithmetic and copies ran while one was open for 0% of the time, Pallas kernels for 11%

profile of v5, /device:TPU:0, one launch (start us, length us, event | category | flops | bytes accessed | tf_op | source)
XLA Modules:
  0.0 52.2 jit_solution(8684259712104111385)
XLA Ops:
  0.6 1.7 %pack_east_west.1 = (f32[64,128]{1,0:T(8,128)S(1)}, f32[64,128]{1,0:T(8,128)S(1)}) custom-call(f32[256,1024]{1,0:T(8,128)} %refs_0_.3, s32[256,1024]{1,0:T(8,128)} %refs_1_.3, f32[4]{0:T(128)} %refs_2_.3, f32[3,3]{1,0:T(4,128)} %taps.5), custom_call_target="tpu_custom_call" | custom-call | tf_op jit(solution)/shard_map/pack_east_west/pallas_call | solution.py:403
  2.3 0.7 %collective-permute-start = (f32[64,128]{1,0:T(8,128)S(1)}, f32[64,128]{1,0:T(8,128)S(1)}, u32[]{:S(2)}, u32[]{:S(2)}) collective-permute-start(f32[64,128]{1,0:T(8,128)S(1)} %get-tuple-element.29), channel_id=1, source_target_pairs={{4,8},{8,4},{12,16},{16,12},{20,24},{24,20},{5,9},{9,5},{13,17},{1... | collective-permute-start | bytes 98312 | tf_op jit(solution)/shard_map/ppermute | solution.py:926
  3.0 5.8 %collective-permute-start.1 = (f32[64,128]{1,0:T(8,128)S(1)}, f32[64,128]{1,0:T(8,128)S(1)}, u32[]{:S(2)}, u32[]{:S(2)}) collective-permute-start(f32[64,128]{1,0:T(8,128)S(1)} %get-tuple-element.30.refs_4_), channel_id=1, source_target_pairs={{0,4},{4,0},{8,12},{12,8},{16,20},{20,16},{24,28},{28,24},{1,5},{5... | collective-permute-start | bytes 98312 | tf_op jit(solution)/shard_map/ppermute | solution.py:927
  8.8 2.5 %pack_all.1 = (f32[9,288,128]{2,1,0:T(8,128)S(1)}, f32[9,288,128]{2,1,0:T(8,128)S(1)}, f32[4,48,256]{2,1,0:T(8,128)S(1)}) custom-call(f32[256,1024]{1,0:T(8,128)} %refs_0_.3, s32[256,1024]{1,0:T(8,128)} %refs_1_.3, f32[4]{0:T(128)} %refs_2_.3, f32[3,3]{1,0:T(4,128)} %taps.5, f32[64,128]{1,0:T(8,128)S(1)} %get-tuple-element.30.refs_4_), custom_call_target="tpu_custom_call" | custom-call | flops 5242880 | bytes 4194304 | tf_op jit(solution)/shard_map/pack_all/pallas_call | solution.py:435
  11.3 0.0 collective-permute-done.got_b
  11.3 0.0 collective-permute-done.1.got_a
  11.3 0.0 copy-start
  11.3 0.3 pack_north_south.1
  11.6 0.7 %collective-permute-start.2 = (f32[22,8,128]{2,1,0:T(8,128)S(1)}, f32[22,8,128]{2,1,0:T(8,128)S(1)}, u32[]{:S(2)}, u32[]{:S(2)}) collective-permute-start(f32[22,8,128]{2,1,0:T(8,128)S(1)} %get-tuple-element.40), channel_id=1, source_target_pairs={{1,2},{2,1},{5,6},{6,5},{9,10},{10,9},{13,14},{14,13},{17,18},{18,... | collective-permute-start | bytes 270344 | tf_op jit(solution)/shard_map/ppermute | solution.py:926
  12.2 2.9 %collective-permute-start.3 = (f32[22,8,128]{2,1,0:T(8,128)S(1)}, f32[22,8,128]{2,1,0:T(8,128)S(1)}, u32[]{:S(2)}, u32[]{:S(2)}) collective-permute-start(f32[22,8,128]{2,1,0:T(8,128)S(1)} %get-tuple-element.41), channel_id=1, source_target_pairs={{0,1},{1,0},{2,3},{3,2},{4,5},{5,4},{6,7},{7,6},{8,9},{9,8},{10,11... | collective-permute-start | bytes 270344 | tf_op jit(solution)/shard_map/ppermute | solution.py:927
  15.2 0.0 copy-done
  15.2 3.0 %inner_strips.1 = (f32[9,288,128]{2,1,0:T(8,128)S(1)}, f32[9,288,128]{2,1,0:T(8,128)S(1)}, f32[9,288,128]{2,1,0:T(8,128)S(1)}, f32[9,288,128]{2,1,0:T(8,128)S(1)}) custom-call(f32[3,3]{1,0:T(4,128)S(1)} %copy-done, f32[9,288,128]{2,1,0:T(8,128)S(1)} %get-tuple-element.34.obs.obs_in, f32[9,288,128]{2,1,0:T(8,128)S(1)} %get-tuple-element.35.cond.cond_in), custom_call_target="tpu_custom_call" | custom-call | flops 14929920 | bytes 7962624 | tf_op jit(solution)/shard_map/inner_strips/pallas_call | solution.py:569
  18.2 0.0 collective-permute-done.2.got_b
  18.2 0.0 collective-permute-done.3.got_a
  18.2 6.2 %first_direction.1 = (f32[9,288,128]{2,1,0:T(8,128)S(1)}, f32[9,288,128]{2,1,0:T(8,128)S(1)}, f32[9,288,128]{2,1,0:T(8,128)S(1)}, f32[9,288,128]{2,1,0:T(8,128)S...) custom-call(f32[3,3]{1,0:T(4,128)S(1)} %copy-done, ...), custom_call_target="tpu_custom_call", output_to_operand_aliasing={{0}: (1, {}), {1}: (2, {}), {2}: (3, {}), {3}: (4, {}), {4}... | custom-call | tf_op jit(solution)/shard_map/first_direction/pallas_call | solution.py:740
  24.4 12.0 %all_to_all.10.got_ref = f32[32,8,128]{2,1,0:T(8,128)S(1)} all-to-all(f32[32,8,128]{2,1,0:T(8,128)S(1)} %get-tuple-element.43), channel_id=1, replica_groups=mesh['cols'=8,'rows'=4] {'cols','rows'}, dimensions={0} | all-to-all | bytes 262144 | tf_op jit(solution)/shard_map/all_to_all | solution.py:943
  36.4 5.3 %second_direction.1 = (f32[9,288,128]{2,1,0:T(8,128)S(1)}, f32[9,288,128]{2,1,0:T(8,128)S(1)}, f32[32,1,128]{2,1,0:T(1,128)S(1)}) custom-call(f32[3,3]{1,0:T(4,128)S(1)} %copy-done, f32[32,8,128]{2,1,0:T(8,128)S(1)} %all_to_all.10.got_ref, f32[32,128]{1,0:T(8,128)S(1)} %get-tuple-element.44.own_ref, f32[5,48,256]{2,1,0:T(8,128)S(1)} %get-tuple-element.45.table_ref, ...), custom_call_target="tpu_custom_call" | custom-call | tf_op jit(solution)/shard_map/second_direction/pallas_call | solution.py:838
  41.7 8.9 %all_to_all.11.sums_ref = f32[32,1,128]{2,1,0:T(1,128)S(1)} all-to-all(f32[32,1,128]{2,1,0:T(1,128)S(1)} %get-tuple-element.51), channel_id=1, replica_groups=mesh['cols'=8,'rows'=4] {'cols','rows'}, dimensions={0} | all-to-all | bytes 32768 | tf_op jit(solution)/shard_map/all_to_all | solution.py:945
  50.6 1.6 %combine.1 = (f32[256,1024]{1,0:T(8,128)}, f32[256,1024]{1,0:T(8,128)}) custom-call(f32[32,1,128]{2,1,0:T(1,128)S(1)} %all_to_all.11.sums_ref, f32[9,288,128]{2,1,0:T(8,128)S(1)} %get-tuple-element.52.p_ref, f32[9,288,128]{2,1,0:T(8,128)S(1)} %get-tuple-element.53.w_ref, f32[9,288,128]{2,1,0:T(8,128)S(1)} %get-tuple-element.54.r_ref, ...), custom_call_target="tpu_custom_call" | custom-call | tf_op jit(solution)/shard_map/combine/pallas_call | solution.py:903
Async XLA Ops:
  2.3 9.0 %collective-permute-start = (f32[64,128]{1,0:T(8,128)S(1)}, f32[64,128]{1,0:T(8,128)S(1)}, u32[]{:S(2)}, u32[]{:S(2)}) collective-permute-start(f32[64,128]{1,0:T(8,128)S(1)} %get-tuple-element.29), channel_id=1, source_target_pairs={{4,8},{8,4},{12,16},{16,12},{20,24},{24,20},{5,9},{9,5},{13,17},{1... | collective-permute-start | bytes 98312 | tf_op jit(solution)/shard_map/ppermute | solution.py:926
  3.0 8.3 %collective-permute-start.1 = (f32[64,128]{1,0:T(8,128)S(1)}, f32[64,128]{1,0:T(8,128)S(1)}, u32[]{:S(2)}, u32[]{:S(2)}) collective-permute-start(f32[64,128]{1,0:T(8,128)S(1)} %get-tuple-element.30.refs_4_), channel_id=1, source_target_pairs={{0,4},{4,0},{8,12},{12,8},{16,20},{20,16},{24,28},{28,24},{1,5},{5... | collective-permute-start | bytes 98312 | tf_op jit(solution)/shard_map/ppermute | solution.py:927
  11.3 3.9 %copy-start = (f32[3,3]{1,0:T(4,128)S(1)}, f32[3,3]{1,0:T(4,128)}, u32[]{:S(2)}) copy-start(f32[3,3]{1,0:T(4,128)} %taps.5) | copy-start | bytes 112
  11.6 6.6 %collective-permute-start.2 = (f32[22,8,128]{2,1,0:T(8,128)S(1)}, f32[22,8,128]{2,1,0:T(8,128)S(1)}, u32[]{:S(2)}, u32[]{:S(2)}) collective-permute-start(f32[22,8,128]{2,1,0:T(8,128)S(1)} %get-tuple-element.40), channel_id=1, source_target_pairs={{1,2},{2,1},{5,6},{6,5},{9,10},{10,9},{13,14},{14,13},{17,18},{18,... | collective-permute-start | bytes 270344 | tf_op jit(solution)/shard_map/ppermute | solution.py:926
  12.2 5.9 %collective-permute-start.3 = (f32[22,8,128]{2,1,0:T(8,128)S(1)}, f32[22,8,128]{2,1,0:T(8,128)S(1)}, u32[]{:S(2)}, u32[]{:S(2)}) collective-permute-start(f32[22,8,128]{2,1,0:T(8,128)S(1)} %get-tuple-element.41), channel_id=1, source_target_pairs={{0,1},{1,0},{2,3},{3,2},{4,5},{5,4},{6,7},{7,6},{8,9},{9,8},{10,11... | collective-permute-start | bytes 270344 | tf_op jit(solution)/shard_map/ppermute | solution.py:927

commit v6 on v5

--- a/solution.py
+++ b/solution.py
@@ -14,6 +14,7 @@
 
 LANES = 128
 HALF = LANES // 2
+COLUMNS = LANES // COARSE
 EDGE = 8
 STRIP = 2 * EDGE
 GROUP = 2
@@ -108,17 +109,49 @@
 
 def from_west(strip):
     lane = iota(strip[0].shape, 1)
-    turned = [roll(part, 1, 1) for part in strip]
-    return [jnp.where(lane == 0, turned[t - 1], turned[t]) for t in range(len(strip))]
+    last, halo = roll(strip[-2], 1, 1), roll(strip[-1], 1, 1)
+    return [
+        jnp.where(lane == 0, halo, last),
+        *strip[:-2],
+        jnp.where(lane == 0, last, halo),
+    ]
 
 
 def from_east(strip):
     lane = iota(strip[0].shape, 1)
-    turned = [roll(part, -1, 1) for part in strip]
-    count = len(strip)
+    first, halo = roll(strip[0], -1, 1), roll(strip[-1], -1, 1)
     return [
-        jnp.where(lane == LANES - 1, turned[(t + 1) % count], turned[t]) for t in range(count)
-    ]
+        *strip[1:-1],
+        jnp.where(lane == LANES - 1, halo, first),
+        jnp.where(lane == LANES - 1, first, halo),
+    ]
+
+
+def swap_blocks(strip):
+    strip = list(strip)
+    block = iota(strip[0].shape, 1) // COLUMNS
+    for apart in (1, 2, 4):
+        low = (block & apart) == 0
+        for one in range(COARSE):
+            if one & apart:
+                continue
+            two = one + apart
+            a, b = strip[one], strip[two]
+            strip[one] = jnp.where(low, a, roll(b, COLUMNS * apart, 1))
+            strip[two] = jnp.where(low, roll(a, -COLUMNS * apart, 1), b)
+    return strip
+
+
+def to_cells(strip):
+    lane = iota(strip[0].shape, 1)
+    turn = (lane % COLUMNS) * COARSE + lane // COLUMNS
+    return swap_blocks([pick_lanes(part, turn) for part in strip])
+
+
+def from_cells(strip):
+    lane = iota(strip[0].shape, 1)
+    turn = (lane % COARSE) * COLUMNS + lane // COARSE
+    return [pick_lanes(part, turn) for part in swap_blocks(strip)]
 
 
 def tap_sums(ref, at, taps, flip):
@@ -180,36 +213,30 @@
 
 
 def spread_cells(cells, spread):
-    tiles = spread.shape[0] - 1
+    spread[0] = cells[:, :LANES]
     lane = iota((cells.shape[0], LANES), 1)
-    for t in range(tiles):
-        spread[t] = pick_lanes(cells[:, :LANES], (lane >> 3) + t * (LANES // COARSE))
-    turn = jnp.where(lane < HALF, 0, LANES - LANES // COARSE)
-    spread[tiles] = pick_lanes(cells[:, LANES:], (lane >> 3) + turn)
+    turn = jnp.where(lane < HALF, 0, LANES - COLUMNS)
+    spread[1] = pick_lanes(cells[:, LANES:], lane // COARSE + turn)
 
 
 def cells_at(spread, at):
     first = at // EDGE + EDGE - 2
     rows = [load(spread, first + index, 1) for index in range(STRIP // EDGE)]
-    return [
+    own, halo = [
         jnp.concatenate([jnp.broadcast_to(row, (EDGE, LANES)) for row in parts], axis=0)
         for parts in zip(*rows)
     ]
+    return [own] * COARSE + [halo]
 
 
 def cell_sums(ref, tiles, down):
-    lane = iota((down, LANES), 1)
-    total = jnp.zeros((down, LANES), jnp.float32)
-    for t in range(tiles):
-        picked = [
+    total = [
+        sum(
             ref[t, pl.ds(2 * EDGE + k, down, stride=COARSE), :] for k in range(COARSE)
-        ]
-        part = sum(picked[1:], picked[0])
-        for by in (1, 2, 4):
-            part = part + roll(part, -by, 1)
-        part = pick_lanes(part, (lane & (LANES // COARSE - 1)) * COARSE)
-        total = jnp.where(lane // (LANES // COARSE) == t, part, total)
-    return total
+        )
+        for t in range(tiles)
+    ]
+    return sum(total[1:], total[0])
 
 
 def side_lanes(has_e, has_w):
@@ -416,13 +443,106 @@
     )(*[in_hbm(array) for array in (observed, class_map, class_weights, taps)])
 
 
-def pack_kernel(tiles, down, *refs):
-    arguments, (obs, cond, coarse_ref), scratch = refs[:4], refs[5:8], refs[8:]
-    settle = reader(range(tiles), arguments, scratch, obs, cond, down)
-    matrix = gather_matrix(tiles)
-    for t in range(tiles):
-        settle(t)
-    for index, part in enumerate(coarse_parts(scratch[3], read_taps(scratch[2]), matrix)):
+def pack_kernel(
+    down,
+    obs_in,
+    class_in,
+    weight_in,
+    taps_in,
+    _,
+    obs,
+    cond,
+    coarse_ref,
+    raw,
+    classes,
+    weights,
+    taps,
+    sums,
+    row_sem,
+    small_sem,
+):
+    tiles = COARSE
+    window = down + 2 * EDGE
+    small = [
+        pltpu.make_async_copy(weight_in, weights, small_sem.at[0]),
+        pltpu.make_async_copy(taps_in, taps, small_sem.at[1]),
+    ]
+
+    def copies(index):
+        rows = pl.ds(pl.multiple_of(index * CHUNK, CHUNK), CHUNK)
+        return (
+            pltpu.make_async_copy(obs_in.at[rows, :], raw.at[rows, :], row_sem.at[0, index]),
+            pltpu.make_async_copy(class_in.at[rows, :], classes.at[rows, :], row_sem.at[1, index]),
+        )
+
+    def request(index, _):
+        for copy in copies(index):
+            copy.start()
+        return 0
+
+    steps = raw.shape[0] // CHUNK
+    for copy in small:
+        copy.start()
+    lax.fori_loop(0, steps, request, 0)
+    sums[...] = jnp.zeros_like(sums)
+    for copy in small:
+        copy.wait()
+    values = [0.5 * weights[class_id] for class_id in range(CLASSES)]
+
+    def work(index, _):
+        for copy in copies(index):
+            copy.wait()
+        at = pl.multiple_of(index * CHUNK, CHUNK)
+        rows = pl.ds(at, CHUNK)
+        level = []
+        for t in range(tiles):
+            kind = classes[rows, t * LANES : (t + 1) * LANES]
+            level.append(
+                jnp.where(
+                    kind < 2,
+                    jnp.where(kind == 0, values[0], values[1]),
+                    jnp.where(kind == 2, values[2], values[3]),
+                )
+            )
+        level = to_cells(level)
+        field = to_cells([raw[rows, t * LANES : (t + 1) * LANES] for t in range(tiles)])
+        store(cond, at + 2 * EDGE, level)
+        store(obs, at + 2 * EDGE, field)
+        return 0
+
+    lax.fori_loop(0, steps, work, 0)
+    for which, ref in enumerate((obs, cond)):
+        for t in range(tiles):
+            picked = [
+                ref[t, pl.ds(2 * EDGE + k, down, stride=COARSE), :] for k in range(COARSE)
+            ]
+            sums[3 * which, t, EDGE : EDGE + down, :] = sum(picked[1:], picked[0])
+            sums[3 * which + 1, t, EDGE : EDGE + down, :] = picked[0]
+            sums[3 * which + 2, t, EDGE : EDGE + down, :] = picked[-1]
+
+    taps = read_taps(taps)
+    span = range(tiles + 1)
+    together = lambda strip: sum(strip[1:tiles], strip[0])
+    join = lambda own, beyond: jnp.concatenate([own, beyond], axis=1)
+    full, head, tail = [load(sums.at[index], 0, window) for index in range(3)]
+    by_tap = [
+        [full[t] - head[t] + roll(head[t], -1, 0) for t in span],
+        full,
+        [full[t] - tail[t] + roll(tail[t], 1, 0) for t in span],
+    ]
+    across = [
+        [sum(taps[a][b] * by_tap[a][t] for a in range(3)) for t in span] for b in range(3)
+    ]
+    right, left = from_east(across[0]), from_west(across[2])
+    strip = [across[1][t] + right[t] + left[t] for t in span]
+    source = join(together(strip), strip[tiles])
+    full, head, tail = [load(sums.at[index], 0, window) for index in range(3, 6)]
+    right = from_east(full)
+    east = join(full[tiles - 1] + right[tiles - 1], right[tiles])
+    south = together([tail[t] + roll(head[t], -1, 0) for t in span])
+    south = join(south, jnp.zeros_like(south))
+    around = east + roll(east, 1, 1) + south + roll(south, 1, 0)
+    for index, part in enumerate((source, east, south, around)):
         coarse_ref[index] = part
 
 
@@ -433,11 +553,19 @@
     field = (tiles + 1, height + 4 * EDGE, LANES)
     pixels = height * breadth
     return pl.pallas_call(
-        functools.partial(pack_kernel, tiles, down),
+        functools.partial(pack_kernel, down),
         in_specs=[HBM] * 4 + [VMEM],
         out_specs=[VMEM] * 3,
         out_shape=floats(field, field, (4, window, 2 * LANES)),
-        scratch_shapes=reader_scratch(tiles, height, window, class_weights, taps),
+        scratch_shapes=[
+            pltpu.VMEM(observed.shape, jnp.float32),
+            pltpu.VMEM(observed.shape, jnp.int32),
+            pltpu.SMEM(class_weights.shape, jnp.float32),
+            pltpu.SMEM(taps.shape, jnp.float32),
+            pltpu.VMEM((6, tiles + 1, window, LANES), jnp.float32),
+            pltpu.SemaphoreType.DMA((2, height // CHUNK)),
+            pltpu.SemaphoreType.DMA((2,)),
+        ],
         compiler_params=params(),
         cost_estimate=pl.CostEstimate(
             flops=20 * pixels, bytes_accessed=16 * pixels, transcendentals=0
@@ -745,7 +873,7 @@
         input_output_aliases={index + 1: index for index in range(6)},
         scratch_shapes=[
             pltpu.VMEM(field, jnp.float32),
-            pltpu.VMEM((tiles + 1, window, LANES), jnp.float32),
+            pltpu.VMEM((2, window, LANES), jnp.float32),
         ],
         compiler_params=params(),
         name="first_direction",
@@ -842,7 +970,7 @@
         out_shape=floats(q.shape, q.shape, (count, 1, LANES)),
         scratch_shapes=[
             pltpu.VMEM(q.shape, jnp.float32),
-            pltpu.VMEM((tiles + 1, window, LANES), jnp.float32),
+            pltpu.VMEM((2, window, LANES), jnp.float32),
         ],
         compiler_params=params(),
         name="second_direction",
@@ -879,8 +1007,8 @@
         p, w, r, q, v = [
             load(ref, at + 2 * EDGE, CHUNK) for ref in (p_ref, w_ref, r_ref, q_ref, v_ref)
         ]
-        one = [on_p * p[t] - on_w * w[t] for t in range(tiles)]
-        two = [r[t] - on_p * q[t] + on_w * v[t] for t in range(tiles)]
+        one = from_cells([on_p * p[t] - on_w * w[t] for t in range(tiles)])
+        two = from_cells([r[t] - on_p * q[t] + on_w * v[t] for t in range(tiles)])
         for t in range(tiles):
             sol[pl.ds(at, CHUNK), t * LANES : (t + 1) * LANES] = one[t]
             res[pl.ds(at, CHUNK), t * LANES : (t + 1) * LANES] = two[t]

time: 52.4 us -> 57.2 us (1.092)
  Pallas kernels: 20.5 us -> 24.3 us
  blocking collectives: 20.9 us -> 21.9 us
    pallas_call x1, Pallas kernels: 1.6 us -> 5.22 us  [combine(): pl.pallas_call(functools.partial(combine_kernel, tiles, height), in_specs...]
    pallas_call x1, Pallas kernels: 2.5 us -> 5.55 us  [pack(): pl.pallas_call(functools.partial(pack_kernel, down), in_specs=[HBM] * 4 +...]
    pallas_call x1, Pallas kernels: 6.23 us -> 5.01 us  [first(): pl.pallas_call(functools.partial(first_kernel, tiles, down), in_specs=[SM...]
    all_to_all x1, blocking collectives: 12 us -> 13 us  [body(): got = lax.all_to_all(chunk, AXES, 0, 0, tiled=True)]
    pallas_call x1, Pallas kernels: 3 us -> 1.97 us  [inner(): pl.pallas_call(inner_kernel, in_specs=[SMEM] + [VMEM] * 2, out_specs=[VME...]
    pallas_call x1, Pallas kernels: 5.26 us -> 4.58 us  [second(): pl.pallas_call(functools.partial(second_kernel, tiles, down), in_specs=[S...]
  transfers between devices with their start and end apart: 4 -> 4, of which waited for: 0 -> 0; matrix products, arithmetic and copies ran while one was open for 0% -> 0% of each run, Pallas kernels for 11% -> 13%
where the time goes in v6:
time: 57.2 us; the launch traced here: 57 us
  Pallas kernels  24.3 us (42%)
  blocking collectives  21.9 us (38%)
  starting transfers between devices  10 us (17%)
  between operations  0.72 us (1%)
    all_to_all x1, blocking collectives, body(): got = lax.all_to_all(chunk, AXES, 0, 0, tiled=True)  13 us
    all_to_all x1, blocking collectives, body(): sums = lax.all_to_all(line, AXES, 0, 0, tiled=True)  8.92 us
    ppermute x2, starting transfers between devices, exchange(): got_a = lax.ppermute(send_a, axis, pairs(0))  8.71 us
    pallas_call x1, Pallas kernels, pack(): pl.pallas_call(functools.partial(pack_kernel, down), in_specs=[HBM] * 4 +...  5.55 us
    pallas_call x1, Pallas kernels, combine(): pl.pallas_call(functools.partial(combine_kernel, tiles, height), in_specs...  5.22 us
    pallas_call x1, Pallas kernels, first(): pl.pallas_call(functools.partial(first_kernel, tiles, down), in_specs=[SM...  5.01 us
    pallas_call x1, Pallas kernels, second(): pl.pallas_call(functools.partial(second_kernel, tiles, down), in_specs=[S...  4.58 us
    pallas_call x1, Pallas kernels, inner(): pl.pallas_call(inner_kernel, in_specs=[SMEM] + [VMEM] * 2, out_specs=[VME...  1.97 us
  transfers between devices with their start and end apart: 4, of which 0 were waited for; matrix products, arithmetic and copies ran while one was open for 0% of the time, Pallas kernels for 13%

profile of v6, /device:TPU:0, one launch (start us, length us, event | category | flops | bytes accessed | tf_op | source)
XLA Modules:
  0.0 57.0 jit_solution(2539650866543997934)
XLA Ops:
  0.6 1.7 %pack_east_west.1 = (f32[64,128]{1,0:T(8,128)S(1)}, f32[64,128]{1,0:T(8,128)S(1)}) custom-call(f32[256,1024]{1,0:T(8,128)} %obs_in.1, s32[256,1024]{1,0:T(8,128)} %class_in.1, f32[4]{0:T(128)} %weight_in.1, f32[3,3]{1,0:T(4,128)} %taps.5), custom_call_target="tpu_custom_call" | custom-call | tf_op jit(solution)/shard_map/pack_east_west/pallas_call | solution.py:430
  2.3 0.7 %collective-permute-start = (f32[64,128]{1,0:T(8,128)S(1)}, f32[64,128]{1,0:T(8,128)S(1)}, u32[]{:S(2)}, u32[]{:S(2)}) collective-permute-start(f32[64,128]{1,0:T(8,128)S(1)} %get-tuple-element.29), channel_id=1, source_target_pairs={{4,8},{8,4},{12,16},{16,12},{20,24},{24,20},{5,9},{9,5},{13,17},{1... | collective-permute-start | bytes 98312 | tf_op jit(solution)/shard_map/ppermute | solution.py:1054
  3.0 5.8 %collective-permute-start.1 = (f32[64,128]{1,0:T(8,128)S(1)}, f32[64,128]{1,0:T(8,128)S(1)}, u32[]{:S(2)}, u32[]{:S(2)}) collective-permute-start(f32[64,128]{1,0:T(8,128)S(1)} %get-tuple-element.30._), channel_id=1, source_target_pairs={{0,4},{4,0},{8,12},{12,8},{16,20},{20,16},{24,28},{28,24},{1,5},{5... | collective-permute-start | bytes 98312 | tf_op jit(solution)/shard_map/ppermute | solution.py:1055
  8.8 5.6 %pack_all.1 = (f32[9,288,128]{2,1,0:T(8,128)S(1)}, f32[9,288,128]{2,1,0:T(8,128)S(1)}, f32[4,48,256]{2,1,0:T(8,128)S(1)}) custom-call(f32[256,1024]{1,0:T(8,128)} %obs_in.1, s32[256,1024]{1,0:T(8,128)} %class_in.1, f32[4]{0:T(128)} %weight_in.1, f32[3,3]{1,0:T(4,128)} %taps.5, f32[64,128]{1,0:T(8,128)S(1)} %get-tuple-element.30._), custom_call_target="tpu_custom_call" | custom-call | flops 5242880 | bytes 4194304 | tf_op jit(solution)/shard_map/pack_all/pallas_call | solution.py:555
  14.3 0.0 collective-permute-done.got_b
  14.3 0.0 collective-permute-done.1.got_a
  14.3 0.0 copy-start
  14.4 0.3 pack_north_south.1
  14.6 0.7 %collective-permute-start.2 = (f32[22,8,128]{2,1,0:T(8,128)S(1)}, f32[22,8,128]{2,1,0:T(8,128)S(1)}, u32[]{:S(2)}, u32[]{:S(2)}) collective-permute-start(f32[22,8,128]{2,1,0:T(8,128)S(1)} %get-tuple-element.40), channel_id=1, source_target_pairs={{1,2},{2,1},{5,6},{6,5},{9,10},{10,9},{13,14},{14,13},{17,18},{18,... | collective-permute-start | bytes 270344 | tf_op jit(solution)/shard_map/ppermute | solution.py:1054
  15.3 2.9 %collective-permute-start.3 = (f32[22,8,128]{2,1,0:T(8,128)S(1)}, f32[22,8,128]{2,1,0:T(8,128)S(1)}, u32[]{:S(2)}, u32[]{:S(2)}) collective-permute-start(f32[22,8,128]{2,1,0:T(8,128)S(1)} %get-tuple-element.41), channel_id=1, source_target_pairs={{0,1},{1,0},{2,3},{3,2},{4,5},{5,4},{6,7},{7,6},{8,9},{9,8},{10,11... | collective-permute-start | bytes 270344 | tf_op jit(solution)/shard_map/ppermute | solution.py:1055
  18.2 0.0 copy-done
  18.2 2.0 %inner_strips.1 = (f32[9,288,128]{2,1,0:T(8,128)S(1)}, f32[9,288,128]{2,1,0:T(8,128)S(1)}, f32[9,288,128]{2,1,0:T(8,128)S(1)}, f32[9,288,128]{2,1,0:T(8,128)S(1)}) custom-call(f32[3,3]{1,0:T(4,128)S(1)} %copy-done, f32[9,288,128]{2,1,0:T(8,128)S(1)} %get-tuple-element.34.obs.obs_in, f32[9,288,128]{2,1,0:T(8,128)S(1)} %get-tuple-element.35.cond.cond_in), custom_call_target="tpu_custom_call" | custom-call | flops 14929920 | bytes 7962624 | tf_op jit(solution)/shard_map/inner_strips/pallas_call | solution.py:697
  20.2 0.0 collective-permute-done.2.got_b
  20.2 0.0 collective-permute-done.3.got_a
  20.2 5.0 %first_direction.1 = (f32[9,288,128]{2,1,0:T(8,128)S(1)}, f32[9,288,128]{2,1,0:T(8,128)S(1)}, f32[9,288,128]{2,1,0:T(8,128)S(1)}, f32[9,288,128]{2,1,0:T(8,128)S...) custom-call(f32[3,3]{1,0:T(4,128)S(1)} %copy-done, ...), custom_call_target="tpu_custom_call", output_to_operand_aliasing={{0}: (1, {}), {1}: (2, {}), {2}: (3, {}), {3}: (4, {}), {4}... | custom-call | tf_op jit(solution)/shard_map/first_direction/pallas_call | solution.py:868
  25.2 13.0 %all_to_all.10.got_ref = f32[32,8,128]{2,1,0:T(8,128)S(1)} all-to-all(f32[32,8,128]{2,1,0:T(8,128)S(1)} %get-tuple-element.43), channel_id=1, replica_groups=mesh['cols'=8,'rows'=4] {'cols','rows'}, dimensions={0} | all-to-all | bytes 262144 | tf_op jit(solution)/shard_map/all_to_all | solution.py:1071
  38.2 4.6 %second_direction.1 = (f32[9,288,128]{2,1,0:T(8,128)S(1)}, f32[9,288,128]{2,1,0:T(8,128)S(1)}, f32[32,1,128]{2,1,0:T(1,128)S(1)}) custom-call(f32[3,3]{1,0:T(4,128)S(1)} %copy-done, f32[32,8,128]{2,1,0:T(8,128)S(1)} %all_to_all.10.got_ref, f32[32,128]{1,0:T(8,128)S(1)} %get-tuple-element.44.own_ref, f32[5,48,256]{2,1,0:T(8,128)S(1)} %get-tuple-element.45.table_ref, ...), custom_call_target="tpu_custom_call" | custom-call | tf_op jit(solution)/shard_map/second_direction/pallas_call | solution.py:966
  42.8 8.9 %all_to_all.11.sums_ref = f32[32,1,128]{2,1,0:T(1,128)S(1)} all-to-all(f32[32,1,128]{2,1,0:T(1,128)S(1)} %get-tuple-element.51), channel_id=1, replica_groups=mesh['cols'=8,'rows'=4] {'cols','rows'}, dimensions={0} | all-to-all | bytes 32768 | tf_op jit(solution)/shard_map/all_to_all | solution.py:1073
  51.7 5.2 %combine.1 = (f32[256,1024]{1,0:T(8,128)}, f32[256,1024]{1,0:T(8,128)}) custom-call(f32[32,1,128]{2,1,0:T(1,128)S(1)} %all_to_all.11.sums_ref, f32[9,288,128]{2,1,0:T(8,128)S(1)} %get-tuple-element.52.p_ref, f32[9,288,128]{2,1,0:T(8,128)S(1)} %get-tuple-element.53.w_ref, f32[9,288,128]{2,1,0:T(8,128)S(1)} %get-tuple-element.54.r_ref, ...), custom_call_target="tpu_custom_call" | custom-call | tf_op jit(solution)/shard_map/combine/pallas_call | solution.py:1031
Async XLA Ops:
  2.3 12.0 %collective-permute-start = (f32[64,128]{1,0:T(8,128)S(1)}, f32[64,128]{1,0:T(8,128)S(1)}, u32[]{:S(2)}, u32[]{:S(2)}) collective-permute-start(f32[64,128]{1,0:T(8,128)S(1)} %get-tuple-element.29), channel_id=1, source_target_pairs={{4,8},{8,4},{12,16},{16,12},{20,24},{24,20},{5,9},{9,5},{13,17},{1... | collective-permute-start | bytes 98312 | tf_op jit(solution)/shard_map/ppermute | solution.py:1054
  3.0 11.4 %collective-permute-start.1 = (f32[64,128]{1,0:T(8,128)S(1)}, f32[64,128]{1,0:T(8,128)S(1)}, u32[]{:S(2)}, u32[]{:S(2)}) collective-permute-start(f32[64,128]{1,0:T(8,128)S(1)} %get-tuple-element.30._), channel_id=1, source_target_pairs={{0,4},{4,0},{8,12},{12,8},{16,20},{20,16},{24,28},{28,24},{1,5},{5... | collective-permute-start | bytes 98312 | tf_op jit(solution)/shard_map/ppermute | solution.py:1055
  14.3 3.9 %copy-start = (f32[3,3]{1,0:T(4,128)S(1)}, f32[3,3]{1,0:T(4,128)}, u32[]{:S(2)}) copy-start(f32[3,3]{1,0:T(4,128)} %taps.5) | copy-start | bytes 112
  14.6 5.6 %collective-permute-start.2 = (f32[22,8,128]{2,1,0:T(8,128)S(1)}, f32[22,8,128]{2,1,0:T(8,128)S(1)}, u32[]{:S(2)}, u32[]{:S(2)}) collective-permute-start(f32[22,8,128]{2,1,0:T(8,128)S(1)} %get-tuple-element.40), channel_id=1, source_target_pairs={{1,2},{2,1},{5,6},{6,5},{9,10},{10,9},{13,14},{14,13},{17,18},{18,... | collective-permute-start | bytes 270344 | tf_op jit(solution)/shard_map/ppermute | solution.py:1054
  15.3 4.9 %collective-permute-start.3 = (f32[22,8,128]{2,1,0:T(8,128)S(1)}, f32[22,8,128]{2,1,0:T(8,128)S(1)}, u32[]{:S(2)}, u32[]{:S(2)}) collective-permute-start(f32[22,8,128]{2,1,0:T(8,128)S(1)} %get-tuple-element.41), channel_id=1, source_target_pairs={{0,1},{1,0},{2,3},{3,2},{4,5},{5,4},{6,7},{7,6},{8,9},{9,8},{10,11... | collective-permute-start | bytes 270344 | tf_op jit(solution)/shard_map/ppermute | solution.py:1055

commit v7 on v5

--- a/solution.py
+++ b/solution.py
@@ -172,7 +172,8 @@
     inverse = [pl.reciprocal(part, approx=True) for part in diag]
     inverse = [inverse[t] * (2.0 - diag[t] * inverse[t]) for t in span]
     inverse[-1] = inverse[-1] * sides
-    return east, south, inverse, conv(obs, at, taps, True)
+    residual = conv(obs, at, taps, True)
+    return east, south, inverse, residual, [residual[t] * inverse[t] for t in span]
 
 
 def pick_lanes(field, lanes):
@@ -229,11 +230,15 @@
         ref[:, ref.shape[1] - EDGE :, :] = empty
 
 
-def product_sum(one, two, count, flags=None):
+def product_sum_rows(one, two, count):
     total = one[0] * two[0]
     for t in range(1, count):
         total = total + one[t] * two[t]
-    return fold(total, flags)
+    return total
+
+
+def product_sum(one, two, count, flags=None):
+    return fold(product_sum_rows(one, two, count), flags)
 
 
 def fold(total, flags=None):
@@ -261,15 +266,32 @@
     return lax.fori_loop(0, steps, work, carry)
 
 
-def jacobi(source, table):
+def jacobi(source, table, work):
     factor, east, west, south, north = [table[index] for index in range(5)]
+    window = source.shape[0]
     source = factor * source
     iterate = source
-    for _ in range(SWEEPS - 1):
+    for sweep_index in range(SWEEPS - 1):
+        place_ref = work.at[sweep_index % 2]
+        for half in range(2):
+            place_ref[half, EDGE : EDGE + window, :] = iterate[
+                :, half * LANES : (half + 1) * LANES
+            ]
+        above, below = [
+            jnp.concatenate(
+                [place_ref[half, EDGE + by : EDGE + by + window, :] for half in range(2)], axis=1
+            )
+            for by in (-1, 1)
+        ]
         across = east * roll(iterate, -1, 1) + west * roll(iterate, 1, 1)
-        along = south * roll(iterate, -1, 0) + north * roll(iterate, 1, 0)
+        along = south * below + north * above
         iterate = ((1.0 - OMEGA) * iterate + source) + (across + along)
     return iterate
+
+
+def clear_work(work):
+    for buffer in range(2):
+        clear_pads(work.at[buffer])
 
 
 def in_pair_order(at, for_before, for_after):
@@ -325,9 +347,10 @@
             picked = [
                 ref[slot, pl.ds(2 * EDGE + k, down, stride=COARSE), :] for k in range(COARSE)
             ]
-            sums[3 * which, slot, EDGE : EDGE + down, :] = sum(picked[1:], picked[0])
-            sums[3 * which + 1, slot, EDGE : EDGE + down, :] = picked[0]
-            sums[3 * which + 2, slot, EDGE : EDGE + down, :] = picked[-1]
+            cells = slice(2 * EDGE, 2 * EDGE + down)
+            sums[3 * which, slot, cells, :] = sum(picked[1:], picked[0])
+            sums[3 * which + 1, slot, cells, :] = picked[0]
+            sums[3 * which + 2, slot, cells, :] = picked[-1]
 
     return settle
 
@@ -337,7 +360,7 @@
         pltpu.VMEM((tiles, height, LANES), jnp.int32),
         pltpu.SMEM(class_weights.shape, jnp.float32),
         pltpu.SMEM(taps.shape, jnp.float32),
-        pltpu.VMEM((6, tiles + 1, window, LANES), jnp.float32),
+        pltpu.VMEM((6, tiles + 1, window + 2 * EDGE, LANES), jnp.float32),
         pltpu.SemaphoreType.DMA((tiles,)),
         pltpu.SemaphoreType.DMA((tiles,)),
         pltpu.SemaphoreType.DMA((2,)),
@@ -345,16 +368,16 @@
 
 
 def coarse_parts(sums, taps, matrix):
-    window = sums.shape[2]
-    whole = lambda index: wide(sums.at[index], 0, window)
-    full, head, tail = whole(0), whole(1), whole(2)
-    by_tap = [full - head + roll(head, -1, 0), full, full - tail + roll(tail, 1, 0)]
+    window = sums.shape[2] - 2 * EDGE
+    whole = lambda index, by=0: wide(sums.at[index], EDGE + by, window)
+    full = whole(0)
+    by_tap = [full - whole(1) + whole(1, 1), full, full - whole(2) + whole(2, -1)]
     across = [sum(taps[a][b] * by_tap[a] for a in range(3)) for b in range(3)]
     source = across[1] + roll(across[0], -1, 1) + roll(across[2], 1, 1)
-    full, head, tail = whole(3), whole(4), whole(5)
+    full = whole(3)
     last = (iota(full.shape, 1) & (COARSE - 1)) == COARSE - 1
     east = jnp.where(last, full + roll(full, -1, 1), 0.0)
-    south = tail + roll(head, -1, 0)
+    south = whole(5) + whole(4, 1)
     cells = split_dot(jnp.concatenate([source, east, south], axis=0), matrix)
     source, east, south = cells[:window], cells[window : 2 * window], cells[2 * window :]
     around = east + roll(east, 1, 1) + south + roll(south, 1, 0)
@@ -550,17 +573,22 @@
     )(got_b, got_a, coarse, obs, cond)
 
 
-def inner_kernel(taps, obs, cond, res_ref, east_ref, south_ref, inv_ref):
+def inner_kernel(taps, obs, cond, res_ref, east_ref, south_ref, inv_ref, u_ref, dot_ref):
     _, _, has_e, has_w = has_sides()
     clear_pads(east_ref, south_ref)
     taps = read_taps(taps)
     sides = side_lanes(has_e, has_w)
 
-    def work(at, _, carry):
+    tiles = obs.shape[0] - 1
+
+    def work(at, start, total):
         fields = begin(obs, cond, at, taps, sides)
-        return list(zip((east_ref, south_ref, inv_ref, res_ref), fields)), carry
-
-    sweep(3 * EDGE, obs.shape[1] - 3 * EDGE, work, 0)
+        flags = [jnp.where(at + by >= start, 1.0, 0.0) for by in range(0, STRIP, EDGE)]
+        total = total + product_sum(fields[3], fields[4], tiles, flags)
+        return list(zip((east_ref, south_ref, inv_ref, res_ref, u_ref), fields)), total
+
+    nothing = jnp.zeros((EDGE, LANES), jnp.float32)
+    dot_ref[...] = sweep(3 * EDGE, obs.shape[1] - 3 * EDGE, work, nothing)
 
 
 def inner(taps, obs, cond):
@@ -569,8 +597,8 @@
     return pl.pallas_call(
         inner_kernel,
         in_specs=[SMEM] + [VMEM] * 2,
-        out_specs=[VMEM] * 4,
-        out_shape=floats(field, field, field, field),
+        out_specs=[VMEM] * 6,
+        out_shape=floats(field, field, field, field, field, (EDGE, LANES)),
         compiler_params=params(),
         cost_estimate=pl.CostEstimate(
             flops=45 * pixels, bytes_accessed=24 * pixels, transcendentals=0
@@ -589,15 +617,18 @@
     east_in,
     south_in,
     inv_in,
+    u_in,
     got_b,
     got_a,
     coarse_in,
+    dot_in,
     obs,
     cond,
     res_ref,
     east_ref,
     south_ref,
     inv_ref,
+    u_ref,
     p_ref,
     q_ref,
     table_ref,
@@ -606,12 +637,14 @@
     dots_ref,
     image,
     spread,
+    work,
 ):
     height = down * COARSE
     window = down + 2 * EDGE
     at_col, at_row, n_cols, n_rows = place()
     has_n, has_s, has_e, has_w = has_sides()
     clear_pads(obs, cond, p_ref, image)
+    clear_work(work)
     from_s, from_n = in_pair_order(
         at_row, lambda index: got_b[index], lambda index: got_a[index]
     )
@@ -655,8 +688,8 @@
         lane < LANES, 1.0, jnp.where(lane < LANES + HALF, has_e, has_w)
     )
     taps = read_taps(taps)
-    total = tap_total(taps, 1)
-    factor = inside * OMEGA / (COARSE * COARSE * total * total + around)
+    taps_sum = tap_total(taps, 1)
+    factor = inside * OMEGA / (COARSE * COARSE * taps_sum * taps_sum + around)
     weights = (east, roll(east, 1, 1), south, roll(south, 1, 0))
     table = [factor] + [factor * weight for weight in weights]
     for index, part in enumerate(table):
@@ -664,16 +697,24 @@
     sides = side_lanes(has_e, has_w)
     half = iota((STRIP, LANES), 0) // EDGE
     pending = []
+    total = dot_in[...]
     for index, known in ((0, has_n), (1, has_s)):
         at = EDGE + index * height
         fields = begin(obs, cond, at, taps, sides)
+        own = jnp.where(half == index, 0.0, 1.0)
+        total = total + fold(own * product_sum_rows(fields[3], fields[4], tiles))
         flag = jnp.where(half == index, known, 1.0)
-        fields = (*fields[:2], [part * flag for part in fields[2]], fields[3])
+        inverse, start = [[part * flag for part in fields[index]] for index in (2, 4)]
+        fields = (*fields[:2], inverse, fields[3], start)
         pending += [
             (ref, at, strip)
-            for ref, strip in zip((east_ref, south_ref, inv_ref, res_ref), fields)
+            for ref, strip in zip((east_ref, south_ref, inv_ref, res_ref, u_ref), fields)
         ]
-    spread_cells(jacobi(source, table), spread)
+    cells = jacobi(source, table, work)
+    spread_cells(cells, spread)
+    inner_cells = slice(EDGE, EDGE + down)
+    total = total + fold(source[inner_cells, :LANES] * cells[inner_cells, :LANES])
+    dots_ref[0] = total
     for ref, at, strip in pending:
         store(ref, at, strip)
 
@@ -684,10 +725,9 @@
             jnp.where((row >= first_row) & (row < 2 * EDGE + height), 1.0, 0.0) for row in rows
         ]
 
-    def begin_p(at, start, total):
-        residual, inverse, cells = load(res_ref, at), load(inv_ref, at), cells_at(spread, at)
-        strip = [residual[t] * inverse[t] + cells[t] for t in range(tiles + 1)]
-        return [(p_ref, strip)], total + product_sum(residual, strip, tiles, flags(at, start))
+    def begin_p(at, _, carry):
+        start, cells = load(u_ref, at), cells_at(spread, at)
+        return [(p_ref, [start[t] + cells[t] for t in range(tiles + 1)])], carry
 
     def blur(at, _, carry):
         strip = conv(p_ref, at, taps, False)
@@ -700,7 +740,7 @@
 
     nothing = jnp.zeros((EDGE, LANES), jnp.float32)
     span = (EDGE, 3 * EDGE + height)
-    dots_ref[0] = sweep(*span, begin_p, nothing)
+    sweep(*span, begin_p, 0)
     sweep(*span, blur, 0)
     mask_rows(image, has_n, has_s)
     dots_ref[1] = sweep(*span, finish, nothing)
@@ -725,13 +765,13 @@
                 chunk_ref[to_col * n_rows + to_row] = piece
 
 
-def first(taps, fields, got_a, got_b, coarse):
+def first(taps, fields, got_a, got_b, coarse, dot):
     field = fields[0].shape
     tiles, height = field[0] - 1, field[1] - 4 * EDGE
     down = height // COARSE
     window = down + 2 * EDGE
     count = lax.axis_size("cols") * lax.axis_size("rows")
-    shapes = [field] * 8 + [
+    shapes = [field] * 9 + [
         (5, window, 2 * LANES),
         (down, LANES),
         (count, EDGE, LANES),
@@ -739,17 +779,18 @@
     ]
     return pl.pallas_call(
         functools.partial(first_kernel, tiles, down),
-        in_specs=[SMEM] + [VMEM] * 9,
+        in_specs=[SMEM] + [VMEM] * 11,
         out_specs=[VMEM] * len(shapes),
         out_shape=floats(*shapes),
-        input_output_aliases={index + 1: index for index in range(6)},
+        input_output_aliases={index + 1: index for index in range(7)},
         scratch_shapes=[
             pltpu.VMEM(field, jnp.float32),
             pltpu.VMEM((tiles + 1, window, LANES), jnp.float32),
+            pltpu.VMEM((2, 2, window + 2 * EDGE, LANES), jnp.float32),
         ],
         compiler_params=params(),
         name="first_direction",
-    )(taps, *fields, got_b, got_a, coarse)[2:]
+    )(taps, *fields, got_b, got_a, coarse, dot)[2:]
 
 
 def second_kernel(
@@ -769,6 +810,7 @@
     out_ref,
     image,
     spread,
+    work,
 ):
     height = down * COARSE
     has_n, has_s, has_e, has_w = has_sides()
@@ -791,34 +833,37 @@
         ],
         axis=0,
     )
-    spread_cells(jacobi(source, table_ref), spread)
+    clear_work(work)
+    spread_cells(jacobi(source, table_ref, work), spread)
     clear_pads(w_ref, image)
     sides = side_lanes(has_e, has_w)
     taps = read_taps(taps)
 
-    def begin_w(at, _, carry):
+    def begin_w(at, start, total):
         field, inverse, cells = load(q_ref, at), load(inv_ref, at), cells_at(spread, at)
-        return [(w_ref, [field[t] * inverse[t] + cells[t] for t in range(tiles + 1)])], carry
+        strip = [field[t] * inverse[t] + cells[t] for t in range(tiles + 1)]
+        first_row = jnp.maximum(start, 2 * EDGE)
+        flags = [
+            jnp.where((row >= first_row) & (row < 2 * EDGE + height), 1.0, 0.0)
+            for row in [at + by for by in range(0, STRIP, EDGE)]
+        ]
+        return [(w_ref, strip)], total + product_sum(field, strip, tiles, flags)
 
     def blur(at, _, carry):
         strip = conv(w_ref, at, taps, False)
         strip[tiles] = strip[tiles] * sides
         return [(image, strip)], carry
 
-    def finish(at, _, totals):
+    def finish(at, _, total):
         here, product = operate(w_ref, image, east_ref, south_ref, at, taps)
-        field = load(q_ref, at)
-        return [(v_ref, product[:tiles])], (
-            totals[0] + product_sum(field, here, tiles),
-            totals[1] + product_sum(here, product, tiles),
-        )
+        return [(v_ref, product[:tiles])], total + product_sum(here, product, tiles)
 
     nothing = jnp.zeros((EDGE, LANES), jnp.float32)
     span = (EDGE, 3 * EDGE + height)
-    sweep(*span, begin_w, 0)
+    dot_qw = sweep(*span, begin_w, nothing)
     sweep(*span, blur, 0)
     mask_rows(image, has_n, has_s)
-    dot_qw, dot_wv = sweep(2 * EDGE, 2 * EDGE + height, finish, (nothing, nothing))
+    dot_wv = sweep(2 * EDGE, 2 * EDGE + height, finish, nothing)
     line = jnp.zeros((1, LANES), jnp.float32)
     block = iota((1, LANES), 1) // (LANES // 4)
     for index, part in enumerate((dots_in[0], dots_in[1], dot_qw, dot_wv)):
@@ -843,6 +888,7 @@
         scratch_shapes=[
             pltpu.VMEM(q.shape, jnp.float32),
             pltpu.VMEM((tiles + 1, window, LANES), jnp.float32),
+            pltpu.VMEM((2, 2, window + 2 * EDGE, LANES), jnp.float32),
         ],
         compiler_params=params(),
         name="second_direction",
@@ -935,10 +981,10 @@
     obs, cond, coarse = pack(*arguments, send_a)
     obs, cond, coarse, send_a, send_b = middle(got_a, got_b, coarse, obs, cond)
     got_a, got_b = exchange(send_a, send_b, "rows")
-    r, east, south, inv = inner(blur_kernel, obs, cond)
-    fields = (obs, cond, r, east, south, inv)
-    r, east, south, inv, p, q, table, own, chunk, dots = first(
-        blur_kernel, fields, got_a, got_b, coarse
+    r, east, south, inv, u, dot = inner(blur_kernel, obs, cond)
+    fields = (obs, cond, r, east, south, inv, u)
+    r, east, south, inv, _, p, q, table, own, chunk, dots = first(
+        blur_kernel, fields, got_a, got_b, coarse, dot
     )
     got = lax.all_to_all(chunk, AXES, 0, 0, tiled=True)
     w, v, line = second(blur_kernel, got, own, table, q, east, south, inv, dots)

time: 52.4 us -> 52.5 us (level)
  transfers between devices with their start and end apart: 4 -> 4, of which waited for: 0 -> 0; matrix products, arithmetic and copies ran while one was open for 0% -> 0% of each run, Pallas kernels for 11% -> 10%
where the time goes in v7:
time: 52.5 us; the launch traced here: 52.2 us
  blocking collectives  21 us (40%)
  Pallas kernels  20.5 us (39%)
  starting transfers between devices  10 us (19%)
  between operations  0.72 us (1%)
    all_to_all x1, blocking collectives, body(): got = lax.all_to_all(chunk, AXES, 0, 0, tiled=True)  12.1 us
    all_to_all x1, blocking collectives, body(): sums = lax.all_to_all(line, AXES, 0, 0, tiled=True)  8.92 us
    ppermute x2, starting transfers between devices, exchange(): got_a = lax.ppermute(send_a, axis, pairs(0))  8.71 us
    pallas_call x1, Pallas kernels, first(): pl.pallas_call(functools.partial(first_kernel, tiles, down), in_specs=[SM...  6.18 us
    pallas_call x1, Pallas kernels, second(): pl.pallas_call(functools.partial(second_kernel, tiles, down), in_specs=[S...  5.32 us
    pallas_call x1, Pallas kernels, inner(): pl.pallas_call(inner_kernel, in_specs=[SMEM] + [VMEM] * 2, out_specs=[VME...  2.93 us
    pallas_call x1, Pallas kernels, pack(): pl.pallas_call(functools.partial(pack_kernel, tiles, down), in_specs=[HBM...  2.52 us
    pallas_call x1, Pallas kernels, edge(): pl.pallas_call(functools.partial(edge_kernel, tiles, down), in_specs=[HBM...  1.68 us
  transfers between devices with their start and end apart: 4, of which 0 were waited for; matrix products, arithmetic and copies ran while one was open for 0% of the time, Pallas kernels for 10%

profile of v7, /device:TPU:0, one launch (start us, length us, event | category | flops | bytes accessed | tf_op | source)
XLA Modules:
  0.0 52.2 jit_solution(16945851297304641521)
XLA Ops:
  0.6 1.7 %pack_east_west.1 = (f32[64,128]{1,0:T(8,128)S(1)}, f32[64,128]{1,0:T(8,128)S(1)}) custom-call(f32[256,1024]{1,0:T(8,128)} %refs_0_.3, s32[256,1024]{1,0:T(8,128)} %refs_1_.3, f32[4]{0:T(128)} %refs_2_.3, f32[3,3]{1,0:T(4,128)} %taps.5), custom_call_target="tpu_custom_call" | custom-call | tf_op jit(solution)/shard_map/pack_east_west/pallas_call | solution.py:426
  2.3 0.7 %collective-permute-start = (f32[64,128]{1,0:T(8,128)S(1)}, f32[64,128]{1,0:T(8,128)S(1)}, u32[]{:S(2)}, u32[]{:S(2)}) collective-permute-start(f32[64,128]{1,0:T(8,128)S(1)} %get-tuple-element.31), channel_id=1, source_target_pairs={{4,8},{8,4},{12,16},{16,12},{20,24},{24,20},{5,9},{9,5},{13,17},{1... | collective-permute-start | bytes 98312 | tf_op jit(solution)/shard_map/ppermute | solution.py:972
  3.0 5.8 %collective-permute-start.1 = (f32[64,128]{1,0:T(8,128)S(1)}, f32[64,128]{1,0:T(8,128)S(1)}, u32[]{:S(2)}, u32[]{:S(2)}) collective-permute-start(f32[64,128]{1,0:T(8,128)S(1)} %get-tuple-element.32.refs_4_), channel_id=1, source_target_pairs={{0,4},{4,0},{8,12},{12,8},{16,20},{20,16},{24,28},{28,24},{1,5},{5... | collective-permute-start | bytes 98312 | tf_op jit(solution)/shard_map/ppermute | solution.py:973
  8.8 2.5 %pack_all.1 = (f32[9,288,128]{2,1,0:T(8,128)S(1)}, f32[9,288,128]{2,1,0:T(8,128)S(1)}, f32[4,48,256]{2,1,0:T(8,128)S(1)}) custom-call(f32[256,1024]{1,0:T(8,128)} %refs_0_.3, s32[256,1024]{1,0:T(8,128)} %refs_1_.3, f32[4]{0:T(128)} %refs_2_.3, f32[3,3]{1,0:T(4,128)} %taps.5, f32[64,128]{1,0:T(8,128)S(1)} %get-tuple-element.32.refs_4_), custom_call_target="tpu_custom_call" | custom-call | flops 5242880 | bytes 4194304 | tf_op jit(solution)/shard_map/pack_all/pallas_call | solution.py:458
  11.3 0.0 collective-permute-done.got_b
  11.3 0.0 collective-permute-done.1.got_a
  11.3 0.0 copy-start
  11.3 0.3 pack_north_south.1
  11.6 0.7 %collective-permute-start.2 = (f32[22,8,128]{2,1,0:T(8,128)S(1)}, f32[22,8,128]{2,1,0:T(8,128)S(1)}, u32[]{:S(2)}, u32[]{:S(2)}) collective-permute-start(f32[22,8,128]{2,1,0:T(8,128)S(1)} %get-tuple-element.43), channel_id=1, source_target_pairs={{1,2},{2,1},{5,6},{6,5},{9,10},{10,9},{13,14},{14,13},{17,18},{18,... | collective-permute-start | bytes 270344 | tf_op jit(solution)/shard_map/ppermute | solution.py:972
  12.3 2.9 %collective-permute-start.3 = (f32[22,8,128]{2,1,0:T(8,128)S(1)}, f32[22,8,128]{2,1,0:T(8,128)S(1)}, u32[]{:S(2)}, u32[]{:S(2)}) collective-permute-start(f32[22,8,128]{2,1,0:T(8,128)S(1)} %get-tuple-element.44), channel_id=1, source_target_pairs={{0,1},{1,0},{2,3},{3,2},{4,5},{5,4},{6,7},{7,6},{8,9},{9,8},{10,11... | collective-permute-start | bytes 270344 | tf_op jit(solution)/shard_map/ppermute | solution.py:973
  15.2 0.0 copy-done
  15.2 2.9 %inner_strips.1 = (f32[9,288,128]{2,1,0:T(8,128)S(1)}, f32[9,288,128]{2,1,0:T(8,128)S(1)}, f32[9,288,128]{2,1,0:T(8,128)S(1)}, f32[9,288,128]{2,1,0:T(8,128)S(1)...) custom-call(f32[3,3]{1,0:T(4,128)S(1)} %copy-done, f32[9,288,128]{2,1,0:T(8,128)S(1)} %get-tuple-element.36.obs.obs_in, ...), custom_call_target="tpu_custom_call" | custom-call | flops 14929920 | bytes 7962624 | tf_op jit(solution)/shard_map/inner_strips/pallas_call | solution.py:597
  18.1 0.0 collective-permute-done.2.got_b
  18.1 0.0 collective-permute-done.3.got_a
  18.2 6.2 %first_direction.1 = (f32[9,288,128]{2,1,0:T(8,128)S(1)}, f32[9,288,128]{2,1,0:T(8,128)S(1)}, f32[9,288,128]{2,1,0:T(8,128)S(1)}, f32[9,288,128]{2,1,0:T(8,128)S...) custom-call(f32[3,3]{1,0:T(4,128)S(1)} %copy-done, ...), custom_call_target="tpu_custom_call", output_to_operand_aliasing={{0}: (1, {}), {1}: (2, {}), {2}: (3, {}), {3}: (4, {}), {4}... | custom-call | tf_op jit(solution)/shard_map/first_direction/pallas_call | solution.py:780
  24.3 12.1 %all_to_all.10.got_ref = f32[32,8,128]{2,1,0:T(8,128)S(1)} all-to-all(f32[32,8,128]{2,1,0:T(8,128)S(1)} %get-tuple-element.47), channel_id=1, replica_groups=mesh['cols'=8,'rows'=4] {'cols','rows'}, dimensions={0} | all-to-all | bytes 262144 | tf_op jit(solution)/shard_map/all_to_all | solution.py:989
  36.4 5.3 %second_direction.1 = (f32[9,288,128]{2,1,0:T(8,128)S(1)}, f32[9,288,128]{2,1,0:T(8,128)S(1)}, f32[32,1,128]{2,1,0:T(1,128)S(1)}) custom-call(f32[3,3]{1,0:T(4,128)S(1)} %copy-done, f32[32,8,128]{2,1,0:T(8,128)S(1)} %all_to_all.10.got_ref, f32[32,128]{1,0:T(8,128)S(1)} %get-tuple-element.48.own_ref, f32[5,48,256]{2,1,0:T(8,128)S(1)} %get-tuple-element.49.table_ref, ...), custom_call_target="tpu_custom_call" | custom-call | tf_op jit(solution)/shard_map/second_direction/pallas_call | solution.py:883
  41.7 8.9 %all_to_all.11.sums_ref = f32[32,1,128]{2,1,0:T(1,128)S(1)} all-to-all(f32[32,1,128]{2,1,0:T(1,128)S(1)} %get-tuple-element.55), channel_id=1, replica_groups=mesh['cols'=8,'rows'=4] {'cols','rows'}, dimensions={0} | all-to-all | bytes 32768 | tf_op jit(solution)/shard_map/all_to_all | solution.py:991
  50.7 1.6 %combine.1 = (f32[256,1024]{1,0:T(8,128)}, f32[256,1024]{1,0:T(8,128)}) custom-call(f32[32,1,128]{2,1,0:T(1,128)S(1)} %all_to_all.11.sums_ref, f32[9,288,128]{2,1,0:T(8,128)S(1)} %get-tuple-element.56.p_ref, f32[9,288,128]{2,1,0:T(8,128)S(1)} %get-tuple-element.57.w_ref, f32[9,288,128]{2,1,0:T(8,128)S(1)} %get-tuple-element.58.r_ref, ...), custom_call_target="tpu_custom_call" | custom-call | tf_op jit(solution)/shard_map/combine/pallas_call | solution.py:949
Async XLA Ops:
  2.3 9.0 %collective-permute-start = (f32[64,128]{1,0:T(8,128)S(1)}, f32[64,128]{1,0:T(8,128)S(1)}, u32[]{:S(2)}, u32[]{:S(2)}) collective-permute-start(f32[64,128]{1,0:T(8,128)S(1)} %get-tuple-element.31), channel_id=1, source_target_pairs={{4,8},{8,4},{12,16},{16,12},{20,24},{24,20},{5,9},{9,5},{13,17},{1... | collective-permute-start | bytes 98312 | tf_op jit(solution)/shard_map/ppermute | solution.py:972
  3.0 8.3 %collective-permute-start.1 = (f32[64,128]{1,0:T(8,128)S(1)}, f32[64,128]{1,0:T(8,128)S(1)}, u32[]{:S(2)}, u32[]{:S(2)}) collective-permute-start(f32[64,128]{1,0:T(8,128)S(1)} %get-tuple-element.32.refs_4_), channel_id=1, source_target_pairs={{0,4},{4,0},{8,12},{12,8},{16,20},{20,16},{24,28},{28,24},{1,5},{5... | collective-permute-start | bytes 98312 | tf_op jit(solution)/shard_map/ppermute | solution.py:973
  11.3 3.9 %copy-start = (f32[3,3]{1,0:T(4,128)S(1)}, f32[3,3]{1,0:T(4,128)}, u32[]{:S(2)}) copy-start(f32[3,3]{1,0:T(4,128)} %taps.5) | copy-start | bytes 112
  11.6 6.5 %collective-permute-start.2 = (f32[22,8,128]{2,1,0:T(8,128)S(1)}, f32[22,8,128]{2,1,0:T(8,128)S(1)}, u32[]{:S(2)}, u32[]{:S(2)}) collective-permute-start(f32[22,8,128]{2,1,0:T(8,128)S(1)} %get-tuple-element.43), channel_id=1, source_target_pairs={{1,2},{2,1},{5,6},{6,5},{9,10},{10,9},{13,14},{14,13},{17,18},{18,... | collective-permute-start | bytes 270344 | tf_op jit(solution)/shard_map/ppermute | solution.py:972
  12.3 5.9 %collective-permute-start.3 = (f32[22,8,128]{2,1,0:T(8,128)S(1)}, f32[22,8,128]{2,1,0:T(8,128)S(1)}, u32[]{:S(2)}, u32[]{:S(2)}) collective-permute-start(f32[22,8,128]{2,1,0:T(8,128)S(1)} %get-tuple-element.44), channel_id=1, source_target_pairs={{0,1},{1,0},{2,3},{3,2},{4,5},{5,4},{6,7},{7,6},{8,9},{9,8},{10,11... | collective-permute-start | bytes 270344 | tf_op jit(solution)/shard_map/ppermute | solution.py:973

commit v8 on v7

--- a/solution.py
+++ b/solution.py
@@ -200,17 +200,20 @@
 
 def cell_sums(ref, tiles, down):
     lane = iota((down, LANES), 1)
-    total = jnp.zeros((down, LANES), jnp.float32)
-    for t in range(tiles):
-        picked = [
-            ref[t, pl.ds(2 * EDGE + k, down, stride=COARSE), :] for k in range(COARSE)
-        ]
-        part = sum(picked[1:], picked[0])
-        for by in (1, 2, 4):
-            part = part + roll(part, -by, 1)
-        part = pick_lanes(part, (lane & (LANES // COARSE - 1)) * COARSE)
-        total = jnp.where(lane // (LANES // COARSE) == t, part, total)
-    return total
+
+    def some(step, total):
+        for t in (2 * step, 2 * step + 1):
+            picked = [
+                ref[t, pl.ds(2 * EDGE + k, down, stride=COARSE), :] for k in range(COARSE)
+            ]
+            part = sum(picked[1:], picked[0])
+            for by in (1, 2, 4):
+                part = part + roll(part, -by, 1)
+            part = pick_lanes(part, (lane & (LANES // COARSE - 1)) * COARSE)
+            total = jnp.where(lane // (LANES // COARSE) == t, part, total)
+        return total
+
+    return lax.fori_loop(0, tiles // 2, some, jnp.zeros((down, LANES), jnp.float32))
 
 
 def side_lanes(has_e, has_w):
@@ -267,26 +270,26 @@
 
 
 def jacobi(source, table, work):
-    factor, east, west, south, north = [table[index] for index in range(5)]
     window = source.shape[0]
-    source = factor * source
-    iterate = source
-    for sweep_index in range(SWEEPS - 1):
-        place_ref = work.at[sweep_index % 2]
+    source = table[0] * source
+
+    def once(index, iterate):
+        rows_ref = work.at[index % 2]
         for half in range(2):
-            place_ref[half, EDGE : EDGE + window, :] = iterate[
+            rows_ref[half, EDGE : EDGE + window, :] = iterate[
                 :, half * LANES : (half + 1) * LANES
             ]
         above, below = [
             jnp.concatenate(
-                [place_ref[half, EDGE + by : EDGE + by + window, :] for half in range(2)], axis=1
+                [rows_ref[half, EDGE + by : EDGE + by + window, :] for half in range(2)], axis=1
             )
             for by in (-1, 1)
         ]
-        across = east * roll(iterate, -1, 1) + west * roll(iterate, 1, 1)
-        along = south * below + north * above
-        iterate = ((1.0 - OMEGA) * iterate + source) + (across + along)
-    return iterate
+        across = table[1] * roll(iterate, -1, 1) + table[2] * roll(iterate, 1, 1)
+        along = table[3] * below + table[4] * above
+        return ((1.0 - OMEGA) * iterate + source) + (across + along)
+
+    return lax.fori_loop(0, SWEEPS - 1, once, source)
 
 
 def clear_work(work):
@@ -696,27 +699,25 @@
         table_ref[index] = part
     sides = side_lanes(has_e, has_w)
     half = iota((STRIP, LANES), 0) // EDGE
-    pending = []
-    total = dot_in[...]
-    for index, known in ((0, has_n), (1, has_s)):
-        at = EDGE + index * height
+
+    def ends(index, total):
+        at = pl.multiple_of(EDGE + index * height, EDGE)
         fields = begin(obs, cond, at, taps, sides)
         own = jnp.where(half == index, 0.0, 1.0)
         total = total + fold(own * product_sum_rows(fields[3], fields[4], tiles))
-        flag = jnp.where(half == index, known, 1.0)
-        inverse, start = [[part * flag for part in fields[index]] for index in (2, 4)]
+        flag = jnp.where(half == index, jnp.where(index == 0, has_n, has_s), 1.0)
+        inverse, start = [[part * flag for part in fields[which]] for which in (2, 4)]
         fields = (*fields[:2], inverse, fields[3], start)
-        pending += [
-            (ref, at, strip)
-            for ref, strip in zip((east_ref, south_ref, inv_ref, res_ref, u_ref), fields)
-        ]
-    cells = jacobi(source, table, work)
+        for ref, strip in zip((east_ref, south_ref, inv_ref, res_ref, u_ref), fields):
+            store(ref, at, strip)
+        return total
+
+    total = lax.fori_loop(0, 2, ends, dot_in[...])
+    cells = jacobi(source, table_ref, work)
     spread_cells(cells, spread)
     inner_cells = slice(EDGE, EDGE + down)
     total = total + fold(source[inner_cells, :LANES] * cells[inner_cells, :LANES])
     dots_ref[0] = total
-    for ref, at, strip in pending:
-        store(ref, at, strip)
 
     def flags(at, start):
         rows = [at + by for by in range(0, STRIP, EDGE)]
@@ -759,10 +760,9 @@
             else:
                 piece = own[:EDGE] if down_by < 0 else own[down - EDGE :]
             to_row, to_col = at_row + down_by, at_col + right_by
-
-            @pl.when((to_row >= 0) & (to_row < n_rows) & (to_col >= 0) & (to_col < n_cols))
-            def _(piece=piece, to_row=to_row, to_col=to_col):
-                chunk_ref[to_col * n_rows + to_row] = piece
+            there = (to_row >= 0) & (to_row < n_rows) & (to_col >= 0) & (to_col < n_cols)
+            slot = jnp.where(there, to_col * n_rows + to_row, at_col * n_rows + at_row)
+            chunk_ref[slot] = piece * jnp.where(there, 1.0, 0.0)
 
 
 def first(taps, fields, got_a, got_b, coarse, dot):

time: 52.5 us -> 53.8 us (1.025)
  Pallas kernels: 20.5 us -> 21.8 us
    pallas_call x1, Pallas kernels: 6.18 us -> 7.4 us  [first(): pl.pallas_call(functools.partial(first_kernel, tiles, down), in_specs=[SM...]
where the time goes in v8:
time: 53.8 us; the launch traced here: 53.5 us
  Pallas kernels  21.8 us (41%)
  blocking collectives  21 us (39%)
  starting transfers between devices  10 us (19%)
  between operations  0.72 us (1%)
    all_to_all x1, blocking collectives, body(): got = lax.all_to_all(chunk, AXES, 0, 0, tiled=True)  12.1 us
    all_to_all x1, blocking collectives, body(): sums = lax.all_to_all(line, AXES, 0, 0, tiled=True)  8.92 us
    ppermute x2, starting transfers between devices, exchange(): got_a = lax.ppermute(send_a, axis, pairs(0))  8.71 us
    pallas_call x1, Pallas kernels, first(): pl.pallas_call(functools.partial(first_kernel, tiles, down), in_specs=[SM...  7.4 us
    pallas_call x1, Pallas kernels, second(): pl.pallas_call(functools.partial(second_kernel, tiles, down), in_specs=[S...  5.39 us
    pallas_call x1, Pallas kernels, inner(): pl.pallas_call(inner_kernel, in_specs=[SMEM] + [VMEM] * 2, out_specs=[VME...  2.93 us
    pallas_call x1, Pallas kernels, pack(): pl.pallas_call(functools.partial(pack_kernel, tiles, down), in_specs=[HBM...  2.52 us
    pallas_call x1, Pallas kernels, edge(): pl.pallas_call(functools.partial(edge_kernel, tiles, down), in_specs=[HBM...  1.68 us
  transfers between devices with their start and end apart: 4, of which 0 were waited for; matrix products, arithmetic and copies ran while one was open for 0% of the time, Pallas kernels for 10%

profile of v8, /device:TPU:0, one launch (start us, length us, event | category | flops | bytes accessed | tf_op | source)
XLA Modules:
  0.0 53.5 jit_solution(13599302172207809086)
XLA Ops:
  0.6 1.7 %pack_east_west.1 = (f32[64,128]{1,0:T(8,128)S(1)}, f32[64,128]{1,0:T(8,128)S(1)}) custom-call(f32[256,1024]{1,0:T(8,128)} %refs_0_.3, s32[256,1024]{1,0:T(8,128)} %refs_1_.3, f32[4]{0:T(128)} %refs_2_.3, f32[3,3]{1,0:T(4,128)} %taps.5), custom_call_target="tpu_custom_call" | custom-call | tf_op jit(solution)/shard_map/pack_east_west/pallas_call | solution.py:429
  2.3 0.7 %collective-permute-start = (f32[64,128]{1,0:T(8,128)S(1)}, f32[64,128]{1,0:T(8,128)S(1)}, u32[]{:S(2)}, u32[]{:S(2)}) collective-permute-start(f32[64,128]{1,0:T(8,128)S(1)} %get-tuple-element.31), channel_id=1, source_target_pairs={{4,8},{8,4},{12,16},{16,12},{20,24},{24,20},{5,9},{9,5},{13,17},{1... | collective-permute-start | bytes 98312 | tf_op jit(solution)/shard_map/ppermute | solution.py:972
  3.0 5.8 %collective-permute-start.1 = (f32[64,128]{1,0:T(8,128)S(1)}, f32[64,128]{1,0:T(8,128)S(1)}, u32[]{:S(2)}, u32[]{:S(2)}) collective-permute-start(f32[64,128]{1,0:T(8,128)S(1)} %get-tuple-element.32.refs_4_), channel_id=1, source_target_pairs={{0,4},{4,0},{8,12},{12,8},{16,20},{20,16},{24,28},{28,24},{1,5},{5... | collective-permute-start | bytes 98312 | tf_op jit(solution)/shard_map/ppermute | solution.py:973
  8.8 2.5 %pack_all.1 = (f32[9,288,128]{2,1,0:T(8,128)S(1)}, f32[9,288,128]{2,1,0:T(8,128)S(1)}, f32[4,48,256]{2,1,0:T(8,128)S(1)}) custom-call(f32[256,1024]{1,0:T(8,128)} %refs_0_.3, s32[256,1024]{1,0:T(8,128)} %refs_1_.3, f32[4]{0:T(128)} %refs_2_.3, f32[3,3]{1,0:T(4,128)} %taps.5, f32[64,128]{1,0:T(8,128)S(1)} %get-tuple-element.32.refs_4_), custom_call_target="tpu_custom_call" | custom-call | flops 5242880 | bytes 4194304 | tf_op jit(solution)/shard_map/pack_all/pallas_call | solution.py:461
  11.3 0.0 collective-permute-done.got_b
  11.3 0.0 collective-permute-done.1.got_a
  11.3 0.0 copy-start
  11.3 0.3 pack_north_south.1
  11.6 0.7 %collective-permute-start.2 = (f32[22,8,128]{2,1,0:T(8,128)S(1)}, f32[22,8,128]{2,1,0:T(8,128)S(1)}, u32[]{:S(2)}, u32[]{:S(2)}) collective-permute-start(f32[22,8,128]{2,1,0:T(8,128)S(1)} %get-tuple-element.43), channel_id=1, source_target_pairs={{1,2},{2,1},{5,6},{6,5},{9,10},{10,9},{13,14},{14,13},{17,18},{18,... | collective-permute-start | bytes 270344 | tf_op jit(solution)/shard_map/ppermute | solution.py:972
  12.3 2.9 %collective-permute-start.3 = (f32[22,8,128]{2,1,0:T(8,128)S(1)}, f32[22,8,128]{2,1,0:T(8,128)S(1)}, u32[]{:S(2)}, u32[]{:S(2)}) collective-permute-start(f32[22,8,128]{2,1,0:T(8,128)S(1)} %get-tuple-element.44), channel_id=1, source_target_pairs={{0,1},{1,0},{2,3},{3,2},{4,5},{5,4},{6,7},{7,6},{8,9},{9,8},{10,11... | collective-permute-start | bytes 270344 | tf_op jit(solution)/shard_map/ppermute | solution.py:973
  15.2 0.0 copy-done
  15.2 2.9 %inner_strips.1 = (f32[9,288,128]{2,1,0:T(8,128)S(1)}, f32[9,288,128]{2,1,0:T(8,128)S(1)}, f32[9,288,128]{2,1,0:T(8,128)S(1)}, f32[9,288,128]{2,1,0:T(8,128)S(1)...) custom-call(f32[3,3]{1,0:T(4,128)S(1)} %copy-done, f32[9,288,128]{2,1,0:T(8,128)S(1)} %get-tuple-element.36.obs.obs_in, ...), custom_call_target="tpu_custom_call" | custom-call | flops 14929920 | bytes 7962624 | tf_op jit(solution)/shard_map/inner_strips/pallas_call | solution.py:600
  18.1 0.0 collective-permute-done.2.got_b
  18.1 0.0 collective-permute-done.3.got_a
  18.2 7.4 %first_direction.1 = (f32[9,288,128]{2,1,0:T(8,128)S(1)}, f32[9,288,128]{2,1,0:T(8,128)S(1)}, f32[9,288,128]{2,1,0:T(8,128)S(1)}, f32[9,288,128]{2,1,0:T(8,128)S...) custom-call(f32[3,3]{1,0:T(4,128)S(1)} %copy-done, ...), custom_call_target="tpu_custom_call", output_to_operand_aliasing={{0}: (1, {}), {1}: (2, {}), {2}: (3, {}), {3}: (4, {}), {4}... | custom-call | tf_op jit(solution)/shard_map/first_direction/pallas_call | solution.py:780
  25.6 12.1 %all_to_all.10.got_ref = f32[32,8,128]{2,1,0:T(8,128)S(1)} all-to-all(f32[32,8,128]{2,1,0:T(8,128)S(1)} %get-tuple-element.47), channel_id=1, replica_groups=mesh['cols'=8,'rows'=4] {'cols','rows'}, dimensions={0} | all-to-all | bytes 262144 | tf_op jit(solution)/shard_map/all_to_all | solution.py:989
  37.6 5.4 %second_direction.1 = (f32[9,288,128]{2,1,0:T(8,128)S(1)}, f32[9,288,128]{2,1,0:T(8,128)S(1)}, f32[32,1,128]{2,1,0:T(1,128)S(1)}) custom-call(f32[3,3]{1,0:T(4,128)S(1)} %copy-done, f32[32,8,128]{2,1,0:T(8,128)S(1)} %all_to_all.10.got_ref, f32[32,128]{1,0:T(8,128)S(1)} %get-tuple-element.48.own_ref, f32[5,48,256]{2,1,0:T(8,128)S(1)} %get-tuple-element.49.table_ref, ...), custom_call_target="tpu_custom_call" | custom-call | tf_op jit(solution)/shard_map/second_direction/pallas_call | solution.py:883
  43.0 8.9 %all_to_all.11.sums_ref = f32[32,1,128]{2,1,0:T(1,128)S(1)} all-to-all(f32[32,1,128]{2,1,0:T(1,128)S(1)} %get-tuple-element.55), channel_id=1, replica_groups=mesh['cols'=8,'rows'=4] {'cols','rows'}, dimensions={0} | all-to-all | bytes 32768 | tf_op jit(solution)/shard_map/all_to_all | solution.py:991
  51.9 1.6 %combine.1 = (f32[256,1024]{1,0:T(8,128)}, f32[256,1024]{1,0:T(8,128)}) custom-call(f32[32,1,128]{2,1,0:T(1,128)S(1)} %all_to_all.11.sums_ref, f32[9,288,128]{2,1,0:T(8,128)S(1)} %get-tuple-element.56.p_ref, f32[9,288,128]{2,1,0:T(8,128)S(1)} %get-tuple-element.57.w_ref, f32[9,288,128]{2,1,0:T(8,128)S(1)} %get-tuple-element.58.r_ref, ...), custom_call_target="tpu_custom_call" | custom-call | tf_op jit(solution)/shard_map/combine/pallas_call | solution.py:949
Async XLA Ops:
  2.3 9.0 %collective-permute-start = (f32[64,128]{1,0:T(8,128)S(1)}, f32[64,128]{1,0:T(8,128)S(1)}, u32[]{:S(2)}, u32[]{:S(2)}) collective-permute-start(f32[64,128]{1,0:T(8,128)S(1)} %get-tuple-element.31), channel_id=1, source_target_pairs={{4,8},{8,4},{12,16},{16,12},{20,24},{24,20},{5,9},{9,5},{13,17},{1... | collective-permute-start | bytes 98312 | tf_op jit(solution)/shard_map/ppermute | solution.py:972
  3.0 8.3 %collective-permute-start.1 = (f32[64,128]{1,0:T(8,128)S(1)}, f32[64,128]{1,0:T(8,128)S(1)}, u32[]{:S(2)}, u32[]{:S(2)}) collective-permute-start(f32[64,128]{1,0:T(8,128)S(1)} %get-tuple-element.32.refs_4_), channel_id=1, source_target_pairs={{0,4},{4,0},{8,12},{12,8},{16,20},{20,16},{24,28},{28,24},{1,5},{5... | collective-permute-start | bytes 98312 | tf_op jit(solution)/shard_map/ppermute | solution.py:973
  11.3 3.9 %copy-start = (f32[3,3]{1,0:T(4,128)S(1)}, f32[3,3]{1,0:T(4,128)}, u32[]{:S(2)}) copy-start(f32[3,3]{1,0:T(4,128)} %taps.5) | copy-start | bytes 112
  11.6 6.5 %collective-permute-start.2 = (f32[22,8,128]{2,1,0:T(8,128)S(1)}, f32[22,8,128]{2,1,0:T(8,128)S(1)}, u32[]{:S(2)}, u32[]{:S(2)}) collective-permute-start(f32[22,8,128]{2,1,0:T(8,128)S(1)} %get-tuple-element.43), channel_id=1, source_target_pairs={{1,2},{2,1},{5,6},{6,5},{9,10},{10,9},{13,14},{14,13},{17,18},{18,... | collective-permute-start | bytes 270344 | tf_op jit(solution)/shard_map/ppermute | solution.py:972
  12.3 5.9 %collective-permute-start.3 = (f32[22,8,128]{2,1,0:T(8,128)S(1)}, f32[22,8,128]{2,1,0:T(8,128)S(1)}, u32[]{:S(2)}, u32[]{:S(2)}) collective-permute-start(f32[22,8,128]{2,1,0:T(8,128)S(1)} %get-tuple-element.44), channel_id=1, source_target_pairs={{0,1},{1,0},{2,3},{3,2},{4,5},{5,4},{6,7},{7,6},{8,9},{9,8},{10,11... | collective-permute-start | bytes 270344 | tf_op jit(solution)/shard_map/ppermute | solution.py:973

commit v9 on v7

--- a/solution.py
+++ b/solution.py
@@ -16,7 +16,6 @@
 HALF = LANES // 2
 EDGE = 8
 STRIP = 2 * EDGE
-GROUP = 2
 CHUNK = 32
 AXES = ("cols", "rows")
 LIMIT = 40 * 1024 * 1024
@@ -248,8 +247,8 @@
     return sum(parts[1:], parts[0])
 
 
-def sweep(first, last, body, carry):
-    width = GROUP * STRIP
+def sweep(group, first, last, body, carry):
+    width = group * STRIP
     steps = -(-(last - first) // width)
 
     def work(index, carry):
@@ -588,7 +587,7 @@
         return list(zip((east_ref, south_ref, inv_ref, res_ref, u_ref), fields)), total
 
     nothing = jnp.zeros((EDGE, LANES), jnp.float32)
-    dot_ref[...] = sweep(3 * EDGE, obs.shape[1] - 3 * EDGE, work, nothing)
+    dot_ref[...] = sweep(5, 3 * EDGE, obs.shape[1] - 3 * EDGE, work, nothing)
 
 
 def inner(taps, obs, cond):
@@ -740,10 +739,10 @@
 
     nothing = jnp.zeros((EDGE, LANES), jnp.float32)
     span = (EDGE, 3 * EDGE + height)
-    sweep(*span, begin_p, 0)
-    sweep(*span, blur, 0)
+    sweep(6, *span, begin_p, 0)
+    sweep(6, *span, blur, 0)
     mask_rows(image, has_n, has_s)
-    dots_ref[1] = sweep(*span, finish, nothing)
+    dots_ref[1] = sweep(6, *span, finish, nothing)
 
     own = cell_sums(q_ref, tiles, down)
     own_ref[...] = own
@@ -759,10 +758,9 @@
             else:
                 piece = own[:EDGE] if down_by < 0 else own[down - EDGE :]
             to_row, to_col = at_row + down_by, at_col + right_by
-
-            @pl.when((to_row >= 0) & (to_row < n_rows) & (to_col >= 0) & (to_col < n_cols))
-            def _(piece=piece, to_row=to_row, to_col=to_col):
-                chunk_ref[to_col * n_rows + to_row] = piece
+            there = (to_row >= 0) & (to_row < n_rows) & (to_col >= 0) & (to_col < n_cols)
+            slot = jnp.where(there, to_col * n_rows + to_row, at_col * n_rows + at_row)
+            chunk_ref[slot] = piece * jnp.where(there, 1.0, 0.0)
 
 
 def first(taps, fields, got_a, got_b, coarse, dot):
@@ -860,10 +858,10 @@
 
     nothing = jnp.zeros((EDGE, LANES), jnp.float32)
     span = (EDGE, 3 * EDGE + height)
-    dot_qw = sweep(*span, begin_w, nothing)
-    sweep(*span, blur, 0)
+    dot_qw = sweep(3, *span, begin_w, nothing)
+    sweep(3, *span, blur, 0)
     mask_rows(image, has_n, has_s)
-    dot_wv = sweep(2 * EDGE, 2 * EDGE + height, finish, nothing)
+    dot_wv = sweep(4, 2 * EDGE, 2 * EDGE + height, finish, nothing)
     line = jnp.zeros((1, LANES), jnp.float32)
     block = iota((1, LANES), 1) // (LANES // 4)
     for index, part in enumerate((dots_in[0], dots_in[1], dot_qw, dot_wv)):

time: 52.5 us -> 52 us (level)
  Pallas kernels: 20.5 us -> 19.7 us
where the time goes in v9:
time: 52 us; the launch traced here: 51.7 us
  blocking collectives  21.2 us (41%)
  Pallas kernels  19.7 us (38%)
  starting transfers between devices  10 us (19%)
  between operations  0.73 us (1%)
    all_to_all x1, blocking collectives, body(): got = lax.all_to_all(chunk, AXES, 0, 0, tiled=True)  12.3 us
    all_to_all x1, blocking collectives, body(): sums = lax.all_to_all(line, AXES, 0, 0, tiled=True)  8.92 us
    ppermute x2, starting transfers between devices, exchange(): got_a = lax.ppermute(send_a, axis, pairs(0))  8.71 us
    pallas_call x1, Pallas kernels, first(): pl.pallas_call(functools.partial(first_kernel, tiles, down), in_specs=[SM...  5.8 us
    pallas_call x1, Pallas kernels, second(): pl.pallas_call(functools.partial(second_kernel, tiles, down), in_specs=[S...  5.19 us
    pallas_call x1, Pallas kernels, inner(): pl.pallas_call(inner_kernel, in_specs=[SMEM] + [VMEM] * 2, out_specs=[VME...  2.66 us
    pallas_call x1, Pallas kernels, pack(): pl.pallas_call(functools.partial(pack_kernel, tiles, down), in_specs=[HBM...  2.52 us
    pallas_call x1, Pallas kernels, edge(): pl.pallas_call(functools.partial(edge_kernel, tiles, down), in_specs=[HBM...  1.68 us
  transfers between devices with their start and end apart: 4, of which 0 were waited for; matrix products, arithmetic and copies ran while one was open for 0% of the time, Pallas kernels for 10%

profile of v9, /device:TPU:0, one launch (start us, length us, event | category | flops | bytes accessed | tf_op | source)
XLA Modules:
  0.0 51.7 jit_solution(7817791411025997951)
XLA Ops:
  0.6 1.7 %pack_east_west.1 = (f32[64,128]{1,0:T(8,128)S(1)}, f32[64,128]{1,0:T(8,128)S(1)}) custom-call(f32[256,1024]{1,0:T(8,128)} %refs_0_.3, s32[256,1024]{1,0:T(8,128)} %refs_1_.3, f32[4]{0:T(128)} %refs_2_.3, f32[3,3]{1,0:T(4,128)} %taps.5), custom_call_target="tpu_custom_call" | custom-call | tf_op jit(solution)/shard_map/pack_east_west/pallas_call | solution.py:425
  2.3 0.7 %collective-permute-start = (f32[64,128]{1,0:T(8,128)S(1)}, f32[64,128]{1,0:T(8,128)S(1)}, u32[]{:S(2)}, u32[]{:S(2)}) collective-permute-start(f32[64,128]{1,0:T(8,128)S(1)} %get-tuple-element.31), channel_id=1, source_target_pairs={{4,8},{8,4},{12,16},{16,12},{20,24},{24,20},{5,9},{9,5},{13,17},{1... | collective-permute-start | bytes 98312 | tf_op jit(solution)/shard_map/ppermute | solution.py:970
  3.0 5.8 %collective-permute-start.1 = (f32[64,128]{1,0:T(8,128)S(1)}, f32[64,128]{1,0:T(8,128)S(1)}, u32[]{:S(2)}, u32[]{:S(2)}) collective-permute-start(f32[64,128]{1,0:T(8,128)S(1)} %get-tuple-element.32.refs_4_), channel_id=1, source_target_pairs={{0,4},{4,0},{8,12},{12,8},{16,20},{20,16},{24,28},{28,24},{1,5},{5... | collective-permute-start | bytes 98312 | tf_op jit(solution)/shard_map/ppermute | solution.py:971
  8.8 2.5 %pack_all.1 = (f32[9,288,128]{2,1,0:T(8,128)S(1)}, f32[9,288,128]{2,1,0:T(8,128)S(1)}, f32[4,48,256]{2,1,0:T(8,128)S(1)}) custom-call(f32[256,1024]{1,0:T(8,128)} %refs_0_.3, s32[256,1024]{1,0:T(8,128)} %refs_1_.3, f32[4]{0:T(128)} %refs_2_.3, f32[3,3]{1,0:T(4,128)} %taps.5, f32[64,128]{1,0:T(8,128)S(1)} %get-tuple-element.32.refs_4_), custom_call_target="tpu_custom_call" | custom-call | flops 5242880 | bytes 4194304 | tf_op jit(solution)/shard_map/pack_all/pallas_call | solution.py:457
  11.3 0.0 collective-permute-done.got_b
  11.3 0.0 collective-permute-done.1.got_a
  11.3 0.0 copy-start
  11.3 0.3 pack_north_south.1
  11.6 0.7 %collective-permute-start.2 = (f32[22,8,128]{2,1,0:T(8,128)S(1)}, f32[22,8,128]{2,1,0:T(8,128)S(1)}, u32[]{:S(2)}, u32[]{:S(2)}) collective-permute-start(f32[22,8,128]{2,1,0:T(8,128)S(1)} %get-tuple-element.43), channel_id=1, source_target_pairs={{1,2},{2,1},{5,6},{6,5},{9,10},{10,9},{13,14},{14,13},{17,18},{18,... | collective-permute-start | bytes 270344 | tf_op jit(solution)/shard_map/ppermute | solution.py:970
  12.3 2.9 %collective-permute-start.3 = (f32[22,8,128]{2,1,0:T(8,128)S(1)}, f32[22,8,128]{2,1,0:T(8,128)S(1)}, u32[]{:S(2)}, u32[]{:S(2)}) collective-permute-start(f32[22,8,128]{2,1,0:T(8,128)S(1)} %get-tuple-element.44), channel_id=1, source_target_pairs={{0,1},{1,0},{2,3},{3,2},{4,5},{5,4},{6,7},{7,6},{8,9},{9,8},{10,11... | collective-permute-start | bytes 270344 | tf_op jit(solution)/shard_map/ppermute | solution.py:971
  15.2 0.0 copy-done
  15.2 2.7 %inner_strips.1 = (f32[9,288,128]{2,1,0:T(8,128)S(1)}, f32[9,288,128]{2,1,0:T(8,128)S(1)}, f32[9,288,128]{2,1,0:T(8,128)S(1)}, f32[9,288,128]{2,1,0:T(8,128)S(1)...) custom-call(f32[3,3]{1,0:T(4,128)S(1)} %copy-done, f32[9,288,128]{2,1,0:T(8,128)S(1)} %get-tuple-element.36.obs.obs_in, ...), custom_call_target="tpu_custom_call" | custom-call | flops 14929920 | bytes 7962624 | tf_op jit(solution)/shard_map/inner_strips/pallas_call | solution.py:596
  17.9 0.0 collective-permute-done.2.got_b
  17.9 0.0 collective-permute-done.3.got_a
  17.9 5.8 %first_direction.1 = (f32[9,288,128]{2,1,0:T(8,128)S(1)}, f32[9,288,128]{2,1,0:T(8,128)S(1)}, f32[9,288,128]{2,1,0:T(8,128)S(1)}, f32[9,288,128]{2,1,0:T(8,128)S...) custom-call(f32[3,3]{1,0:T(4,128)S(1)} %copy-done, ...), custom_call_target="tpu_custom_call", output_to_operand_aliasing={{0}: (1, {}), {1}: (2, {}), {2}: (3, {}), {3}: (4, {}), {4}... | custom-call | tf_op jit(solution)/shard_map/first_direction/pallas_call | solution.py:778
  23.7 12.3 %all_to_all.10.got_ref = f32[32,8,128]{2,1,0:T(8,128)S(1)} all-to-all(f32[32,8,128]{2,1,0:T(8,128)S(1)} %get-tuple-element.47), channel_id=1, replica_groups=mesh['cols'=8,'rows'=4] {'cols','rows'}, dimensions={0} | all-to-all | bytes 262144 | tf_op jit(solution)/shard_map/all_to_all | solution.py:987
  36.0 5.2 %second_direction.1 = (f32[9,288,128]{2,1,0:T(8,128)S(1)}, f32[9,288,128]{2,1,0:T(8,128)S(1)}, f32[32,1,128]{2,1,0:T(1,128)S(1)}) custom-call(f32[3,3]{1,0:T(4,128)S(1)} %copy-done, f32[32,8,128]{2,1,0:T(8,128)S(1)} %all_to_all.10.got_ref, f32[32,128]{1,0:T(8,128)S(1)} %get-tuple-element.48.own_ref, f32[5,48,256]{2,1,0:T(8,128)S(1)} %get-tuple-element.49.table_ref, ...), custom_call_target="tpu_custom_call" | custom-call | tf_op jit(solution)/shard_map/second_direction/pallas_call | solution.py:881
  41.2 8.9 %all_to_all.11.sums_ref = f32[32,1,128]{2,1,0:T(1,128)S(1)} all-to-all(f32[32,1,128]{2,1,0:T(1,128)S(1)} %get-tuple-element.55), channel_id=1, replica_groups=mesh['cols'=8,'rows'=4] {'cols','rows'}, dimensions={0} | all-to-all | bytes 32768 | tf_op jit(solution)/shard_map/all_to_all | solution.py:989
  50.1 1.6 %combine.1 = (f32[256,1024]{1,0:T(8,128)}, f32[256,1024]{1,0:T(8,128)}) custom-call(f32[32,1,128]{2,1,0:T(1,128)S(1)} %all_to_all.11.sums_ref, f32[9,288,128]{2,1,0:T(8,128)S(1)} %get-tuple-element.56.p_ref, f32[9,288,128]{2,1,0:T(8,128)S(1)} %get-tuple-element.57.w_ref, f32[9,288,128]{2,1,0:T(8,128)S(1)} %get-tuple-element.58.r_ref, ...), custom_call_target="tpu_custom_call" | custom-call | tf_op jit(solution)/shard_map/combine/pallas_call | solution.py:947
Async XLA Ops:
  2.3 9.0 %collective-permute-start = (f32[64,128]{1,0:T(8,128)S(1)}, f32[64,128]{1,0:T(8,128)S(1)}, u32[]{:S(2)}, u32[]{:S(2)}) collective-permute-start(f32[64,128]{1,0:T(8,128)S(1)} %get-tuple-element.31), channel_id=1, source_target_pairs={{4,8},{8,4},{12,16},{16,12},{20,24},{24,20},{5,9},{9,5},{13,17},{1... | collective-permute-start | bytes 98312 | tf_op jit(solution)/shard_map/ppermute | solution.py:970
  3.0 8.3 %collective-permute-start.1 = (f32[64,128]{1,0:T(8,128)S(1)}, f32[64,128]{1,0:T(8,128)S(1)}, u32[]{:S(2)}, u32[]{:S(2)}) collective-permute-start(f32[64,128]{1,0:T(8,128)S(1)} %get-tuple-element.32.refs_4_), channel_id=1, source_target_pairs={{0,4},{4,0},{8,12},{12,8},{16,20},{20,16},{24,28},{28,24},{1,5},{5... | collective-permute-start | bytes 98312 | tf_op jit(solution)/shard_map/ppermute | solution.py:971
  11.3 3.9 %copy-start = (f32[3,3]{1,0:T(4,128)S(1)}, f32[3,3]{1,0:T(4,128)}, u32[]{:S(2)}) copy-start(f32[3,3]{1,0:T(4,128)} %taps.5) | copy-start | bytes 112
  11.6 6.3 %collective-permute-start.2 = (f32[22,8,128]{2,1,0:T(8,128)S(1)}, f32[22,8,128]{2,1,0:T(8,128)S(1)}, u32[]{:S(2)}, u32[]{:S(2)}) collective-permute-start(f32[22,8,128]{2,1,0:T(8,128)S(1)} %get-tuple-element.43), channel_id=1, source_target_pairs={{1,2},{2,1},{5,6},{6,5},{9,10},{10,9},{13,14},{14,13},{17,18},{18,... | collective-permute-start | bytes 270344 | tf_op jit(solution)/shard_map/ppermute | solution.py:970
  12.3 5.6 %collective-permute-start.3 = (f32[22,8,128]{2,1,0:T(8,128)S(1)}, f32[22,8,128]{2,1,0:T(8,128)S(1)}, u32[]{:S(2)}, u32[]{:S(2)}) collective-permute-start(f32[22,8,128]{2,1,0:T(8,128)S(1)} %get-tuple-element.44), channel_id=1, source_target_pairs={{0,1},{1,0},{2,3},{3,2},{4,5},{5,4},{6,7},{7,6},{8,9},{9,8},{10,11... | collective-permute-start | bytes 270344 | tf_op jit(solution)/shard_map/ppermute | solution.py:971

commit v10 on v9

--- a/solution.py
+++ b/solution.py
@@ -16,7 +16,7 @@
 HALF = LANES // 2
 EDGE = 8
 STRIP = 2 * EDGE
-CHUNK = 32
+CHUNK = 64
 AXES = ("cols", "rows")
 LIMIT = 40 * 1024 * 1024
 
@@ -739,10 +739,10 @@
 
     nothing = jnp.zeros((EDGE, LANES), jnp.float32)
     span = (EDGE, 3 * EDGE + height)
-    sweep(6, *span, begin_p, 0)
-    sweep(6, *span, blur, 0)
+    sweep(3, *span, begin_p, 0)
+    sweep(3, *span, blur, 0)
     mask_rows(image, has_n, has_s)
-    dots_ref[1] = sweep(6, *span, finish, nothing)
+    dots_ref[1] = sweep(3, *span, finish, nothing)
 
     own = cell_sums(q_ref, tiles, down)
     own_ref[...] = own
@@ -986,7 +986,7 @@
     )
     got = lax.all_to_all(chunk, AXES, 0, 0, tiled=True)
     w, v, line = second(blur_kernel, got, own, table, q, east, south, inv, dots)
-    sums = lax.all_to_all(line, AXES, 0, 0, tiled=True)
+    sums = lax.all_to_all(line, AXES[::-1], 0, 0, tiled=True)
     return tuple(combine(sums, p, w, r, q, v))
 
 

time: 52 us -> 52 us (level)
  no operation moved by 1% of the time
where the time goes in v10:
time: 52 us; the launch traced here: 51.7 us
  blocking collectives  21.2 us (41%)
  Pallas kernels  19.7 us (38%)
  starting transfers between devices  10 us (19%)
  between operations  0.73 us (1%)
    all_to_all x1, blocking collectives, body(): got = lax.all_to_all(chunk, AXES, 0, 0, tiled=True)  12.3 us
    all_to_all x1, blocking collectives, body(): sums = lax.all_to_all(line, AXES[::-1], 0, 0, tiled=True)  8.89 us
    ppermute x2, starting transfers between devices, exchange(): got_a = lax.ppermute(send_a, axis, pairs(0))  8.71 us
    pallas_call x1, Pallas kernels, first(): pl.pallas_call(functools.partial(first_kernel, tiles, down), in_specs=[SM...  5.87 us
    pallas_call x1, Pallas kernels, second(): pl.pallas_call(functools.partial(second_kernel, tiles, down), in_specs=[S...  5.19 us
    pallas_call x1, Pallas kernels, inner(): pl.pallas_call(inner_kernel, in_specs=[SMEM] + [VMEM] * 2, out_specs=[VME...  2.66 us
    pallas_call x1, Pallas kernels, pack(): pl.pallas_call(functools.partial(pack_kernel, tiles, down), in_specs=[HBM...  2.52 us
    pallas_call x1, Pallas kernels, edge(): pl.pallas_call(functools.partial(edge_kernel, tiles, down), in_specs=[HBM...  1.68 us
  transfers between devices with their start and end apart: 4, of which 0 were waited for; matrix products, arithmetic and copies ran while one was open for 0% of the time, Pallas kernels for 10%

profile of v10, /device:TPU:0, one launch (start us, length us, event | category | flops | bytes accessed | tf_op | source)
XLA Modules:
  0.0 51.7 jit_solution(13148634259053356464)
XLA Ops:
  0.6 1.7 %pack_east_west.1 = (f32[64,128]{1,0:T(8,128)S(1)}, f32[64,128]{1,0:T(8,128)S(1)}) custom-call(f32[256,1024]{1,0:T(8,128)} %refs_0_.3, s32[256,1024]{1,0:T(8,128)} %refs_1_.3, f32[4]{0:T(128)} %refs_2_.3, f32[3,3]{1,0:T(4,128)} %taps.5), custom_call_target="tpu_custom_call" | custom-call | tf_op jit(solution)/shard_map/pack_east_west/pallas_call | solution.py:425
  2.3 0.7 %collective-permute-start = (f32[64,128]{1,0:T(8,128)S(1)}, f32[64,128]{1,0:T(8,128)S(1)}, u32[]{:S(2)}, u32[]{:S(2)}) collective-permute-start(f32[64,128]{1,0:T(8,128)S(1)} %get-tuple-element.31), channel_id=1, source_target_pairs={{4,8},{8,4},{12,16},{16,12},{20,24},{24,20},{5,9},{9,5},{13,17},{1... | collective-permute-start | bytes 98312 | tf_op jit(solution)/shard_map/ppermute | solution.py:970
  3.0 5.8 %collective-permute-start.1 = (f32[64,128]{1,0:T(8,128)S(1)}, f32[64,128]{1,0:T(8,128)S(1)}, u32[]{:S(2)}, u32[]{:S(2)}) collective-permute-start(f32[64,128]{1,0:T(8,128)S(1)} %get-tuple-element.32.refs_4_), channel_id=1, source_target_pairs={{0,4},{4,0},{8,12},{12,8},{16,20},{20,16},{24,28},{28,24},{1,5},{5... | collective-permute-start | bytes 98312 | tf_op jit(solution)/shard_map/ppermute | solution.py:971
  8.8 2.5 %pack_all.1 = (f32[9,288,128]{2,1,0:T(8,128)S(1)}, f32[9,288,128]{2,1,0:T(8,128)S(1)}, f32[4,48,256]{2,1,0:T(8,128)S(1)}) custom-call(f32[256,1024]{1,0:T(8,128)} %refs_0_.3, s32[256,1024]{1,0:T(8,128)} %refs_1_.3, f32[4]{0:T(128)} %refs_2_.3, f32[3,3]{1,0:T(4,128)} %taps.5, f32[64,128]{1,0:T(8,128)S(1)} %get-tuple-element.32.refs_4_), custom_call_target="tpu_custom_call" | custom-call | flops 5242880 | bytes 4194304 | tf_op jit(solution)/shard_map/pack_all/pallas_call | solution.py:457
  11.3 0.0 collective-permute-done.got_b
  11.3 0.0 collective-permute-done.1.got_a
  11.3 0.0 copy-start
  11.3 0.3 pack_north_south.1
  11.6 0.7 %collective-permute-start.2 = (f32[22,8,128]{2,1,0:T(8,128)S(1)}, f32[22,8,128]{2,1,0:T(8,128)S(1)}, u32[]{:S(2)}, u32[]{:S(2)}) collective-permute-start(f32[22,8,128]{2,1,0:T(8,128)S(1)} %get-tuple-element.43), channel_id=1, source_target_pairs={{1,2},{2,1},{5,6},{6,5},{9,10},{10,9},{13,14},{14,13},{17,18},{18,... | collective-permute-start | bytes 270344 | tf_op jit(solution)/shard_map/ppermute | solution.py:970
  12.3 2.9 %collective-permute-start.3 = (f32[22,8,128]{2,1,0:T(8,128)S(1)}, f32[22,8,128]{2,1,0:T(8,128)S(1)}, u32[]{:S(2)}, u32[]{:S(2)}) collective-permute-start(f32[22,8,128]{2,1,0:T(8,128)S(1)} %get-tuple-element.44), channel_id=1, source_target_pairs={{0,1},{1,0},{2,3},{3,2},{4,5},{5,4},{6,7},{7,6},{8,9},{9,8},{10,11... | collective-permute-start | bytes 270344 | tf_op jit(solution)/shard_map/ppermute | solution.py:971
  15.2 0.0 copy-done
  15.2 2.7 %inner_strips.1 = (f32[9,288,128]{2,1,0:T(8,128)S(1)}, f32[9,288,128]{2,1,0:T(8,128)S(1)}, f32[9,288,128]{2,1,0:T(8,128)S(1)}, f32[9,288,128]{2,1,0:T(8,128)S(1)...) custom-call(f32[3,3]{1,0:T(4,128)S(1)} %copy-done, f32[9,288,128]{2,1,0:T(8,128)S(1)} %get-tuple-element.36.obs.obs_in, ...), custom_call_target="tpu_custom_call" | custom-call | flops 14929920 | bytes 7962624 | tf_op jit(solution)/shard_map/inner_strips/pallas_call | solution.py:596
  17.9 0.0 collective-permute-done.2.got_b
  17.9 0.0 collective-permute-done.3.got_a
  17.9 5.9 %first_direction.1 = (f32[9,288,128]{2,1,0:T(8,128)S(1)}, f32[9,288,128]{2,1,0:T(8,128)S(1)}, f32[9,288,128]{2,1,0:T(8,128)S(1)}, f32[9,288,128]{2,1,0:T(8,128)S...) custom-call(f32[3,3]{1,0:T(4,128)S(1)} %copy-done, ...), custom_call_target="tpu_custom_call", output_to_operand_aliasing={{0}: (1, {}), {1}: (2, {}), {2}: (3, {}), {3}: (4, {}), {4}... | custom-call | tf_op jit(solution)/shard_map/first_direction/pallas_call | solution.py:778
  23.8 12.3 %all_to_all.10.got_ref = f32[32,8,128]{2,1,0:T(8,128)S(1)} all-to-all(f32[32,8,128]{2,1,0:T(8,128)S(1)} %get-tuple-element.47), channel_id=1, replica_groups=mesh['cols'=8,'rows'=4] {'cols','rows'}, dimensions={0} | all-to-all | bytes 262144 | tf_op jit(solution)/shard_map/all_to_all | solution.py:987
  36.1 5.2 %second_direction.1 = (f32[9,288,128]{2,1,0:T(8,128)S(1)}, f32[9,288,128]{2,1,0:T(8,128)S(1)}, f32[32,1,128]{2,1,0:T(1,128)S(1)}) custom-call(f32[3,3]{1,0:T(4,128)S(1)} %copy-done, f32[32,8,128]{2,1,0:T(8,128)S(1)} %all_to_all.10.got_ref, f32[32,128]{1,0:T(8,128)S(1)} %get-tuple-element.48.own_ref, f32[5,48,256]{2,1,0:T(8,128)S(1)} %get-tuple-element.49.table_ref, ...), custom_call_target="tpu_custom_call" | custom-call | tf_op jit(solution)/shard_map/second_direction/pallas_call | solution.py:881
  41.3 8.9 %all_to_all.11.sums_ref = f32[32,1,128]{2,1,0:T(1,128)S(1)} all-to-all(f32[32,1,128]{2,1,0:T(1,128)S(1)} %get-tuple-element.55), channel_id=1, replica_groups=mesh['cols'=8,'rows'=4] {'rows','cols'}, dimensions={0} | all-to-all | bytes 32768 | tf_op jit(solution)/shard_map/all_to_all | solution.py:989
  50.2 1.5 %combine.1 = (f32[256,1024]{1,0:T(8,128)}, f32[256,1024]{1,0:T(8,128)}) custom-call(f32[32,1,128]{2,1,0:T(1,128)S(1)} %all_to_all.11.sums_ref, f32[9,288,128]{2,1,0:T(8,128)S(1)} %get-tuple-element.56.p_ref, f32[9,288,128]{2,1,0:T(8,128)S(1)} %get-tuple-element.57.w_ref, f32[9,288,128]{2,1,0:T(8,128)S(1)} %get-tuple-element.58.r_ref, ...), custom_call_target="tpu_custom_call" | custom-call | tf_op jit(solution)/shard_map/combine/pallas_call | solution.py:947
Async XLA Ops:
  2.3 9.0 %collective-permute-start = (f32[64,128]{1,0:T(8,128)S(1)}, f32[64,128]{1,0:T(8,128)S(1)}, u32[]{:S(2)}, u32[]{:S(2)}) collective-permute-start(f32[64,128]{1,0:T(8,128)S(1)} %get-tuple-element.31), channel_id=1, source_target_pairs={{4,8},{8,4},{12,16},{16,12},{20,24},{24,20},{5,9},{9,5},{13,17},{1... | collective-permute-start | bytes 98312 | tf_op jit(solution)/shard_map/ppermute | solution.py:970
  3.0 8.3 %collective-permute-start.1 = (f32[64,128]{1,0:T(8,128)S(1)}, f32[64,128]{1,0:T(8,128)S(1)}, u32[]{:S(2)}, u32[]{:S(2)}) collective-permute-start(f32[64,128]{1,0:T(8,128)S(1)} %get-tuple-element.32.refs_4_), channel_id=1, source_target_pairs={{0,4},{4,0},{8,12},{12,8},{16,20},{20,16},{24,28},{28,24},{1,5},{5... | collective-permute-start | bytes 98312 | tf_op jit(solution)/shard_map/ppermute | solution.py:971
  11.3 3.9 %copy-start = (f32[3,3]{1,0:T(4,128)S(1)}, f32[3,3]{1,0:T(4,128)}, u32[]{:S(2)}) copy-start(f32[3,3]{1,0:T(4,128)} %taps.5) | copy-start | bytes 112
  11.6 6.3 %collective-permute-start.2 = (f32[22,8,128]{2,1,0:T(8,128)S(1)}, f32[22,8,128]{2,1,0:T(8,128)S(1)}, u32[]{:S(2)}, u32[]{:S(2)}) collective-permute-start(f32[22,8,128]{2,1,0:T(8,128)S(1)} %get-tuple-element.43), channel_id=1, source_target_pairs={{1,2},{2,1},{5,6},{6,5},{9,10},{10,9},{13,14},{14,13},{17,18},{18,... | collective-permute-start | bytes 270344 | tf_op jit(solution)/shard_map/ppermute | solution.py:970
  12.3 5.6 %collective-permute-start.3 = (f32[22,8,128]{2,1,0:T(8,128)S(1)}, f32[22,8,128]{2,1,0:T(8,128)S(1)}, u32[]{:S(2)}, u32[]{:S(2)}) collective-permute-start(f32[22,8,128]{2,1,0:T(8,128)S(1)} %get-tuple-element.44), channel_id=1, source_target_pairs={{0,1},{1,0},{2,3},{3,2},{4,5},{5,4},{6,7},{7,6},{8,9},{9,8},{10,11... | collective-permute-start | bytes 270344 | tf_op jit(solution)/shard_map/ppermute | solution.py:971

commit v11 on v10

--- a/solution.py
+++ b/solution.py
@@ -16,6 +16,7 @@
 HALF = LANES // 2
 EDGE = 8
 STRIP = 2 * EDGE
+REACH = 5
 CHUNK = 64
 AXES = ("cols", "rows")
 LIMIT = 40 * 1024 * 1024
@@ -297,8 +298,8 @@
     even = at % 2 == 0
     if callable(for_before):
         return (
-            lambda index: jnp.where(even, for_after(index), for_before(index)),
-            lambda index: jnp.where(even, for_before(index), for_after(index)),
+            lambda *args: jnp.where(even, for_after(*args), for_before(*args)),
+            lambda *args: jnp.where(even, for_before(*args), for_after(*args)),
         )
     return jnp.where(even, for_after, for_before), jnp.where(even, for_before, for_after)
 
@@ -390,29 +391,29 @@
     window = down + 2 * EDGE
     settle = reader((0, tiles - 1), arguments, scratch, obs, cond, down)
     matrix = gather_matrix(2)
-    for slot, begin_row in ((0, 0), (1, LANES - EDGE)):
+    fine = [[], []]
+    for slot, begin_row in ((0, 0), (1, LANES - REACH)):
         settle(slot)
-        for which, ref in enumerate((obs, cond)):
+        for ref in (obs, cond):
             turned = jnp.transpose(ref[slot, 2 * EDGE : 2 * EDGE + height, :])
-            turned = turned[begin_row : begin_row + EDGE]
+            turned = turned[begin_row : begin_row + REACH]
             for half in range(halves):
-                at = (which * halves + half) * EDGE
-                message[slot, at : at + EDGE, :] = turned[:, half * LANES : (half + 1) * LANES]
+                fine[slot].append(turned[:, half * LANES : (half + 1) * LANES])
     parts = coarse_parts(scratch[3], read_taps(scratch[2]), matrix)
     spare = jnp.zeros((2 * LANES - 4 * window, 2 * LANES), jnp.float32)
     stack = jnp.concatenate(parts + [spare], axis=0)
     left = jnp.transpose(stack[:, :LANES])
     right = jnp.transpose(stack[:, LANES:])
-    base = 2 * halves * EDGE
     past = 2 * LANES // COARSE
-    for slot, pieces in (
-        (0, (left[:EDGE], right[LANES - EDGE :])),
-        (1, (left[past - EDGE : past], left[past : past + EDGE])),
+    split = lambda piece: [piece[:, half * LANES : (half + 1) * LANES] for half in range(2)]
+    for slot, main, over in (
+        (0, left[:EDGE], right[LANES - 1 :]),
+        (1, left[past - EDGE : past], left[past : past + 1]),
     ):
-        for index, piece in enumerate(pieces):
-            for half in range(2):
-                at = base + (2 * index + half) * EDGE
-                message[slot, at : at + EDGE, :] = piece[:, half * LANES : (half + 1) * LANES]
+        rows = split(main) + fine[slot] + split(over)
+        filled = sum(piece.shape[0] for piece in rows)
+        rows.append(jnp.zeros((message.shape[1] - filled, LANES), jnp.float32))
+        message[slot] = jnp.concatenate(rows, axis=0)
     send_a[...], send_b[...] = in_pair_order(place()[0], message[0], message[1])
 
 
@@ -421,7 +422,8 @@
     tiles, down = breadth // LANES, height // COARSE
     window = down + 2 * EDGE
     field = (3, height + 4 * EDGE, LANES)
-    strip = ((2 * (height // LANES) + 4) * EDGE, LANES)
+    rows = 2 * EDGE + 2 * REACH * (height // LANES) + 2
+    strip = (-(-rows // EDGE) * EDGE, LANES)
     return pl.pallas_call(
         functools.partial(edge_kernel, tiles, down),
         in_specs=[HBM] * 4,
@@ -466,6 +468,13 @@
         ),
         name="pack_all",
     )(*[in_hbm(array) for array in (observed, class_map, class_weights, taps)], after)
+
+
+def message_rows(tiles):
+    rest = EDGE
+    fine = rest + 2 * tiles
+    sides = fine + tiles * EDGE
+    return 0, rest, fine, sides, sides + EDGE
 
 
 def merge_sides(parts):
@@ -503,26 +512,28 @@
     halves = height // LANES
     at_col, at_row, _, _ = place()
     from_e, from_w = in_pair_order(at_col, got_b[...], got_a[...])
-    gap = jnp.zeros((LANES - 2 * EDGE, LANES), jnp.float32)
+    zeros = lambda rows: jnp.zeros((rows, LANES), jnp.float32)
 
     def turned(low, high):
-        return jnp.transpose(jnp.concatenate([low, gap, high], axis=0))
+        low = [low, zeros(EDGE - low.shape[0])] if low.shape[0] < EDGE else [low]
+        high = [zeros(EDGE - high.shape[0]), high] if high.shape[0] < EDGE else [high]
+        return jnp.transpose(jnp.concatenate([*low, zeros(LANES - 2 * EDGE), *high], axis=0))
 
     for which, field in enumerate((obs, cond)):
         for half in range(halves):
-            at = (which * halves + half) * EDGE
+            at = 2 * EDGE + REACH * (which * halves + half)
             begin_row = 2 * EDGE + half * LANES
             field[tiles, begin_row : begin_row + LANES, :] = turned(
-                from_e[at : at + EDGE], from_w[at : at + EDGE]
+                from_e[at : at + REACH], from_w[at : at + REACH]
             )
-    base = 2 * halves * EDGE
-
-    def piece(strip, index, half):
-        at = base + (2 * index + half) * EDGE
-        return strip[at : at + EDGE]
-
-    left = [turned(piece(from_w, 1, half), piece(from_e, 1, half)) for half in range(2)]
-    right = [turned(piece(from_e, 0, half), piece(from_w, 0, half)) for half in range(2)]
+    main = lambda strip, half: strip[half * EDGE : (half + 1) * EDGE]
+
+    def over(strip, half):
+        at = 2 * EDGE + 2 * REACH * halves + half
+        return strip[at : at + 1]
+
+    left = [turned(over(from_w, half), over(from_e, half)) for half in range(2)]
+    right = [turned(main(from_e, half), main(from_w, half)) for half in range(2)]
     left = jnp.concatenate(left, axis=0)
     right = jnp.concatenate(right, axis=0)
     window = down + 2 * EDGE
@@ -530,36 +541,49 @@
         rows = slice(index * window, (index + 1) * window)
         coarse_ref[index, :, :LANES] = coarse_in[index, :, :LANES] + left[rows]
         coarse_ref[index, :, LANES:] = coarse_in[index, :, LANES:] + right[rows]
-    fields = (obs, cond)
-    for slot, begin_row, first_row, over_row in (
-        (0, 2 * EDGE, EDGE, EDGE - 1),
-        (1, EDGE + height, window - 2 * EDGE, window - EDGE),
+    row = iota((EDGE, LANES), 0)
+    over_at, rest_at, fine_at, sides_at, coarse_at = message_rows(tiles)
+    for slot, begin_row, reach_row, first_row, over_row in (
+        (0, 2 * EDGE, 2 * EDGE, EDGE, EDGE - 1),
+        (1, EDGE + height, 2 * EDGE + height - REACH, window - 2 * EDGE, window - EDGE),
     ):
-        pieces = [field[t, begin_row : begin_row + EDGE, :] for field in fields for t in range(tiles)]
+        for t in range(tiles):
+            at = fine_at + t * EDGE
+            message[slot, at : at + EDGE, :] = jnp.where(
+                row < REACH,
+                obs[t, reach_row : reach_row + EDGE, :],
+                cond[t, reach_row - REACH : reach_row - REACH + EDGE, :],
+            )
+        for begin_tile in range(0, tiles, 4):
+            rest = None
+            for index in range(4):
+                at = reach_row + EDGE - REACH - 2 * index
+                piece = cond[begin_tile + index, at : at + EDGE, :]
+                rest = piece if rest is None else jnp.where(row < 2 * index, rest, piece)
+            at = rest_at + begin_tile * 2
+            message[slot, at : at + EDGE, :] = rest
         rows = slice(first_row, first_row + EDGE)
-        pieces += [coarse_ref[index, rows, :LANES] for index in range(4)]
+        for index in range(4):
+            at = coarse_at + index * EDGE
+            message[slot, at : at + EDGE, :] = coarse_ref[index, rows, :LANES]
         beyond = [coarse_ref[index, rows, LANES:] for index in range(4)]
-        beyond += [field[tiles, begin_row : begin_row + EDGE, :] for field in fields]
-        pieces.append(merge_sides(beyond))
-        pieces.append(
-            jnp.concatenate(
-                [
-                    coarse_ref[index, over_row : over_row + 1, half * LANES : (half + 1) * LANES]
-                    for index in range(4)
-                    for half in range(2)
-                ],
-                axis=0,
-            )
+        beyond += [field[tiles, begin_row : begin_row + EDGE, :] for field in (obs, cond)]
+        message[slot, sides_at : sides_at + EDGE, :] = merge_sides(beyond)
+        message[slot, over_at : over_at + EDGE, :] = jnp.concatenate(
+            [
+                coarse_ref[index, over_row : over_row + 1, half * LANES : (half + 1) * LANES]
+                for index in range(4)
+                for half in range(2)
+            ],
+            axis=0,
         )
-        for index, piece in enumerate(pieces):
-            message[slot, index] = piece
     send_a[...], send_b[...] = in_pair_order(at_row, message[0], message[1])
 
 
 def middle(got_a, got_b, coarse, obs, cond):
     tiles, height = obs.shape[0] - 1, obs.shape[1] - 4 * EDGE
     down = height // COARSE
-    long = (2 * tiles + 6, EDGE, LANES)
+    long = (message_rows(tiles)[-1] + 4 * EDGE, LANES)
     return pl.pallas_call(
         functools.partial(middle_kernel, tiles, down),
         in_specs=[VMEM] * 5,
@@ -645,14 +669,26 @@
     clear_pads(obs, cond, p_ref, image)
     clear_work(work)
     from_s, from_n = in_pair_order(
-        at_row, lambda index: got_b[index], lambda index: got_a[index]
+        at_row,
+        lambda at, rows=EDGE: got_b[at : at + rows, :],
+        lambda at, rows=EDGE: got_a[at : at + rows, :],
     )
-
-    for which, field in enumerate((obs, cond)):
-        for t in range(tiles):
-            field[t, EDGE : 2 * EDGE, :] = from_n(which * tiles + t)
-            field[t, 2 * EDGE + height : 3 * EDGE + height, :] = from_s(which * tiles + t)
-    sides_n, sides_s = [split_sides(strip(2 * tiles + 4), 6) for strip in (from_n, from_s)]
+    over_at, rest_at, fine_at, sides_at, coarse_at = message_rows(tiles)
+    row = iota((EDGE, LANES), 0)
+    short = EDGE - REACH
+    for t in range(tiles):
+        at = fine_at + t * EDGE
+        rest = rest_at + 2 * t
+        begin_row = 2 * EDGE + height
+        obs[t, EDGE : 2 * EDGE, :] = jnp.where(row >= short, from_n(at - short), 0.0)
+        obs[t, begin_row : begin_row + EDGE, :] = jnp.where(row < REACH, from_s(at), 0.0)
+        near, far = from_n(at + REACH - short), from_n(rest - 2 * short)
+        near = jnp.where(row < short, 0.0, near)
+        cond[t, EDGE : 2 * EDGE, :] = jnp.where(row < 2 * short, near, far)
+        near, far = from_s(at + REACH), from_s(rest - short)
+        far = jnp.where(row < REACH, far, 0.0)
+        cond[t, begin_row : begin_row + EDGE, :] = jnp.where(row < short, near, far)
+    sides_n, sides_s = [split_sides(strip(sides_at), 6) for strip in (from_n, from_s)]
     for which, field in enumerate((obs, cond)):
         field[tiles, EDGE : 2 * EDGE, :] = sides_n[4 + which]
         field[tiles, 2 * EDGE + height : 3 * EDGE + height, :] = sides_s[4 + which]
@@ -663,14 +699,14 @@
         def over(strip, row):
             line = [
                 jnp.broadcast_to(
-                    strip((2 * tiles + 5, pl.ds(2 * index + half, 1))), (EDGE, LANES)
+                    strip(over_at + 2 * index + half, 1), (EDGE, LANES)
                 )
                 for half in range(2)
             ]
             return jnp.where(edge_row == row, jnp.concatenate(line, axis=1), 0.0)
 
         def rows(strip, beyond):
-            return jnp.concatenate([strip(2 * tiles + index), beyond[index]], axis=1)
+            return jnp.concatenate([strip(coarse_at + index * EDGE), beyond[index]], axis=1)
 
         parts = [coarse_in[index, at : at + EDGE, :] for at in range(0, window, EDGE)]
         parts[0] = parts[0] + rows(from_n, sides_n)

time: 52 us -> 51.7 us (level)
  no operation moved by 1% of the time
where the time goes in v11:
time: 51.7 us; the launch traced here: 51.5 us
  blocking collectives  20.9 us (40%)
  Pallas kernels  19.8 us (38%)
  starting transfers between devices  10 us (19%)
  between operations  0.73 us (1%)
    all_to_all x1, blocking collectives, body(): got = lax.all_to_all(chunk, AXES, 0, 0, tiled=True)  12.1 us
    all_to_all x1, blocking collectives, body(): sums = lax.all_to_all(line, AXES[::-1], 0, 0, tiled=True)  8.89 us
    ppermute x2, starting transfers between devices, exchange(): got_a = lax.ppermute(send_a, axis, pairs(0))  8.71 us
    pallas_call x1, Pallas kernels, first(): pl.pallas_call(functools.partial(first_kernel, tiles, down), in_specs=[SM...  5.88 us
    pallas_call x1, Pallas kernels, second(): pl.pallas_call(functools.partial(second_kernel, tiles, down), in_specs=[S...  5.19 us
    pallas_call x1, Pallas kernels, inner(): pl.pallas_call(inner_kernel, in_specs=[SMEM] + [VMEM] * 2, out_specs=[VME...  2.66 us
    pallas_call x1, Pallas kernels, pack(): pl.pallas_call(functools.partial(pack_kernel, tiles, down), in_specs=[HBM...  2.51 us
    pallas_call x1, Pallas kernels, edge(): pl.pallas_call(functools.partial(edge_kernel, tiles, down), in_specs=[HBM...  1.69 us
  transfers between devices with their start and end apart: 4, of which 0 were waited for; matrix products, arithmetic and copies ran while one was open for 0% of the time, Pallas kernels for 10%

profile of v11, /device:TPU:0, one launch (start us, length us, event | category | flops | bytes accessed | tf_op | source)
XLA Modules:
  0.0 51.5 jit_solution(7908848471819935163)
XLA Ops:
  0.6 1.7 %pack_east_west.1 = (f32[40,128]{1,0:T(8,128)S(1)}, f32[40,128]{1,0:T(8,128)S(1)}) custom-call(f32[256,1024]{1,0:T(8,128)} %refs_0_.3, s32[256,1024]{1,0:T(8,128)} %refs_1_.3, f32[4]{0:T(128)} %refs_2_.3, f32[3,3]{1,0:T(4,128)} %taps.5), custom_call_target="tpu_custom_call" | custom-call | tf_op jit(solution)/shard_map/pack_east_west/pallas_call | solution.py:427
  2.3 0.7 %collective-permute-start = (f32[40,128]{1,0:T(8,128)S(1)}, f32[40,128]{1,0:T(8,128)S(1)}, u32[]{:S(2)}, u32[]{:S(2)}) collective-permute-start(f32[40,128]{1,0:T(8,128)S(1)} %get-tuple-element.31), channel_id=1, source_target_pairs={{4,8},{8,4},{12,16},{16,12},{20,24},{24,20},{5,9},{9,5},{13,17},{1... | collective-permute-start | bytes 61448 | tf_op jit(solution)/shard_map/ppermute | solution.py:1006
  3.0 5.8 %collective-permute-start.1 = (f32[40,128]{1,0:T(8,128)S(1)}, f32[40,128]{1,0:T(8,128)S(1)}, u32[]{:S(2)}, u32[]{:S(2)}) collective-permute-start(f32[40,128]{1,0:T(8,128)S(1)} %get-tuple-element.32.refs_4_), channel_id=1, source_target_pairs={{0,4},{4,0},{8,12},{12,8},{16,20},{20,16},{24,28},{28,24},{1,5},{5... | collective-permute-start | bytes 61448 | tf_op jit(solution)/shard_map/ppermute | solution.py:1007
  8.8 2.5 %pack_all.1 = (f32[9,288,128]{2,1,0:T(8,128)S(1)}, f32[9,288,128]{2,1,0:T(8,128)S(1)}, f32[4,48,256]{2,1,0:T(8,128)S(1)}) custom-call(f32[256,1024]{1,0:T(8,128)} %refs_0_.3, s32[256,1024]{1,0:T(8,128)} %refs_1_.3, f32[4]{0:T(128)} %refs_2_.3, f32[3,3]{1,0:T(4,128)} %taps.5, f32[40,128]{1,0:T(8,128)S(1)} %get-tuple-element.32.refs_4_), custom_call_target="tpu_custom_call" | custom-call | flops 5242880 | bytes 4194304 | tf_op jit(solution)/shard_map/pack_all/pallas_call | solution.py:459
  11.3 0.0 collective-permute-done.got_b
  11.3 0.0 collective-permute-done.1.got_a
  11.3 0.0 copy-start
  11.3 0.3 pack_north_south.1
  11.6 0.7 %collective-permute-start.2 = (f32[128,128]{1,0:T(8,128)S(1)}, f32[128,128]{1,0:T(8,128)S(1)}, u32[]{:S(2)}, u32[]{:S(2)}) collective-permute-start(f32[128,128]{1,0:T(8,128)S(1)} %get-tuple-element.43), channel_id=1, source_target_pairs={{1,2},{2,1},{5,6},{6,5},{9,10},{10,9},{13,14},{14,13},{17,18},{18,... | collective-permute-start | bytes 196616 | tf_op jit(solution)/shard_map/ppermute | solution.py:1006
  12.3 2.9 %collective-permute-start.3 = (f32[128,128]{1,0:T(8,128)S(1)}, f32[128,128]{1,0:T(8,128)S(1)}, u32[]{:S(2)}, u32[]{:S(2)}) collective-permute-start(f32[128,128]{1,0:T(8,128)S(1)} %get-tuple-element.44), channel_id=1, source_target_pairs={{0,1},{1,0},{2,3},{3,2},{4,5},{5,4},{6,7},{7,6},{8,9},{9,8},{10,11... | collective-permute-start | bytes 196616 | tf_op jit(solution)/shard_map/ppermute | solution.py:1007
  15.2 0.0 copy-done
  15.2 2.7 %inner_strips.1 = (f32[9,288,128]{2,1,0:T(8,128)S(1)}, f32[9,288,128]{2,1,0:T(8,128)S(1)}, f32[9,288,128]{2,1,0:T(8,128)S(1)}, f32[9,288,128]{2,1,0:T(8,128)S(1)...) custom-call(f32[3,3]{1,0:T(4,128)S(1)} %copy-done, f32[9,288,128]{2,1,0:T(8,128)S(1)} %get-tuple-element.36.obs.obs_in, ...), custom_call_target="tpu_custom_call" | custom-call | flops 14929920 | bytes 7962624 | tf_op jit(solution)/shard_map/inner_strips/pallas_call | solution.py:620
  17.9 0.0 collective-permute-done.2.got_b
  17.9 0.0 collective-permute-done.3.got_a
  17.9 5.9 %first_direction.1 = (f32[9,288,128]{2,1,0:T(8,128)S(1)}, f32[9,288,128]{2,1,0:T(8,128)S(1)}, f32[9,288,128]{2,1,0:T(8,128)S(1)}, f32[9,288,128]{2,1,0:T(8,128)S...) custom-call(f32[3,3]{1,0:T(4,128)S(1)} %copy-done, ...), custom_call_target="tpu_custom_call", output_to_operand_aliasing={{0}: (1, {}), {1}: (2, {}), {2}: (3, {}), {3}: (4, {}), {4}... | custom-call | tf_op jit(solution)/shard_map/first_direction/pallas_call | solution.py:814
  23.8 12.1 %all_to_all.10.got_ref = f32[32,8,128]{2,1,0:T(8,128)S(1)} all-to-all(f32[32,8,128]{2,1,0:T(8,128)S(1)} %get-tuple-element.47), channel_id=1, replica_groups=mesh['cols'=8,'rows'=4] {'cols','rows'}, dimensions={0} | all-to-all | bytes 262144 | tf_op jit(solution)/shard_map/all_to_all | solution.py:1023
  35.8 5.2 %second_direction.1 = (f32[9,288,128]{2,1,0:T(8,128)S(1)}, f32[9,288,128]{2,1,0:T(8,128)S(1)}, f32[32,1,128]{2,1,0:T(1,128)S(1)}) custom-call(f32[3,3]{1,0:T(4,128)S(1)} %copy-done, f32[32,8,128]{2,1,0:T(8,128)S(1)} %all_to_all.10.got_ref, f32[32,128]{1,0:T(8,128)S(1)} %get-tuple-element.48.own_ref, f32[5,48,256]{2,1,0:T(8,128)S(1)} %get-tuple-element.49.table_ref, ...), custom_call_target="tpu_custom_call" | custom-call | tf_op jit(solution)/shard_map/second_direction/pallas_call | solution.py:917
  41.0 8.9 %all_to_all.11.sums_ref = f32[32,1,128]{2,1,0:T(1,128)S(1)} all-to-all(f32[32,1,128]{2,1,0:T(1,128)S(1)} %get-tuple-element.55), channel_id=1, replica_groups=mesh['cols'=8,'rows'=4] {'rows','cols'}, dimensions={0} | all-to-all | bytes 32768 | tf_op jit(solution)/shard_map/all_to_all | solution.py:1025
  49.9 1.5 %combine.1 = (f32[256,1024]{1,0:T(8,128)}, f32[256,1024]{1,0:T(8,128)}) custom-call(f32[32,1,128]{2,1,0:T(1,128)S(1)} %all_to_all.11.sums_ref, f32[9,288,128]{2,1,0:T(8,128)S(1)} %get-tuple-element.56.p_ref, f32[9,288,128]{2,1,0:T(8,128)S(1)} %get-tuple-element.57.w_ref, f32[9,288,128]{2,1,0:T(8,128)S(1)} %get-tuple-element.58.r_ref, ...), custom_call_target="tpu_custom_call" | custom-call | tf_op jit(solution)/shard_map/combine/pallas_call | solution.py:983
Async XLA Ops:
  2.3 9.0 %collective-permute-start = (f32[40,128]{1,0:T(8,128)S(1)}, f32[40,128]{1,0:T(8,128)S(1)}, u32[]{:S(2)}, u32[]{:S(2)}) collective-permute-start(f32[40,128]{1,0:T(8,128)S(1)} %get-tuple-element.31), channel_id=1, source_target_pairs={{4,8},{8,4},{12,16},{16,12},{20,24},{24,20},{5,9},{9,5},{13,17},{1... | collective-permute-start | bytes 61448 | tf_op jit(solution)/shard_map/ppermute | solution.py:1006
  3.0 8.3 %collective-permute-start.1 = (f32[40,128]{1,0:T(8,128)S(1)}, f32[40,128]{1,0:T(8,128)S(1)}, u32[]{:S(2)}, u32[]{:S(2)}) collective-permute-start(f32[40,128]{1,0:T(8,128)S(1)} %get-tuple-element.32.refs_4_), channel_id=1, source_target_pairs={{0,4},{4,0},{8,12},{12,8},{16,20},{20,16},{24,28},{28,24},{1,5},{5... | collective-permute-start | bytes 61448 | tf_op jit(solution)/shard_map/ppermute | solution.py:1007
  11.3 3.9 %copy-start = (f32[3,3]{1,0:T(4,128)S(1)}, f32[3,3]{1,0:T(4,128)}, u32[]{:S(2)}) copy-start(f32[3,3]{1,0:T(4,128)} %taps.5) | copy-start | bytes 112
  11.6 6.3 %collective-permute-start.2 = (f32[128,128]{1,0:T(8,128)S(1)}, f32[128,128]{1,0:T(8,128)S(1)}, u32[]{:S(2)}, u32[]{:S(2)}) collective-permute-start(f32[128,128]{1,0:T(8,128)S(1)} %get-tuple-element.43), channel_id=1, source_target_pairs={{1,2},{2,1},{5,6},{6,5},{9,10},{10,9},{13,14},{14,13},{17,18},{18,... | collective-permute-start | bytes 196616 | tf_op jit(solution)/shard_map/ppermute | solution.py:1006
  12.3 5.6 %collective-permute-start.3 = (f32[128,128]{1,0:T(8,128)S(1)}, f32[128,128]{1,0:T(8,128)S(1)}, u32[]{:S(2)}, u32[]{:S(2)}) collective-permute-start(f32[128,128]{1,0:T(8,128)S(1)} %get-tuple-element.44), channel_id=1, source_target_pairs={{0,1},{1,0},{2,3},{3,2},{4,5},{5,4},{6,7},{7,6},{8,9},{9,8},{10,11... | collective-permute-start | bytes 196616 | tf_op jit(solution)/shard_map/ppermute | solution.py:1007

commit v12 on v11

--- a/solution.py
+++ b/solution.py
@@ -17,6 +17,7 @@
 EDGE = 8
 STRIP = 2 * EDGE
 REACH = 5
+PIECE = EDGE + 1
 CHUNK = 64
 AXES = ("cols", "rows")
 LIMIT = 40 * 1024 * 1024
@@ -73,12 +74,14 @@
 
 def split_dot(field, matrix):
     rows = field.shape[0]
-    high = field.astype(jnp.bfloat16)
-    low = (field - high.astype(jnp.float32)).astype(jnp.bfloat16)
-    both = jnp.dot(
-        jnp.concatenate([high, low], axis=0), matrix, preferred_element_type=jnp.float32
+    parts, rest = [], field
+    for _ in range(3):
+        parts.append(rest.astype(jnp.bfloat16))
+        rest = rest - parts[-1].astype(jnp.float32)
+    product = jnp.dot(
+        jnp.concatenate(parts, axis=0), matrix, preferred_element_type=jnp.float32
     )
-    return both[:rows] + both[rows:]
+    return product[:rows] + (product[rows : 2 * rows] + product[2 * rows :])
 
 
 def roll(field, by, axis):
@@ -264,6 +267,27 @@
         return carry
 
     return lax.fori_loop(0, steps, work, carry)
+
+
+def sum_line(parts):
+    line = jnp.zeros((1, LANES), jnp.float32)
+    block = iota((1, LANES), 1) // (LANES // 4)
+    for index, part in enumerate(parts):
+        part = jnp.sum(part, axis=0, keepdims=True)
+        part = part + roll(part, LANES // 2, 1)
+        part = part + roll(part, LANES // 4, 1)
+        line = jnp.where(block == index, part, line)
+    return line
+
+
+def line_totals(lines, count):
+    while len(lines) > 1:
+        lines = [sum(lines[at + 1 : at + 2], lines[at]) for at in range(0, len(lines), 2)]
+    block = iota((1, LANES), 1) // (LANES // 4)
+    return [
+        jnp.sum(jnp.where(block == index, lines[0], 0.0), axis=1, keepdims=True)
+        for index in range(count)
+    ]
 
 
 def jacobi(source, table, work):
@@ -657,7 +681,6 @@
     table_ref,
     own_ref,
     chunk_ref,
-    dots_ref,
     image,
     spread,
     work,
@@ -727,7 +750,7 @@
     factor = inside * OMEGA / (COARSE * COARSE * taps_sum * taps_sum + around)
     weights = (east, roll(east, 1, 1), south, roll(south, 1, 0))
     table = [factor] + [factor * weight for weight in weights]
-    for index, part in enumerate(table):
+    for index, part in enumerate([*table, source]):
         table_ref[index] = part
     sides = side_lanes(has_e, has_w)
     half = iota((STRIP, LANES), 0) // EDGE
@@ -749,7 +772,7 @@
     spread_cells(cells, spread)
     inner_cells = slice(EDGE, EDGE + down)
     total = total + fold(source[inner_cells, :LANES] * cells[inner_cells, :LANES])
-    dots_ref[0] = total
+    dot_rp = total
     for ref, at, strip in pending:
         store(ref, at, strip)
 
@@ -778,7 +801,7 @@
     sweep(3, *span, begin_p, 0)
     sweep(3, *span, blur, 0)
     mask_rows(image, has_n, has_s)
-    dots_ref[1] = sweep(3, *span, finish, nothing)
+    dot_pq = sweep(3, *span, finish, nothing)
 
     own = cell_sums(q_ref, tiles, down)
     own_ref[...] = own
@@ -796,7 +819,10 @@
             to_row, to_col = at_row + down_by, at_col + right_by
             there = (to_row >= 0) & (to_row < n_rows) & (to_col >= 0) & (to_col < n_cols)
             slot = jnp.where(there, to_col * n_rows + to_row, at_col * n_rows + at_row)
-            chunk_ref[slot] = piece * jnp.where(there, 1.0, 0.0)
+            chunk_ref[pl.ds(slot * PIECE, EDGE), 0, :] = piece * jnp.where(there, 1.0, 0.0)
+    line = sum_line((dot_rp, dot_pq))
+    for at in range(EDGE, chunk_ref.shape[0], PIECE):
+        chunk_ref[at] = line
 
 
 def first(taps, fields, got_a, got_b, coarse, dot):
@@ -806,10 +832,9 @@
     window = down + 2 * EDGE
     count = lax.axis_size("cols") * lax.axis_size("rows")
     shapes = [field] * 9 + [
-        (5, window, 2 * LANES),
+        (6, window, 2 * LANES),
         (down, LANES),
-        (count, EDGE, LANES),
-        (2, EDGE, LANES),
+        (count * PIECE, 1, LANES),
     ]
     return pl.pallas_call(
         functools.partial(first_kernel, tiles, down),
@@ -834,14 +859,15 @@
     got_ref,
     own_ref,
     table_ref,
+    res_ref,
     q_ref,
     east_ref,
     south_ref,
     inv_ref,
-    dots_in,
     w_ref,
     v_ref,
     out_ref,
+    known_ref,
     image,
     spread,
     work,
@@ -854,7 +880,8 @@
     def got(down_by, right_by):
         to_row, to_col = at_row + down_by, at_col + right_by
         there = (to_row >= 0) & (to_row < n_rows) & (to_col >= 0) & (to_col < n_cols)
-        return got_ref[jnp.where(there, to_col * n_rows + to_row, me)]
+        slot = jnp.where(there, to_col * n_rows + to_row, me)
+        return got_ref[pl.ds(slot * PIECE, EDGE), 0, :]
 
     low = iota((EDGE, LANES), 1) < HALF
     gap = jnp.zeros((LANES - 2 * EDGE, LANES), jnp.float32)
@@ -868,20 +895,34 @@
         axis=0,
     )
     clear_work(work)
+    rp, pq = line_totals(
+        [got_ref[at] for at in range(EDGE, got_ref.shape[0], PIECE)], 2
+    )
+    step = rp / pq
+    for index, value in enumerate((step, rp, pq)):
+        known_ref[index] = jnp.broadcast_to(value, (EDGE, LANES))
+    source = table_ref[5] - jnp.broadcast_to(step, source.shape) * source
     spread_cells(jacobi(source, table_ref, work), spread)
+    step = jnp.broadcast_to(step, (STRIP, LANES))
     clear_pads(w_ref, image)
     sides = side_lanes(has_e, has_w)
     taps = read_taps(taps)
 
-    def begin_w(at, start, total):
-        field, inverse, cells = load(q_ref, at), load(inv_ref, at), cells_at(spread, at)
-        strip = [field[t] * inverse[t] + cells[t] for t in range(tiles + 1)]
+    def begin_w(at, start, totals):
+        right, field, inverse = load(res_ref, at), load(q_ref, at), load(inv_ref, at)
+        cells = cells_at(spread, at)
+        span = range(tiles + 1)
+        residual = [right[t] - step * field[t] for t in span]
+        strip = [residual[t] * inverse[t] + cells[t] for t in span]
         first_row = jnp.maximum(start, 2 * EDGE)
         flags = [
             jnp.where((row >= first_row) & (row < 2 * EDGE + height), 1.0, 0.0)
             for row in [at + by for by in range(0, STRIP, EDGE)]
         ]
-        return [(w_ref, strip)], total + product_sum(field, strip, tiles, flags)
+        return [(w_ref, strip)], (
+            totals[0] + product_sum(residual, strip, tiles, flags),
+            totals[1] + product_sum(strip, field, tiles, flags),
+        )
 
     def blur(at, _, carry):
         strip = conv(w_ref, at, taps, False)
@@ -894,22 +935,16 @@
 
     nothing = jnp.zeros((EDGE, LANES), jnp.float32)
     span = (EDGE, 3 * EDGE + height)
-    dot_qw = sweep(3, *span, begin_w, nothing)
+    dot_rz, dot_zq = sweep(3, *span, begin_w, (nothing, nothing))
     sweep(3, *span, blur, 0)
     mask_rows(image, has_n, has_s)
-    dot_wv = sweep(4, 2 * EDGE, 2 * EDGE + height, finish, nothing)
-    line = jnp.zeros((1, LANES), jnp.float32)
-    block = iota((1, LANES), 1) // (LANES // 4)
-    for index, part in enumerate((dots_in[0], dots_in[1], dot_qw, dot_wv)):
-        part = jnp.sum(part, axis=0, keepdims=True)
-        part = part + roll(part, LANES // 2, 1)
-        part = part + roll(part, LANES // 4, 1)
-        line = jnp.where(block == index, part, line)
+    dot_zz = sweep(4, 2 * EDGE, 2 * EDGE + height, finish, nothing)
+    line = sum_line((dot_rz, dot_zq, dot_zz))
     for index in range(out_ref.shape[0]):
         out_ref[index] = line
 
 
-def second(taps, got, own, table, q, east, south, inv, dots):
+def second(taps, got, own, table, r, q, east, south, inv):
     tiles, height = q.shape[0] - 1, q.shape[1] - 4 * EDGE
     down = height // COARSE
     window = down + 2 * EDGE
@@ -917,8 +952,8 @@
     return pl.pallas_call(
         functools.partial(second_kernel, tiles, down),
         in_specs=[SMEM] + [VMEM] * 8,
-        out_specs=[VMEM] * 3,
-        out_shape=floats(q.shape, q.shape, (count, 1, LANES)),
+        out_specs=[VMEM] * 4,
+        out_shape=floats(q.shape, q.shape, (count, 1, LANES), (3, EDGE, LANES)),
         scratch_shapes=[
             pltpu.VMEM(q.shape, jnp.float32),
             pltpu.VMEM((tiles + 1, window, LANES), jnp.float32),
@@ -926,26 +961,18 @@
         ],
         compiler_params=params(),
         name="second_direction",
-    )(taps, got, own, table, q, east, south, inv, dots)
+    )(taps, got, own, table, r, q, east, south, inv)
 
 
 def combine_kernel(
-    tiles, height, sums_ref, p_ref, w_ref, r_ref, q_ref, v_ref, sol_out, res_out, sol, res, sem
+    tiles, height, sums_ref, known_ref, p_ref, w_ref, r_ref, q_ref, v_ref, sol_out, res_out, sol, res, sem
 ):
-    line = sums_ref[0]
-    for index in range(1, sums_ref.shape[0]):
-        line = line + sums_ref[index]
-    block = iota((1, LANES), 1) // (LANES // 4)
-    pick = lambda index: jnp.sum(jnp.where(block == index, line, 0.0), axis=1, keepdims=True)
-    rp, pq, qw, wv = [pick(index) for index in range(4)]
-    step = rp / pq
-    rp_next = step * step * qw - rp
-    ratio = rp_next / rp
-    lead = 1.0 + ratio
-    curvature = lead * lead * pq - 2.0 * lead * step * qw + step * step * wv
-    step_next = rp_next / curvature
-    on_p = jnp.broadcast_to(step + step_next * lead, (CHUNK, LANES))
-    on_w = jnp.broadcast_to(step_next * step, (CHUNK, LANES))
+    rz, zq, zz = line_totals([sums_ref[index] for index in range(sums_ref.shape[0])], 3)
+    step, rp, pq = [known_ref[index, :1, :] for index in range(3)]
+    ratio = rz / rp
+    step_next = rz / (zz + ratio * (2.0 * zq + ratio * pq))
+    on_w = jnp.broadcast_to(step_next, (CHUNK, LANES))
+    on_p = jnp.broadcast_to(step + step_next * ratio, (CHUNK, LANES))
 
     def copies(index):
         rows = pl.ds(pl.multiple_of(index * CHUNK, CHUNK), CHUNK)
@@ -959,8 +986,8 @@
         p, w, r, q, v = [
             load(ref, at + 2 * EDGE, CHUNK) for ref in (p_ref, w_ref, r_ref, q_ref, v_ref)
         ]
-        one = [on_p * p[t] - on_w * w[t] for t in range(tiles)]
-        two = [r[t] - on_p * q[t] + on_w * v[t] for t in range(tiles)]
+        one = [on_p * p[t] + on_w * w[t] for t in range(tiles)]
+        two = [r[t] - on_p * q[t] - on_w * v[t] for t in range(tiles)]
         for t in range(tiles):
             sol[pl.ds(at, CHUNK), t * LANES : (t + 1) * LANES] = one[t]
             res[pl.ds(at, CHUNK), t * LANES : (t + 1) * LANES] = two[t]
@@ -977,12 +1004,12 @@
     lax.fori_loop(0, height // CHUNK, settle, 0)
 
 
-def combine(sums, p, w, r, q, v):
+def combine(sums, known, p, w, r, q, v):
     tiles, height = q.shape[0] - 1, q.shape[1] - 4 * EDGE
     shape = (height, tiles * LANES)
     return pl.pallas_call(
         functools.partial(combine_kernel, tiles, height),
-        in_specs=[VMEM] * 6,
+        in_specs=[VMEM] * 7,
         out_specs=[HBM] * 2,
         out_shape=floats(shape, shape),
         scratch_shapes=[
@@ -992,7 +1019,7 @@
         ],
         compiler_params=params(),
         name="combine",
-    )(sums, p, w, r, q, v)
+    )(sums, known, p, w, r, q, v)
 
 
 def exchange(send_a, send_b, axis):
@@ -1017,13 +1044,13 @@
     got_a, got_b = exchange(send_a, send_b, "rows")
     r, east, south, inv, u, dot = inner(blur_kernel, obs, cond)
     fields = (obs, cond, r, east, south, inv, u)
-    r, east, south, inv, _, p, q, table, own, chunk, dots = first(
+    r, east, south, inv, _, p, q, table, own, chunk = first(
         blur_kernel, fields, got_a, got_b, coarse, dot
     )
     got = lax.all_to_all(chunk, AXES, 0, 0, tiled=True)
-    w, v, line = second(blur_kernel, got, own, table, q, east, south, inv, dots)
+    w, v, line, known = second(blur_kernel, got, own, table, r, q, east, south, inv)
     sums = lax.all_to_all(line, AXES[::-1], 0, 0, tiled=True)
-    return tuple(combine(sums, p, w, r, q, v))
+    return tuple(combine(sums, known, p, w, r, q, v))
 
 
 def solution(mesh):

time: 51.7 us -> 52.4 us (1.014)
  no operation moved by 1% of the time
where the time goes in v12:
time: 52.4 us; the launch traced here: 52.1 us
  blocking collectives  21.3 us (41%)
  Pallas kernels  20.1 us (38%)
  starting transfers between devices  10 us (19%)
  between operations  0.73 us (1%)
    all_to_all x1, blocking collectives, body(): got = lax.all_to_all(chunk, AXES, 0, 0, tiled=True)  12.2 us
    all_to_all x1, blocking collectives, body(): sums = lax.all_to_all(line, AXES[::-1], 0, 0, tiled=True)  9.06 us
    ppermute x2, starting transfers between devices, exchange(): got_a = lax.ppermute(send_a, axis, pairs(0))  8.71 us
    pallas_call x1, Pallas kernels, first(): pl.pallas_call(functools.partial(first_kernel, tiles, down), in_specs=[SM...  6.01 us
    pallas_call x1, Pallas kernels, second(): pl.pallas_call(functools.partial(second_kernel, tiles, down), in_specs=[S...  5.28 us
    pallas_call x1, Pallas kernels, inner(): pl.pallas_call(inner_kernel, in_specs=[SMEM] + [VMEM] * 2, out_specs=[VME...  2.68 us
    pallas_call x1, Pallas kernels, pack(): pl.pallas_call(functools.partial(pack_kernel, tiles, down), in_specs=[HBM...  2.6 us
    pallas_call x1, Pallas kernels, edge(): pl.pallas_call(functools.partial(edge_kernel, tiles, down), in_specs=[HBM...  1.73 us
  transfers between devices with their start and end apart: 4, of which 0 were waited for; matrix products, arithmetic and copies ran while one was open for 0% of the time, Pallas kernels for 10%

profile of v12, /device:TPU:0, one launch (start us, length us, event | category | flops | bytes accessed | tf_op | source)
XLA Modules:
  0.0 52.1 jit_solution(10360060714043623195)
XLA Ops:
  0.6 1.7 %pack_east_west.1 = (f32[40,128]{1,0:T(8,128)S(1)}, f32[40,128]{1,0:T(8,128)S(1)}) custom-call(f32[256,1024]{1,0:T(8,128)} %refs_0_.3, s32[256,1024]{1,0:T(8,128)} %refs_1_.3, f32[4]{0:T(128)} %refs_2_.3, f32[3,3]{1,0:T(4,128)} %taps.5), custom_call_target="tpu_custom_call" | custom-call | tf_op jit(solution)/shard_map/pack_east_west/pallas_call | solution.py:451
  2.4 0.7 %collective-permute-start = (f32[40,128]{1,0:T(8,128)S(1)}, f32[40,128]{1,0:T(8,128)S(1)}, u32[]{:S(2)}, u32[]{:S(2)}) collective-permute-start(f32[40,128]{1,0:T(8,128)S(1)} %get-tuple-element.31), channel_id=1, source_target_pairs={{4,8},{8,4},{12,16},{16,12},{20,24},{24,20},{5,9},{9,5},{13,17},{1... | collective-permute-start | bytes 61448 | tf_op jit(solution)/shard_map/ppermute | solution.py:1033
  3.0 5.8 %collective-permute-start.1 = (f32[40,128]{1,0:T(8,128)S(1)}, f32[40,128]{1,0:T(8,128)S(1)}, u32[]{:S(2)}, u32[]{:S(2)}) collective-permute-start(f32[40,128]{1,0:T(8,128)S(1)} %get-tuple-element.32.refs_4_), channel_id=1, source_target_pairs={{0,4},{4,0},{8,12},{12,8},{16,20},{20,16},{24,28},{28,24},{1,5},{5... | collective-permute-start | bytes 61448 | tf_op jit(solution)/shard_map/ppermute | solution.py:1034
  8.8 2.6 %pack_all.1 = (f32[9,288,128]{2,1,0:T(8,128)S(1)}, f32[9,288,128]{2,1,0:T(8,128)S(1)}, f32[4,48,256]{2,1,0:T(8,128)S(1)}) custom-call(f32[256,1024]{1,0:T(8,128)} %refs_0_.3, s32[256,1024]{1,0:T(8,128)} %refs_1_.3, f32[4]{0:T(128)} %refs_2_.3, f32[3,3]{1,0:T(4,128)} %taps.5, f32[40,128]{1,0:T(8,128)S(1)} %get-tuple-element.32.refs_4_), custom_call_target="tpu_custom_call" | custom-call | flops 5242880 | bytes 4194304 | tf_op jit(solution)/shard_map/pack_all/pallas_call | solution.py:483
  11.4 0.0 collective-permute-done.got_b
  11.5 0.0 collective-permute-done.1.got_a
  11.5 0.0 copy-start
  11.5 0.3 pack_north_south.1
  11.8 0.7 %collective-permute-start.2 = (f32[128,128]{1,0:T(8,128)S(1)}, f32[128,128]{1,0:T(8,128)S(1)}, u32[]{:S(2)}, u32[]{:S(2)}) collective-permute-start(f32[128,128]{1,0:T(8,128)S(1)} %get-tuple-element.43), channel_id=1, source_target_pairs={{1,2},{2,1},{5,6},{6,5},{9,10},{10,9},{13,14},{14,13},{17,18},{18,... | collective-permute-start | bytes 196616 | tf_op jit(solution)/shard_map/ppermute | solution.py:1033
  12.4 2.9 %collective-permute-start.3 = (f32[128,128]{1,0:T(8,128)S(1)}, f32[128,128]{1,0:T(8,128)S(1)}, u32[]{:S(2)}, u32[]{:S(2)}) collective-permute-start(f32[128,128]{1,0:T(8,128)S(1)} %get-tuple-element.44), channel_id=1, source_target_pairs={{0,1},{1,0},{2,3},{3,2},{4,5},{5,4},{6,7},{7,6},{8,9},{9,8},{10,11... | collective-permute-start | bytes 196616 | tf_op jit(solution)/shard_map/ppermute | solution.py:1034
  15.3 0.0 copy-done
  15.3 2.7 %inner_strips.1 = (f32[9,288,128]{2,1,0:T(8,128)S(1)}, f32[9,288,128]{2,1,0:T(8,128)S(1)}, f32[9,288,128]{2,1,0:T(8,128)S(1)}, f32[9,288,128]{2,1,0:T(8,128)S(1)...) custom-call(f32[3,3]{1,0:T(4,128)S(1)} %copy-done, f32[9,288,128]{2,1,0:T(8,128)S(1)} %get-tuple-element.36.obs.obs_in, ...), custom_call_target="tpu_custom_call" | custom-call | flops 14929920 | bytes 7962624 | tf_op jit(solution)/shard_map/inner_strips/pallas_call | solution.py:644
  18.0 0.0 collective-permute-done.2.got_b
  18.0 0.0 collective-permute-done.3.got_a
  18.0 6.0 %first_direction.1 = (f32[9,288,128]{2,1,0:T(8,128)S(1)}, f32[9,288,128]{2,1,0:T(8,128)S(1)}, f32[9,288,128]{2,1,0:T(8,128)S(1)}, f32[9,288,128]{2,1,0:T(8,128)S...) custom-call(f32[3,3]{1,0:T(4,128)S(1)} %copy-done, ...), custom_call_target="tpu_custom_call", output_to_operand_aliasing={{0}: (1, {}), {1}: (2, {}), {2}: (3, {}), {3}: (4, {}), {4}... | custom-call | tf_op jit(solution)/shard_map/first_direction/pallas_call | solution.py:839
  24.1 12.2 %all_to_all.10.got_ref = f32[288,1,128]{2,1,0:T(1,128)S(1)} all-to-all(f32[288,1,128]{2,1,0:T(1,128)S(1)} %get-tuple-element.47), channel_id=1, replica_groups=mesh['cols'=8,'rows'=4] {'cols','rows'}, dimensions={0} | all-to-all | bytes 294912 | tf_op jit(solution)/shard_map/all_to_all | solution.py:1050
  36.3 5.3 %second_direction.1 = (f32[9,288,128]{2,1,0:T(8,128)S(1)}, f32[9,288,128]{2,1,0:T(8,128)S(1)}, f32[32,1,128]{2,1,0:T(1,128)S(1)}, f32[3,8,128]{2,1,0:T(8,128)S(1)}) custom-call(f32[3,3]{1,0:T(4,128)S(1)} %copy-done, f32[288,1,128]{2,1,0:T(1,128)S(1)} %all_to_all.10.got_ref, f32[32,128]{1,0:T(8,128)S(1)} %get-tuple-element.48.own_ref, ...), custom_call_target="tpu_custom_call" | custom-call | tf_op jit(solution)/shard_map/second_direction/pallas_call | solution.py:952
  41.6 9.1 %all_to_all.11.sums_ref = f32[32,1,128]{2,1,0:T(1,128)S(1)} all-to-all(f32[32,1,128]{2,1,0:T(1,128)S(1)} %get-tuple-element.55), channel_id=1, replica_groups=mesh['cols'=8,'rows'=4] {'rows','cols'}, dimensions={0} | all-to-all | bytes 32768 | tf_op jit(solution)/shard_map/all_to_all | solution.py:1052
  50.6 1.5 %combine.1 = (f32[256,1024]{1,0:T(8,128)}, f32[256,1024]{1,0:T(8,128)}) custom-call(f32[32,1,128]{2,1,0:T(1,128)S(1)} %all_to_all.11.sums_ref, f32[3,8,128]{2,1,0:T(8,128)S(1)} %get-tuple-element.56.known_ref, f32[9,288,128]{2,1,0:T(8,128)S(1)} %get-tuple-element.57.p_ref, f32[9,288,128]{2,1,0:T(8,128)S(1)} %get-tuple-element.58.w_ref, ...), custom_call_target="tpu_custom_call" | custom-call | tf_op jit(solution)/shard_map/combine/pallas_call | solution.py:1010
Async XLA Ops:
  2.4 9.1 %collective-permute-start = (f32[40,128]{1,0:T(8,128)S(1)}, f32[40,128]{1,0:T(8,128)S(1)}, u32[]{:S(2)}, u32[]{:S(2)}) collective-permute-start(f32[40,128]{1,0:T(8,128)S(1)} %get-tuple-element.31), channel_id=1, source_target_pairs={{4,8},{8,4},{12,16},{16,12},{20,24},{24,20},{5,9},{9,5},{13,17},{1... | collective-permute-start | bytes 61448 | tf_op jit(solution)/shard_map/ppermute | solution.py:1033
  3.0 8.4 %collective-permute-start.1 = (f32[40,128]{1,0:T(8,128)S(1)}, f32[40,128]{1,0:T(8,128)S(1)}, u32[]{:S(2)}, u32[]{:S(2)}) collective-permute-start(f32[40,128]{1,0:T(8,128)S(1)} %get-tuple-element.32.refs_4_), channel_id=1, source_target_pairs={{0,4},{4,0},{8,12},{12,8},{16,20},{20,16},{24,28},{28,24},{1,5},{5... | collective-permute-start | bytes 61448 | tf_op jit(solution)/shard_map/ppermute | solution.py:1034
  11.5 3.9 %copy-start = (f32[3,3]{1,0:T(4,128)S(1)}, f32[3,3]{1,0:T(4,128)}, u32[]{:S(2)}) copy-start(f32[3,3]{1,0:T(4,128)} %taps.5) | copy-start | bytes 112
  11.8 6.3 %collective-permute-start.2 = (f32[128,128]{1,0:T(8,128)S(1)}, f32[128,128]{1,0:T(8,128)S(1)}, u32[]{:S(2)}, u32[]{:S(2)}) collective-permute-start(f32[128,128]{1,0:T(8,128)S(1)} %get-tuple-element.43), channel_id=1, source_target_pairs={{1,2},{2,1},{5,6},{6,5},{9,10},{10,9},{13,14},{14,13},{17,18},{18,... | collective-permute-start | bytes 196616 | tf_op jit(solution)/shard_map/ppermute | solution.py:1033
  12.4 5.6 %collective-permute-start.3 = (f32[128,128]{1,0:T(8,128)S(1)}, f32[128,128]{1,0:T(8,128)S(1)}, u32[]{:S(2)}, u32[]{:S(2)}) collective-permute-start(f32[128,128]{1,0:T(8,128)S(1)} %get-tuple-element.44), channel_id=1, source_target_pairs={{0,1},{1,0},{2,3},{3,2},{4,5},{5,4},{6,7},{7,6},{8,9},{9,8},{10,11... | collective-permute-start | bytes 196616 | tf_op jit(solution)/shard_map/ppermute | solution.py:1034

commit v13 on v12

--- a/solution.py
+++ b/solution.py
@@ -807,7 +807,8 @@
     own_ref[...] = own
     spare = jnp.zeros((LANES - down, LANES), jnp.float32)
     turned = jnp.transpose(jnp.concatenate([own, spare], axis=0))
-    chunk_ref[...] = jnp.zeros_like(chunk_ref)
+    me = at_col * n_rows + at_row
+    chunk_ref[pl.ds(me * PIECE, EDGE), 0, :] = jnp.zeros((EDGE, LANES), jnp.float32)
     for down_by in (-1, 0, 1):
         for right_by in (-1, 0, 1):
             if down_by == 0 and right_by == 0:
@@ -818,7 +819,7 @@
                 piece = own[:EDGE] if down_by < 0 else own[down - EDGE :]
             to_row, to_col = at_row + down_by, at_col + right_by
             there = (to_row >= 0) & (to_row < n_rows) & (to_col >= 0) & (to_col < n_cols)
-            slot = jnp.where(there, to_col * n_rows + to_row, at_col * n_rows + at_row)
+            slot = jnp.where(there, to_col * n_rows + to_row, me)
             chunk_ref[pl.ds(slot * PIECE, EDGE), 0, :] = piece * jnp.where(there, 1.0, 0.0)
     line = sum_line((dot_rp, dot_pq))
     for at in range(EDGE, chunk_ref.shape[0], PIECE):
@@ -899,7 +900,7 @@
         [got_ref[at] for at in range(EDGE, got_ref.shape[0], PIECE)], 2
     )
     step = rp / pq
-    for index, value in enumerate((step, rp, pq)):
+    for index, value in enumerate((step, rp)):
         known_ref[index] = jnp.broadcast_to(value, (EDGE, LANES))
     source = table_ref[5] - jnp.broadcast_to(step, source.shape) * source
     spread_cells(jacobi(source, table_ref, work), spread)
@@ -908,7 +909,7 @@
     sides = side_lanes(has_e, has_w)
     taps = read_taps(taps)
 
-    def begin_w(at, start, totals):
+    def begin_w(at, start, total):
         right, field, inverse = load(res_ref, at), load(q_ref, at), load(inv_ref, at)
         cells = cells_at(spread, at)
         span = range(tiles + 1)
@@ -919,10 +920,7 @@
             jnp.where((row >= first_row) & (row < 2 * EDGE + height), 1.0, 0.0)
             for row in [at + by for by in range(0, STRIP, EDGE)]
         ]
-        return [(w_ref, strip)], (
-            totals[0] + product_sum(residual, strip, tiles, flags),
-            totals[1] + product_sum(strip, field, tiles, flags),
-        )
+        return [(w_ref, strip)], total + product_sum(residual, strip, tiles, flags)
 
     def blur(at, _, carry):
         strip = conv(w_ref, at, taps, False)
@@ -935,11 +933,11 @@
 
     nothing = jnp.zeros((EDGE, LANES), jnp.float32)
     span = (EDGE, 3 * EDGE + height)
-    dot_rz, dot_zq = sweep(3, *span, begin_w, (nothing, nothing))
+    dot_rz = sweep(3, *span, begin_w, nothing)
     sweep(3, *span, blur, 0)
     mask_rows(image, has_n, has_s)
     dot_zz = sweep(4, 2 * EDGE, 2 * EDGE + height, finish, nothing)
-    line = sum_line((dot_rz, dot_zq, dot_zz))
+    line = sum_line((dot_rz, dot_zz))
     for index in range(out_ref.shape[0]):
         out_ref[index] = line
 
@@ -953,7 +951,7 @@
         functools.partial(second_kernel, tiles, down),
         in_specs=[SMEM] + [VMEM] * 8,
         out_specs=[VMEM] * 4,
-        out_shape=floats(q.shape, q.shape, (count, 1, LANES), (3, EDGE, LANES)),
+        out_shape=floats(q.shape, q.shape, (count, 1, LANES), (2, EDGE, LANES)),
         scratch_shapes=[
             pltpu.VMEM(q.shape, jnp.float32),
             pltpu.VMEM((tiles + 1, window, LANES), jnp.float32),
@@ -967,10 +965,10 @@
 def combine_kernel(
     tiles, height, sums_ref, known_ref, p_ref, w_ref, r_ref, q_ref, v_ref, sol_out, res_out, sol, res, sem
 ):
-    rz, zq, zz = line_totals([sums_ref[index] for index in range(sums_ref.shape[0])], 3)
-    step, rp, pq = [known_ref[index, :1, :] for index in range(3)]
+    rz, zz = line_totals([sums_ref[index] for index in range(sums_ref.shape[0])], 2)
+    step, rp = [known_ref[index, :1, :] for index in range(2)]
     ratio = rz / rp
-    step_next = rz / (zz + ratio * (2.0 * zq + ratio * pq))
+    step_next = rz / (zz - ratio * (rz / step))
     on_w = jnp.broadcast_to(step_next, (CHUNK, LANES))
     on_p = jnp.broadcast_to(step + step_next * ratio, (CHUNK, LANES))
 

time: 52.4 us -> 52.3 us (level)
  no operation moved by 1% of the time
where the time goes in v13:
time: 52.3 us; the launch traced here: 52 us
  blocking collectives  21.3 us (41%)
  Pallas kernels  20 us (38%)
  starting transfers between devices  10 us (19%)
  between operations  0.73 us (1%)
    all_to_all x1, blocking collectives, body(): got = lax.all_to_all(chunk, AXES, 0, 0, tiled=True)  12.2 us
    all_to_all x1, blocking collectives, body(): sums = lax.all_to_all(line, AXES[::-1], 0, 0, tiled=True)  9.06 us
    ppermute x2, starting transfers between devices, exchange(): got_a = lax.ppermute(send_a, axis, pairs(0))  8.71 us
    pallas_call x1, Pallas kernels, first(): pl.pallas_call(functools.partial(first_kernel, tiles, down), in_specs=[SM...  5.94 us
    pallas_call x1, Pallas kernels, second(): pl.pallas_call(functools.partial(second_kernel, tiles, down), in_specs=[S...  5.26 us
    pallas_call x1, Pallas kernels, inner(): pl.pallas_call(inner_kernel, in_specs=[SMEM] + [VMEM] * 2, out_specs=[VME...  2.68 us
    pallas_call x1, Pallas kernels, pack(): pl.pallas_call(functools.partial(pack_kernel, tiles, down), in_specs=[HBM...  2.6 us
    pallas_call x1, Pallas kernels, edge(): pl.pallas_call(functools.partial(edge_kernel, tiles, down), in_specs=[HBM...  1.73 us
  transfers between devices with their start and end apart: 4, of which 0 were waited for; matrix products, arithmetic and copies ran while one was open for 0% of the time, Pallas kernels for 10%

profile of v13, /device:TPU:0, one launch (start us, length us, event | category | flops | bytes accessed | tf_op | source)
XLA Modules:
  0.0 52.0 jit_solution(17539898257804745374)
XLA Ops:
  0.6 1.7 %pack_east_west.1 = (f32[40,128]{1,0:T(8,128)S(1)}, f32[40,128]{1,0:T(8,128)S(1)}) custom-call(f32[256,1024]{1,0:T(8,128)} %refs_0_.3, s32[256,1024]{1,0:T(8,128)} %refs_1_.3, f32[4]{0:T(128)} %refs_2_.3, f32[3,3]{1,0:T(4,128)} %taps.5), custom_call_target="tpu_custom_call" | custom-call | tf_op jit(solution)/shard_map/pack_east_west/pallas_call | solution.py:451
  2.4 0.7 %collective-permute-start = (f32[40,128]{1,0:T(8,128)S(1)}, f32[40,128]{1,0:T(8,128)S(1)}, u32[]{:S(2)}, u32[]{:S(2)}) collective-permute-start(f32[40,128]{1,0:T(8,128)S(1)} %get-tuple-element.31), channel_id=1, source_target_pairs={{4,8},{8,4},{12,16},{16,12},{20,24},{24,20},{5,9},{9,5},{13,17},{1... | collective-permute-start | bytes 61448 | tf_op jit(solution)/shard_map/ppermute | solution.py:1031
  3.0 5.8 %collective-permute-start.1 = (f32[40,128]{1,0:T(8,128)S(1)}, f32[40,128]{1,0:T(8,128)S(1)}, u32[]{:S(2)}, u32[]{:S(2)}) collective-permute-start(f32[40,128]{1,0:T(8,128)S(1)} %get-tuple-element.32.refs_4_), channel_id=1, source_target_pairs={{0,4},{4,0},{8,12},{12,8},{16,20},{20,16},{24,28},{28,24},{1,5},{5... | collective-permute-start | bytes 61448 | tf_op jit(solution)/shard_map/ppermute | solution.py:1032
  8.8 2.6 %pack_all.1 = (f32[9,288,128]{2,1,0:T(8,128)S(1)}, f32[9,288,128]{2,1,0:T(8,128)S(1)}, f32[4,48,256]{2,1,0:T(8,128)S(1)}) custom-call(f32[256,1024]{1,0:T(8,128)} %refs_0_.3, s32[256,1024]{1,0:T(8,128)} %refs_1_.3, f32[4]{0:T(128)} %refs_2_.3, f32[3,3]{1,0:T(4,128)} %taps.5, f32[40,128]{1,0:T(8,128)S(1)} %get-tuple-element.32.refs_4_), custom_call_target="tpu_custom_call" | custom-call | flops 5242880 | bytes 4194304 | tf_op jit(solution)/shard_map/pack_all/pallas_call | solution.py:483
  11.4 0.0 collective-permute-done.got_b
  11.5 0.0 collective-permute-done.1.got_a
  11.5 0.0 copy-start
  11.5 0.3 pack_north_south.1
  11.7 0.7 %collective-permute-start.2 = (f32[128,128]{1,0:T(8,128)S(1)}, f32[128,128]{1,0:T(8,128)S(1)}, u32[]{:S(2)}, u32[]{:S(2)}) collective-permute-start(f32[128,128]{1,0:T(8,128)S(1)} %get-tuple-element.43), channel_id=1, source_target_pairs={{1,2},{2,1},{5,6},{6,5},{9,10},{10,9},{13,14},{14,13},{17,18},{18,... | collective-permute-start | bytes 196616 | tf_op jit(solution)/shard_map/ppermute | solution.py:1031
  12.4 2.9 %collective-permute-start.3 = (f32[128,128]{1,0:T(8,128)S(1)}, f32[128,128]{1,0:T(8,128)S(1)}, u32[]{:S(2)}, u32[]{:S(2)}) collective-permute-start(f32[128,128]{1,0:T(8,128)S(1)} %get-tuple-element.44), channel_id=1, source_target_pairs={{0,1},{1,0},{2,3},{3,2},{4,5},{5,4},{6,7},{7,6},{8,9},{9,8},{10,11... | collective-permute-start | bytes 196616 | tf_op jit(solution)/shard_map/ppermute | solution.py:1032
  15.3 0.0 copy-done
  15.3 2.7 %inner_strips.1 = (f32[9,288,128]{2,1,0:T(8,128)S(1)}, f32[9,288,128]{2,1,0:T(8,128)S(1)}, f32[9,288,128]{2,1,0:T(8,128)S(1)}, f32[9,288,128]{2,1,0:T(8,128)S(1)...) custom-call(f32[3,3]{1,0:T(4,128)S(1)} %copy-done, f32[9,288,128]{2,1,0:T(8,128)S(1)} %get-tuple-element.36.obs.obs_in, ...), custom_call_target="tpu_custom_call" | custom-call | flops 14929920 | bytes 7962624 | tf_op jit(solution)/shard_map/inner_strips/pallas_call | solution.py:644
  18.0 0.0 collective-permute-done.2.got_b
  18.0 0.0 collective-permute-done.3.got_a
  18.0 5.9 %first_direction.1 = (f32[9,288,128]{2,1,0:T(8,128)S(1)}, f32[9,288,128]{2,1,0:T(8,128)S(1)}, f32[9,288,128]{2,1,0:T(8,128)S(1)}, f32[9,288,128]{2,1,0:T(8,128)S...) custom-call(f32[3,3]{1,0:T(4,128)S(1)} %copy-done, ...), custom_call_target="tpu_custom_call", output_to_operand_aliasing={{0}: (1, {}), {1}: (2, {}), {2}: (3, {}), {3}: (4, {}), {4}... | custom-call | tf_op jit(solution)/shard_map/first_direction/pallas_call | solution.py:840
  24.0 12.2 %all_to_all.10.got_ref = f32[288,1,128]{2,1,0:T(1,128)S(1)} all-to-all(f32[288,1,128]{2,1,0:T(1,128)S(1)} %get-tuple-element.47), channel_id=1, replica_groups=mesh['cols'=8,'rows'=4] {'cols','rows'}, dimensions={0} | all-to-all | bytes 294912 | tf_op jit(solution)/shard_map/all_to_all | solution.py:1048
  36.2 5.3 %second_direction.1 = (f32[9,288,128]{2,1,0:T(8,128)S(1)}, f32[9,288,128]{2,1,0:T(8,128)S(1)}, f32[32,1,128]{2,1,0:T(1,128)S(1)}, f32[2,8,128]{2,1,0:T(8,128)S(1)}) custom-call(f32[3,3]{1,0:T(4,128)S(1)} %copy-done, f32[288,1,128]{2,1,0:T(1,128)S(1)} %all_to_all.10.got_ref, f32[32,128]{1,0:T(8,128)S(1)} %get-tuple-element.48.own_ref, ...), custom_call_target="tpu_custom_call" | custom-call | tf_op jit(solution)/shard_map/second_direction/pallas_call | solution.py:950
  41.5 9.1 %all_to_all.11.sums_ref = f32[32,1,128]{2,1,0:T(1,128)S(1)} all-to-all(f32[32,1,128]{2,1,0:T(1,128)S(1)} %get-tuple-element.55), channel_id=1, replica_groups=mesh['cols'=8,'rows'=4] {'rows','cols'}, dimensions={0} | all-to-all | bytes 32768 | tf_op jit(solution)/shard_map/all_to_all | solution.py:1050
  50.5 1.5 %combine.1 = (f32[256,1024]{1,0:T(8,128)}, f32[256,1024]{1,0:T(8,128)}) custom-call(f32[32,1,128]{2,1,0:T(1,128)S(1)} %all_to_all.11.sums_ref, f32[2,8,128]{2,1,0:T(8,128)S(1)} %get-tuple-element.56.known_ref, f32[9,288,128]{2,1,0:T(8,128)S(1)} %get-tuple-element.57.p_ref, f32[9,288,128]{2,1,0:T(8,128)S(1)} %get-tuple-element.58.w_ref, ...), custom_call_target="tpu_custom_call" | custom-call | tf_op jit(solution)/shard_map/combine/pallas_call | solution.py:1008
Async XLA Ops:
  2.4 9.1 %collective-permute-start = (f32[40,128]{1,0:T(8,128)S(1)}, f32[40,128]{1,0:T(8,128)S(1)}, u32[]{:S(2)}, u32[]{:S(2)}) collective-permute-start(f32[40,128]{1,0:T(8,128)S(1)} %get-tuple-element.31), channel_id=1, source_target_pairs={{4,8},{8,4},{12,16},{16,12},{20,24},{24,20},{5,9},{9,5},{13,17},{1... | collective-permute-start | bytes 61448 | tf_op jit(solution)/shard_map/ppermute | solution.py:1031
  3.0 8.4 %collective-permute-start.1 = (f32[40,128]{1,0:T(8,128)S(1)}, f32[40,128]{1,0:T(8,128)S(1)}, u32[]{:S(2)}, u32[]{:S(2)}) collective-permute-start(f32[40,128]{1,0:T(8,128)S(1)} %get-tuple-element.32.refs_4_), channel_id=1, source_target_pairs={{0,4},{4,0},{8,12},{12,8},{16,20},{20,16},{24,28},{28,24},{1,5},{5... | collective-permute-start | bytes 61448 | tf_op jit(solution)/shard_map/ppermute | solution.py:1032
  11.5 3.9 %copy-start = (f32[3,3]{1,0:T(4,128)S(1)}, f32[3,3]{1,0:T(4,128)}, u32[]{:S(2)}) copy-start(f32[3,3]{1,0:T(4,128)} %taps.5) | copy-start | bytes 112
  11.7 6.3 %collective-permute-start.2 = (f32[128,128]{1,0:T(8,128)S(1)}, f32[128,128]{1,0:T(8,128)S(1)}, u32[]{:S(2)}, u32[]{:S(2)}) collective-permute-start(f32[128,128]{1,0:T(8,128)S(1)} %get-tuple-element.43), channel_id=1, source_target_pairs={{1,2},{2,1},{5,6},{6,5},{9,10},{10,9},{13,14},{14,13},{17,18},{18,... | collective-permute-start | bytes 196616 | tf_op jit(solution)/shard_map/ppermute | solution.py:1031
  12.4 5.6 %collective-permute-start.3 = (f32[128,128]{1,0:T(8,128)S(1)}, f32[128,128]{1,0:T(8,128)S(1)}, u32[]{:S(2)}, u32[]{:S(2)}) collective-permute-start(f32[128,128]{1,0:T(8,128)S(1)} %get-tuple-element.44), channel_id=1, source_target_pairs={{0,1},{1,0},{2,3},{3,2},{4,5},{5,4},{6,7},{7,6},{8,9},{9,8},{10,11... | collective-permute-start | bytes 196616 | tf_op jit(solution)/shard_map/ppermute | solution.py:1032

commit v14 on v13

--- a/solution.py
+++ b/solution.py
@@ -18,7 +18,7 @@
 STRIP = 2 * EDGE
 REACH = 5
 PIECE = EDGE + 1
-CHUNK = 64
+CHUNK = 128
 AXES = ("cols", "rows")
 LIMIT = 40 * 1024 * 1024
 
@@ -798,7 +798,7 @@
 
     nothing = jnp.zeros((EDGE, LANES), jnp.float32)
     span = (EDGE, 3 * EDGE + height)
-    sweep(3, *span, begin_p, 0)
+    sweep(6, *span, begin_p, 0)
     sweep(3, *span, blur, 0)
     mask_rows(image, has_n, has_s)
     dot_pq = sweep(3, *span, finish, nothing)
@@ -933,7 +933,7 @@
 
     nothing = jnp.zeros((EDGE, LANES), jnp.float32)
     span = (EDGE, 3 * EDGE + height)
-    dot_rz = sweep(3, *span, begin_w, nothing)
+    dot_rz = sweep(6, *span, begin_w, nothing)
     sweep(3, *span, blur, 0)
     mask_rows(image, has_n, has_s)
     dot_zz = sweep(4, 2 * EDGE, 2 * EDGE + height, finish, nothing)

time: 52.3 us -> 52.2 us (level)
  no operation moved by 1% of the time
where the time goes in v14:
time: 52.2 us; the launch traced here: 52 us
  blocking collectives  21.3 us (41%)
  Pallas kernels  20 us (38%)
  starting transfers between devices  10 us (19%)
  between operations  0.73 us (1%)
    all_to_all x1, blocking collectives, body(): got = lax.all_to_all(chunk, AXES, 0, 0, tiled=True)  12.2 us
    all_to_all x1, blocking collectives, body(): sums = lax.all_to_all(line, AXES[::-1], 0, 0, tiled=True)  9.06 us
    ppermute x2, starting transfers between devices, exchange(): got_a = lax.ppermute(send_a, axis, pairs(0))  8.71 us
    pallas_call x1, Pallas kernels, first(): pl.pallas_call(functools.partial(first_kernel, tiles, down), in_specs=[SM...  5.93 us
    pallas_call x1, Pallas kernels, second(): pl.pallas_call(functools.partial(second_kernel, tiles, down), in_specs=[S...  5.23 us
    pallas_call x1, Pallas kernels, inner(): pl.pallas_call(inner_kernel, in_specs=[SMEM] + [VMEM] * 2, out_specs=[VME...  2.68 us
    pallas_call x1, Pallas kernels, pack(): pl.pallas_call(functools.partial(pack_kernel, tiles, down), in_specs=[HBM...  2.6 us
    pallas_call x1, Pallas kernels, edge(): pl.pallas_call(functools.partial(edge_kernel, tiles, down), in_specs=[HBM...  1.73 us
  transfers between devices with their start and end apart: 4, of which 0 were waited for; matrix products, arithmetic and copies ran while one was open for 0% of the time, Pallas kernels for 10%

profile of v14, /device:TPU:0, one launch (start us, length us, event | category | flops | bytes accessed | tf_op | source)
XLA Modules:
  0.0 52.0 jit_solution(1547017044626988355)
XLA Ops:
  0.6 1.7 %pack_east_west.1 = (f32[40,128]{1,0:T(8,128)S(1)}, f32[40,128]{1,0:T(8,128)S(1)}) custom-call(f32[256,1024]{1,0:T(8,128)} %refs_0_.3, s32[256,1024]{1,0:T(8,128)} %refs_1_.3, f32[4]{0:T(128)} %refs_2_.3, f32[3,3]{1,0:T(4,128)} %taps.5), custom_call_target="tpu_custom_call" | custom-call | tf_op jit(solution)/shard_map/pack_east_west/pallas_call | solution.py:451
  2.4 0.7 %collective-permute-start = (f32[40,128]{1,0:T(8,128)S(1)}, f32[40,128]{1,0:T(8,128)S(1)}, u32[]{:S(2)}, u32[]{:S(2)}) collective-permute-start(f32[40,128]{1,0:T(8,128)S(1)} %get-tuple-element.31), channel_id=1, source_target_pairs={{4,8},{8,4},{12,16},{16,12},{20,24},{24,20},{5,9},{9,5},{13,17},{1... | collective-permute-start | bytes 61448 | tf_op jit(solution)/shard_map/ppermute | solution.py:1031
  3.0 5.8 %collective-permute-start.1 = (f32[40,128]{1,0:T(8,128)S(1)}, f32[40,128]{1,0:T(8,128)S(1)}, u32[]{:S(2)}, u32[]{:S(2)}) collective-permute-start(f32[40,128]{1,0:T(8,128)S(1)} %get-tuple-element.32.refs_4_), channel_id=1, source_target_pairs={{0,4},{4,0},{8,12},{12,8},{16,20},{20,16},{24,28},{28,24},{1,5},{5... | collective-permute-start | bytes 61448 | tf_op jit(solution)/shard_map/ppermute | solution.py:1032
  8.8 2.6 %pack_all.1 = (f32[9,288,128]{2,1,0:T(8,128)S(1)}, f32[9,288,128]{2,1,0:T(8,128)S(1)}, f32[4,48,256]{2,1,0:T(8,128)S(1)}) custom-call(f32[256,1024]{1,0:T(8,128)} %refs_0_.3, s32[256,1024]{1,0:T(8,128)} %refs_1_.3, f32[4]{0:T(128)} %refs_2_.3, f32[3,3]{1,0:T(4,128)} %taps.5, f32[40,128]{1,0:T(8,128)S(1)} %get-tuple-element.32.refs_4_), custom_call_target="tpu_custom_call" | custom-call | flops 5242880 | bytes 4194304 | tf_op jit(solution)/shard_map/pack_all/pallas_call | solution.py:483
  11.4 0.0 collective-permute-done.got_b
  11.5 0.0 collective-permute-done.1.got_a
  11.5 0.0 copy-start
  11.5 0.3 pack_north_south.1
  11.7 0.7 %collective-permute-start.2 = (f32[128,128]{1,0:T(8,128)S(1)}, f32[128,128]{1,0:T(8,128)S(1)}, u32[]{:S(2)}, u32[]{:S(2)}) collective-permute-start(f32[128,128]{1,0:T(8,128)S(1)} %get-tuple-element.43), channel_id=1, source_target_pairs={{1,2},{2,1},{5,6},{6,5},{9,10},{10,9},{13,14},{14,13},{17,18},{18,... | collective-permute-start | bytes 196616 | tf_op jit(solution)/shard_map/ppermute | solution.py:1031
  12.4 2.9 %collective-permute-start.3 = (f32[128,128]{1,0:T(8,128)S(1)}, f32[128,128]{1,0:T(8,128)S(1)}, u32[]{:S(2)}, u32[]{:S(2)}) collective-permute-start(f32[128,128]{1,0:T(8,128)S(1)} %get-tuple-element.44), channel_id=1, source_target_pairs={{0,1},{1,0},{2,3},{3,2},{4,5},{5,4},{6,7},{7,6},{8,9},{9,8},{10,11... | collective-permute-start | bytes 196616 | tf_op jit(solution)/shard_map/ppermute | solution.py:1032
  15.3 0.0 copy-done
  15.3 2.7 %inner_strips.1 = (f32[9,288,128]{2,1,0:T(8,128)S(1)}, f32[9,288,128]{2,1,0:T(8,128)S(1)}, f32[9,288,128]{2,1,0:T(8,128)S(1)}, f32[9,288,128]{2,1,0:T(8,128)S(1)...) custom-call(f32[3,3]{1,0:T(4,128)S(1)} %copy-done, f32[9,288,128]{2,1,0:T(8,128)S(1)} %get-tuple-element.36.obs.obs_in, ...), custom_call_target="tpu_custom_call" | custom-call | flops 14929920 | bytes 7962624 | tf_op jit(solution)/shard_map/inner_strips/pallas_call | solution.py:644
  18.0 0.0 collective-permute-done.2.got_b
  18.0 0.0 collective-permute-done.3.got_a
  18.0 5.9 %first_direction.1 = (f32[9,288,128]{2,1,0:T(8,128)S(1)}, f32[9,288,128]{2,1,0:T(8,128)S(1)}, f32[9,288,128]{2,1,0:T(8,128)S(1)}, f32[9,288,128]{2,1,0:T(8,128)S...) custom-call(f32[3,3]{1,0:T(4,128)S(1)} %copy-done, ...), custom_call_target="tpu_custom_call", output_to_operand_aliasing={{0}: (1, {}), {1}: (2, {}), {2}: (3, {}), {3}: (4, {}), {4}... | custom-call | tf_op jit(solution)/shard_map/first_direction/pallas_call | solution.py:840
  24.0 12.2 %all_to_all.10.got_ref = f32[288,1,128]{2,1,0:T(1,128)S(1)} all-to-all(f32[288,1,128]{2,1,0:T(1,128)S(1)} %get-tuple-element.47), channel_id=1, replica_groups=mesh['cols'=8,'rows'=4] {'cols','rows'}, dimensions={0} | all-to-all | bytes 294912 | tf_op jit(solution)/shard_map/all_to_all | solution.py:1048
  36.2 5.2 %second_direction.1 = (f32[9,288,128]{2,1,0:T(8,128)S(1)}, f32[9,288,128]{2,1,0:T(8,128)S(1)}, f32[32,1,128]{2,1,0:T(1,128)S(1)}, f32[2,8,128]{2,1,0:T(8,128)S(1)}) custom-call(f32[3,3]{1,0:T(4,128)S(1)} %copy-done, f32[288,1,128]{2,1,0:T(1,128)S(1)} %all_to_all.10.got_ref, f32[32,128]{1,0:T(8,128)S(1)} %get-tuple-element.48.own_ref, ...), custom_call_target="tpu_custom_call" | custom-call | tf_op jit(solution)/shard_map/second_direction/pallas_call | solution.py:950
  41.4 9.1 %all_to_all.11.sums_ref = f32[32,1,128]{2,1,0:T(1,128)S(1)} all-to-all(f32[32,1,128]{2,1,0:T(1,128)S(1)} %get-tuple-element.55), channel_id=1, replica_groups=mesh['cols'=8,'rows'=4] {'rows','cols'}, dimensions={0} | all-to-all | bytes 32768 | tf_op jit(solution)/shard_map/all_to_all | solution.py:1050
  50.5 1.5 %combine.1 = (f32[256,1024]{1,0:T(8,128)}, f32[256,1024]{1,0:T(8,128)}) custom-call(f32[32,1,128]{2,1,0:T(1,128)S(1)} %all_to_all.11.sums_ref, f32[2,8,128]{2,1,0:T(8,128)S(1)} %get-tuple-element.56.known_ref, f32[9,288,128]{2,1,0:T(8,128)S(1)} %get-tuple-element.57.p_ref, f32[9,288,128]{2,1,0:T(8,128)S(1)} %get-tuple-element.58.w_ref, ...), custom_call_target="tpu_custom_call" | custom-call | tf_op jit(solution)/shard_map/combine/pallas_call | solution.py:1008
Async XLA Ops:
  2.4 9.1 %collective-permute-start = (f32[40,128]{1,0:T(8,128)S(1)}, f32[40,128]{1,0:T(8,128)S(1)}, u32[]{:S(2)}, u32[]{:S(2)}) collective-permute-start(f32[40,128]{1,0:T(8,128)S(1)} %get-tuple-element.31), channel_id=1, source_target_pairs={{4,8},{8,4},{12,16},{16,12},{20,24},{24,20},{5,9},{9,5},{13,17},{1... | collective-permute-start | bytes 61448 | tf_op jit(solution)/shard_map/ppermute | solution.py:1031
  3.0 8.4 %collective-permute-start.1 = (f32[40,128]{1,0:T(8,128)S(1)}, f32[40,128]{1,0:T(8,128)S(1)}, u32[]{:S(2)}, u32[]{:S(2)}) collective-permute-start(f32[40,128]{1,0:T(8,128)S(1)} %get-tuple-element.32.refs_4_), channel_id=1, source_target_pairs={{0,4},{4,0},{8,12},{12,8},{16,20},{20,16},{24,28},{28,24},{1,5},{5... | collective-permute-start | bytes 61448 | tf_op jit(solution)/shard_map/ppermute | solution.py:1032
  11.5 3.9 %copy-start = (f32[3,3]{1,0:T(4,128)S(1)}, f32[3,3]{1,0:T(4,128)}, u32[]{:S(2)}) copy-start(f32[3,3]{1,0:T(4,128)} %taps.5) | copy-start | bytes 112
  11.7 6.3 %collective-permute-start.2 = (f32[128,128]{1,0:T(8,128)S(1)}, f32[128,128]{1,0:T(8,128)S(1)}, u32[]{:S(2)}, u32[]{:S(2)}) collective-permute-start(f32[128,128]{1,0:T(8,128)S(1)} %get-tuple-element.43), channel_id=1, source_target_pairs={{1,2},{2,1},{5,6},{6,5},{9,10},{10,9},{13,14},{14,13},{17,18},{18,... | collective-permute-start | bytes 196616 | tf_op jit(solution)/shard_map/ppermute | solution.py:1031
  12.4 5.6 %collective-permute-start.3 = (f32[128,128]{1,0:T(8,128)S(1)}, f32[128,128]{1,0:T(8,128)S(1)}, u32[]{:S(2)}, u32[]{:S(2)}) collective-permute-start(f32[128,128]{1,0:T(8,128)S(1)} %get-tuple-element.44), channel_id=1, source_target_pairs={{0,1},{1,0},{2,3},{3,2},{4,5},{5,4},{6,7},{7,6},{8,9},{9,8},{10,11... | collective-permute-start | bytes 196616 | tf_op jit(solution)/shard_map/ppermute | solution.py:1032

commit v15 on v13

--- a/solution.py
+++ b/solution.py
@@ -201,19 +201,20 @@
     ]
 
 
-def cell_sums(ref, tiles, down):
-    lane = iota((down, LANES), 1)
-    total = jnp.zeros((down, LANES), jnp.float32)
+def cell_sums(ref, tiles, down, matrix):
+    rows = []
     for t in range(tiles):
         picked = [
             ref[t, pl.ds(2 * EDGE + k, down, stride=COARSE), :] for k in range(COARSE)
         ]
-        part = sum(picked[1:], picked[0])
-        for by in (1, 2, 4):
-            part = part + roll(part, -by, 1)
-        part = pick_lanes(part, (lane & (LANES // COARSE - 1)) * COARSE)
-        total = jnp.where(lane // (LANES // COARSE) == t, part, total)
-    return total
+        rows.append(sum(picked[1:], picked[0]))
+    return split_dot(jnp.concatenate(rows, axis=1), matrix)
+
+
+def cell_matrix(tiles):
+    shape = (tiles * LANES, LANES)
+    hit = iota(shape, 0) // COARSE == iota(shape, 1)
+    return jnp.where(hit, 1.0, 0.0).astype(jnp.bfloat16)
 
 
 def side_lanes(has_e, has_w):
@@ -620,13 +621,14 @@
     )(got_b, got_a, coarse, obs, cond)
 
 
-def inner_kernel(taps, obs, cond, res_ref, east_ref, south_ref, inv_ref, u_ref, dot_ref):
+def inner_kernel(taps, obs, cond, res_ref, east_ref, south_ref, inv_ref, u_ref, dot_ref, cells_ref):
     _, _, has_e, has_w = has_sides()
     clear_pads(east_ref, south_ref)
     taps = read_taps(taps)
     sides = side_lanes(has_e, has_w)
 
     tiles = obs.shape[0] - 1
+    cells_ref[...] = cell_matrix(tiles)
 
     def work(at, start, total):
         fields = begin(obs, cond, at, taps, sides)
@@ -644,8 +646,9 @@
     return pl.pallas_call(
         inner_kernel,
         in_specs=[SMEM] + [VMEM] * 2,
-        out_specs=[VMEM] * 6,
-        out_shape=floats(field, field, field, field, field, (EDGE, LANES)),
+        out_specs=[VMEM] * 7,
+        out_shape=floats(field, field, field, field, field, (EDGE, LANES))
+        + [jax.ShapeDtypeStruct(((field[0] - 1) * LANES, LANES), jnp.bfloat16)],
         compiler_params=params(),
         cost_estimate=pl.CostEstimate(
             flops=45 * pixels, bytes_accessed=24 * pixels, transcendentals=0
@@ -669,6 +672,7 @@
     got_a,
     coarse_in,
     dot_in,
+    cells_in,
     obs,
     cond,
     res_ref,
@@ -803,7 +807,7 @@
     mask_rows(image, has_n, has_s)
     dot_pq = sweep(3, *span, finish, nothing)
 
-    own = cell_sums(q_ref, tiles, down)
+    own = cell_sums(q_ref, tiles, down, cells_in[...])
     own_ref[...] = own
     spare = jnp.zeros((LANES - down, LANES), jnp.float32)
     turned = jnp.transpose(jnp.concatenate([own, spare], axis=0))
@@ -826,7 +830,7 @@
         chunk_ref[at] = line
 
 
-def first(taps, fields, got_a, got_b, coarse, dot):
+def first(taps, fields, got_a, got_b, coarse, dot, matrix):
     field = fields[0].shape
     tiles, height = field[0] - 1, field[1] - 4 * EDGE
     down = height // COARSE
@@ -839,7 +843,7 @@
     ]
     return pl.pallas_call(
         functools.partial(first_kernel, tiles, down),
-        in_specs=[SMEM] + [VMEM] * 11,
+        in_specs=[SMEM] + [VMEM] * 12,
         out_specs=[VMEM] * len(shapes),
         out_shape=floats(*shapes),
         input_output_aliases={index + 1: index for index in range(7)},
@@ -850,7 +854,7 @@
         ],
         compiler_params=params(),
         name="first_direction",
-    )(taps, *fields, got_b, got_a, coarse, dot)[2:]
+    )(taps, *fields, got_b, got_a, coarse, dot, matrix)[2:]
 
 
 def second_kernel(
@@ -1040,10 +1044,10 @@
     obs, cond, coarse = pack(*arguments, send_a)
     obs, cond, coarse, send_a, send_b = middle(got_a, got_b, coarse, obs, cond)
     got_a, got_b = exchange(send_a, send_b, "rows")
-    r, east, south, inv, u, dot = inner(blur_kernel, obs, cond)
+    r, east, south, inv, u, dot, matrix = inner(blur_kernel, obs, cond)
     fields = (obs, cond, r, east, south, inv, u)
     r, east, south, inv, _, p, q, table, own, chunk = first(
-        blur_kernel, fields, got_a, got_b, coarse, dot
+        blur_kernel, fields, got_a, got_b, coarse, dot, matrix
     )
     got = lax.all_to_all(chunk, AXES, 0, 0, tiled=True)
     w, v, line, known = second(blur_kernel, got, own, table, r, q, east, south, inv)

time: 52.3 us -> 52.2 us (level)
  no operation moved by 1% of the time
where the time goes in v15:
time: 52.2 us; the launch traced here: 51.9 us
  blocking collectives  21.2 us (41%)
  Pallas kernels  19.9 us (38%)
  starting transfers between devices  10 us (19%)
  between operations  0.73 us (1%)
    all_to_all x1, blocking collectives, body(): got = lax.all_to_all(chunk, AXES, 0, 0, tiled=True)  12.2 us
    all_to_all x1, blocking collectives, body(): sums = lax.all_to_all(line, AXES[::-1], 0, 0, tiled=True)  9.06 us
    ppermute x2, starting transfers between devices, exchange(): got_a = lax.ppermute(send_a, axis, pairs(0))  8.71 us
    pallas_call x1, Pallas kernels, first(): pl.pallas_call(functools.partial(first_kernel, tiles, down), in_specs=[SM...  5.83 us
    pallas_call x1, Pallas kernels, second(): pl.pallas_call(functools.partial(second_kernel, tiles, down), in_specs=[S...  5.26 us
    pallas_call x1, Pallas kernels, inner(): pl.pallas_call(inner_kernel, in_specs=[SMEM] + [VMEM] * 2, out_specs=[VME...  2.74 us
    pallas_call x1, Pallas kernels, pack(): pl.pallas_call(functools.partial(pack_kernel, tiles, down), in_specs=[HBM...  2.6 us
    pallas_call x1, Pallas kernels, edge(): pl.pallas_call(functools.partial(edge_kernel, tiles, down), in_specs=[HBM...  1.73 us
  transfers between devices with their start and end apart: 4, of which 0 were waited for; matrix products, arithmetic and copies ran while one was open for 0% of the time, Pallas kernels for 10%

profile of v15, /device:TPU:0, one launch (start us, length us, event | category | flops | bytes accessed | tf_op | source)
XLA Modules:
  0.0 51.9 jit_solution(16801504778854452673)
XLA Ops:
  0.6 1.7 %pack_east_west.1 = (f32[40,128]{1,0:T(8,128)S(1)}, f32[40,128]{1,0:T(8,128)S(1)}) custom-call(f32[256,1024]{1,0:T(8,128)} %refs_0_.3, s32[256,1024]{1,0:T(8,128)} %refs_1_.3, f32[4]{0:T(128)} %refs_2_.3, f32[3,3]{1,0:T(4,128)} %taps.5), custom_call_target="tpu_custom_call" | custom-call | tf_op jit(solution)/shard_map/pack_east_west/pallas_call | solution.py:452
  2.4 0.7 %collective-permute-start = (f32[40,128]{1,0:T(8,128)S(1)}, f32[40,128]{1,0:T(8,128)S(1)}, u32[]{:S(2)}, u32[]{:S(2)}) collective-permute-start(f32[40,128]{1,0:T(8,128)S(1)} %get-tuple-element.32), channel_id=1, source_target_pairs={{4,8},{8,4},{12,16},{16,12},{20,24},{24,20},{5,9},{9,5},{13,17},{1... | collective-permute-start | bytes 61448 | tf_op jit(solution)/shard_map/ppermute | solution.py:1035
  3.0 5.8 %collective-permute-start.1 = (f32[40,128]{1,0:T(8,128)S(1)}, f32[40,128]{1,0:T(8,128)S(1)}, u32[]{:S(2)}, u32[]{:S(2)}) collective-permute-start(f32[40,128]{1,0:T(8,128)S(1)} %get-tuple-element.33.refs_4_), channel_id=1, source_target_pairs={{0,4},{4,0},{8,12},{12,8},{16,20},{20,16},{24,28},{28,24},{1,5},{5... | collective-permute-start | bytes 61448 | tf_op jit(solution)/shard_map/ppermute | solution.py:1036
  8.8 2.6 %pack_all.1 = (f32[9,288,128]{2,1,0:T(8,128)S(1)}, f32[9,288,128]{2,1,0:T(8,128)S(1)}, f32[4,48,256]{2,1,0:T(8,128)S(1)}) custom-call(f32[256,1024]{1,0:T(8,128)} %refs_0_.3, s32[256,1024]{1,0:T(8,128)} %refs_1_.3, f32[4]{0:T(128)} %refs_2_.3, f32[3,3]{1,0:T(4,128)} %taps.5, f32[40,128]{1,0:T(8,128)S(1)} %get-tuple-element.33.refs_4_), custom_call_target="tpu_custom_call" | custom-call | flops 5242880 | bytes 4194304 | tf_op jit(solution)/shard_map/pack_all/pallas_call | solution.py:484
  11.4 0.0 collective-permute-done.got_b
  11.5 0.0 collective-permute-done.1.got_a
  11.5 0.0 copy-start
  11.5 0.3 pack_north_south.1
  11.8 0.7 %collective-permute-start.2 = (f32[128,128]{1,0:T(8,128)S(1)}, f32[128,128]{1,0:T(8,128)S(1)}, u32[]{:S(2)}, u32[]{:S(2)}) collective-permute-start(f32[128,128]{1,0:T(8,128)S(1)} %get-tuple-element.44), channel_id=1, source_target_pairs={{1,2},{2,1},{5,6},{6,5},{9,10},{10,9},{13,14},{14,13},{17,18},{18,... | collective-permute-start | bytes 196616 | tf_op jit(solution)/shard_map/ppermute | solution.py:1035
  12.4 2.9 %collective-permute-start.3 = (f32[128,128]{1,0:T(8,128)S(1)}, f32[128,128]{1,0:T(8,128)S(1)}, u32[]{:S(2)}, u32[]{:S(2)}) collective-permute-start(f32[128,128]{1,0:T(8,128)S(1)} %get-tuple-element.45), channel_id=1, source_target_pairs={{0,1},{1,0},{2,3},{3,2},{4,5},{5,4},{6,7},{7,6},{8,9},{9,8},{10,11... | collective-permute-start | bytes 196616 | tf_op jit(solution)/shard_map/ppermute | solution.py:1036
  15.3 0.0 copy-done
  15.3 2.7 %inner_strips.1 = (f32[9,288,128]{2,1,0:T(8,128)S(1)}, f32[9,288,128]{2,1,0:T(8,128)S(1)}, f32[9,288,128]{2,1,0:T(8,128)S(1)}, f32[9,288,128]{2,1,0:T(8,128)S(1)...) custom-call(f32[3,3]{1,0:T(4,128)S(1)} %copy-done, ...), custom_call_target="tpu_custom_call" | custom-call | flops 14929920 | bytes 7962624 | tf_op jit(solution)/shard_map/inner_strips/pallas_call | solution.py:646
  18.1 0.0 collective-permute-done.2.got_b
  18.1 0.0 collective-permute-done.3.got_a
  18.1 5.8 %first_direction.1 = (f32[9,288,128]{2,1,0:T(8,128)S(1)}, f32[9,288,128]{2,1,0:T(8,128)S(1)}, f32[9,288,128]{2,1,0:T(8,128)S(1)}, f32[9,288,128]{2,1,0:T(8,128)S...) custom-call(f32[3,3]{1,0:T(4,128)S(1)} %copy-done, ...), custom_call_target="tpu_custom_call", output_to_operand_aliasing={{0}: (1, {}), {1}: (2, {}), {2}: (3, {}), {3}: (4, {}), {4}... | custom-call | tf_op jit(solution)/shard_map/first_direction/pallas_call | solution.py:844
  23.9 12.2 %all_to_all.10.got_ref = f32[288,1,128]{2,1,0:T(1,128)S(1)} all-to-all(f32[288,1,128]{2,1,0:T(1,128)S(1)} %get-tuple-element.49), channel_id=1, replica_groups=mesh['cols'=8,'rows'=4] {'cols','rows'}, dimensions={0} | all-to-all | bytes 294912 | tf_op jit(solution)/shard_map/all_to_all | solution.py:1052
  36.1 5.3 %second_direction.1 = (f32[9,288,128]{2,1,0:T(8,128)S(1)}, f32[9,288,128]{2,1,0:T(8,128)S(1)}, f32[32,1,128]{2,1,0:T(1,128)S(1)}, f32[2,8,128]{2,1,0:T(8,128)S(1)}) custom-call(f32[3,3]{1,0:T(4,128)S(1)} %copy-done, f32[288,1,128]{2,1,0:T(1,128)S(1)} %all_to_all.10.got_ref, f32[32,128]{1,0:T(8,128)S(1)} %get-tuple-element.50.own_ref, ...), custom_call_target="tpu_custom_call" | custom-call | tf_op jit(solution)/shard_map/second_direction/pallas_call | solution.py:954
  41.4 9.1 %all_to_all.11.sums_ref = f32[32,1,128]{2,1,0:T(1,128)S(1)} all-to-all(f32[32,1,128]{2,1,0:T(1,128)S(1)} %get-tuple-element.57), channel_id=1, replica_groups=mesh['cols'=8,'rows'=4] {'rows','cols'}, dimensions={0} | all-to-all | bytes 32768 | tf_op jit(solution)/shard_map/all_to_all | solution.py:1054
  50.4 1.5 %combine.1 = (f32[256,1024]{1,0:T(8,128)}, f32[256,1024]{1,0:T(8,128)}) custom-call(f32[32,1,128]{2,1,0:T(1,128)S(1)} %all_to_all.11.sums_ref, f32[2,8,128]{2,1,0:T(8,128)S(1)} %get-tuple-element.58.known_ref, f32[9,288,128]{2,1,0:T(8,128)S(1)} %get-tuple-element.59.p_ref, f32[9,288,128]{2,1,0:T(8,128)S(1)} %get-tuple-element.60.w_ref, ...), custom_call_target="tpu_custom_call" | custom-call | tf_op jit(solution)/shard_map/combine/pallas_call | solution.py:1012
Async XLA Ops:
  2.4 9.1 %collective-permute-start = (f32[40,128]{1,0:T(8,128)S(1)}, f32[40,128]{1,0:T(8,128)S(1)}, u32[]{:S(2)}, u32[]{:S(2)}) collective-permute-start(f32[40,128]{1,0:T(8,128)S(1)} %get-tuple-element.32), channel_id=1, source_target_pairs={{4,8},{8,4},{12,16},{16,12},{20,24},{24,20},{5,9},{9,5},{13,17},{1... | collective-permute-start | bytes 61448 | tf_op jit(solution)/shard_map/ppermute | solution.py:1035
  3.0 8.4 %collective-permute-start.1 = (f32[40,128]{1,0:T(8,128)S(1)}, f32[40,128]{1,0:T(8,128)S(1)}, u32[]{:S(2)}, u32[]{:S(2)}) collective-permute-start(f32[40,128]{1,0:T(8,128)S(1)} %get-tuple-element.33.refs_4_), channel_id=1, source_target_pairs={{0,4},{4,0},{8,12},{12,8},{16,20},{20,16},{24,28},{28,24},{1,5},{5... | collective-permute-start | bytes 61448 | tf_op jit(solution)/shard_map/ppermute | solution.py:1036
  11.5 3.9 %copy-start = (f32[3,3]{1,0:T(4,128)S(1)}, f32[3,3]{1,0:T(4,128)}, u32[]{:S(2)}) copy-start(f32[3,3]{1,0:T(4,128)} %taps.5) | copy-start | bytes 112
  11.8 6.3 %collective-permute-start.2 = (f32[128,128]{1,0:T(8,128)S(1)}, f32[128,128]{1,0:T(8,128)S(1)}, u32[]{:S(2)}, u32[]{:S(2)}) collective-permute-start(f32[128,128]{1,0:T(8,128)S(1)} %get-tuple-element.44), channel_id=1, source_target_pairs={{1,2},{2,1},{5,6},{6,5},{9,10},{10,9},{13,14},{14,13},{17,18},{18,... | collective-permute-start | bytes 196616 | tf_op jit(solution)/shard_map/ppermute | solution.py:1035
  12.4 5.7 %collective-permute-start.3 = (f32[128,128]{1,0:T(8,128)S(1)}, f32[128,128]{1,0:T(8,128)S(1)}, u32[]{:S(2)}, u32[]{:S(2)}) collective-permute-start(f32[128,128]{1,0:T(8,128)S(1)} %get-tuple-element.45), channel_id=1, source_target_pairs={{0,1},{1,0},{2,3},{3,2},{4,5},{5,4},{6,7},{7,6},{8,9},{9,8},{10,11... | collective-permute-start | bytes 196616 | tf_op jit(solution)/shard_map/ppermute | solution.py:1036

commit v16 on v15

--- a/solution.py
+++ b/solution.py
@@ -19,7 +19,7 @@
 REACH = 5
 PIECE = EDGE + 1
 CHUNK = 64
-AXES = ("cols", "rows")
+AXES = ("rows", "cols")
 LIMIT = 40 * 1024 * 1024
 
 
@@ -811,7 +811,7 @@
     own_ref[...] = own
     spare = jnp.zeros((LANES - down, LANES), jnp.float32)
     turned = jnp.transpose(jnp.concatenate([own, spare], axis=0))
-    me = at_col * n_rows + at_row
+    me = at_row * n_cols + at_col
     chunk_ref[pl.ds(me * PIECE, EDGE), 0, :] = jnp.zeros((EDGE, LANES), jnp.float32)
     for down_by in (-1, 0, 1):
         for right_by in (-1, 0, 1):
@@ -823,7 +823,7 @@
                 piece = own[:EDGE] if down_by < 0 else own[down - EDGE :]
             to_row, to_col = at_row + down_by, at_col + right_by
             there = (to_row >= 0) & (to_row < n_rows) & (to_col >= 0) & (to_col < n_cols)
-            slot = jnp.where(there, to_col * n_rows + to_row, me)
+            slot = jnp.where(there, to_row * n_cols + to_col, me)
             chunk_ref[pl.ds(slot * PIECE, EDGE), 0, :] = piece * jnp.where(there, 1.0, 0.0)
     line = sum_line((dot_rp, dot_pq))
     for at in range(EDGE, chunk_ref.shape[0], PIECE):
@@ -880,12 +880,12 @@
     height = down * COARSE
     has_n, has_s, has_e, has_w = has_sides()
     at_col, at_row, n_cols, n_rows = place()
-    me = at_col * n_rows + at_row
+    me = at_row * n_cols + at_col
 
     def got(down_by, right_by):
         to_row, to_col = at_row + down_by, at_col + right_by
         there = (to_row >= 0) & (to_row < n_rows) & (to_col >= 0) & (to_col < n_cols)
-        slot = jnp.where(there, to_col * n_rows + to_row, me)
+        slot = jnp.where(there, to_row * n_cols + to_col, me)
         return got_ref[pl.ds(slot * PIECE, EDGE), 0, :]
 
     low = iota((EDGE, LANES), 1) < HALF
@@ -1051,7 +1051,7 @@
     )
     got = lax.all_to_all(chunk, AXES, 0, 0, tiled=True)
     w, v, line, known = second(blur_kernel, got, own, table, r, q, east, south, inv)
-    sums = lax.all_to_all(line, AXES[::-1], 0, 0, tiled=True)
+    sums = lax.all_to_all(line, AXES, 0, 0, tiled=True)
     return tuple(combine(sums, known, p, w, r, q, v))
 
 

time: 52.2 us -> 52.2 us (level)
    all_to_all x1, blocking collectives: 12.2 us -> 11.6 us  [body(): got = lax.all_to_all(chunk, AXES, 0, 0, tiled=True)]
    all_to_all x1, blocking collectives: 9.06 us -> 9.64 us  [body(): sums = lax.all_to_all(line, AXES, 0, 0, tiled=True)]
where the time goes in v16:
time: 52.2 us; the launch traced here: 51.9 us
  blocking collectives  21.2 us (41%)
  Pallas kernels  20 us (38%)
  starting transfers between devices  10 us (19%)
  between operations  0.73 us (1%)
    all_to_all x1, blocking collectives, body(): got = lax.all_to_all(chunk, AXES, 0, 0, tiled=True)  11.6 us
    all_to_all x1, blocking collectives, body(): sums = lax.all_to_all(line, AXES, 0, 0, tiled=True)  9.64 us
    ppermute x2, starting transfers between devices, exchange(): got_a = lax.ppermute(send_a, axis, pairs(0))  8.71 us
    pallas_call x1, Pallas kernels, first(): pl.pallas_call(functools.partial(first_kernel, tiles, down), in_specs=[SM...  5.83 us
    pallas_call x1, Pallas kernels, second(): pl.pallas_call(functools.partial(second_kernel, tiles, down), in_specs=[S...  5.27 us
    pallas_call x1, Pallas kernels, inner(): pl.pallas_call(inner_kernel, in_specs=[SMEM] + [VMEM] * 2, out_specs=[VME...  2.74 us
    pallas_call x1, Pallas kernels, pack(): pl.pallas_call(functools.partial(pack_kernel, tiles, down), in_specs=[HBM...  2.6 us
    pallas_call x1, Pallas kernels, edge(): pl.pallas_call(functools.partial(edge_kernel, tiles, down), in_specs=[HBM...  1.73 us
  transfers between devices with their start and end apart: 4, of which 0 were waited for; matrix products, arithmetic and copies ran while one was open for 0% of the time, Pallas kernels for 10%

profile of v16, /device:TPU:0, one launch (start us, length us, event | category | flops | bytes accessed | tf_op | source)
XLA Modules:
  0.0 51.9 jit_solution(4225682732730271472)
XLA Ops:
  0.6 1.7 %pack_east_west.1 = (f32[40,128]{1,0:T(8,128)S(1)}, f32[40,128]{1,0:T(8,128)S(1)}) custom-call(f32[256,1024]{1,0:T(8,128)} %refs_0_.3, s32[256,1024]{1,0:T(8,128)} %refs_1_.3, f32[4]{0:T(128)} %refs_2_.3, f32[3,3]{1,0:T(4,128)} %taps.5), custom_call_target="tpu_custom_call" | custom-call | tf_op jit(solution)/shard_map/pack_east_west/pallas_call | solution.py:452
  2.4 0.7 %collective-permute-start = (f32[40,128]{1,0:T(8,128)S(1)}, f32[40,128]{1,0:T(8,128)S(1)}, u32[]{:S(2)}, u32[]{:S(2)}) collective-permute-start(f32[40,128]{1,0:T(8,128)S(1)} %get-tuple-element.32), channel_id=1, source_target_pairs={{4,8},{8,4},{12,16},{16,12},{20,24},{24,20},{5,9},{9,5},{13,17},{1... | collective-permute-start | bytes 61448 | tf_op jit(solution)/shard_map/ppermute | solution.py:1035
  3.0 5.8 %collective-permute-start.1 = (f32[40,128]{1,0:T(8,128)S(1)}, f32[40,128]{1,0:T(8,128)S(1)}, u32[]{:S(2)}, u32[]{:S(2)}) collective-permute-start(f32[40,128]{1,0:T(8,128)S(1)} %get-tuple-element.33.refs_4_), channel_id=1, source_target_pairs={{0,4},{4,0},{8,12},{12,8},{16,20},{20,16},{24,28},{28,24},{1,5},{5... | collective-permute-start | bytes 61448 | tf_op jit(solution)/shard_map/ppermute | solution.py:1036
  8.8 2.6 %pack_all.1 = (f32[9,288,128]{2,1,0:T(8,128)S(1)}, f32[9,288,128]{2,1,0:T(8,128)S(1)}, f32[4,48,256]{2,1,0:T(8,128)S(1)}) custom-call(f32[256,1024]{1,0:T(8,128)} %refs_0_.3, s32[256,1024]{1,0:T(8,128)} %refs_1_.3, f32[4]{0:T(128)} %refs_2_.3, f32[3,3]{1,0:T(4,128)} %taps.5, f32[40,128]{1,0:T(8,128)S(1)} %get-tuple-element.33.refs_4_), custom_call_target="tpu_custom_call" | custom-call | flops 5242880 | bytes 4194304 | tf_op jit(solution)/shard_map/pack_all/pallas_call | solution.py:484
  11.4 0.0 collective-permute-done.got_b
  11.5 0.0 collective-permute-done.1.got_a
  11.5 0.0 copy-start
  11.5 0.3 pack_north_south.1
  11.8 0.7 %collective-permute-start.2 = (f32[128,128]{1,0:T(8,128)S(1)}, f32[128,128]{1,0:T(8,128)S(1)}, u32[]{:S(2)}, u32[]{:S(2)}) collective-permute-start(f32[128,128]{1,0:T(8,128)S(1)} %get-tuple-element.44), channel_id=1, source_target_pairs={{1,2},{2,1},{5,6},{6,5},{9,10},{10,9},{13,14},{14,13},{17,18},{18,... | collective-permute-start | bytes 196616 | tf_op jit(solution)/shard_map/ppermute | solution.py:1035
  12.4 2.9 %collective-permute-start.3 = (f32[128,128]{1,0:T(8,128)S(1)}, f32[128,128]{1,0:T(8,128)S(1)}, u32[]{:S(2)}, u32[]{:S(2)}) collective-permute-start(f32[128,128]{1,0:T(8,128)S(1)} %get-tuple-element.45), channel_id=1, source_target_pairs={{0,1},{1,0},{2,3},{3,2},{4,5},{5,4},{6,7},{7,6},{8,9},{9,8},{10,11... | collective-permute-start | bytes 196616 | tf_op jit(solution)/shard_map/ppermute | solution.py:1036
  15.3 0.0 copy-done
  15.3 2.7 %inner_strips.1 = (f32[9,288,128]{2,1,0:T(8,128)S(1)}, f32[9,288,128]{2,1,0:T(8,128)S(1)}, f32[9,288,128]{2,1,0:T(8,128)S(1)}, f32[9,288,128]{2,1,0:T(8,128)S(1)...) custom-call(f32[3,3]{1,0:T(4,128)S(1)} %copy-done, ...), custom_call_target="tpu_custom_call" | custom-call | flops 14929920 | bytes 7962624 | tf_op jit(solution)/shard_map/inner_strips/pallas_call | solution.py:646
  18.1 0.0 collective-permute-done.2.got_b
  18.1 0.0 collective-permute-done.3.got_a
  18.1 5.8 %first_direction.1 = (f32[9,288,128]{2,1,0:T(8,128)S(1)}, f32[9,288,128]{2,1,0:T(8,128)S(1)}, f32[9,288,128]{2,1,0:T(8,128)S(1)}, f32[9,288,128]{2,1,0:T(8,128)S...) custom-call(f32[3,3]{1,0:T(4,128)S(1)} %copy-done, ...), custom_call_target="tpu_custom_call", output_to_operand_aliasing={{0}: (1, {}), {1}: (2, {}), {2}: (3, {}), {3}: (4, {}), {4}... | custom-call | tf_op jit(solution)/shard_map/first_direction/pallas_call | solution.py:844
  23.9 11.6 %all_to_all.10.got_ref = f32[288,1,128]{2,1,0:T(1,128)S(1)} all-to-all(f32[288,1,128]{2,1,0:T(1,128)S(1)} %get-tuple-element.49), channel_id=1, replica_groups=mesh['cols'=8,'rows'=4] {'rows','cols'}, dimensions={0} | all-to-all | bytes 294912 | tf_op jit(solution)/shard_map/all_to_all | solution.py:1052
  35.5 5.3 %second_direction.1 = (f32[9,288,128]{2,1,0:T(8,128)S(1)}, f32[9,288,128]{2,1,0:T(8,128)S(1)}, f32[32,1,128]{2,1,0:T(1,128)S(1)}, f32[2,8,128]{2,1,0:T(8,128)S(1)}) custom-call(f32[3,3]{1,0:T(4,128)S(1)} %copy-done, f32[288,1,128]{2,1,0:T(1,128)S(1)} %all_to_all.10.got_ref, f32[32,128]{1,0:T(8,128)S(1)} %get-tuple-element.50.own_ref, ...), custom_call_target="tpu_custom_call" | custom-call | tf_op jit(solution)/shard_map/second_direction/pallas_call | solution.py:954
  40.8 9.6 %all_to_all.11.sums_ref = f32[32,1,128]{2,1,0:T(1,128)S(1)} all-to-all(f32[32,1,128]{2,1,0:T(1,128)S(1)} %get-tuple-element.57), channel_id=1, replica_groups=mesh['cols'=8,'rows'=4] {'rows','cols'}, dimensions={0} | all-to-all | bytes 32768 | tf_op jit(solution)/shard_map/all_to_all | solution.py:1054
  50.4 1.5 %combine.1 = (f32[256,1024]{1,0:T(8,128)}, f32[256,1024]{1,0:T(8,128)}) custom-call(f32[32,1,128]{2,1,0:T(1,128)S(1)} %all_to_all.11.sums_ref, f32[2,8,128]{2,1,0:T(8,128)S(1)} %get-tuple-element.58.known_ref, f32[9,288,128]{2,1,0:T(8,128)S(1)} %get-tuple-element.59.p_ref, f32[9,288,128]{2,1,0:T(8,128)S(1)} %get-tuple-element.60.w_ref, ...), custom_call_target="tpu_custom_call" | custom-call | tf_op jit(solution)/shard_map/combine/pallas_call | solution.py:1012
Async XLA Ops:
  2.4 9.1 %collective-permute-start = (f32[40,128]{1,0:T(8,128)S(1)}, f32[40,128]{1,0:T(8,128)S(1)}, u32[]{:S(2)}, u32[]{:S(2)}) collective-permute-start(f32[40,128]{1,0:T(8,128)S(1)} %get-tuple-element.32), channel_id=1, source_target_pairs={{4,8},{8,4},{12,16},{16,12},{20,24},{24,20},{5,9},{9,5},{13,17},{1... | collective-permute-start | bytes 61448 | tf_op jit(solution)/shard_map/ppermute | solution.py:1035
  3.0 8.4 %collective-permute-start.1 = (f32[40,128]{1,0:T(8,128)S(1)}, f32[40,128]{1,0:T(8,128)S(1)}, u32[]{:S(2)}, u32[]{:S(2)}) collective-permute-start(f32[40,128]{1,0:T(8,128)S(1)} %get-tuple-element.33.refs_4_), channel_id=1, source_target_pairs={{0,4},{4,0},{8,12},{12,8},{16,20},{20,16},{24,28},{28,24},{1,5},{5... | collective-permute-start | bytes 61448 | tf_op jit(solution)/shard_map/ppermute | solution.py:1036
  11.5 3.9 %copy-start = (f32[3,3]{1,0:T(4,128)S(1)}, f32[3,3]{1,0:T(4,128)}, u32[]{:S(2)}) copy-start(f32[3,3]{1,0:T(4,128)} %taps.5) | copy-start | bytes 112
  11.8 6.3 %collective-permute-start.2 = (f32[128,128]{1,0:T(8,128)S(1)}, f32[128,128]{1,0:T(8,128)S(1)}, u32[]{:S(2)}, u32[]{:S(2)}) collective-permute-start(f32[128,128]{1,0:T(8,128)S(1)} %get-tuple-element.44), channel_id=1, source_target_pairs={{1,2},{2,1},{5,6},{6,5},{9,10},{10,9},{13,14},{14,13},{17,18},{18,... | collective-permute-start | bytes 196616 | tf_op jit(solution)/shard_map/ppermute | solution.py:1035
  12.4 5.7 %collective-permute-start.3 = (f32[128,128]{1,0:T(8,128)S(1)}, f32[128,128]{1,0:T(8,128)S(1)}, u32[]{:S(2)}, u32[]{:S(2)}) collective-permute-start(f32[128,128]{1,0:T(8,128)S(1)} %get-tuple-element.45), channel_id=1, source_target_pairs={{0,1},{1,0},{2,3},{3,2},{4,5},{5,4},{6,7},{7,6},{8,9},{9,8},{10,11... | collective-permute-start | bytes 196616 | tf_op jit(solution)/shard_map/ppermute | solution.py:1036

commit v17 on v15

--- a/solution.py
+++ b/solution.py
@@ -803,7 +803,7 @@
     nothing = jnp.zeros((EDGE, LANES), jnp.float32)
     span = (EDGE, 3 * EDGE + height)
     sweep(3, *span, begin_p, 0)
-    sweep(3, *span, blur, 0)
+    sweep(6, *span, blur, 0)
     mask_rows(image, has_n, has_s)
     dot_pq = sweep(3, *span, finish, nothing)
 
@@ -938,7 +938,7 @@
     nothing = jnp.zeros((EDGE, LANES), jnp.float32)
     span = (EDGE, 3 * EDGE + height)
     dot_rz = sweep(3, *span, begin_w, nothing)
-    sweep(3, *span, blur, 0)
+    sweep(6, *span, blur, 0)
     mask_rows(image, has_n, has_s)
     dot_zz = sweep(4, 2 * EDGE, 2 * EDGE + height, finish, nothing)
     line = sum_line((dot_rz, dot_zz))

time: 52.2 us -> 51.9 us (level)
  no operation moved by 1% of the time
where the time goes in v17:
time: 51.9 us; the launch traced here: 51.7 us
  blocking collectives  21.2 us (41%)
  Pallas kernels  19.7 us (38%)
  starting transfers between devices  10 us (19%)
  between operations  0.73 us (1%)
    all_to_all x1, blocking collectives, body(): got = lax.all_to_all(chunk, AXES, 0, 0, tiled=True)  12.2 us
    all_to_all x1, blocking collectives, body(): sums = lax.all_to_all(line, AXES[::-1], 0, 0, tiled=True)  9.06 us
    ppermute x2, starting transfers between devices, exchange(): got_a = lax.ppermute(send_a, axis, pairs(0))  8.71 us
    pallas_call x1, Pallas kernels, first(): pl.pallas_call(functools.partial(first_kernel, tiles, down), in_specs=[SM...  5.72 us
    pallas_call x1, Pallas kernels, second(): pl.pallas_call(functools.partial(second_kernel, tiles, down), in_specs=[S...  5.13 us
    pallas_call x1, Pallas kernels, inner(): pl.pallas_call(inner_kernel, in_specs=[SMEM] + [VMEM] * 2, out_specs=[VME...  2.74 us
    pallas_call x1, Pallas kernels, pack(): pl.pallas_call(functools.partial(pack_kernel, tiles, down), in_specs=[HBM...  2.6 us
    pallas_call x1, Pallas kernels, edge(): pl.pallas_call(functools.partial(edge_kernel, tiles, down), in_specs=[HBM...  1.73 us
  transfers between devices with their start and end apart: 4, of which 0 were waited for; matrix products, arithmetic and copies ran while one was open for 0% of the time, Pallas kernels for 10%

profile of v17, /device:TPU:0, one launch (start us, length us, event | category | flops | bytes accessed | tf_op | source)
XLA Modules:
  0.0 51.7 jit_solution(3496944632117313635)
XLA Ops:
  0.6 1.7 %pack_east_west.1 = (f32[40,128]{1,0:T(8,128)S(1)}, f32[40,128]{1,0:T(8,128)S(1)}) custom-call(f32[256,1024]{1,0:T(8,128)} %refs_0_.3, s32[256,1024]{1,0:T(8,128)} %refs_1_.3, f32[4]{0:T(128)} %refs_2_.3, f32[3,3]{1,0:T(4,128)} %taps.5), custom_call_target="tpu_custom_call" | custom-call | tf_op jit(solution)/shard_map/pack_east_west/pallas_call | solution.py:452
  2.4 0.7 %collective-permute-start = (f32[40,128]{1,0:T(8,128)S(1)}, f32[40,128]{1,0:T(8,128)S(1)}, u32[]{:S(2)}, u32[]{:S(2)}) collective-permute-start(f32[40,128]{1,0:T(8,128)S(1)} %get-tuple-element.32), channel_id=1, source_target_pairs={{4,8},{8,4},{12,16},{16,12},{20,24},{24,20},{5,9},{9,5},{13,17},{1... | collective-permute-start | bytes 61448 | tf_op jit(solution)/shard_map/ppermute | solution.py:1035
  3.0 5.8 %collective-permute-start.1 = (f32[40,128]{1,0:T(8,128)S(1)}, f32[40,128]{1,0:T(8,128)S(1)}, u32[]{:S(2)}, u32[]{:S(2)}) collective-permute-start(f32[40,128]{1,0:T(8,128)S(1)} %get-tuple-element.33.refs_4_), channel_id=1, source_target_pairs={{0,4},{4,0},{8,12},{12,8},{16,20},{20,16},{24,28},{28,24},{1,5},{5... | collective-permute-start | bytes 61448 | tf_op jit(solution)/shard_map/ppermute | solution.py:1036
  8.8 2.6 %pack_all.1 = (f32[9,288,128]{2,1,0:T(8,128)S(1)}, f32[9,288,128]{2,1,0:T(8,128)S(1)}, f32[4,48,256]{2,1,0:T(8,128)S(1)}) custom-call(f32[256,1024]{1,0:T(8,128)} %refs_0_.3, s32[256,1024]{1,0:T(8,128)} %refs_1_.3, f32[4]{0:T(128)} %refs_2_.3, f32[3,3]{1,0:T(4,128)} %taps.5, f32[40,128]{1,0:T(8,128)S(1)} %get-tuple-element.33.refs_4_), custom_call_target="tpu_custom_call" | custom-call | flops 5242880 | bytes 4194304 | tf_op jit(solution)/shard_map/pack_all/pallas_call | solution.py:484
  11.4 0.0 collective-permute-done.got_b
  11.5 0.0 collective-permute-done.1.got_a
  11.5 0.0 copy-start
  11.5 0.3 pack_north_south.1
  11.8 0.7 %collective-permute-start.2 = (f32[128,128]{1,0:T(8,128)S(1)}, f32[128,128]{1,0:T(8,128)S(1)}, u32[]{:S(2)}, u32[]{:S(2)}) collective-permute-start(f32[128,128]{1,0:T(8,128)S(1)} %get-tuple-element.44), channel_id=1, source_target_pairs={{1,2},{2,1},{5,6},{6,5},{9,10},{10,9},{13,14},{14,13},{17,18},{18,... | collective-permute-start | bytes 196616 | tf_op jit(solution)/shard_map/ppermute | solution.py:1035
  12.4 2.9 %collective-permute-start.3 = (f32[128,128]{1,0:T(8,128)S(1)}, f32[128,128]{1,0:T(8,128)S(1)}, u32[]{:S(2)}, u32[]{:S(2)}) collective-permute-start(f32[128,128]{1,0:T(8,128)S(1)} %get-tuple-element.45), channel_id=1, source_target_pairs={{0,1},{1,0},{2,3},{3,2},{4,5},{5,4},{6,7},{7,6},{8,9},{9,8},{10,11... | collective-permute-start | bytes 196616 | tf_op jit(solution)/shard_map/ppermute | solution.py:1036
  15.3 0.0 copy-done
  15.3 2.7 %inner_strips.1 = (f32[9,288,128]{2,1,0:T(8,128)S(1)}, f32[9,288,128]{2,1,0:T(8,128)S(1)}, f32[9,288,128]{2,1,0:T(8,128)S(1)}, f32[9,288,128]{2,1,0:T(8,128)S(1)...) custom-call(f32[3,3]{1,0:T(4,128)S(1)} %copy-done, ...), custom_call_target="tpu_custom_call" | custom-call | flops 14929920 | bytes 7962624 | tf_op jit(solution)/shard_map/inner_strips/pallas_call | solution.py:646
  18.1 0.0 collective-permute-done.2.got_b
  18.1 0.0 collective-permute-done.3.got_a
  18.1 5.7 %first_direction.1 = (f32[9,288,128]{2,1,0:T(8,128)S(1)}, f32[9,288,128]{2,1,0:T(8,128)S(1)}, f32[9,288,128]{2,1,0:T(8,128)S(1)}, f32[9,288,128]{2,1,0:T(8,128)S...) custom-call(f32[3,3]{1,0:T(4,128)S(1)} %copy-done, ...), custom_call_target="tpu_custom_call", output_to_operand_aliasing={{0}: (1, {}), {1}: (2, {}), {2}: (3, {}), {3}: (4, {}), {4}... | custom-call | tf_op jit(solution)/shard_map/first_direction/pallas_call | solution.py:844
  23.8 12.2 %all_to_all.10.got_ref = f32[288,1,128]{2,1,0:T(1,128)S(1)} all-to-all(f32[288,1,128]{2,1,0:T(1,128)S(1)} %get-tuple-element.49), channel_id=1, replica_groups=mesh['cols'=8,'rows'=4] {'cols','rows'}, dimensions={0} | all-to-all | bytes 294912 | tf_op jit(solution)/shard_map/all_to_all | solution.py:1052
  36.0 5.1 %second_direction.1 = (f32[9,288,128]{2,1,0:T(8,128)S(1)}, f32[9,288,128]{2,1,0:T(8,128)S(1)}, f32[32,1,128]{2,1,0:T(1,128)S(1)}, f32[2,8,128]{2,1,0:T(8,128)S(1)}) custom-call(f32[3,3]{1,0:T(4,128)S(1)} %copy-done, f32[288,1,128]{2,1,0:T(1,128)S(1)} %all_to_all.10.got_ref, f32[32,128]{1,0:T(8,128)S(1)} %get-tuple-element.50.own_ref, ...), custom_call_target="tpu_custom_call" | custom-call | tf_op jit(solution)/shard_map/second_direction/pallas_call | solution.py:954
  41.1 9.1 %all_to_all.11.sums_ref = f32[32,1,128]{2,1,0:T(1,128)S(1)} all-to-all(f32[32,1,128]{2,1,0:T(1,128)S(1)} %get-tuple-element.57), channel_id=1, replica_groups=mesh['cols'=8,'rows'=4] {'rows','cols'}, dimensions={0} | all-to-all | bytes 32768 | tf_op jit(solution)/shard_map/all_to_all | solution.py:1054
  50.2 1.5 %combine.1 = (f32[256,1024]{1,0:T(8,128)}, f32[256,1024]{1,0:T(8,128)}) custom-call(f32[32,1,128]{2,1,0:T(1,128)S(1)} %all_to_all.11.sums_ref, f32[2,8,128]{2,1,0:T(8,128)S(1)} %get-tuple-element.58.known_ref, f32[9,288,128]{2,1,0:T(8,128)S(1)} %get-tuple-element.59.p_ref, f32[9,288,128]{2,1,0:T(8,128)S(1)} %get-tuple-element.60.w_ref, ...), custom_call_target="tpu_custom_call" | custom-call | tf_op jit(solution)/shard_map/combine/pallas_call | solution.py:1012
Async XLA Ops:
  2.4 9.1 %collective-permute-start = (f32[40,128]{1,0:T(8,128)S(1)}, f32[40,128]{1,0:T(8,128)S(1)}, u32[]{:S(2)}, u32[]{:S(2)}) collective-permute-start(f32[40,128]{1,0:T(8,128)S(1)} %get-tuple-element.32), channel_id=1, source_target_pairs={{4,8},{8,4},{12,16},{16,12},{20,24},{24,20},{5,9},{9,5},{13,17},{1... | collective-permute-start | bytes 61448 | tf_op jit(solution)/shard_map/ppermute | solution.py:1035
  3.0 8.4 %collective-permute-start.1 = (f32[40,128]{1,0:T(8,128)S(1)}, f32[40,128]{1,0:T(8,128)S(1)}, u32[]{:S(2)}, u32[]{:S(2)}) collective-permute-start(f32[40,128]{1,0:T(8,128)S(1)} %get-tuple-element.33.refs_4_), channel_id=1, source_target_pairs={{0,4},{4,0},{8,12},{12,8},{16,20},{20,16},{24,28},{28,24},{1,5},{5... | collective-permute-start | bytes 61448 | tf_op jit(solution)/shard_map/ppermute | solution.py:1036
  11.5 3.9 %copy-start = (f32[3,3]{1,0:T(4,128)S(1)}, f32[3,3]{1,0:T(4,128)}, u32[]{:S(2)}) copy-start(f32[3,3]{1,0:T(4,128)} %taps.5) | copy-start | bytes 112
  11.8 6.3 %collective-permute-start.2 = (f32[128,128]{1,0:T(8,128)S(1)}, f32[128,128]{1,0:T(8,128)S(1)}, u32[]{:S(2)}, u32[]{:S(2)}) collective-permute-start(f32[128,128]{1,0:T(8,128)S(1)} %get-tuple-element.44), channel_id=1, source_target_pairs={{1,2},{2,1},{5,6},{6,5},{9,10},{10,9},{13,14},{14,13},{17,18},{18,... | collective-permute-start | bytes 196616 | tf_op jit(solution)/shard_map/ppermute | solution.py:1035
  12.4 5.7 %collective-permute-start.3 = (f32[128,128]{1,0:T(8,128)S(1)}, f32[128,128]{1,0:T(8,128)S(1)}, u32[]{:S(2)}, u32[]{:S(2)}) collective-permute-start(f32[128,128]{1,0:T(8,128)S(1)} %get-tuple-element.45), channel_id=1, source_target_pairs={{0,1},{1,0},{2,3},{3,2},{4,5},{5,4},{6,7},{7,6},{8,9},{9,8},{10,11... | collective-permute-start | bytes 196616 | tf_op jit(solution)/shard_map/ppermute | solution.py:1036
